TPU v7x, 512 devices: a whole 4x4x16 slice. The times are simulated.
512 devices in a mesh: dp: 4 (over x), expert: 128 (over y, z, core).
Axes of the slice: x: 4, y: 4, z: 16, core: 2. Of those that a mesh axis runs over, the one named last changes fastest.
Arguments:
- grad_out: bfloat16 [8192, 2048], P(('dp', 'expert')), may hold values from -4 to 4
- x_codes: bfloat16 [8192, 2048], P(('dp', 'expert')), may hold values from -6 to 6
- x_scales: bfloat16 [8192, 16], P(('dp', 'expert')), may hold values from 0.25 to 4
- combine: bfloat16 [8192, 8], P(('dp', 'expert')), may hold values from 0.049804688 to 1
- expert_ids: int32 [8192, 8], P(('dp', 'expert')), may hold values from 0 to 127, all different within a row; in each aligned block of 16 rows (0 to 15, 16 to 31, ...) at most 2 rows name the same one
- w_gate: bfloat16 [128, 768, 2048], P('expert', 'dp'), may hold values from -0.125 to 0.125
- w_up: bfloat16 [128, 768, 2048], P('expert', 'dp'), may hold values from -0.125 to 0.125
- w_down: bfloat16 [128, 768, 2048], P('expert', 'dp'), may hold values from -0.21875 to 0.21875
Outputs:
- grad_in: bfloat16 [8192, 2048], P(('dp', 'expert'))
- grad_combine: float32 [8192, 8], P(('dp', 'expert'))
- grad_gate: bfloat16 [128, 768, 2048], P('expert', 'dp')
- grad_up: bfloat16 [128, 768, 2048], P('expert', 'dp')
- grad_down: bfloat16 [128, 768, 2048], P('expert', 'dp')
Inputs may be any that keep to these rules, and one draw needn't show every extreme that they name: `expert_ids`: each token names 8 different experts. Among the 16 tokens of one device no expert is named more than 2 times, and on some devices some expert is named exactly 2 times.
All inputs are finite; a program needn't handle non-finite values.
Results may differ from a plain program's by a relative error of at most 0.015.
Values may be sent and summed in bfloat16 or wider, within the bound.
No kernel may reach another device: no remote copies, remote signals or barrier semaphores. Data moves between devices by JAX's collectives and lax.ppermute only.
A program may use at most 128 MiB of HBM per device.

v0:
```python
import jax
import jax.numpy as jnp
from jax import lax
from jax.sharding import PartitionSpec as P

BLOCK = 128


def slot_table(flat_ids, experts, capacity):
    onehot = (flat_ids[:, None] == jnp.arange(experts, dtype=jnp.int32)[None, :]).astype(jnp.int32)
    before = jnp.cumsum(onehot, axis=0) - onehot
    position = jnp.sum(before * onehot, axis=1)
    slot_index = flat_ids * capacity + position
    return jnp.arange(experts * capacity, dtype=jnp.int32)[:, None] == slot_index[None, :]


def token_owner(placed, tokens, picks):
    return jnp.sum(placed.reshape(placed.shape[0], tokens, picks).astype(jnp.int32), axis=2)


def build_rows(grad_out, x_codes, x_scales, combine, expert_ids, experts, capacity):
    tokens, picks = expert_ids.shape
    placed = slot_table(expert_ids.reshape(-1), experts, capacity)
    owner = token_owner(placed, tokens, picks).astype(jnp.bfloat16)
    grad_rows = jnp.dot(owner, grad_out, preferred_element_type=jnp.float32).astype(jnp.bfloat16)
    code_rows = jnp.dot(owner, x_codes, preferred_element_type=jnp.float32).astype(jnp.bfloat16)
    scale_rows = jnp.dot(owner, x_scales, preferred_element_type=jnp.float32).astype(jnp.bfloat16)
    weight_rows = jnp.dot(
        placed.astype(jnp.bfloat16), combine.reshape(-1), preferred_element_type=jnp.float32
    ).astype(jnp.bfloat16)
    return (
        grad_rows.reshape(experts, capacity, -1),
        code_rows.reshape(experts, capacity, -1),
        scale_rows.reshape(experts, capacity, -1),
        weight_rows.reshape(experts, capacity),
    )


def body(grad_out, x_codes, x_scales, combine, expert_ids, w_gate, w_up, w_down):
    tokens, picks = expert_ids.shape
    width = grad_out.shape[1]
    groups = lax.axis_size("dp")
    experts = w_gate.shape[0] * lax.axis_size("expert")
    capacity = min(tokens, max(2, 2 * tokens * picks // experts))
    grad_rows, code_rows, scale_rows, weight_rows = build_rows(
        grad_out, x_codes, x_scales, combine, expert_ids, experts, capacity
    )
    grad_rows, code_rows, scale_rows, weight_rows = (
        lax.all_to_all(grad_rows, "expert", split_axis=0, concat_axis=0, tiled=True),
        lax.all_to_all(code_rows, "expert", split_axis=0, concat_axis=0, tiled=True),
        lax.all_to_all(scale_rows, "expert", split_axis=0, concat_axis=0, tiled=True),
        lax.all_to_all(weight_rows, "expert", split_axis=0, concat_axis=0, tiled=True),
    )
    grad_rows, code_rows, scale_rows, weight_rows = (
        lax.all_gather(grad_rows[None], "dp", axis=0, tiled=True),
        lax.all_gather(code_rows[None], "dp", axis=0, tiled=True),
        lax.all_gather(scale_rows[None], "dp", axis=0, tiled=True),
        lax.all_gather(weight_rows[None], "dp", axis=0, tiled=True),
    )
    rows = groups * experts * capacity
    scale_count = width // BLOCK
    grad_flat = grad_rows.reshape(rows, width)
    x_rows = (
        (
            code_rows.reshape(rows, scale_count, BLOCK).astype(jnp.float32)
            * scale_rows.reshape(rows, scale_count, 1).astype(jnp.float32)
        )
        .reshape(rows, width)
        .astype(jnp.bfloat16)
    )
    weight_flat = weight_rows.reshape(rows).astype(jnp.float32)
    share = w_gate.shape[1]
    stacked_w = jnp.concatenate([w_gate[0], w_up[0]], axis=0)
    down_w = w_down[0]
    both_pre = lax.dot_general(
        x_rows, stacked_w, (((1,), (1,)), ((), ())), preferred_element_type=jnp.float32
    )
    gate_pre = both_pre[:, :share]
    up_pre = both_pre[:, share:]
    sigmoid_gate = jax.nn.sigmoid(gate_pre)
    activated = gate_pre * sigmoid_gate
    hidden = (activated * up_pre).astype(jnp.bfloat16)
    scaled = (weight_flat[:, None] * grad_flat.astype(jnp.float32)).astype(jnp.bfloat16)
    backward = lax.dot_general(
        grad_flat, down_w, (((1,), (1,)), ((), ())), preferred_element_type=jnp.float32
    )
    partial_comb = jnp.sum(backward * hidden.astype(jnp.float32), axis=1)
    grad_hidden = weight_flat[:, None] * backward
    grad_gate_pre = (
        grad_hidden * up_pre * sigmoid_gate * (1.0 + gate_pre * (1.0 - sigmoid_gate))
    ).astype(jnp.bfloat16)
    grad_up_pre = (grad_hidden * activated).astype(jnp.bfloat16)
    grad_both_pre = jnp.concatenate([grad_gate_pre, grad_up_pre], axis=1)
    grad_down = lax.dot_general(
        hidden, scaled, (((0,), (0,)), ((), ())), preferred_element_type=jnp.float32
    ).astype(jnp.bfloat16)
    grad_stacked = lax.dot_general(
        grad_both_pre, x_rows, (((0,), (0,)), ((), ())), preferred_element_type=jnp.float32
    ).astype(jnp.bfloat16)
    grad_gate = grad_stacked[:share]
    grad_up = grad_stacked[share:]
    input_part = jnp.dot(grad_both_pre, stacked_w, preferred_element_type=jnp.float32)
    summed = lax.psum_scatter(
        input_part.reshape(groups, experts, capacity, width).astype(jnp.bfloat16),
        "dp",
        scatter_dimension=0,
        tiled=True,
    ).astype(jnp.float32)
    comb_all = lax.psum(partial_comb, "dp")
    own_terms = lax.dynamic_slice_in_dim(
        comb_all, lax.axis_index("dp") * (experts * capacity), experts * capacity
    )
    back_grad, back_comb = (
        lax.all_to_all(
            summed.reshape(experts, capacity, width).astype(jnp.bfloat16),
            "expert",
            split_axis=0,
            concat_axis=0,
            tiled=True,
        ).astype(jnp.float32),
        lax.all_to_all(
            own_terms.reshape(experts, capacity).astype(jnp.bfloat16),
            "expert",
            split_axis=0,
            concat_axis=0,
            tiled=True,
        ).astype(jnp.float32),
    )
    placed = slot_table(expert_ids.reshape(-1), experts, capacity)
    owner = token_owner(placed, tokens, picks).astype(jnp.float32)
    grad_in = lax.dot_general(
        owner,
        back_grad.reshape(experts * capacity, width),
        (((0,), (0,)), ((), ())),
        precision=lax.Precision.HIGHEST,
    ).astype(jnp.bfloat16)
    grad_combine = lax.dot_general(
        placed.astype(jnp.float32),
        back_comb.reshape(experts * capacity),
        (((0,), (0,)), ((), ())),
        precision=lax.Precision.HIGHEST,
    ).reshape(tokens, picks)
    return (grad_in, grad_combine, grad_gate[None], grad_up[None], grad_down[None])


def solution(mesh):
    in_specs = (
        P(("dp", "expert"), None),
        P(("dp", "expert"), None),
        P(("dp", "expert"), None),
        P(("dp", "expert"), None),
        P(("dp", "expert"), None),
        P("expert", "dp", None),
        P("expert", "dp", None),
        P("expert", "dp", None),
    )
    out_specs = (
        P(("dp", "expert"), None),
        P(("dp", "expert"), None),
        P("expert", "dp", None),
        P("expert", "dp", None),
        P("expert", "dp", None),
    )
    return jax.shard_map(body, mesh=mesh, in_specs=in_specs, out_specs=out_specs, check_vma=False)
```

profile of v0, /device:TPU:6, one launch (start us, length us, event | category | flops | bytes accessed | tf_op | source)
XLA Modules:
  0.0 397.3 jit_solution(18235403229023424888)
XLA Ops:
  7.2 0.8 copy.52
  8.2 0.2 reduce_window_sum.12
  8.4 0.2 select_reduce_fusion
  8.8 1.3 convolution_convert_fusion.2
  10.1 0.7 reshape.130
  10.8 75.5 %all_to_all.36 = bf16[128,2,2048]{2,1,0:T(2,128)(2,1)} all-to-all(bf16[128,2,2048]{2,1,0:T(2,128)(2,1)S(1)} %reshape.130), channel_id=1, replica_groups=mesh['dp'=4,'expert'=128] {'expert'}, dimensions={0} | all-to-all | bytes 2097152 | tf_op jit(solution)/shard_map/all_to_all | solution.py:50
  86.4 0.4 convolution_convert_fusion.3
  86.9 0.7 reshape.128
  87.6 62.7 %all_to_all.37 = bf16[128,2,2048]{2,1,0:T(2,128)(2,1)} all-to-all(bf16[128,2,2048]{2,1,0:T(2,128)(2,1)S(1)} %reshape.128), channel_id=1, replica_groups=mesh['dp'=4,'expert'=128] {'expert'}, dimensions={0} | all-to-all | bytes 2097152 | tf_op jit(solution)/shard_map/all_to_all | solution.py:49
  150.8 0.8 all_to_all.29
  151.6 7.2 %all-to-all-start = ((bf16[128,1,2]{2,1,0:T(2,128)(2,1)}), bf16[128,1,2]{2,1,0:T(2,128)(2,1)S(1)}, u32[]{:S(2)}, u32[]{:S(2)}) async-start(bf16[128,1,2]{2,1,0:T(2,128)(2,1)} %all_to_all.29), calls=%async_computation | async-start | bytes 131072 | tf_op jit(solution)/shard_map/all_to_all | solution.py:52
  158.8 0.2 convolution_convert_fusion.5
  159.0 0.7 copy.58
  159.7 14.5 %all-to-all-done = bf16[128,1,2]{2,1,0:T(2,128)(2,1)S(1)} async-done(((bf16[128,1,2]{2,1,0:T(2,128)(2,1)}), bf16[128,1,2]{2,1,0:T(2,128)(2,1)S(1)}, u32[]{:S(2)}, u32[]{:S(2)}) %all-to-all-start) | async-done | bytes 544 | tf_op jit(solution)/shard_map/all_to_all | solution.py:52
  174.2 6.1 %all-to-all-start.3 = ((bf16[128,2,16]{2,1,0:T(2,128)(2,1)}), bf16[128,2,16]{2,1,0:T(2,128)(2,1)S(1)}, u32[]{:S(2)}, u32[]{:S(2)}) async-start(bf16[128,2,16]{2,1,0:T(2,128)(2,1)} %bitcast.2), calls=%async_computation.3 | async-start | bytes 131072 | tf_op jit(solution)/shard_map/all_to_all | solution.py:51
  180.5 6.7 %all-gather = bf16[512,1,2]{0,2,1:T(2,128)(2,1)S(1)} all-gather(bf16[128,1,2]{0,2,1:T(2,128)(2,1)S(1)} %copy.56), channel_id=2, replica_groups=mesh['dp'=4,'expert'=128] {'dp'}, dimensions={0}, use_global_device_ids=true | all-gather | bytes 2560 | tf_op jit(solution)/shard_map/all_gather | solution.py:58
  187.2 0.2 copy.57
  187.4 0.2 reshape.134
  187.5 8.3 %all-to-all-done.3 = bf16[128,2,16]{2,1,0:T(2,128)(2,1)S(1)} async-done(((bf16[128,2,16]{2,1,0:T(2,128)(2,1)}), bf16[128,2,16]{2,1,0:T(2,128)(2,1)S(1)}, u32[]{:S(2)}, u32[]{:S(2)}) %all-to-all-start.3) | async-done | bytes 8224 | tf_op jit(solution)/shard_map/all_to_all | solution.py:51
  195.9 10.2 %all-gather.3 = bf16[512,2,16]{0,2,1:T(8,128)(2,1)S(1)} all-gather(bf16[128,2,16]{0,2,1:T(8,128)(2,1)S(1)} %copy.59), channel_id=5, replica_groups=mesh['dp'=4,'expert'=128] {'dp'}, dimensions={0}, use_global_device_ids=true | all-gather | bytes 40960 | tf_op jit(solution)/shard_map/all_gather | solution.py:57
  206.2 0.2 copy.60
  206.4 7.6 %reshape.135 = f32[1024,2048]{1,0:T(8,128)} reshape(bf16[512,2,2048]{2,1,0:T(2,128)(2,1)} %all-gather.9.cloned.1.call-done) | data formatting | bytes 12582912 | tf_op jit(solution)/shard_map/convert_element_type | solution.py:65
  214.0 6.0 %mul.74 = f32[1024,16,128]{2,1,0:T(8,128)} broadcast(f32[1024,16]{1,0:T(8,128)S(1)} %bitcast.39), dimensions={0,1} | broadcast | bytes 8454144 | tf_op jit(solution)/shard_map/mul | solution.py:65
  219.9 8.6 %fusion = bf16[1024,2048]{1,0:T(8,128)(2,1)S(1)} fusion(f32[1024,2048]{1,0:T(8,128)} %reshape.135, f32[128,8,16,128]{3,2,1,0:T(8,128)} %bitcast.38), kind=kLoop, calls=%fused_computation.1 | loop fusion | flops 4194304 | bytes 20971520 | tf_op jit(solution)/shard_map/convert_element_type | solution.py:69
  228.5 1.9 copy-done.2
  230.5 4.1 %fusion.5 = f32[1024,384]{0,1:T(8,128)} fusion(bf16[1024,2048]{1,0:T(8,128)(2,1)S(1)} %fusion, bf16[192,2048]{1,0:T(8,128)(2,1)S(1)} %bitcast.42, bf16[192,2048]{1,0:T(8,128)(2,1)} %bitcast.44), kind=kOutput, calls=%fused_computation.14 | convolution fusion | flops 1613758464 | bytes 7340032 | tf_op jit(solution)/shard_map/dot_general | solution.py:75
  234.6 7.3 %reshape.129 = bf16[1024,2048]{1,0:T(8,128)(2,1)} reshape(bf16[512,2,2048]{2,1,0:T(2,128)(2,1)} %all-gather.7.cloned.1.call-done) | data formatting | bytes 8388608 | tf_op jit(solution)/shard_map/reshape | solution.py:62
  241.9 4.5 %multiply_reduce_fusion = (f32[1024]{0:T(1024)S(1)}, bf16[1024,192]{0,1:T(8,128)(2,1)S(1)}, bf16[1024,192]{0,1:T(8,128)(2,1)S(1)}, bf16[1024,192]{0,1:T(8,128)(2,1)S(1)}) fusion(f32[1024,384]{0,1:T(8,128)} %fusion.5, f32[1024]{0:T(1024)S(1)} %reshape.134, bf16[1024,2048]{1,0:T(8,128)(2,1)} %reshape.129, bf16[1,192,2048]{2,1,0:T(8,128)(2,1)S(1)} %copy-done), kind=kOutput, calls=%fused_computation.20 | convolution fusion | flops 809040896 | bytes 7741440 | tf_op jit(solution)/shard_map/dot_general | solution.py:84
  246.4 0.7 copy-done.9
  247.3 4.3 %convolution_convert_fusion = bf16[1024,2048]{1,0:T(8,128)(2,1)} fusion(bf16[192,2048]{1,0:T(8,128)(2,1)S(1)} %bitcast.43, bf16[192,2048]{1,0:T(8,128)(2,1)S(1)} %bitcast.45, bf16[1024,192]{0,1:T(8,128)(2,1)S(1)} %get-tuple-element.9, bf16[1024,192]{0,1:T(8,128)(2,1)S(1)} %get-tuple-element.10), kind=kOutput, calls=%fused_computation.5 | convolution fusion | flops 1617428480 | bytes 6553600 | tf_op jit(solution)/shard_map/dot_general | solution.py:102
  251.6 7.7 %convert_element_type.130 = bf16[4,128,2,2048]{3,2,1,0:T(2,128)(2,1)} reshape(bf16[1024,2048]{1,0:T(8,128)(2,1)} %convolution_convert_fusion) | data formatting | bytes 8388608 | tf_op jit(solution)/shard_map/convert_element_type | solution.py:104
  259.2 6.0 %copy.61 = bf16[4,128,2,2048]{3,1,2,0:T(8,128)(2,1)} copy(bf16[4,128,2,2048]{3,2,1,0:T(2,128)(2,1)} %convert_element_type.130) | data formatting | bytes 8388608 | tf_op jit(solution)/shard_map/convert_element_type | solution.py:104
  265.2 8.0 %psum.7 = bf16[1024]{0:T(1024)(128)(2,1)S(1)} all-reduce(f32[1024]{0:T(1024)S(1)} %get-tuple-element.5), channel_id=1, replica_groups=mesh['dp'=4,'expert'=128] {'dp'}, use_global_device_ids=true, to_apply=%region_5.6 | all-reduce | flops 1024 | bytes 6144 | tf_op jit(solution)/shard_map/psum | solution.py:109
  273.3 0.8 convert_element_type.147
  274.1 10.6 %all-to-all-start.5 = ((bf16[128,1,2]{2,1,0:T(2,128)(2,1)}), bf16[128,1,2]{2,1,0:T(2,128)(2,1)S(1)}, u32[]{:S(2)}, u32[]{:S(2)}) async-start(bf16[128,1,2]{2,1,0:T(2,128)(2,1)} %convert_element_type.147), calls=%async_computation.6 | async-start | bytes 131072 | tf_op jit(solution)/shard_map/all_to_all | solution.py:121
  284.7 28.4 %reduce-scatter.2.cloned.1.call-done = bf16[1,128,2,2048]{3,1,2,0:T(8,128)(2,1)} async-done(((bf16[4,128,2,2048]{3,1,2,0:T(8,128)(2,1)}), bf16[1,128,2,2048]{3,1,2,0:T(8,128)(2,1)}) %reduce-scatter.2.cloned.1.call-update) | async-done | bytes 1048592 | tf_op jit(solution)/shard_map/reduce_scatter | solution.py:103
  313.1 3.4 copy.62
  316.5 17.0 %all-to-all-start.4 = ((bf16[128,2,2048]{2,1,0:T(2,128)(2,1)}), bf16[128,2,2048]{2,1,0:T(2,128)(2,1)S(1)}, u32[]{:S(2)}, u32[]{:S(2)}) async-start(bf16[128,2,2048]{2,1,0:T(2,128)(2,1)} %copy.62), calls=%async_computation.5 | async-start | bytes 2097152 | tf_op jit(solution)/shard_map/all_to_all | solution.py:114
  333.5 4.3 %fusion.4 = bf16[1,192,2048]{2,1,0:T(8,128)(2,1)} fusion(bf16[1024,192]{0,1:T(8,128)(2,1)S(1)} %get-tuple-element.6, bf16[1024,2048]{1,0:T(8,128)(2,1)} %reshape.129, f32[1024]{0:T(1024)S(1)} %reshape.134), kind=kOutput, calls=%fused_computation.10 | convolution fusion | flops 811991040 | bytes 5378048 | tf_op jit(solution)/shard_map/dot_general | solution.py:94
  337.9 1.8 convolution_convert_fusion.1
  339.7 1.2 slice_bitcast_fusion
  341.0 0.2 reduce
  341.1 0.1 reshape.150
  341.3 0.3 fusion.11
  341.6 0.7 copy.64
  342.3 46.9 %all-to-all-done.4 = bf16[128,2,2048]{2,1,0:T(2,128)(2,1)S(1)} async-done(((bf16[128,2,2048]{2,1,0:T(2,128)(2,1)}), bf16[128,2,2048]{2,1,0:T(2,128)(2,1)S(1)}, u32[]{:S(2)}, u32[]{:S(2)}) %all-to-all-start.4) | async-done | bytes 1048608 | tf_op jit(solution)/shard_map/all_to_all | solution.py:114
  389.2 0.4 reshape.132
  389.6 1.2 convolution_convert_fusion.4
  (46 shorter events, 1.3 us)
Async XLA Ops:
  7.2 234.7 %copy-start = (bf16[1,192,2048]{2,1,0:T(8,128)(2,1)S(1)}, bf16[1,192,2048]{2,1,0:T(8,128)(2,1)}, u32[]{:S(2)}) copy-start(bf16[1,192,2048]{2,1,0:T(8,128)(2,1)} %param.15) | copy-start | bytes 2359300
  7.2 79.3 %copy-start.4 = (bf16[16,2048]{1,0:T(8,128)(2,1)S(1)}, bf16[16,2048]{1,0:T(8,128)(2,1)}, u32[]{:S(2)}) copy-start(bf16[16,2048]{1,0:T(8,128)(2,1)} %param.8) | copy-start | bytes 196612
  7.2 199.2 %all-gather.9.cloned.1.call-start = ((), (), s32[]{:S(2)}) async-start(), calls=%async_computation.9 | async-start | bytes 5242880 | tf_op jit(solution)/shard_map/all_gather | solution.py:56
  86.4 64.0 %copy-start.5 = (bf16[16,8]{0,1:T(8,128)(2,1)S(1)}, bf16[16,8]{0,1:T(8,128)(2,1)}, u32[]{:S(2)}) copy-start(bf16[16,8]{0,1:T(8,128)(2,1)} %param.11) | copy-start | bytes 772
  86.4 72.4 %copy-start.8 = (bf16[16,16]{1,0:T(8,128)(2,1)S(1)}, bf16[16,16]{1,0:T(8,128)(2,1)}, u32[]{:S(2)}) copy-start(bf16[16,16]{1,0:T(8,128)(2,1)} %param.10) | copy-start | bytes 1540
  86.4 148.2 %all-gather.7.cloned.1.call-start = ((), (), s32[]{:S(2)}) async-start(), calls=%async_computation.8 | async-start | bytes 5242880 | tf_op jit(solution)/shard_map/all_gather | solution.py:55
  151.6 22.7 %all-to-all-start = ((bf16[128,1,2]{2,1,0:T(2,128)(2,1)}), bf16[128,1,2]{2,1,0:T(2,128)(2,1)S(1)}, u32[]{:S(2)}, u32[]{:S(2)}) async-start(bf16[128,1,2]{2,1,0:T(2,128)(2,1)} %all_to_all.29), calls=%async_computation | async-start | bytes 131072 | tf_op jit(solution)/shard_map/all_to_all | solution.py:52
  174.2 21.6 %all-to-all-start.3 = ((bf16[128,2,16]{2,1,0:T(2,128)(2,1)}), bf16[128,2,16]{2,1,0:T(2,128)(2,1)S(1)}, u32[]{:S(2)}, u32[]{:S(2)}) async-start(bf16[128,2,16]{2,1,0:T(2,128)(2,1)} %bitcast.2), calls=%async_computation.3 | async-start | bytes 131072 | tf_op jit(solution)/shard_map/all_to_all | solution.py:51
  180.4 132.7 %reduce-scatter.2.cloned.1.call-start = ((), (), s32[]{:S(2)}) async-start(), calls=%async_computation.7 | async-start | bytes 5242880 | tf_op jit(solution)/shard_map/reduce_scatter | solution.py:103
  219.9 10.5 %copy-start.6 = (bf16[1,192,2048]{2,1,0:T(8,128)(2,1)S(1)}, bf16[1,192,2048]{2,1,0:T(8,128)(2,1)}, u32[]{:S(2)}) copy-start(bf16[1,192,2048]{2,1,0:T(8,128)(2,1)} %param.14) | copy-start | bytes 2359300
  228.5 2.0 copy-start.2
  241.9 5.4 %copy-start.7 = (bf16[1,192,2048]{2,1,0:T(8,128)(2,1)S(1)}, bf16[1,192,2048]{2,1,0:T(8,128)(2,1)}, u32[]{:S(2)}) copy-start(bf16[1,192,2048]{2,1,0:T(8,128)(2,1)} %param.13) | copy-start | bytes 2359300
  246.4 0.7 copy-start.9
  246.4 0.9 copy-start.11
  274.1 42.4 %all-to-all-start.5 = ((bf16[128,1,2]{2,1,0:T(2,128)(2,1)}), bf16[128,1,2]{2,1,0:T(2,128)(2,1)S(1)}, u32[]{:S(2)}, u32[]{:S(2)}) async-start(bf16[128,1,2]{2,1,0:T(2,128)(2,1)} %convert_element_type.147), calls=%async_computation.6 | async-start | bytes 131072 | tf_op jit(solution)/shard_map/all_to_all | solution.py:121
  316.5 21.4 %copy-start.10 = (bf16[1024,192]{0,1:T(8,128)(2,1)S(1)}, bf16[1024,192]{0,1:T(8,128)(2,1)}, u32[]{:S(2)}) copy-start(bf16[1024,192]{0,1:T(8,128)(2,1)} %copy-done.9) | copy-start | bytes 1179652
  316.5 21.4 %copy-start.12 = (bf16[1024,192]{0,1:T(8,128)(2,1)S(1)}, bf16[1024,192]{0,1:T(8,128)(2,1)}, u32[]{:S(2)}) copy-start(bf16[1024,192]{0,1:T(8,128)(2,1)} %copy-done.11) | copy-start | bytes 1179652
  316.5 72.7 %all-to-all-start.4 = ((bf16[128,2,2048]{2,1,0:T(2,128)(2,1)}), bf16[128,2,2048]{2,1,0:T(2,128)(2,1)S(1)}, u32[]{:S(2)}, u32[]{:S(2)}) async-start(bf16[128,2,2048]{2,1,0:T(2,128)(2,1)} %copy.62), calls=%async_computation.5 | async-start | bytes 2097152 | tf_op jit(solution)/shard_map/all_to_all | solution.py:114
  333.5 4.3 %copy-start.3 = (bf16[1024,2048]{1,0:T(8,128)(2,1)S(1)}, bf16[1024,2048]{1,0:T(8,128)(2,1)}, u32[]{:S(2)}) copy-start(bf16[1024,2048]{1,0:T(8,128)(2,1)} %copy-done.2) | copy-start | bytes 12582916
  337.9 52.9 %copy-start.1 = (bf16[1,192,2048]{2,1,0:T(8,128)(2,1)S(1)}, bf16[1,192,2048]{2,1,0:T(8,128)(2,1)}, u32[]{:S(2)}) copy-start(bf16[1,192,2048]{2,1,0:T(8,128)(2,1)} %param.15) | copy-start | bytes 2359300
Sparse Core Ops, SparseCore 0:
  86.5 45.7 all-gather.8
  150.5 45.7 all-gather.6
  265.4 47.7 reduce-scatter.1
where the time goes:
time: 400 us; the launch traced here: 397 us
  blocking collectives  163 us (41%)
  waiting for transfers between devices  98.2 us (25%)
  local copies, waits for them, and re-layouts  48.9 us (12%)
  starting transfers between devices  41 us (10%)
  matrix products  22.7 us (6%)
  between operations  14 us (4%)
  other arithmetic  9.32 us (2%)
    all_to_all x1, blocking collectives, body(): lax.all_to_all(code_rows, 'expert', split_axis=0, concat_axis=0, tiled=True)  75.5 us
    all_to_all x1, blocking collectives, body(): lax.all_to_all(grad_rows, 'expert', split_axis=0, concat_axis=0, tiled=True)  62.7 us
    all_to_all x1, waiting for transfers between devices, body(): lax.all_to_all(summed.reshape(experts, capacity, width).astype(jnp.bfloat...  46.9 us
    reduce_scatter x1, waiting for transfers between devices, body(): lax.psum_scatter(input_part.reshape(groups, experts, capacity, width).ast...  28.4 us
    all_to_all x1, starting transfers between devices, body(): lax.all_to_all(summed.reshape(experts, capacity, width).astype(jnp.bfloat...  17 us
    all_to_all x1, waiting for transfers between devices, body(): lax.all_to_all(weight_rows, 'expert', split_axis=0, concat_axis=0, tiled=...  14.5 us
    convert_element_type x2, local copies, waits for them, and re-layouts, body(): input_part.reshape(groups, experts, capacity, width).astype(jnp.bfloat16)  13.6 us
    all_to_all x1, starting transfers between devices, body(): lax.all_to_all(own_terms.reshape(experts, capacity).astype(jnp.bfloat16),...  10.6 us
  transfers between devices with their start and end apart: 7, of which 4 were waited for; matrix products, arithmetic and copies ran while one was open for 11% of the time, Pallas kernels for 0%

commit v1 on v0

v1 whole, which is shorter than its diff:
```python
import jax
import jax.numpy as jnp
from jax import lax
from jax.sharding import Mesh, PartitionSpec as P

BLOCK = 128
Y, Z, CORE = 4, 16, 2
DP = 4
F32, BF16 = jnp.float32, jnp.bfloat16
WEIGHTS = "pp"
GRADS = "pp"


def shift(a, k):
    return lax.ppermute(a, "dp", [(i, (i + k) % DP) for i in range(DP)])


def nt(a, b):
    return lax.dot_general(a, b, (((1,), (1,)), ((), ())), preferred_element_type=F32)


def tn(a, b):
    return lax.dot_general(a, b, (((0,), (0,)), ((), ())), preferred_element_type=F32)


def gather_weights(mine):
    half = mine.shape[0] // 2
    from_prev, from_next = shift(mine, 1), shift(mine, -1)
    top, bottom = shift(from_prev[:half], 1), shift(from_next[half:], -1)
    return from_next, from_prev, jnp.concatenate([top, bottom], axis=0)


def scatter_grads(own, nxt, prv, far):
    half = own.shape[0] // 2
    far_top, far_bottom = shift(far[:half], 1), shift(far[half:], -1)
    next_bottom, prev_top = shift(nxt[half:], 1), shift(prv[:half], -1)
    next_top = shift((nxt[:half].astype(F32) + far_top.astype(F32)).astype(BF16), 1)
    prev_bottom = shift((prv[half:].astype(F32) + far_bottom.astype(F32)).astype(BF16), -1)
    top = own[:half].astype(F32) + prev_top.astype(F32) + next_top.astype(F32)
    bottom = own[half:].astype(F32) + next_bottom.astype(F32) + prev_bottom.astype(F32)
    return jnp.concatenate([top, bottom], axis=0).astype(BF16)


def expert_block(x_rows, grad_rows, scaled, weight, w):
    share = w.shape[0] // 3
    both = nt(x_rows, w[: 2 * share])
    gate, up = both[:, :share], both[:, share:]
    back = nt(grad_rows, w[2 * share :])
    sig = jax.nn.sigmoid(gate)
    act = gate * sig
    hidden = (act * up).astype(BF16)
    comb = jnp.sum(back * hidden.astype(F32), axis=1)
    gh = weight * back
    d_gate = (gh * up * sig * (1.0 + gate * (1.0 - sig))).astype(BF16)
    d_up = (gh * act).astype(BF16)
    d_both = jnp.concatenate([d_gate, d_up], axis=1)
    part = jnp.dot(d_both, w[: 2 * share], preferred_element_type=F32).astype(BF16)
    d_w = jnp.concatenate([tn(d_both, x_rows).astype(BF16), tn(hidden, scaled).astype(BF16)], axis=0)
    return part, comb, d_w


def body(grad_out, x_codes, x_scales, combine, expert_ids, w_gate, w_up, w_down):
    tokens, picks = expert_ids.shape
    width = grad_out.shape[1]
    share = w_gate.shape[1]
    experts = Y * Z * CORE
    capacity = 2
    z, y, core = lax.axis_index("z"), lax.axis_index("y"), lax.axis_index("core")
    mine = jnp.concatenate([w_gate[0], w_up[0], w_down[0]], axis=0)
    w_next, w_prev, w_far = gather_weights(mine)

    x = (
        (x_codes.astype(F32).reshape(tokens, width // BLOCK, BLOCK) * x_scales.astype(F32)[:, :, None])
        .reshape(tokens, width)
        .astype(BF16)
    )
    names = (expert_ids[:, :, None] == jnp.arange(experts, dtype=jnp.int32)).astype(F32)
    dense = jnp.sum(names * combine.astype(F32)[:, :, None], axis=1)
    payload = jnp.concatenate([x, grad_out, dense.astype(BF16)], axis=1)
    seen = lax.all_gather(payload, "z", axis=0, tiled=True)

    count = Z * tokens
    slots = Z * capacity
    lanes = lax.broadcasted_iota(jnp.int32, (experts, Y * CORE), 0)
    dest = lax.broadcasted_iota(jnp.int32, (experts, Y * CORE), 1)
    pick_dest = (lanes == ((dest // CORE) * Z + z) * CORE + dest % CORE).astype(BF16)
    member = (seen[:, 2 * width :] != 0).astype(BF16)
    local = jnp.dot(member, pick_dest, preferred_element_type=F32)
    ti = lax.broadcasted_iota(jnp.int32, (count, count), 0)
    tj = lax.broadcasted_iota(jnp.int32, (count, count), 1)
    earlier = ((ti // tokens == tj // tokens) & (tj < ti)).astype(BF16)
    before = jnp.dot(earlier, local.astype(BF16), preferred_element_type=F32)
    slot_of = before.astype(jnp.int32) + (lax.broadcasted_iota(jnp.int32, before.shape, 0) // tokens) * capacity
    slot_of = jnp.where(local > 0, slot_of, -1)
    select = (slot_of.T[:, None, :] == lax.broadcasted_iota(jnp.int32, (Y * CORE, slots, count), 1)).astype(BF16)
    sent = jnp.dot(select.reshape(Y * CORE * slots, count), seen, preferred_element_type=F32).astype(BF16)
    rows = lax.all_to_all(
        sent.reshape(Y * CORE, slots, -1), ("y", "core"), split_axis=0, concat_axis=0, tiled=True
    ).reshape(Y * CORE * slots, -1)

    x_rows, grad_rows = rows[:, :width], rows[:, width : 2 * width]
    me = (y * Z + z) * CORE + core
    at = lax.broadcasted_iota(jnp.int32, (1, experts), 1) == me
    weight = jnp.sum(jnp.where(at, rows[:, 2 * width :].astype(F32), 0.0), axis=1, keepdims=True)
    scaled = (weight * grad_rows.astype(F32)).astype(BF16)

    outs = [expert_block(x_rows, grad_rows, scaled, weight, w) for w in (w_far, w_next, w_prev, mine)]
    total = sum(o[0].astype(F32) for o in outs)
    comb = sum(o[1] for o in outs)
    far, nxt, prv, own = (o[2] for o in outs)
    d_w = scatter_grads(own, nxt, prv, far)

    high = comb.astype(BF16)
    low = (comb - high.astype(F32)).astype(BF16)
    tail = jnp.concatenate([high[:, None], low[:, None], jnp.zeros((comb.shape[0], 126), BF16)], axis=1)
    back = jnp.concatenate([total.astype(BF16), tail], axis=1)
    back = back.reshape(Y, CORE, Z, capacity, -1).transpose(0, 2, 1, 3, 4).reshape(experts, capacity, -1)
    home = lax.all_to_all(back, ("y", "z", "core"), split_axis=0, concat_axis=0, tiled=True)
    home = home.reshape(experts * capacity, -1)

    named = jnp.sum(names, axis=1)
    th = lax.broadcasted_iota(jnp.int32, (tokens, tokens), 0)
    tk = lax.broadcasted_iota(jnp.int32, (tokens, tokens), 1)
    prior = jnp.dot((tk < th).astype(F32), named)
    cap = lax.broadcasted_iota(jnp.int32, (1, 1, capacity), 2)
    owner = (named[:, :, None] > 0) & (prior[:, :, None].astype(jnp.int32) == cap)
    owner = owner.reshape(tokens, experts * capacity).astype(BF16)
    grad_in = jnp.dot(owner, home[:, :width], preferred_element_type=F32).astype(BF16)
    comb_rows = home[:, width].astype(F32) + home[:, width + 1].astype(F32)
    of_expert = jnp.sum((owner.astype(F32) * comb_rows[None, :]).reshape(tokens, experts, capacity), axis=2)
    grad_combine = jnp.sum(names * of_expert[:, None, :], axis=2)
    return (
        grad_in,
        grad_combine,
        d_w[None, :share],
        d_w[None, share : 2 * share],
        d_w[None, 2 * share :],
    )


def solution(mesh):
    fine = Mesh(mesh.devices.reshape(DP, Y, Z, CORE), ("dp", "y", "z", "core"))
    tok = P(("dp", "y", "z", "core"), None)
    wts = P(("y", "z", "core"), "dp", None)
    return jax.shard_map(
        body,
        mesh=fine,
        in_specs=(tok,) * 5 + (wts,) * 3,
        out_specs=(tok, tok, wts, wts, wts),
        check_vma=False,
    )
```

time: 400 us -> 281 us (0.70)
  blocking collectives: 163 us -> 0 us
  waiting for transfers between devices: 98.2 us -> 130 us
  local copies, waits for them, and re-layouts: 48.9 us -> 20.9 us
  matrix products: 22.7 us -> 38 us
  starting transfers between devices: 41 us -> 53.3 us
  other arithmetic: 9.32 us -> 19.1 us
    all_to_all x2 -> x0, blocking collectives: 138 us -> none  [the longest x1 75.5 us: body(): lax.all_to_all(code_rows, 'expert', split_axis=0, concat_axis=0, tiled=True)]
    all_gather x2 -> x1, waiting for transfers between devices: 0.02 us -> 64.9 us  [body(): seen = lax.all_gather(payload, 'z', axis=0, tiled=True)]
    all_to_all x4 -> x2, waiting for transfers between devices: 69.7 us -> 15.8 us  [the longest x1 15.8 us: body(): lax.all_to_all(sent.reshape(Y * CORE, slots, -1), ('y', 'core'), split_ax...]
    ppermute x0 -> x10, waiting for transfers between devices: none -> 49.5 us  [shift(): return lax.ppermute(a, 'dp', [(i, (i + k) % DP) for i in range(DP)])]
    ppermute x0 -> x10, starting transfers between devices: none -> 38.2 us  [shift(): return lax.ppermute(a, 'dp', [(i, (i + k) % DP) for i in range(DP)])]
    reduce_scatter x1 -> x0, waiting for transfers between devices: 28.4 us -> none  [body(): lax.psum_scatter(input_part.reshape(groups, experts, capacity, width).ast...]
    all_to_all x4 -> x2, starting transfers between devices: 40.9 us -> 15 us  [the longest x1 10.7 us: body(): lax.all_to_all(back, ('y', 'z', 'core'), split_axis=0, concat_axis=0, til...]
    convert_element_type x9 -> x4, local copies, waits for them, and re-layouts: 26.6 us -> 1.23 us  [the longest x1 0.76 us: body(): dense = jnp.sum(names * combine.astype(F32)[:, :, None], axis=1)]
  transfers between devices with their start and end apart: 7 -> 13, of which waited for: 4 -> 6; matrix products, arithmetic and copies ran while one was open for 11% -> 22% of each run, Pallas kernels for 0% -> 0%
where the time goes in v1:
time: 281 us; the launch traced here: 276 us
  waiting for transfers between devices  130 us (46%)
  starting transfers between devices  53.3 us (19%)
  matrix products  38 us (14%)
  local copies, waits for them, and re-layouts  20.9 us (7%)
  other arithmetic  19.1 us (7%)
  between operations  14.6 us (5%)
    all_gather x1, waiting for transfers between devices, body(): seen = lax.all_gather(payload, 'z', axis=0, tiled=True)  64.9 us
    ppermute x10, waiting for transfers between devices, shift(): return lax.ppermute(a, 'dp', [(i, (i + k) % DP) for i in range(DP)])  49.5 us
    ppermute x10, starting transfers between devices, shift(): return lax.ppermute(a, 'dp', [(i, (i + k) % DP) for i in range(DP)])  38.2 us
    dot_general x8, matrix products, nt(): lax.dot_general(a, b, (((1,), (1,)), ((), ())), preferred_element_type=F32)  15.9 us
    all_to_all x1, waiting for transfers between devices, body(): lax.all_to_all(sent.reshape(Y * CORE, slots, -1), ('y', 'core'), split_ax...  15.8 us
    all_to_all x1, starting transfers between devices, body(): lax.all_to_all(back, ('y', 'z', 'core'), split_axis=0, concat_axis=0, til...  10.7 us
    concatenate x3, local copies, waits for them, and re-layouts, body(): back = jnp.concatenate([total.astype(BF16), tail], axis=1)  9.24 us
    dot_general x8, matrix products, tn(): lax.dot_general(a, b, (((0,), (0,)), ((), ())), preferred_element_type=F32)  8.01 us
  transfers between devices with their start and end apart: 13, of which 6 were waited for; matrix products, arithmetic and copies ran while one was open for 22% of the time, Pallas kernels for 0%

profile of v1, /device:TPU:6, one launch (start us, length us, event | category | flops | bytes accessed | tf_op | source)
XLA Modules:
  0.0 276.1 jit_solution(6282669146607549834)
XLA Ops:
  10.5 1.5 pad_maximum_fusion.16
  12.1 3.4 %pad_maximum_fusion = bf16[576,2048]{1,0:T(8,128)(2,1)} fusion(bf16[192,2048]{1,0:T(8,128)(2,1)} %bitcast.62, bf16[192,2048]{1,0:T(8,128)(2,1)} %bitcast.56, bf16[192,2048]{1,0:T(8,128)(2,1)} %bitcast.59), kind=kLoop, calls=%fused_computation.21 | loop fusion | flops 7077888 | bytes 4718592 | tf_op jit(solution)/shard_map/concatenate | solution.py:69
  15.4 7.7 %collective-permute-start.2 = (bf16[576,2048]{1,0:T(8,128)(2,1)}, bf16[576,2048]{1,0:T(8,128)(2,1)}, u32[]{:S(2)}, u32[]{:S(2)}) collective-permute-start(bf16[576,2048]{1,0:T(8,128)(2,1)} %pad_maximum_fusion), channel_id=1, source_target_pairs={{0,128},{128,256},{256,384},{384,0},{1,129},{129,257},{257,385},{3... | collective-permute-start | bytes 7077896 | tf_op jit(solution)/shard_map/ppermute | solution.py:15
  23.2 1.9 collective-permute-start
  25.3 64.9 %all-gather.2.cloned.1.call-done = bf16[256,4224]{1,0:T(8,128)(2,1)} async-done(((bf16[16,4224]{1,0:T(8,128)(2,1)}), bf16[256,4224]{1,0:T(8,128)(2,1)}) %all-gather.2.cloned.1.call-update) | async-done | bytes 2162704 | tf_op jit(solution)/shard_map/all_gather | solution.py:80
  91.6 3.7 %convolution_convert_fusion = bf16[256,4224]{1,0:T(8,128)(2,1)} fusion(pred[256,256]{1,0:T(32,128)(4,1)S(1)} %bitcast_compare_fusion, bf16[256,4224]{1,0:T(8,128)(2,1)} %all-gather.2.cloned.1.call-done), kind=kOutput, calls=%fused_computation | convolution fusion | flops 554729472 | bytes 4390912 | tf_op jit(solution)/shard_map/dot_general | solution.py:96
  95.3 4.3 %all-to-all-start = ((bf16[8,32,4224]{2,1,0:T(8,128)(2,1)}), bf16[8,32,4224]{2,1,0:T(8,128)(2,1)S(1)}, u32[]{:S(2)}, u32[]{:S(2)}) async-start(bf16[8,32,4224]{2,1,0:T(8,128)(2,1)} %bitcast.54), calls=%async_computation | async-start | bytes 4325376 | tf_op jit(solution)/shard_map/all_to_all | solution.py:97
  99.6 2.5 slice.147
  102.2 2.8 collective-permute-start.1
  104.9 2.5 slice.150
  107.4 4.3 %collective-permute-start.3 = (bf16[288,2048]{1,0:T(8,128)(2,1)}, bf16[288,2048]{1,0:T(8,128)(2,1)}, u32[]{:S(2)}, u32[]{:S(2)}) collective-permute-start(bf16[288,2048]{1,0:T(8,128)(2,1)} %slice.150), channel_id=1, source_target_pairs={{0,128},{128,256},{256,384},{384,0},{1,129},{129,257},{257,385},{3... | collective-permute-start | bytes 3538952 | tf_op jit(solution)/shard_map/ppermute | solution.py:15
  111.7 15.8 %all-to-all-done = bf16[8,32,4224]{2,1,0:T(8,128)(2,1)S(1)} async-done(((bf16[8,32,4224]{2,1,0:T(8,128)(2,1)}), bf16[8,32,4224]{2,1,0:T(8,128)(2,1)S(1)}, u32[]{:S(2)}, u32[]{:S(2)}) %all-to-all-start) | async-done | bytes 2162720 | tf_op jit(solution)/shard_map/all_to_all | solution.py:97
  127.5 1.8 fusion.17
  129.5 1.1 multiply_reduce_fusion
  130.6 2.0 fusion.9
  132.7 2.3 multiply_reduce_fusion.1
  135.0 2.0 fusion.12
  137.0 2.3 multiply_reduce_fusion.2
  139.4 2.0 fusion.25
  141.4 2.2 multiply_reduce_fusion.3
  143.9 1.4 convolution_convert_fusion.9
  145.8 1.6 pad_maximum_fusion.3
  147.4 2.9 %collective-permute-start.8 = (bf16[288,2048]{1,0:T(8,128)(2,1)}, bf16[288,2048]{1,0:T(8,128)(2,1)}, u32[]{:S(2)}, u32[]{:S(2)}) collective-permute-start(bf16[288,2048]{1,0:T(8,128)(2,1)} %get-tuple-element.29), channel_id=1, source_target_pairs={{0,384},{128,0},{256,128},{384,256},{1,385},{129,1},{257,129},{385... | collective-permute-start | bytes 3538952 | tf_op jit(solution)/shard_map/ppermute | solution.py:15
  151.1 1.8 convolution_convert_fusion.2
  152.8 2.2 fusion.4
  155.0 2.1 fusion.5
  157.2 2.2 fusion.7
  159.4 1.5 concatenate.54
  160.9 2.5 copy.83
  163.8 5.3 %concatenate.55 = bf16[4,2,16,2,2176]{4,3,1,2,0:T(2,128)(2,1)} concatenate(bf16[4,2,16,2,2048]{4,3,1,2,0:T(2,128)(2,1)S(1)} %copy.83, bf16[4,2,16,2,1]{4,3,1,2,0:T(2,128)(2,1)S(1)} %copy.84, bf16[4,2,16,2,1]{4,3,1,2,0:T(2,128)(2,1)S(1)} %copy.85, bf16[4,2,16,2,126]{4,3,1,2,0:T(2,128)(2,1)S(1)} %broadcast_in_dim.43), dimensions={4} | concatenate | bytes 2228224 | tf_op jit(solution)/shard_map/concatenate | solution.py:116
  169.0 10.7 %all-to-all-start.1 = ((bf16[128,2,2176]{2,1,0:T(2,128)(2,1)}), bf16[128,2,2176]{2,1,0:T(2,128)(2,1)S(1)}, u32[]{:S(2)}, u32[]{:S(2)}) async-start(bf16[128,2,2176]{2,1,0:T(2,128)(2,1)} %bitcast.55), calls=%async_computation.1 | async-start | bytes 2228224 | tf_op jit(solution)/shard_map/all_to_all | solution.py:118
  179.8 5.3 %collective-permute-start.5 = (bf16[288,2048]{1,0:T(8,128)(2,1)}, bf16[288,2048]{1,0:T(8,128)(2,1)S(1)}, u32[]{:S(2)}, u32[]{:S(2)}) collective-permute-start(bf16[288,2048]{1,0:T(8,128)(2,1)} %get-tuple-element.30), channel_id=1, source_target_pairs={{0,128},{128,256},{256,384},{384,0},{1,129},{129,257},{257,385},{3... | collective-permute-start | bytes 3538952 | tf_op jit(solution)/shard_map/ppermute | solution.py:15
  185.6 1.2 pad_maximum_fusion.5
  186.8 4.0 %collective-permute-start.7 = (bf16[288,2048]{1,0:T(8,128)(2,1)}, bf16[288,2048]{1,0:T(8,128)(2,1)}, u32[]{:S(2)}, u32[]{:S(2)}) collective-permute-start(bf16[288,2048]{1,0:T(8,128)(2,1)} %pad_maximum_fusion.5), channel_id=1, source_target_pairs={{0,128},{128,256},{256,384},{384,0},{1,129},{129,257},{257,385},{3... | collective-permute-start | bytes 3538952 | tf_op jit(solution)/shard_map/ppermute | solution.py:15
  191.4 1.1 slice.167
  192.5 1.9 collective-permute-start.4
  194.9 2.8 %add_convert_fusion.1 = bf16[288,2048]{1,0:T(8,128)(2,1)} fusion(bf16[288,2048]{1,0:T(8,128)(2,1)} %collective-permute-done.8, bf16[192,2048]{1,0:T(8,128)(2,1)S(1)} %convolution_convert_fusion.10, bf16[384,2048]{1,0:T(8,128)(2,1)S(1)} %convolution_convert_fusion.3), kind=kLoop, calls=%fused_computation.23 | loop fusion | flops 4128768 | bytes 4718592 | tf_op jit(solution)/shard_map/convert_element_type | solution.py:38
  197.8 1.9 collective-permute-start.9
  199.7 12.1 %collective-permute-done.5 = bf16[288,2048]{1,0:T(8,128)(2,1)S(1)} collective-permute-done((bf16[288,2048]{1,0:T(8,128)(2,1)}, bf16[288,2048]{1,0:T(8,128)(2,1)S(1)}, u32[]{:S(2)}, u32[]{:S(2)}) %collective-permute-start.5) | collective-permute-done | bytes 1179680 | tf_op jit(solution)/shard_map/ppermute | solution.py:15
  211.8 1.5 add_convert_fusion.3
  213.3 5.5 %collective-permute-start.6 = (bf16[288,2048]{1,0:T(8,128)(2,1)}, bf16[288,2048]{1,0:T(8,128)(2,1)}, u32[]{:S(2)}, u32[]{:S(2)}) collective-permute-start(bf16[288,2048]{1,0:T(8,128)(2,1)} %add_convert_fusion.3), channel_id=1, source_target_pairs={{0,128},{128,256},{256,384},{384,0},{1,129},{129,257},{257,385},{3... | collective-permute-start | bytes 3538952 | tf_op jit(solution)/shard_map/ppermute | solution.py:15
  220.7 1.4 convolution_convert_fusion.12
  222.1 1.5 convolution_convert_fusion.4
  223.5 13.5 %collective-permute-done.7 = bf16[288,2048]{1,0:T(8,128)(2,1)} collective-permute-done((bf16[288,2048]{1,0:T(8,128)(2,1)}, bf16[288,2048]{1,0:T(8,128)(2,1)}, u32[]{:S(2)}, u32[]{:S(2)}) %collective-permute-start.7) | collective-permute-done | bytes 1179680 | tf_op jit(solution)/shard_map/ppermute | solution.py:15
  237.1 11.1 %collective-permute-done.9 = bf16[288,2048]{1,0:T(8,128)(2,1)} collective-permute-done((bf16[288,2048]{1,0:T(8,128)(2,1)}, bf16[288,2048]{1,0:T(8,128)(2,1)}, u32[]{:S(2)}, u32[]{:S(2)}) %collective-permute-start.9) | collective-permute-done | bytes 1179680 | tf_op jit(solution)/shard_map/ppermute | solution.py:15
  248.1 12.8 %collective-permute-done.6 = bf16[288,2048]{1,0:T(8,128)(2,1)} collective-permute-done((bf16[288,2048]{1,0:T(8,128)(2,1)}, bf16[288,2048]{1,0:T(8,128)(2,1)}, u32[]{:S(2)}, u32[]{:S(2)}) %collective-permute-start.6) | collective-permute-done | bytes 1179680 | tf_op jit(solution)/shard_map/ppermute | solution.py:15
  260.9 3.8 %add_convert_fusion = (bf16[288,2048]{1,0:T(8,128)(2,1)S(1)}, bf16[288,2048]{1,0:T(8,128)(2,1)S(1)}) fusion(bf16[288,2048]{1,0:T(8,128)(2,1)} %collective-permute-done.9, bf16[288,2048]{1,0:T(8,128)(2,1)} %collective-permute-done.7, bf16[192,2048]{1,0:T(8,128)(2,1)S(1)} %convolution_convert_fusion.12, bf16[384,2048]{1,0:T(8,128)(2,1)S(1)} %convolution_convert_fusion.4, ...), kind=kLoop, calls=%fused_computation.22 | loop fusion | flops 8847360 | bytes 10616832 | tf_op jit(solution)/shard_map/convert.1
  264.7 1.5 slice_bitcast_fusion
  (91 shorter events, 13.5 us)
Async XLA Ops:
  7.2 83.0 %all-gather.2.cloned.1.call-start = ((), (), s32[]{:S(2)}) async-start(), calls=%async_computation.2 | async-start | bytes 2297856 | tf_op jit(solution)/shard_map/all_gather | solution.py:80
  8.0 0.8 copy-start.11
  8.8 209.9 %copy-start.13 = (f32[16,128]{1,0:T(8,128)}, f32[16,128]{1,0:T(8,128)S(1)}, u32[]{:S(2)}) copy-start(f32[16,128]{1,0:T(8,128)S(1)} %get-tuple-element.15) | copy-start | bytes 24580
  15.4 89.5 %collective-permute-start.2 = (bf16[576,2048]{1,0:T(8,128)(2,1)}, bf16[576,2048]{1,0:T(8,128)(2,1)}, u32[]{:S(2)}, u32[]{:S(2)}) collective-permute-start(bf16[576,2048]{1,0:T(8,128)(2,1)} %pad_maximum_fusion), channel_id=1, source_target_pairs={{0,128},{128,256},{256,384},{384,0},{1,129},{129,257},{257,385},{3... | collective-permute-start | bytes 7077896 | tf_op jit(solution)/shard_map/ppermute | solution.py:15
  23.2 76.4 %collective-permute-start = (bf16[576,2048]{1,0:T(8,128)(2,1)}, bf16[576,2048]{1,0:T(8,128)(2,1)}, u32[]{:S(2)}, u32[]{:S(2)}) collective-permute-start(bf16[576,2048]{1,0:T(8,128)(2,1)} %pad_maximum_fusion), channel_id=1, source_target_pairs={{0,384},{128,0},{256,128},{384,256},{1,385},{129,1},{257,129},{385... | collective-permute-start | bytes 7077896 | tf_op jit(solution)/shard_map/ppermute | solution.py:15
  95.3 32.2 %all-to-all-start = ((bf16[8,32,4224]{2,1,0:T(8,128)(2,1)}), bf16[8,32,4224]{2,1,0:T(8,128)(2,1)S(1)}, u32[]{:S(2)}, u32[]{:S(2)}) async-start(bf16[8,32,4224]{2,1,0:T(8,128)(2,1)} %bitcast.54), calls=%async_computation | async-start | bytes 4325376 | tf_op jit(solution)/shard_map/all_to_all | solution.py:97
  99.6 27.9 %copy-start.1 = (bf16[1,192,2048]{2,1,0:T(8,128)(2,1)S(1)}, bf16[1,192,2048]{2,1,0:T(8,128)(2,1)}, u32[]{:S(2)}) copy-start(bf16[1,192,2048]{2,1,0:T(8,128)(2,1)} %param.14) | copy-start | bytes 2359300
  102.2 37.2 %collective-permute-start.1 = (bf16[288,2048]{1,0:T(8,128)(2,1)}, bf16[288,2048]{1,0:T(8,128)(2,1)}, u32[]{:S(2)}, u32[]{:S(2)}) collective-permute-start(bf16[288,2048]{1,0:T(8,128)(2,1)} %slice.147), channel_id=1, source_target_pairs={{0,384},{128,0},{256,128},{384,256},{1,385},{129,1},{257,129},{385... | collective-permute-start | bytes 3538952 | tf_op jit(solution)/shard_map/ppermute | solution.py:15
  107.4 31.9 %collective-permute-start.3 = (bf16[288,2048]{1,0:T(8,128)(2,1)}, bf16[288,2048]{1,0:T(8,128)(2,1)}, u32[]{:S(2)}, u32[]{:S(2)}) collective-permute-start(bf16[288,2048]{1,0:T(8,128)(2,1)} %slice.150), channel_id=1, source_target_pairs={{0,128},{128,256},{256,384},{384,0},{1,129},{129,257},{257,385},{3... | collective-permute-start | bytes 3538952 | tf_op jit(solution)/shard_map/ppermute | solution.py:15
  127.5 1.9 copy-start.3
  129.5 65.0 %copy-start.15 = (f32[256]{0:T(256)}, f32[256]{0:T(256)S(1)}, u32[]{:S(2)}) copy-start(f32[256]{0:T(256)S(1)} %select_reduce_fusion) | copy-start | bytes 3076
  130.6 19.7 %copy-start.4 = (bf16[256,192]{0,1:T(8,128)(2,1)}, bf16[256,192]{0,1:T(8,128)(2,1)S(1)}, u32[]{:S(2)}) copy-start(bf16[256,192]{0,1:T(8,128)(2,1)S(1)} %get-tuple-element.49) | copy-start | bytes 294916
  135.0 20.1 %copy-start.5 = (bf16[256,192]{0,1:T(8,128)(2,1)}, bf16[256,192]{0,1:T(8,128)(2,1)S(1)}, u32[]{:S(2)}) copy-start(bf16[256,192]{0,1:T(8,128)(2,1)S(1)} %get-tuple-element.46) | copy-start | bytes 294916
  145.8 4.5 %copy-start.2 = (bf16[1,192,2048]{2,1,0:T(8,128)(2,1)S(1)}, bf16[1,192,2048]{2,1,0:T(8,128)(2,1)}, u32[]{:S(2)}) copy-start(bf16[1,192,2048]{2,1,0:T(8,128)(2,1)} %param.13) | copy-start | bytes 2359300
  147.4 3.7 %copy-start.9 = (bf16[256,192]{0,1:T(8,128)(2,1)S(1)}, bf16[256,192]{0,1:T(8,128)(2,1)}, u32[]{:S(2)}) copy-start(bf16[256,192]{0,1:T(8,128)(2,1)} %get-tuple-element.42) | copy-start | bytes 294916
  147.4 3.7 %copy-start.10 = (bf16[256,192]{0,1:T(8,128)(2,1)S(1)}, bf16[256,192]{0,1:T(8,128)(2,1)}, u32[]{:S(2)}) copy-start(bf16[256,192]{0,1:T(8,128)(2,1)} %get-tuple-element.43) | copy-start | bytes 294916
  147.4 47.5 %collective-permute-start.8 = (bf16[288,2048]{1,0:T(8,128)(2,1)}, bf16[288,2048]{1,0:T(8,128)(2,1)}, u32[]{:S(2)}, u32[]{:S(2)}) collective-permute-start(bf16[288,2048]{1,0:T(8,128)(2,1)} %get-tuple-element.29), channel_id=1, source_target_pairs={{0,384},{128,0},{256,128},{384,256},{1,385},{129,1},{257,129},{385... | collective-permute-start | bytes 3538952 | tf_op jit(solution)/shard_map/ppermute | solution.py:15
  152.8 2.2 copy-start.7
  169.0 16.0 %copy-start.17 = (bf16[256,192]{0,1:T(8,128)(2,1)S(1)}, bf16[256,192]{0,1:T(8,128)(2,1)}, u32[]{:S(2)}) copy-start(bf16[256,192]{0,1:T(8,128)(2,1)} %get-tuple-element.20) | copy-start | bytes 294916
  169.0 97.2 %all-to-all-start.1 = ((bf16[128,2,2176]{2,1,0:T(2,128)(2,1)}), bf16[128,2,2176]{2,1,0:T(2,128)(2,1)S(1)}, u32[]{:S(2)}, u32[]{:S(2)}) async-start(bf16[128,2,2176]{2,1,0:T(2,128)(2,1)} %bitcast.55), calls=%async_computation.1 | async-start | bytes 2228224 | tf_op jit(solution)/shard_map/all_to_all | solution.py:118
  179.8 5.8 %copy-start = (bf16[384,2048]{1,0:T(8,128)(2,1)S(1)}, bf16[384,2048]{1,0:T(8,128)(2,1)}, u32[]{:S(2)}) copy-start(bf16[384,2048]{1,0:T(8,128)(2,1)} %convolution_convert_fusion.2) | copy-start | bytes 4718596
  179.8 32.0 %collective-permute-start.5 = (bf16[288,2048]{1,0:T(8,128)(2,1)}, bf16[288,2048]{1,0:T(8,128)(2,1)S(1)}, u32[]{:S(2)}, u32[]{:S(2)}) collective-permute-start(bf16[288,2048]{1,0:T(8,128)(2,1)} %get-tuple-element.30), channel_id=1, source_target_pairs={{0,128},{128,256},{256,384},{384,0},{1,129},{129,257},{257,385},{3... | collective-permute-start | bytes 3538952 | tf_op jit(solution)/shard_map/ppermute | solution.py:15
  185.6 5.2 %copy-start.6 = (bf16[256,192]{0,1:T(8,128)(2,1)S(1)}, bf16[256,192]{0,1:T(8,128)(2,1)}, u32[]{:S(2)}) copy-start(bf16[256,192]{0,1:T(8,128)(2,1)} %copy-done.5) | copy-start | bytes 294916
  185.6 5.2 %copy-start.8 = (bf16[256,192]{0,1:T(8,128)(2,1)S(1)}, bf16[256,192]{0,1:T(8,128)(2,1)}, u32[]{:S(2)}) copy-start(bf16[256,192]{0,1:T(8,128)(2,1)} %get-tuple-element.47) | copy-start | bytes 294916
  186.8 7.7 %copy-start.16 = (bf16[256,192]{0,1:T(8,128)(2,1)S(1)}, bf16[256,192]{0,1:T(8,128)(2,1)}, u32[]{:S(2)}) copy-start(bf16[256,192]{0,1:T(8,128)(2,1)} %get-tuple-element.24) | copy-start | bytes 294916
  186.8 50.3 %collective-permute-start.7 = (bf16[288,2048]{1,0:T(8,128)(2,1)}, bf16[288,2048]{1,0:T(8,128)(2,1)}, u32[]{:S(2)}, u32[]{:S(2)}) collective-permute-start(bf16[288,2048]{1,0:T(8,128)(2,1)} %pad_maximum_fusion.5), channel_id=1, source_target_pairs={{0,128},{128,256},{256,384},{384,0},{1,129},{129,257},{257,385},{3... | collective-permute-start | bytes 3538952 | tf_op jit(solution)/shard_map/ppermute | solution.py:15
  192.5 44.5 %collective-permute-start.4 = (bf16[288,2048]{1,0:T(8,128)(2,1)}, bf16[288,2048]{1,0:T(8,128)(2,1)}, u32[]{:S(2)}, u32[]{:S(2)}) collective-permute-start(bf16[288,2048]{1,0:T(8,128)(2,1)} %slice.167), channel_id=1, source_target_pairs={{0,384},{128,0},{256,128},{384,256},{1,385},{129,1},{257,129},{385... | collective-permute-start | bytes 3538952 | tf_op jit(solution)/shard_map/ppermute | solution.py:15
  197.8 50.4 %collective-permute-start.9 = (bf16[288,2048]{1,0:T(8,128)(2,1)}, bf16[288,2048]{1,0:T(8,128)(2,1)}, u32[]{:S(2)}, u32[]{:S(2)}) collective-permute-start(bf16[288,2048]{1,0:T(8,128)(2,1)} %add_convert_fusion.1), channel_id=1, source_target_pairs={{0,384},{128,0},{256,128},{384,256},{1,385},{129,1},{257,129},{385... | collective-permute-start | bytes 3538952 | tf_op jit(solution)/shard_map/ppermute | solution.py:15
  213.3 47.7 %collective-permute-start.6 = (bf16[288,2048]{1,0:T(8,128)(2,1)}, bf16[288,2048]{1,0:T(8,128)(2,1)}, u32[]{:S(2)}, u32[]{:S(2)}) collective-permute-start(bf16[288,2048]{1,0:T(8,128)(2,1)} %add_convert_fusion.3), channel_id=1, source_target_pairs={{0,128},{128,256},{256,384},{384,0},{1,129},{129,257},{257,385},{3... | collective-permute-start | bytes 3538952 | tf_op jit(solution)/shard_map/ppermute | solution.py:15
  266.2 1.2 copy-start.12
  266.2 2.1 copy-start.14
Sparse Core Ops, SparseCore 0:
  12.2 77.9 all-gather.1

commit v2 on v1

v2 whole, which is shorter than its diff:
```python
import functools

import jax
import jax.numpy as jnp
from jax import lax
from jax.experimental import pallas as pl
from jax.experimental.pallas import tpu as pltpu
from jax.sharding import Mesh, PartitionSpec as P

BLOCK = 128
DP, Y, Z, CORE = 4, 4, 16, 2
STRIDE = 4
YC = Y * CORE
CAP = 2
F32, BF16 = jnp.float32, jnp.bfloat16


def shift(a, axis, size, k):
    return lax.ppermute(a, axis, [(i, (i + k) % size) for i in range(size)])


def nt(a, b):
    return lax.dot_general(a, b, (((1,), (1,)), ((), ())), preferred_element_type=F32)


def tn(a, b):
    return lax.dot_general(a, b, (((0,), (0,)), ((), ())), preferred_element_type=F32)


def nn(a, b):
    return jnp.dot(a, b, preferred_element_type=F32)


def gather_weights(mine):
    half = mine.shape[0] // 2
    from_prev, from_next = shift(mine, "dp", DP, 1), shift(mine, "dp", DP, -1)
    top, bottom = shift(from_prev[:half], "dp", DP, 1), shift(from_next[half:], "dp", DP, -1)
    return from_next, from_prev, top, bottom


def add(a, b):
    return (a.astype(F32) + b.astype(F32)).astype(BF16)


def block_kernel(last, rows_ref, own_ref, top_ref, bottom_ref, comb_ref, *refs):
    if last:
        part_a, part_b, part_c, perm_ref, d_top, d_bottom, back_ref = refs
    else:
        d_top, d_bottom, part_ref, comb_out = refs
    width = top_ref.shape[1]
    half = top_ref.shape[0]
    share = 2 * half // 3
    rest = half - share
    x = rows_ref[:, :width]
    grad = rows_ref[:, width : 2 * width]
    weight = jnp.sum(rows_ref[:, 2 * width :].astype(F32) * own_ref[...], axis=1, keepdims=True)
    w_gate = top_ref[:share]
    w_up = jnp.concatenate([top_ref[share:], bottom_ref[:rest]], axis=0)
    w_down = bottom_ref[rest:]
    gate = nt(x, w_gate)
    up = nt(x, w_up)
    back = nt(grad, w_down)
    sig = jax.nn.sigmoid(gate)
    act = gate * sig
    hidden = (act * up).astype(BF16)
    comb = comb_ref[...] + jnp.sum(back * hidden.astype(F32), axis=1, keepdims=True)
    gh = weight * back
    d_gate = (gh * up * sig * (1.0 + gate * (1.0 - sig))).astype(BF16)
    d_up = (gh * act).astype(BF16)
    scaled = (weight * grad.astype(F32)).astype(BF16)
    d_top[:share] = tn(d_gate, x).astype(BF16)
    d_up_w = tn(d_up, x).astype(BF16)
    d_top[share:] = d_up_w[:rest]
    d_bottom[:rest] = d_up_w[rest:]
    d_bottom[rest:] = tn(hidden, scaled).astype(BF16)
    part = (nn(d_gate, w_gate) + nn(d_up, w_up)).astype(BF16)
    if last:
        total = part.astype(F32) + part_a[...].astype(F32) + part_b[...].astype(F32) + part_c[...].astype(F32)
        perm = perm_ref[...]
        back_ref[:, :width] = nn(perm, total.astype(BF16)).astype(BF16)
        high = comb.astype(BF16)
        low = (comb - high.astype(F32)).astype(BF16)
        lane = lax.broadcasted_iota(jnp.int32, high.shape, 1)
        tail = jnp.where(lane == 0, high.astype(F32), jnp.where(lane == 1, low.astype(F32), 0.0))
        back_ref[:, width:] = nn(perm, tail.astype(BF16)).astype(BF16)
    else:
        part_ref[...] = part
        comb_out[...] = comb


def expert_block(rows, own, weights, comb, last=()):
    n, width = rows.shape[0], weights[0].shape[1]
    if len(weights) == 1:
        half = weights[0].shape[0] // 2
        w_specs = [pl.BlockSpec((half, width), lambda i, k=k: (k, 0)) for k in range(2)]
        weights = weights * 2
    else:
        half = weights[0].shape[0]
        w_specs = [pl.BlockSpec((half, width), lambda i: (0, 0))] * 2
    whole = lambda a: pl.BlockSpec(a.shape, lambda i: (0,) * a.ndim)
    sds = jax.ShapeDtypeStruct
    out = [sds((half, width), BF16), sds((half, width), BF16)]
    out += [sds((n, width + 128), BF16)] if last else [sds((n, width), BF16), sds((n, 128), F32)]
    return pl.pallas_call(
        functools.partial(block_kernel, bool(last)),
        grid=(1,),
        out_shape=out,
        in_specs=[whole(rows), whole(own), *w_specs, whole(comb), *[whole(a) for a in last]],
        out_specs=[whole(o) for o in out],
        compiler_params=pltpu.CompilerParams(vmem_limit_bytes=40 * 2**20),
        cost_estimate=pl.CostEstimate(flops=2 * 8 * n * 256 * width, bytes_accessed=9 * 2**20, transcendentals=n * 192),
    )(rows, own, *weights, comb, *last)


def dispatch(chunk, z, tokens, width):
    n = chunk.shape[0]
    lane = lax.broadcasted_iota(jnp.int32, (YC * Z, YC), 0)
    dest = lax.broadcasted_iota(jnp.int32, (YC * Z, YC), 1)
    member = (chunk[:, 2 * width :] != 0).astype(BF16)
    local = nn(member, (lane == dest * Z + z).astype(BF16))
    ti = lax.broadcasted_iota(jnp.int32, (n, n), 0)
    tj = lax.broadcasted_iota(jnp.int32, (n, n), 1)
    earlier = ((ti // tokens == tj // tokens) & (tj < ti)).astype(BF16)
    before = nn(earlier, local.astype(BF16)).astype(jnp.int32)
    slot = before + (lax.broadcasted_iota(jnp.int32, before.shape, 0) // tokens) * CAP
    slot = jnp.where(local > 0, slot, -1)
    slots = n // tokens * CAP
    select = slot.T[:, None, :] == lax.broadcasted_iota(jnp.int32, (YC, slots, n), 1)
    sent = nn(select.astype(BF16).reshape(YC * slots, n), chunk).astype(BF16)
    got = lax.all_to_all(sent.reshape(YC, slots, -1), ("y", "core"), split_axis=0, concat_axis=0, tiled=True)
    return got.reshape(YC * slots, -1)


def body(grad_out, x_codes, x_scales, combine, expert_ids, w_gate, w_up, w_down):
    tokens, picks = expert_ids.shape
    width = grad_out.shape[1]
    share = w_gate.shape[1]
    experts = YC * Z
    z = lax.axis_index("z")
    yc = lax.axis_index("y") * CORE + lax.axis_index("core")
    mine = jnp.concatenate([w_gate[0], w_up[0], w_down[0]], axis=0)
    w_next, w_prev, far_top, far_bottom = gather_weights(mine)

    x = (
        (x_codes.astype(F32).reshape(tokens, width // BLOCK, BLOCK) * x_scales.astype(F32)[:, :, None])
        .reshape(tokens, width)
        .astype(BF16)
    )
    ranks = expert_ids // (Z * CORE) * (Z * CORE) + expert_ids % CORE * Z + expert_ids // CORE % Z
    names = (ranks[:, :, None] == jnp.arange(experts, dtype=jnp.int32)).astype(F32)
    dense = jnp.sum(names * combine.astype(F32)[:, :, None], axis=1)
    payload = jnp.concatenate([x, grad_out, dense.astype(BF16)], axis=1)
    groups = [list(range(r, Z, STRIDE)) for r in range(STRIDE)]
    seen = lax.all_gather(payload, "z", axis=0, tiled=True, axis_index_groups=groups)
    mid = seen.shape[0] // 2
    others = (
        shift(seen, "z", Z, -1),
        shift(seen, "z", Z, 1),
        shift(seen[:mid], "z", Z, -2),
        shift(seen[mid:], "z", Z, 2),
    )
    first = dispatch(seen, z, tokens, width)
    rows = jnp.concatenate([first, dispatch(jnp.concatenate(others, axis=0), z, tokens, width)], axis=0)

    own = (lax.broadcasted_iota(jnp.int32, (1, experts), 1) == yc * Z + z).astype(F32)
    comb = jnp.zeros((rows.shape[0], 128), F32)
    f_top, f_bottom, part_f, comb = expert_block(rows, own, (far_top, far_bottom), comb)
    n_top, n_bottom, part_n, comb = expert_block(rows, own, (w_next,), comb)
    p_top, p_bottom, part_p, comb = expert_block(rows, own, (w_prev,), comb)
    q = lax.broadcasted_iota(jnp.int32, (rows.shape[0], 1), 0)
    q_yc, q_z, q_cap = q // (Z * CAP), q // CAP % Z, q % CAP
    kind = (q_z - z + Z) % STRIDE
    per = Z // STRIDE * CAP
    place = q_z // STRIDE * CAP + q_cap
    at = jnp.where(
        kind == 0,
        q_yc * per + place,
        YC * per + q_yc * 3 * per + jnp.where(kind == 1, 0, jnp.where(kind == 3, per, 2 * per)) + place,
    )
    perm = (at == lax.broadcasted_iota(jnp.int32, (rows.shape[0], rows.shape[0]), 1)).astype(BF16)
    o_top, o_bottom, back = expert_block(rows, own, (mine,), comb, (part_f, part_n, part_p, perm))

    got_f_top, got_f_bottom = shift(f_top, "dp", DP, 1), shift(f_bottom, "dp", DP, -1)
    got_n_bottom, got_p_top = shift(n_bottom, "dp", DP, 1), shift(p_top, "dp", DP, -1)
    got_n_top = shift(add(n_top, got_f_top), "dp", DP, 1)
    got_p_bottom = shift(add(p_bottom, got_f_bottom), "dp", DP, -1)

    home = lax.all_to_all(
        back.reshape(experts, CAP, -1), ("y", "core", "z"), split_axis=0, concat_axis=0, tiled=True
    ).reshape(experts * CAP, -1)
    named = jnp.sum(names, axis=1)
    th = lax.broadcasted_iota(jnp.int32, (tokens, tokens), 0)
    tk = lax.broadcasted_iota(jnp.int32, (tokens, tokens), 1)
    prior = nn((tk < th).astype(BF16), named.astype(BF16)).astype(jnp.int32)
    owner = (named[:, :, None] > 0) & (prior[:, :, None] == lax.broadcasted_iota(jnp.int32, (1, 1, CAP), 2))
    owner = owner.reshape(tokens, experts * CAP).astype(BF16)
    grad_in = nn(owner, home[:, :width]).astype(BF16)
    comb_rows = home[:, width].astype(F32) + home[:, width + 1].astype(F32)
    of_expert = jnp.sum((owner.astype(F32) * comb_rows[None, :]).reshape(tokens, experts, CAP), axis=2)
    grad_combine = jnp.sum(names * of_expert[:, None, :], axis=2)

    rest = f_top.shape[0] - share
    top = lambda s: (o_top[s].astype(F32) + got_p_top[s].astype(F32) + got_n_top[s].astype(F32)).astype(BF16)
    bottom = lambda s: (
        o_bottom[s].astype(F32) + got_n_bottom[s].astype(F32) + got_p_bottom[s].astype(F32)
    ).astype(BF16)
    grad_up = jnp.concatenate([top(slice(share, None)), bottom(slice(0, rest))], axis=0)
    return grad_in, grad_combine, top(slice(0, share))[None], grad_up[None], bottom(slice(rest, None))[None]


def solution(mesh):
    fine = Mesh(mesh.devices.reshape(DP, Y, Z, CORE), ("dp", "y", "z", "core"))
    tok = P(("dp", "y", "z", "core"), None)
    wts = P(("y", "z", "core"), "dp", None)
    return jax.shard_map(
        body,
        mesh=fine,
        in_specs=(tok,) * 5 + (wts,) * 3,
        out_specs=(tok, tok, wts, wts, wts),
        check_vma=False,
    )
```

time: 281 us -> 247 us (0.88); the launches traced: 276 us -> 245 us
  waiting for transfers between devices: 130 us -> 72.4 us
  blocking collectives: 0 us -> 35 us
  matrix products: 38 us -> 5.47 us
  Pallas kernels: 0 us -> 18 us
  between operations: 14.6 us -> 1.07 us
  starting transfers between devices: 53.3 us -> 64.8 us
  local copies, waits for them, and re-layouts: 20.9 us -> 27 us
    all_gather x1 -> x0, waiting for transfers between devices: 64.9 us -> none  [body(): seen = lax.all_gather(payload, 'z', axis=0, tiled=True)]
    all_gather x0 -> x1, blocking collectives: none -> 35 us  [body(): lax.all_gather(payload, 'z', axis=0, tiled=True, axis_index_groups=groups)]
    dot_general x25 -> x8, matrix products: 38 us -> 5.47 us  [nn(): return jnp.dot(a, b, preferred_element_type=F32)]
    ppermute x10 -> x14, waiting for transfers between devices: 49.5 us -> 72.4 us  [shift(): return lax.ppermute(a, axis, [(i, (i + k) % size) for i in range(size)])]
    pallas_call x0 -> x4, Pallas kernels: none -> 18 us  [expert_block(): pl.pallas_call(functools.partial(block_kernel, bool(last)), grid=(1,), ou...]
    all_to_all x2 -> x3, waiting for transfers between devices: 15.8 us -> 0.01 us  [the longest x2 0.01 us: dispatch(): lax.all_to_all(sent.reshape(YC, slots, -1), ('y', 'core'), split_axis=0,...]
    concatenate x3 -> x1, local copies, waits for them, and re-layouts: 9.24 us -> 0.03 us  [body(): jnp.concatenate(others, axis=0)]
    unnamed x38 -> x32, local copies, waits for them, and re-layouts: 1.5 us -> 8.81 us
  transfers between devices with their start and end apart: 13 -> 17, of which waited for: 6 -> 7; matrix products, arithmetic and copies ran while one was open for 22% -> 17% of each run, Pallas kernels for 0% -> 5%
where the time goes in v2:
time: 247 us; the launch traced here: 245 us
  waiting for transfers between devices  72.4 us (29%)
  starting transfers between devices  64.8 us (26%)
  blocking collectives  35 us (14%)
  local copies, waits for them, and re-layouts  27 us (11%)
  other arithmetic  21.4 us (9%)
  Pallas kernels  18 us (7%)
  matrix products  5.47 us (2%)
    ppermute x14, waiting for transfers between devices, shift(): return lax.ppermute(a, axis, [(i, (i + k) % size) for i in range(size)])  72.4 us
    ppermute x14, starting transfers between devices, shift(): return lax.ppermute(a, axis, [(i, (i + k) % size) for i in range(size)])  42.7 us
    all_gather x1, blocking collectives, body(): lax.all_gather(payload, 'z', axis=0, tiled=True, axis_index_groups=groups)  35 us
    pallas_call x4, Pallas kernels, expert_block(): pl.pallas_call(functools.partial(block_kernel, bool(last)), grid=(1,), ou...  18 us
    all_to_all x1, starting transfers between devices, body(): lax.all_to_all(back.reshape(experts, CAP, -1), ('y', 'core', 'z'), split_...  13.2 us
    all_to_all x2, starting transfers between devices, dispatch(): lax.all_to_all(sent.reshape(YC, slots, -1), ('y', 'core'), split_axis=0,...  8.92 us
    unnamed x32, local copies, waits for them, and re-layouts  8.81 us
    convert_element_type x2, other arithmetic, add(): return (a.astype(F32) + b.astype(F32)).astype(BF16)  5.66 us
  transfers between devices with their start and end apart: 17, of which 7 were waited for; matrix products, arithmetic and copies ran while one was open for 17% of the time, Pallas kernels for 5%

profile of v2, /device:TPU:6, one launch (start us, length us, event | category | flops | bytes accessed | tf_op | source)
XLA Modules:
  0.0 245.3 jit_solution(9227488517474750858)
XLA Ops:
  4.9 35.0 %all_gather.3 = bf16[64,4224]{1,0:T(8,128)(2,1)S(1)} all-gather(bf16[16,4224]{1,0:T(8,128)(2,1)S(1)} %pad_maximum_fusion.2), channel_id=1, replica_groups={{0,8,16,24},{2,10,18,26},{4,12,20,28},{6,14,22,30},{1,9,17,25},{3,11,19..., dimensions={0}, use_global_device_ids=true | all-gather | bytes 675840 | tf_op jit(solution)/shard_map/all_gather | solution.py:154
  39.9 1.9 collective-permute-start
  41.8 3.9 %collective-permute-start.1 = (bf16[64,4224]{1,0:T(8,128)(2,1)S(1)}, bf16[64,4224]{1,0:T(8,128)(2,1)}, u32[]{:S(2)}, u32[]{:S(2)}) collective-permute-start(bf16[64,4224]{1,0:T(8,128)(2,1)S(1)} %all_gather.3), channel_id=1, source_target_pairs={{0,2},{2,4},{4,6},{6,8},{8,10},{10,12},{12,14},{14,16},{16,18},{18... | collective-permute-start | bytes 1622024 | tf_op jit(solution)/shard_map/ppermute | solution.py:19
  45.8 1.7 pad_maximum_fusion.top_ref.bottom_ref
  47.4 2.4 collective-permute-start.4
  49.8 3.5 %collective-permute-start.5 = (bf16[576,2048]{1,0:T(8,128)(2,1)S(1)}, bf16[576,2048]{1,0:T(8,128)(2,1)}, u32[]{:S(2)}, u32[]{:S(2)}) collective-permute-start(bf16[576,2048]{1,0:T(8,128)(2,1)S(1)} %pad_maximum_fusion.top_ref.bottom_ref), channel_id=1, source_target_pairs={{0,384},{128,0},{256,128},{384,256},{1,385},{129,1},{257,129},{385... | collective-permute-start | bytes 7077896 | tf_op jit(solution)/shard_map/ppermute | solution.py:19
  54.1 2.4 collective-permute-start.2
  57.0 1.2 fusion
  58.2 4.5 %all-to-all-start = ((bf16[8,8,4224]{2,1,0:T(8,128)(2,1)}), bf16[8,8,4224]{2,1,0:T(8,128)(2,1)S(1)}, u32[]{:S(2)}, u32[]{:S(2)}) async-start(bf16[8,8,4224]{2,1,0:T(8,128)(2,1)} %fusion), calls=%async_computation | async-start | bytes 1081344 | tf_op jit(solution)/shard_map/all_to_all | solution.py:130
  62.8 4.3 %collective-permute-start.3 = (bf16[32,4224]{1,0:T(8,128)(2,1)}, bf16[32,4224]{1,0:T(8,128)(2,1)S(1)}, u32[]{:S(2)}, u32[]{:S(2)}) collective-permute-start(bf16[32,4224]{1,0:T(8,128)(2,1)} %get-tuple-element.42), channel_id=1, source_target_pairs={{0,4},{2,6},{4,8},{6,10},{8,12},{10,14},{12,16},{14,18},{16,20},{1... | collective-permute-start | bytes 811016 | tf_op jit(solution)/shard_map/ppermute | solution.py:19
  67.1 1.1 constant_dynamic-update-slice_fusion.3
  68.2 1.1 constant_dynamic-update-slice_fusion.2
  70.3 6.3 %collective-permute-done.3 = bf16[32,4224]{1,0:T(8,128)(2,1)S(1)} collective-permute-done((bf16[32,4224]{1,0:T(8,128)(2,1)}, bf16[32,4224]{1,0:T(8,128)(2,1)S(1)}, u32[]{:S(2)}, u32[]{:S(2)}) %collective-permute-start.3) | collective-permute-done | bytes 270368 | tf_op jit(solution)/shard_map/ppermute | solution.py:19
  77.2 1.8 convolution_convert_fusion
  79.8 4.4 %all-to-all-start.1 = ((bf16[8,24,4224]{2,1,0:T(8,128)(2,1)}), bf16[8,24,4224]{2,1,0:T(8,128)(2,1)}, u32[]{:S(2)}, u32[]{:S(2)}) async-start(bf16[8,24,4224]{2,1,0:T(8,128)(2,1)} %bitcast.34), calls=%async_computation.1 | async-start | bytes 3244032 | tf_op jit(solution)/shard_map/all_to_all | solution.py:130
  84.2 13.4 %collective-permute-done.4.top_ref.bottom_ref = bf16[576,2048]{1,0:T(8,128)(2,1)} collective-permute-done((bf16[576,2048]{1,0:T(8,128)(2,1)S(1)}, bf16[576,2048]{1,0:T(8,128)(2,1)}, u32[]{:S(2)}, u32[]{:S(2)}) %collective-permute-start.4) | collective-permute-done | bytes 2359328 | tf_op jit(solution)/shard_map/ppermute | solution.py:19
  97.6 2.4 slice.88
  100.0 3.6 %collective-permute-start.6 = (bf16[288,2048]{1,0:T(8,128)(2,1)}, bf16[288,2048]{1,0:T(8,128)(2,1)S(1)}, u32[]{:S(2)}, u32[]{:S(2)}) collective-permute-start(bf16[288,2048]{1,0:T(8,128)(2,1)} %slice.88), channel_id=1, source_target_pairs={{0,128},{128,256},{256,384},{384,0},{1,129},{129,257},{257,385},{3... | collective-permute-start | bytes 3538952 | tf_op jit(solution)/shard_map/ppermute | solution.py:19
  103.6 2.4 slice.89
  106.1 2.2 collective-permute-start.7
  108.4 1.7 pad_maximum_fusion.1.rows_ref
  110.1 14.1 %collective-permute-done.6.top_ref = bf16[288,2048]{1,0:T(8,128)(2,1)S(1)} collective-permute-done((bf16[288,2048]{1,0:T(8,128)(2,1)}, bf16[288,2048]{1,0:T(8,128)(2,1)S(1)}, u32[]{:S(2)}, u32[]{:S(2)}) %collective-permute-start.6) | collective-permute-done | bytes 1179680 | tf_op jit(solution)/shard_map/ppermute | solution.py:19
  124.1 7.1 %collective-permute-done.7.bottom_ref = bf16[288,2048]{1,0:T(8,128)(2,1)} collective-permute-done((bf16[288,2048]{1,0:T(8,128)(2,1)}, bf16[288,2048]{1,0:T(8,128)(2,1)}, u32[]{:S(2)}, u32[]{:S(2)}) %collective-permute-start.7) | collective-permute-done | bytes 1179680 | tf_op jit(solution)/shard_map/ppermute | solution.py:19
  131.2 4.8 %shard_map.119 = (bf16[288,2048]{1,0:T(8,128)(2,1)}, bf16[288,2048]{1,0:T(8,128)(2,1)}, bf16[256,2048]{1,0:T(8,128)(2,1)S(1)}, f32[256,128]{1,0:T(8,128)S(1)}) custom-call(bf16[256,4224]{1,0:T(8,128)(2,1)S(1)} %pad_maximum_fusion.1.rows_ref, f32[1,128]{1,0:T(1,128)S(1)} %compare_convert_fusion.own_ref, bf16[288,2048]{1,0:T(8,128)(2,1)S(1)} %collective-permute-done.6.top_ref, ...), custom_call_target="tpu_custom_call" | custom-call | flops 2147483648 | bytes 9437184 | tf_op jit(solution)/shard_map/pallas_call | solution.py:104
  136.1 1.9 collective-permute-start.9
  138.1 4.1 %collective-permute-start.12 = (bf16[288,2048]{1,0:T(8,128)(2,1)}, bf16[288,2048]{1,0:T(8,128)(2,1)}, u32[]{:S(2)}, u32[]{:S(2)}) collective-permute-start(bf16[288,2048]{1,0:T(8,128)(2,1)} %get-tuple-element.34), channel_id=1, source_target_pairs={{0,384},{128,0},{256,128},{384,256},{1,385},{129,1},{257,129},{385... | collective-permute-start | bytes 3538952 | tf_op jit(solution)/shard_map/ppermute | solution.py:19
  142.2 5.0 %shard_map.120 = (bf16[288,2048]{1,0:T(8,128)(2,1)S(1)}, bf16[288,2048]{1,0:T(8,128)(2,1)}, bf16[256,2048]{1,0:T(8,128)(2,1)S(1)}, f32[256,128]{1,0:T(8,128)S(1)}) custom-call(bf16[256,4224]{1,0:T(8,128)(2,1)S(1)} %pad_maximum_fusion.1.rows_ref, f32[1,128]{1,0:T(1,128)S(1)} %compare_convert_fusion.own_ref, ...), custom_call_target="tpu_custom_call" | custom-call | flops 2147483648 | bytes 9437184 | tf_op jit(solution)/shard_map/pallas_call | solution.py:104
  148.3 4.8 %shard_map.121 = (bf16[288,2048]{1,0:T(8,128)(2,1)}, bf16[288,2048]{1,0:T(8,128)(2,1)S(1)}, bf16[256,2048]{1,0:T(8,128)(2,1)S(1)}, f32[256,128]{1,0:T(8,128)S(1)}) custom-call(bf16[256,4224]{1,0:T(8,128)(2,1)S(1)} %pad_maximum_fusion.1.rows_ref, f32[1,128]{1,0:T(1,128)S(1)} %compare_convert_fusion.own_ref, ...), custom_call_target="tpu_custom_call" | custom-call | flops 2147483648 | bytes 9437184 | tf_op jit(solution)/shard_map/pallas_call | solution.py:104
  153.1 3.3 %shard_map.122 = (bf16[288,2048]{1,0:T(8,128)(2,1)S(1)}, bf16[288,2048]{1,0:T(8,128)(2,1)S(1)}, bf16[256,2176]{1,0:T(8,128)(2,1)S(1)}) custom-call(bf16[256,4224]{1,0:T(8,128)(2,1)S(1)} %pad_maximum_fusion.1.rows_ref, f32[1,128]{1,0:T(1,128)S(1)} %compare_convert_fusion.own_ref, bf16[576,2048]{1,0:T(8,128)(2,1)S(1)} %pad_maximum_fusion.top_ref.bottom_ref, ...), custom_call_target="tpu_custom_call" | custom-call | flops 2147483648 | bytes 9437184 | tf_op jit(solution)/shard_map/pallas_call | solution.py:104
  159.5 2.3 reshape.274
  161.8 13.2 %all-to-all-start.2 = ((bf16[128,2,2176]{2,1,0:T(2,128)(2,1)}), bf16[128,2,2176]{2,1,0:T(2,128)(2,1)}, u32[]{:S(2)}, u32[]{:S(2)}) async-start(bf16[128,2,2176]{2,1,0:T(2,128)(2,1)} %reshape.274), calls=%async_computation.2 | async-start | bytes 2228224 | tf_op jit(solution)/shard_map/all_to_all | solution.py:188
  175.1 3.1 %collective-permute-start.11 = (bf16[288,2048]{1,0:T(8,128)(2,1)}, bf16[288,2048]{1,0:T(8,128)(2,1)}, u32[]{:S(2)}, u32[]{:S(2)}) collective-permute-start(bf16[288,2048]{1,0:T(8,128)(2,1)} %get-tuple-element.32), channel_id=1, source_target_pairs={{0,128},{128,256},{256,384},{384,0},{1,129},{129,257},{257,385},{3... | collective-permute-start | bytes 3538952 | tf_op jit(solution)/shard_map/ppermute | solution.py:19
  178.2 2.7 %collective-permute-start.8 = (bf16[288,2048]{1,0:T(8,128)(2,1)}, bf16[288,2048]{1,0:T(8,128)(2,1)}, u32[]{:S(2)}, u32[]{:S(2)}) collective-permute-start(bf16[288,2048]{1,0:T(8,128)(2,1)} %get-tuple-element.28), channel_id=1, source_target_pairs={{0,384},{128,0},{256,128},{384,256},{1,385},{129,1},{257,129},{385... | collective-permute-start | bytes 3538952 | tf_op jit(solution)/shard_map/ppermute | solution.py:19
  180.9 2.8 %add_convert_fusion.1 = bf16[288,2048]{1,0:T(8,128)(2,1)} fusion(bf16[288,2048]{1,0:T(8,128)(2,1)} %collective-permute-done.9, bf16[288,2048]{1,0:T(8,128)(2,1)S(1)} %copy-done.1), kind=kLoop, calls=%fused_computation.5 | loop fusion | flops 2359296 | bytes 3538944 | tf_op jit(solution)/shard_map/convert_element_type | solution.py:42
  183.7 4.3 %collective-permute-start.10 = (bf16[288,2048]{1,0:T(8,128)(2,1)}, bf16[288,2048]{1,0:T(8,128)(2,1)}, u32[]{:S(2)}, u32[]{:S(2)}) collective-permute-start(bf16[288,2048]{1,0:T(8,128)(2,1)} %add_convert_fusion.1), channel_id=1, source_target_pairs={{0,128},{128,256},{256,384},{384,0},{1,129},{129,257},{257,385},{3... | collective-permute-start | bytes 3538952 | tf_op jit(solution)/shard_map/ppermute | solution.py:19
  188.1 2.9 %add_convert_fusion = bf16[288,2048]{1,0:T(8,128)(2,1)} fusion(bf16[288,2048]{1,0:T(8,128)(2,1)} %collective-permute-done.12, bf16[288,2048]{1,0:T(8,128)(2,1)S(1)} %get-tuple-element.33), kind=kLoop, calls=%fused_computation.4 | loop fusion | flops 2359296 | bytes 3538944 | tf_op jit(solution)/shard_map/convert_element_type | solution.py:42
  191.0 2.3 collective-permute-start.13
  194.0 1.4 copy.28
  197.4 1.5 and.172
  199.6 1.5 eq.131
  201.1 9.4 %collective-permute-done.8 = bf16[288,2048]{1,0:T(8,128)(2,1)} collective-permute-done((bf16[288,2048]{1,0:T(8,128)(2,1)}, bf16[288,2048]{1,0:T(8,128)(2,1)}, u32[]{:S(2)}, u32[]{:S(2)}) %collective-permute-start.8) | collective-permute-done | bytes 1179680 | tf_op jit(solution)/shard_map/ppermute | solution.py:19
  210.5 19.4 %collective-permute-done.10 = bf16[288,2048]{1,0:T(8,128)(2,1)} collective-permute-done((bf16[288,2048]{1,0:T(8,128)(2,1)}, bf16[288,2048]{1,0:T(8,128)(2,1)}, u32[]{:S(2)}, u32[]{:S(2)}) %collective-permute-start.10) | collective-permute-done | bytes 1179680 | tf_op jit(solution)/shard_map/ppermute | solution.py:19
  230.0 1.3 add_convert_fusion.5
  231.3 2.7 %collective-permute-done.13 = bf16[288,2048]{1,0:T(8,128)(2,1)S(1)} collective-permute-done((bf16[288,2048]{1,0:T(8,128)(2,1)}, bf16[288,2048]{1,0:T(8,128)(2,1)S(1)}, u32[]{:S(2)}, u32[]{:S(2)}) %collective-permute-start.13) | collective-permute-done | bytes 1179680 | tf_op jit(solution)/shard_map/ppermute | solution.py:19
  234.0 1.1 add_convert_fusion.4
  236.0 2.4 fusion.7
  238.4 2.6 %fusion.6 = bf16[1,192,2048]{2,1,0:T(8,128)(2,1)} fusion(bf16[288,2048]{1,0:T(8,128)(2,1)} %collective-permute-done.10, bf16[288,2048]{1,0:T(8,128)(2,1)} %collective-permute-done.8, bf16[288,2048]{1,0:T(8,128)(2,1)S(1)} %copy-done.3), kind=kLoop, calls=%fused_computation.18 | loop fusion | flops 2359296 | bytes 3145728 | tf_op jit(solution)/shard_map/broadcast_in_dim | solution.py:208
  241.1 1.5 reshape.275
  (80 shorter events, 19.3 us)
Async XLA Ops:
  1.4 0.8 copy-start.11
  2.2 43.6 %copy-start.8 = (bf16[1,192,2048]{2,1,0:T(8,128)(2,1)S(1)}, bf16[1,192,2048]{2,1,0:T(8,128)(2,1)}, u32[]{:S(2)}) copy-start(bf16[1,192,2048]{2,1,0:T(8,128)(2,1)} %param.15) | copy-start | bytes 2359300
  39.9 22.9 %collective-permute-start = (bf16[64,4224]{1,0:T(8,128)(2,1)S(1)}, bf16[64,4224]{1,0:T(8,128)(2,1)}, u32[]{:S(2)}, u32[]{:S(2)}) collective-permute-start(bf16[64,4224]{1,0:T(8,128)(2,1)S(1)} %all_gather.3), channel_id=1, source_target_pairs={{0,30},{2,0},{4,2},{6,4},{8,6},{10,8},{12,10},{14,12},{16,14},{18,... | collective-permute-start | bytes 1622024 | tf_op jit(solution)/shard_map/ppermute | solution.py:19
  41.8 26.4 %collective-permute-start.1 = (bf16[64,4224]{1,0:T(8,128)(2,1)S(1)}, bf16[64,4224]{1,0:T(8,128)(2,1)}, u32[]{:S(2)}, u32[]{:S(2)}) collective-permute-start(bf16[64,4224]{1,0:T(8,128)(2,1)S(1)} %all_gather.3), channel_id=1, source_target_pairs={{0,2},{2,4},{4,6},{6,8},{8,10},{10,12},{12,14},{14,16},{16,18},{18... | collective-permute-start | bytes 1622024 | tf_op jit(solution)/shard_map/ppermute | solution.py:19
  47.4 50.2 %collective-permute-start.4 = (bf16[576,2048]{1,0:T(8,128)(2,1)S(1)}, bf16[576,2048]{1,0:T(8,128)(2,1)}, u32[]{:S(2)}, u32[]{:S(2)}) collective-permute-start(bf16[576,2048]{1,0:T(8,128)(2,1)S(1)} %pad_maximum_fusion.top_ref.bottom_ref), channel_id=1, source_target_pairs={{0,128},{128,256},{256,384},{384,0},{1,129},{129,257},{257,385},{3... | collective-permute-start | bytes 7077896 | tf_op jit(solution)/shard_map/ppermute | solution.py:19
  49.8 53.8 %collective-permute-start.5 = (bf16[576,2048]{1,0:T(8,128)(2,1)S(1)}, bf16[576,2048]{1,0:T(8,128)(2,1)}, u32[]{:S(2)}, u32[]{:S(2)}) collective-permute-start(bf16[576,2048]{1,0:T(8,128)(2,1)S(1)} %pad_maximum_fusion.top_ref.bottom_ref), channel_id=1, source_target_pairs={{0,384},{128,0},{256,128},{384,256},{1,385},{129,1},{257,129},{385... | collective-permute-start | bytes 7077896 | tf_op jit(solution)/shard_map/ppermute | solution.py:19
  54.1 15.2 %collective-permute-start.2 = (bf16[32,4224]{1,0:T(8,128)(2,1)}, bf16[32,4224]{1,0:T(8,128)(2,1)}, u32[]{:S(2)}, u32[]{:S(2)}) collective-permute-start(bf16[32,4224]{1,0:T(8,128)(2,1)} %get-tuple-element.43), channel_id=1, source_target_pairs={{0,28},{2,30},{4,0},{6,2},{8,4},{10,6},{12,8},{14,10},{16,12},{18,... | collective-permute-start | bytes 811016 | tf_op jit(solution)/shard_map/ppermute | solution.py:19
  58.2 20.8 %all-to-all-start = ((bf16[8,8,4224]{2,1,0:T(8,128)(2,1)}), bf16[8,8,4224]{2,1,0:T(8,128)(2,1)S(1)}, u32[]{:S(2)}, u32[]{:S(2)}) async-start(bf16[8,8,4224]{2,1,0:T(8,128)(2,1)} %fusion), calls=%async_computation | async-start | bytes 1081344 | tf_op jit(solution)/shard_map/all_to_all | solution.py:130
  62.8 13.9 %collective-permute-start.3 = (bf16[32,4224]{1,0:T(8,128)(2,1)}, bf16[32,4224]{1,0:T(8,128)(2,1)S(1)}, u32[]{:S(2)}, u32[]{:S(2)}) collective-permute-start(bf16[32,4224]{1,0:T(8,128)(2,1)} %get-tuple-element.42), channel_id=1, source_target_pairs={{0,4},{2,6},{4,8},{6,10},{8,12},{10,14},{12,16},{14,18},{16,20},{1... | collective-permute-start | bytes 811016 | tf_op jit(solution)/shard_map/ppermute | solution.py:19
  79.0 0.8 copy-start.7
  79.8 28.6 %all-to-all-start.1 = ((bf16[8,24,4224]{2,1,0:T(8,128)(2,1)}), bf16[8,24,4224]{2,1,0:T(8,128)(2,1)}, u32[]{:S(2)}, u32[]{:S(2)}) async-start(bf16[8,24,4224]{2,1,0:T(8,128)(2,1)} %bitcast.34), calls=%async_computation.1 | async-start | bytes 3244032 | tf_op jit(solution)/shard_map/all_to_all | solution.py:130
  100.0 24.1 %collective-permute-start.6 = (bf16[288,2048]{1,0:T(8,128)(2,1)}, bf16[288,2048]{1,0:T(8,128)(2,1)S(1)}, u32[]{:S(2)}, u32[]{:S(2)}) collective-permute-start(bf16[288,2048]{1,0:T(8,128)(2,1)} %slice.88), channel_id=1, source_target_pairs={{0,128},{128,256},{256,384},{384,0},{1,129},{129,257},{257,385},{3... | collective-permute-start | bytes 3538952 | tf_op jit(solution)/shard_map/ppermute | solution.py:19
  106.1 25.1 %collective-permute-start.7 = (bf16[288,2048]{1,0:T(8,128)(2,1)}, bf16[288,2048]{1,0:T(8,128)(2,1)}, u32[]{:S(2)}, u32[]{:S(2)}) collective-permute-start(bf16[288,2048]{1,0:T(8,128)(2,1)} %slice.89), channel_id=1, source_target_pairs={{0,384},{128,0},{256,128},{384,256},{1,385},{129,1},{257,129},{385... | collective-permute-start | bytes 3538952 | tf_op jit(solution)/shard_map/ppermute | solution.py:19
  136.1 44.9 %collective-permute-start.9 = (bf16[288,2048]{1,0:T(8,128)(2,1)}, bf16[288,2048]{1,0:T(8,128)(2,1)}, u32[]{:S(2)}, u32[]{:S(2)}) collective-permute-start(bf16[288,2048]{1,0:T(8,128)(2,1)} %get-tuple-element.30), channel_id=1, source_target_pairs={{0,128},{128,256},{256,384},{384,0},{1,129},{129,257},{257,385},{3... | collective-permute-start | bytes 3538952 | tf_op jit(solution)/shard_map/ppermute | solution.py:19
  138.1 50.0 %collective-permute-start.12 = (bf16[288,2048]{1,0:T(8,128)(2,1)}, bf16[288,2048]{1,0:T(8,128)(2,1)}, u32[]{:S(2)}, u32[]{:S(2)}) collective-permute-start(bf16[288,2048]{1,0:T(8,128)(2,1)} %get-tuple-element.34), channel_id=1, source_target_pairs={{0,384},{128,0},{256,128},{384,256},{1,385},{129,1},{257,129},{385... | collective-permute-start | bytes 3538952 | tf_op jit(solution)/shard_map/ppermute | solution.py:19
  147.2 1.1 copy-start
  156.4 1.0 copy-start.2
  157.5 1.0 copy-start.4
  158.5 1.0 copy-start.6
  161.8 19.1 %copy-start.1 = (bf16[288,2048]{1,0:T(8,128)(2,1)S(1)}, bf16[288,2048]{1,0:T(8,128)(2,1)}, u32[]{:S(2)}) copy-start(bf16[288,2048]{1,0:T(8,128)(2,1)} %copy-done) | copy-start | bytes 3538948
  161.8 79.3 %all-to-all-start.2 = ((bf16[128,2,2176]{2,1,0:T(2,128)(2,1)}), bf16[128,2,2176]{2,1,0:T(2,128)(2,1)}, u32[]{:S(2)}, u32[]{:S(2)}) async-start(bf16[128,2,2176]{2,1,0:T(2,128)(2,1)} %reshape.274), calls=%async_computation.2 | async-start | bytes 2228224 | tf_op jit(solution)/shard_map/all_to_all | solution.py:188
  175.1 56.2 %collective-permute-start.11 = (bf16[288,2048]{1,0:T(8,128)(2,1)}, bf16[288,2048]{1,0:T(8,128)(2,1)}, u32[]{:S(2)}, u32[]{:S(2)}) collective-permute-start(bf16[288,2048]{1,0:T(8,128)(2,1)} %get-tuple-element.32), channel_id=1, source_target_pairs={{0,128},{128,256},{256,384},{384,0},{1,129},{129,257},{257,385},{3... | collective-permute-start | bytes 3538952 | tf_op jit(solution)/shard_map/ppermute | solution.py:19
  178.2 32.3 %collective-permute-start.8 = (bf16[288,2048]{1,0:T(8,128)(2,1)}, bf16[288,2048]{1,0:T(8,128)(2,1)}, u32[]{:S(2)}, u32[]{:S(2)}) collective-permute-start(bf16[288,2048]{1,0:T(8,128)(2,1)} %get-tuple-element.28), channel_id=1, source_target_pairs={{0,384},{128,0},{256,128},{384,256},{1,385},{129,1},{257,129},{385... | collective-permute-start | bytes 3538952 | tf_op jit(solution)/shard_map/ppermute | solution.py:19
  183.7 46.2 %collective-permute-start.10 = (bf16[288,2048]{1,0:T(8,128)(2,1)}, bf16[288,2048]{1,0:T(8,128)(2,1)}, u32[]{:S(2)}, u32[]{:S(2)}) collective-permute-start(bf16[288,2048]{1,0:T(8,128)(2,1)} %add_convert_fusion.1), channel_id=1, source_target_pairs={{0,128},{128,256},{256,384},{384,0},{1,129},{129,257},{257,385},{3... | collective-permute-start | bytes 3538952 | tf_op jit(solution)/shard_map/ppermute | solution.py:19
  188.1 41.9 %copy-start.3 = (bf16[288,2048]{1,0:T(8,128)(2,1)S(1)}, bf16[288,2048]{1,0:T(8,128)(2,1)}, u32[]{:S(2)}) copy-start(bf16[288,2048]{1,0:T(8,128)(2,1)} %copy-done.2) | copy-start | bytes 3538948
  191.0 43.0 %copy-start.5 = (bf16[288,2048]{1,0:T(8,128)(2,1)S(1)}, bf16[288,2048]{1,0:T(8,128)(2,1)}, u32[]{:S(2)}) copy-start(bf16[288,2048]{1,0:T(8,128)(2,1)} %copy-done.4) | copy-start | bytes 3538948
  191.0 43.0 %collective-permute-start.13 = (bf16[288,2048]{1,0:T(8,128)(2,1)}, bf16[288,2048]{1,0:T(8,128)(2,1)S(1)}, u32[]{:S(2)}, u32[]{:S(2)}) collective-permute-start(bf16[288,2048]{1,0:T(8,128)(2,1)} %add_convert_fusion), channel_id=1, source_target_pairs={{0,384},{128,0},{256,128},{384,256},{1,385},{129,1},{257,129},{385... | collective-permute-start | bytes 3538952 | tf_op jit(solution)/shard_map/ppermute | solution.py:19
  241.1 1.9 copy-start.9
  241.1 2.3 copy-start.12
  241.1 3.2 %copy-start.10 = (pred[16,256]{0,1:T(32,128)(4,1)S(1)}, pred[16,256]{0,1:T(32,128)(4,1)}, u32[]{:S(2)}) copy-start(pred[16,256]{0,1:T(32,128)(4,1)} %and.172) | copy-start | bytes 12292
  241.1 3.2 %copy-start.13 = (s32[256]{0:T(256)S(1)}, s32[256]{0:T(256)}, u32[]{:S(2)}) copy-start(s32[256]{0:T(256)} %eq.131) | copy-start | bytes 3076

commit v3 on v2

--- a/solution.py
+++ b/solution.py
@@ -12,6 +12,8 @@
 STRIDE = 4
 YC = Y * CORE
 CAP = 2
+VM = 28
+SUM_FLOPS = 10**12
 F32, BF16 = jnp.float32, jnp.bfloat16
 
 
@@ -35,14 +37,56 @@
     half = mine.shape[0] // 2
     from_prev, from_next = shift(mine, "dp", DP, 1), shift(mine, "dp", DP, -1)
     top, bottom = shift(from_prev[:half], "dp", DP, 1), shift(from_next[half:], "dp", DP, -1)
-    return from_next, from_prev, top, bottom
-
-
-def add(a, b):
-    return (a.astype(F32) + b.astype(F32)).astype(BF16)
-
-
-def block_kernel(last, rows_ref, own_ref, top_ref, bottom_ref, comb_ref, *refs):
+    return (from_next,), (from_prev,), (top, bottom)
+
+
+def sum_kernel(n_ref, from_far_top, p_ref, from_far_bottom, _, __, gate_ref, low_ref, high_ref, down_ref):
+    step = pl.program_id(0)
+    top = (n_ref[...].astype(F32) + from_far_top[...].astype(F32)).astype(BF16)
+    bottom = (p_ref[...].astype(F32) + from_far_bottom[...].astype(F32)).astype(BF16)
+
+    @pl.when(step < 2)
+    def _():
+        gate_ref[...] = top
+
+    @pl.when(step == 2)
+    def _():
+        low_ref[...] = top
+
+    @pl.when(step == 0)
+    def _():
+        high_ref[...] = bottom
+
+    @pl.when(step > 0)
+    def _():
+        down_ref[...] = bottom
+
+
+def forward_sums(n_top, from_far_top, p_bottom, from_far_bottom, *arrived):
+    half, width = n_top.shape
+    part = half // 3
+    block = (part, width)
+    walk = pl.BlockSpec(block, lambda i: (i, 0))
+    one = pl.BlockSpec(block, lambda i: (0, 0))
+    sds = jax.ShapeDtypeStruct
+    return pl.pallas_call(
+        sum_kernel,
+        grid=(3,),
+        in_specs=[walk] * 4 + [pl.BlockSpec(memory_space=pl.ANY)] * 2,
+        out_specs=[
+            pl.BlockSpec(block, lambda i: (jnp.minimum(i, 1), 0)),
+            one,
+            one,
+            pl.BlockSpec(block, lambda i: (jnp.maximum(i - 1, 0), 0)),
+        ],
+        out_shape=[sds((k * part, width), BF16) for k in (2, 1, 1, 2)],
+        compiler_params=pltpu.CompilerParams(vmem_limit_bytes=16 * 2**20),
+        cost_estimate=pl.CostEstimate(flops=SUM_FLOPS, bytes_accessed=2**20, transcendentals=0),
+    )(n_top, from_far_top, p_bottom, from_far_bottom, *arrived)
+
+
+def block_kernel(last, count, *refs):
+    rows, (own_ref, top_ref, bottom_ref, comb_ref), refs = refs[:count], refs[count : count + 4], refs[count + 4 :]
     if last:
         part_a, part_b, part_c, perm_ref, d_top, d_bottom, back_ref = refs
     else:
@@ -51,9 +95,10 @@
     half = top_ref.shape[0]
     share = 2 * half // 3
     rest = half - share
-    x = rows_ref[:, :width]
-    grad = rows_ref[:, width : 2 * width]
-    weight = jnp.sum(rows_ref[:, 2 * width :].astype(F32) * own_ref[...], axis=1, keepdims=True)
+    take = lambda a, b: jnp.concatenate([r[:, a:b] for r in rows], axis=0)
+    x = take(0, width)
+    grad = take(width, 2 * width)
+    weight = jnp.sum(take(2 * width, 2 * width + 128).astype(F32) * own_ref[...], axis=1, keepdims=True)
     w_gate = top_ref[:share]
     w_up = jnp.concatenate([top_ref[share:], bottom_ref[:rest]], axis=0)
     w_down = bottom_ref[rest:]
@@ -89,27 +134,28 @@
 
 
 def expert_block(rows, own, weights, comb, last=()):
-    n, width = rows.shape[0], weights[0].shape[1]
+    n = sum(r.shape[0] for r in rows)
+    whole = lambda a: pl.BlockSpec(a.shape, lambda i: (0,) * len(a.shape))
     if len(weights) == 1:
-        half = weights[0].shape[0] // 2
+        half, width = weights[0].shape[0] // 2, weights[0].shape[1]
         w_specs = [pl.BlockSpec((half, width), lambda i, k=k: (k, 0)) for k in range(2)]
         weights = weights * 2
     else:
-        half = weights[0].shape[0]
-        w_specs = [pl.BlockSpec((half, width), lambda i: (0, 0))] * 2
-    whole = lambda a: pl.BlockSpec(a.shape, lambda i: (0,) * a.ndim)
+        half, width = weights[0].shape
+        w_specs = [whole(w) for w in weights]
+    operands = (*rows, own, *weights, comb, *last)
     sds = jax.ShapeDtypeStruct
-    out = [sds((half, width), BF16), sds((half, width), BF16)]
+    out = [pltpu.HBM((half, width), BF16), pltpu.HBM((half, width), BF16)]
     out += [sds((n, width + 128), BF16)] if last else [sds((n, width), BF16), sds((n, 128), F32)]
     return pl.pallas_call(
-        functools.partial(block_kernel, bool(last)),
+        functools.partial(block_kernel, bool(last), len(rows)),
         grid=(1,),
         out_shape=out,
-        in_specs=[whole(rows), whole(own), *w_specs, whole(comb), *[whole(a) for a in last]],
+        in_specs=[*[whole(r) for r in rows], whole(own), *w_specs, whole(comb), *[whole(a) for a in last]],
         out_specs=[whole(o) for o in out],
-        compiler_params=pltpu.CompilerParams(vmem_limit_bytes=40 * 2**20),
+        compiler_params=pltpu.CompilerParams(vmem_limit_bytes=VM * 2**20),
         cost_estimate=pl.CostEstimate(flops=2 * 8 * n * 256 * width, bytes_accessed=9 * 2**20, transcendentals=n * 192),
-    )(rows, own, *weights, comb, *last)
+    )(*operands)
 
 
 def dispatch(chunk, z, tokens, width):
@@ -139,7 +185,7 @@
     z = lax.axis_index("z")
     yc = lax.axis_index("y") * CORE + lax.axis_index("core")
     mine = jnp.concatenate([w_gate[0], w_up[0], w_down[0]], axis=0)
-    w_next, w_prev, far_top, far_bottom = gather_weights(mine)
+    w_next, w_prev, w_far = gather_weights(mine)
 
     x = (
         (x_codes.astype(F32).reshape(tokens, width // BLOCK, BLOCK) * x_scales.astype(F32)[:, :, None])
@@ -151,39 +197,35 @@
     dense = jnp.sum(names * combine.astype(F32)[:, :, None], axis=1)
     payload = jnp.concatenate([x, grad_out, dense.astype(BF16)], axis=1)
     groups = [list(range(r, Z, STRIDE)) for r in range(STRIDE)]
-    seen = lax.all_gather(payload, "z", axis=0, tiled=True, axis_index_groups=groups)
+    copies = jnp.broadcast_to(payload, (Z // STRIDE, *payload.shape))
+    seen = lax.all_to_all(copies, "z", split_axis=0, concat_axis=0, axis_index_groups=groups, tiled=True)
+    seen = seen.reshape(-1, payload.shape[1])
     mid = seen.shape[0] // 2
-    others = (
-        shift(seen, "z", Z, -1),
-        shift(seen, "z", Z, 1),
-        shift(seen[:mid], "z", Z, -2),
-        shift(seen[mid:], "z", Z, 2),
-    )
-    first = dispatch(seen, z, tokens, width)
-    rows = jnp.concatenate([first, dispatch(jnp.concatenate(others, axis=0), z, tokens, width)], axis=0)
+    ahead, behind = shift(seen, "z", Z, -1), shift(seen, "z", Z, 1)
+    across = jnp.concatenate([shift(seen[:mid], "z", Z, -2), shift(seen[mid:], "z", Z, 2)], axis=0)
+    rows = tuple(dispatch(c, z, tokens, width) for c in (seen, ahead, behind, across))
 
     own = (lax.broadcasted_iota(jnp.int32, (1, experts), 1) == yc * Z + z).astype(F32)
-    comb = jnp.zeros((rows.shape[0], 128), F32)
-    f_top, f_bottom, part_f, comb = expert_block(rows, own, (far_top, far_bottom), comb)
-    n_top, n_bottom, part_n, comb = expert_block(rows, own, (w_next,), comb)
-    p_top, p_bottom, part_p, comb = expert_block(rows, own, (w_prev,), comb)
-    q = lax.broadcasted_iota(jnp.int32, (rows.shape[0], 1), 0)
-    q_yc, q_z, q_cap = q // (Z * CAP), q // CAP % Z, q % CAP
-    kind = (q_z - z + Z) % STRIDE
-    per = Z // STRIDE * CAP
-    place = q_z // STRIDE * CAP + q_cap
-    at = jnp.where(
-        kind == 0,
-        q_yc * per + place,
-        YC * per + q_yc * 3 * per + jnp.where(kind == 1, 0, jnp.where(kind == 3, per, 2 * per)) + place,
-    )
-    perm = (at == lax.broadcasted_iota(jnp.int32, (rows.shape[0], rows.shape[0]), 1)).astype(BF16)
+    count = YC * Z * CAP
+    comb = jnp.zeros((count, 128), F32)
+    f_top, f_bottom, part_f, comb = expert_block(rows, own, w_far, comb)
+    n_top, n_bottom, part_n, comb = expert_block(rows, own, w_next, comb)
+    p_top, p_bottom, part_p, comb = expert_block(rows, own, w_prev, comb)
+    q = lax.broadcasted_iota(jnp.int32, (count, 1), 0)
+    q_yc, q_cap = q // (Z * CAP), q % CAP
+    q_z = q // CAP % Z
+    kind, index = (q_z - z + Z) % STRIDE, q_z // STRIDE
+    base = jnp.where(kind == 0, 0, jnp.where(kind == 1, 1, jnp.where(kind == 3, 2, 3)))
+    at = base * (count // STRIDE) + q_yc * (STRIDE * CAP) + index * CAP + q_cap
+    perm = (at == lax.broadcasted_iota(jnp.int32, (count, count), 1)).astype(BF16)
     o_top, o_bottom, back = expert_block(rows, own, (mine,), comb, (part_f, part_n, part_p, perm))
 
     got_f_top, got_f_bottom = shift(f_top, "dp", DP, 1), shift(f_bottom, "dp", DP, -1)
     got_n_bottom, got_p_top = shift(n_bottom, "dp", DP, 1), shift(p_top, "dp", DP, -1)
-    got_n_top = shift(add(n_top, got_f_top), "dp", DP, 1)
-    got_p_bottom = shift(add(p_bottom, got_f_bottom), "dp", DP, -1)
+    rest = f_top.shape[0] - share
+    gate, low, high, down = forward_sums(n_top, got_f_top, p_bottom, got_f_bottom, got_n_bottom, got_p_top)
+    got_gate, got_down = shift(gate, "dp", DP, 1), shift(down, "dp", DP, -1)
+    got_low, got_high = shift(low, "dp", DP, 1), shift(high, "dp", DP, -1)
 
     home = lax.all_to_all(
         back.reshape(experts, CAP, -1), ("y", "core", "z"), split_axis=0, concat_axis=0, tiled=True
@@ -199,13 +241,14 @@
     of_expert = jnp.sum((owner.astype(F32) * comb_rows[None, :]).reshape(tokens, experts, CAP), axis=2)
     grad_combine = jnp.sum(names * of_expert[:, None, :], axis=2)
 
-    rest = f_top.shape[0] - share
-    top = lambda s: (o_top[s].astype(F32) + got_p_top[s].astype(F32) + got_n_top[s].astype(F32)).astype(BF16)
-    bottom = lambda s: (
-        o_bottom[s].astype(F32) + got_n_bottom[s].astype(F32) + got_p_bottom[s].astype(F32)
-    ).astype(BF16)
-    grad_up = jnp.concatenate([top(slice(share, None)), bottom(slice(0, rest))], axis=0)
-    return grad_in, grad_combine, top(slice(0, share))[None], grad_up[None], bottom(slice(rest, None))[None]
+    got_low, got_high, grad_in, grad_combine = lax.optimization_barrier((got_low, got_high, grad_in, grad_combine))
+    three = lambda a, b, c: (a.astype(F32) + b.astype(F32) + c.astype(F32)).astype(BF16)
+    grad_gate = three(o_top[:share], got_p_top[:share], got_gate)
+    grad_down = three(o_bottom[rest:], got_n_bottom[rest:], got_down)
+    low = three(o_top[share:], got_p_top[share:], got_low)
+    high = three(o_bottom[:rest], got_n_bottom[:rest], got_high)
+    grad_up = jnp.concatenate([low, high], axis=0)
+    return grad_in, grad_combine, grad_gate[None], grad_up[None], grad_down[None]
 
 
 def solution(mesh):

time: 247 us -> 261 us (1.057)
  the two profiles are of different devices: /device:TPU:6 before, /device:TPU:65 now
where the time goes in v3:
time: 261 us; the launch traced here: 259 us
  starting transfers between devices  102 us (39%)
  waiting for transfers between devices  85.6 us (33%)
  Pallas kernels  25.7 us (10%)
  local copies, waits for them, and re-layouts  17.3 us (7%)
  other arithmetic  14.6 us (6%)
  matrix products  12.5 us (5%)
    ppermute x16, starting transfers between devices, shift(): return lax.ppermute(a, axis, [(i, (i + k) % size) for i in range(size)])  53.6 us
    ppermute x16, waiting for transfers between devices, shift(): return lax.ppermute(a, axis, [(i, (i + k) % size) for i in range(size)])  32.3 us
    all_to_all x4, starting transfers between devices, dispatch(): lax.all_to_all(sent.reshape(YC, slots, -1), ('y', 'core'), split_axis=0,...  23.7 us
    all_to_all x1, waiting for transfers between devices, body(): lax.all_to_all(copies, 'z', split_axis=0, concat_axis=0, axis_index_group...  22.1 us
    pallas_call x4, Pallas kernels, expert_block(): pl.pallas_call(functools.partial(block_kernel, bool(last), len(rows)), gr...  21.9 us
    all_to_all x4, waiting for transfers between devices, dispatch(): lax.all_to_all(sent.reshape(YC, slots, -1), ('y', 'core'), split_axis=0,...  16.2 us
    all_to_all x1, waiting for transfers between devices, body(): lax.all_to_all(back.reshape(experts, CAP, -1), ('y', 'core', 'z'), split_...  15 us
    all_to_all x1, starting transfers between devices, body(): lax.all_to_all(copies, 'z', split_axis=0, concat_axis=0, axis_index_group...  13 us
  transfers between devices with their start and end apart: 22, of which 9 were waited for; matrix products, arithmetic and copies ran while one was open for 12% of the time, Pallas kernels for 8%

profile of v3, /device:TPU:65, one launch (start us, length us, event | category | flops | bytes accessed | tf_op | source)
XLA Modules:
  0.0 259.2 jit_solution(5257738268839693184)
XLA Ops:
  6.3 13.0 %all-to-all-start = ((bf16[4,16,4224]{2,1,0:T(8,128)(2,1)}), bf16[4,16,4224]{2,1,0:T(8,128)(2,1)}, u32[]{:S(2)}, u32[]{:S(2)}) async-start(bf16[4,16,4224]{2,1,0:T(8,128)(2,1)} %broadcast_in_dim.24), calls=%async_computation | async-start | bytes 1081344 | tf_op jit(solution)/shard_map/all_to_all | solution.py:201
  19.3 1.6 pad_maximum_fusion.refs_5_.refs_6_
  20.9 4.4 %collective-permute-start.4 = (bf16[576,2048]{1,0:T(8,128)(2,1)S(1)}, bf16[576,2048]{1,0:T(8,128)(2,1)}, u32[]{:S(2)}, u32[]{:S(2)}) collective-permute-start(bf16[576,2048]{1,0:T(8,128)(2,1)S(1)} %pad_maximum_fusion.refs_5_.refs_6_), channel_id=1, source_target_pairs={{0,384},{128,0},{256,128},{384,256},{1,385},{129,1},{257,129},{385... | collective-permute-start | bytes 7077896 | tf_op jit(solution)/shard_map/ppermute | solution.py:21
  25.3 1.9 collective-permute-start.5
  27.4 22.1 %all-to-all-done = bf16[4,16,4224]{2,1,0:T(8,128)(2,1)} async-done(((bf16[4,16,4224]{2,1,0:T(8,128)(2,1)}), bf16[4,16,4224]{2,1,0:T(8,128)(2,1)}, u32[]{:S(2)}, u32[]{:S(2)}) %all-to-all-start) | async-done | bytes 540704 | tf_op jit(solution)/shard_map/all_to_all | solution.py:201
  49.5 2.7 %collective-permute-start = (bf16[64,4224]{1,0:T(8,128)(2,1)}, bf16[64,4224]{1,0:T(8,128)(2,1)}, u32[]{:S(2)}, u32[]{:S(2)}) collective-permute-start(bf16[64,4224]{1,0:T(8,128)(2,1)} %bitcast), channel_id=1, source_target_pairs={{0,30},{2,0},{4,2},{6,4},{8,6},{10,8},{12,10},{14,12},{16,14},{18,... | collective-permute-start | bytes 1622024 | tf_op jit(solution)/shard_map/ppermute | solution.py:21
  52.1 2.6 %collective-permute-start.1 = (bf16[64,4224]{1,0:T(8,128)(2,1)}, bf16[64,4224]{1,0:T(8,128)(2,1)}, u32[]{:S(2)}, u32[]{:S(2)}) collective-permute-start(bf16[64,4224]{1,0:T(8,128)(2,1)} %bitcast), channel_id=1, source_target_pairs={{0,2},{2,4},{4,6},{6,8},{8,10},{10,12},{12,14},{14,16},{16,18},{18... | collective-permute-start | bytes 1622024 | tf_op jit(solution)/shard_map/ppermute | solution.py:21
  55.7 1.8 fusion.83
  57.4 2.4 collective-permute-start.2
  60.1 2.1 fusion
  62.2 8.3 %all-to-all-start.1 = ((bf16[8,8,4224]{2,1,0:T(8,128)(2,1)}), bf16[8,8,4224]{2,1,0:T(8,128)(2,1)S(1)}, u32[]{:S(2)}, u32[]{:S(2)}) async-start(bf16[8,8,4224]{2,1,0:T(8,128)(2,1)} %fusion), calls=%async_computation.1 | async-start | bytes 1081344 | tf_op jit(solution)/shard_map/all_to_all | solution.py:176
  70.5 4.5 %collective-permute-done.2 = bf16[32,4224]{1,0:T(8,128)(2,1)S(1)} collective-permute-done((bf16[32,4224]{1,0:T(8,128)(2,1)}, bf16[32,4224]{1,0:T(8,128)(2,1)S(1)}, u32[]{:S(2)}, u32[]{:S(2)}) %collective-permute-start.2) | collective-permute-done | bytes 270368 | tf_op jit(solution)/shard_map/ppermute | solution.py:21
  75.1 6.3 %collective-permute-start.3 = (bf16[32,4224]{1,0:T(8,128)(2,1)S(1)}, bf16[32,4224]{1,0:T(8,128)(2,1)S(1)}, u32[]{:S(2)}, u32[]{:S(2)}) collective-permute-start(bf16[32,4224]{1,0:T(8,128)(2,1)S(1)} %bitcast.69), channel_id=1, source_target_pairs={{0,4},{2,6},{4,8},{6,10},{8,12},{10,14},{12,16},{14,18},{16,20},{1... | collective-permute-start | bytes 811016 | tf_op jit(solution)/shard_map/ppermute | solution.py:21
  81.4 9.7 %collective-permute-done.3 = bf16[32,4224]{1,0:T(8,128)(2,1)S(1)} collective-permute-done((bf16[32,4224]{1,0:T(8,128)(2,1)S(1)}, bf16[32,4224]{1,0:T(8,128)(2,1)S(1)}, u32[]{:S(2)}, u32[]{:S(2)}) %collective-permute-start.3) | collective-permute-done | bytes 270368 | tf_op jit(solution)/shard_map/ppermute | solution.py:21
  92.7 5.1 %all-to-all-start.4 = ((bf16[8,8,4224]{2,1,0:T(8,128)(2,1)}), bf16[8,8,4224]{2,1,0:T(8,128)(2,1)S(1)}, u32[]{:S(2)}, u32[]{:S(2)}) async-start(bf16[8,8,4224]{2,1,0:T(8,128)(2,1)} %fusion.3), calls=%async_computation.4 | async-start | bytes 1081344 | tf_op jit(solution)/shard_map/all_to_all | solution.py:176
  98.9 2.5 slice.90
  101.4 3.2 %collective-permute-start.6 = (bf16[288,2048]{1,0:T(8,128)(2,1)}, bf16[288,2048]{1,0:T(8,128)(2,1)}, u32[]{:S(2)}, u32[]{:S(2)}) collective-permute-start(bf16[288,2048]{1,0:T(8,128)(2,1)} %slice.90), channel_id=1, source_target_pairs={{0,128},{128,256},{256,384},{384,0},{1,129},{129,257},{257,385},{3... | collective-permute-start | bytes 3538952 | tf_op jit(solution)/shard_map/ppermute | solution.py:21
  104.6 2.5 slice.91
  107.1 3.2 %collective-permute-start.7 = (bf16[288,2048]{1,0:T(8,128)(2,1)}, bf16[288,2048]{1,0:T(8,128)(2,1)}, u32[]{:S(2)}, u32[]{:S(2)}) collective-permute-start(bf16[288,2048]{1,0:T(8,128)(2,1)} %slice.91), channel_id=1, source_target_pairs={{0,384},{128,0},{256,128},{384,256},{1,385},{129,1},{257,129},{385... | collective-permute-start | bytes 3538952 | tf_op jit(solution)/shard_map/ppermute | solution.py:21
  110.4 2.2 fusion.1
  112.6 5.4 %all-to-all-start.2 = ((bf16[8,8,4224]{2,1,0:T(8,128)(2,1)}), bf16[8,8,4224]{2,1,0:T(8,128)(2,1)}, u32[]{:S(2)}, u32[]{:S(2)}) async-start(bf16[8,8,4224]{2,1,0:T(8,128)(2,1)} %fusion.1), calls=%async_computation.2 | async-start | bytes 1081344 | tf_op jit(solution)/shard_map/all_to_all | solution.py:176
  119.0 2.2 fusion.2
  121.2 6.4 %all-to-all-done.2 = bf16[8,8,4224]{2,1,0:T(8,128)(2,1)} async-done(((bf16[8,8,4224]{2,1,0:T(8,128)(2,1)}), bf16[8,8,4224]{2,1,0:T(8,128)(2,1)}, u32[]{:S(2)}, u32[]{:S(2)}) %all-to-all-start.2) | async-done | bytes 540704 | tf_op jit(solution)/shard_map/all_to_all | solution.py:176
  127.7 4.9 %all-to-all-start.3 = ((bf16[8,8,4224]{2,1,0:T(8,128)(2,1)}), bf16[8,8,4224]{2,1,0:T(8,128)(2,1)}, u32[]{:S(2)}, u32[]{:S(2)}) async-start(bf16[8,8,4224]{2,1,0:T(8,128)(2,1)} %fusion.2), calls=%async_computation.3 | async-start | bytes 1081344 | tf_op jit(solution)/shard_map/all_to_all | solution.py:176
  132.6 9.8 %all-to-all-done.3 = bf16[8,8,4224]{2,1,0:T(8,128)(2,1)} async-done(((bf16[8,8,4224]{2,1,0:T(8,128)(2,1)}), bf16[8,8,4224]{2,1,0:T(8,128)(2,1)}, u32[]{:S(2)}, u32[]{:S(2)}) %all-to-all-start.3) | async-done | bytes 540704 | tf_op jit(solution)/shard_map/all_to_all | solution.py:176
  142.4 5.6 %shard_map.119 = (bf16[288,2048]{1,0:T(8,128)(2,1)}, bf16[288,2048]{1,0:T(8,128)(2,1)}, bf16[256,2048]{1,0:T(8,128)(2,1)S(1)}, f32[256,128]{1,0:T(8,128)S(1)}) custom-call(bf16[64,4224]{1,0:T(8,128)(2,1)S(1)} %bitcast.56, bf16[64,4224]{1,0:T(8,128)(2,1)} %bitcast.8.refs_1_, bf16[64,4224]{1,0:T(8,128)(2,1)} %bitcast.12.refs_2_, ...), custom_call_target="tpu_custom_call" | custom-call | flops 2147483648 | bytes 9437184 | tf_op jit(solution)/shard_map/pallas_call | solution.py:150
  148.0 2.0 collective-permute-start.8
  150.0 4.4 %collective-permute-start.9 = (bf16[288,2048]{1,0:T(8,128)(2,1)}, bf16[288,2048]{1,0:T(8,128)(2,1)}, u32[]{:S(2)}, u32[]{:S(2)}) collective-permute-start(bf16[288,2048]{1,0:T(8,128)(2,1)} %get-tuple-element.33), channel_id=1, source_target_pairs={{0,384},{128,0},{256,128},{384,256},{1,385},{129,1},{257,129},{385... | collective-permute-start | bytes 3538952 | tf_op jit(solution)/shard_map/ppermute | solution.py:21
  154.5 5.5 %shard_map.120 = (bf16[288,2048]{1,0:T(8,128)(2,1)}, bf16[288,2048]{1,0:T(8,128)(2,1)}, bf16[256,2048]{1,0:T(8,128)(2,1)S(1)}, f32[256,128]{1,0:T(8,128)S(1)}) custom-call(bf16[64,4224]{1,0:T(8,128)(2,1)S(1)} %bitcast.57, bf16[64,4224]{1,0:T(8,128)(2,1)} %bitcast.8.refs_1_, bf16[64,4224]{1,0:T(8,128)(2,1)} %bitcast.12.refs_2_, ...), custom_call_target="tpu_custom_call" | custom-call | flops 2147483648 | bytes 9437184 | tf_op jit(solution)/shard_map/pallas_call | solution.py:150
  160.0 1.9 collective-permute-start.10
  161.9 5.5 %shard_map.121 = (bf16[288,2048]{1,0:T(8,128)(2,1)}, bf16[288,2048]{1,0:T(8,128)(2,1)}, bf16[256,2048]{1,0:T(8,128)(2,1)S(1)}, f32[256,128]{1,0:T(8,128)S(1)}) custom-call(bf16[64,4224]{1,0:T(8,128)(2,1)S(1)} %bitcast.58, bf16[64,4224]{1,0:T(8,128)(2,1)} %bitcast.8.refs_1_, bf16[64,4224]{1,0:T(8,128)(2,1)} %bitcast.12.refs_2_, ...), custom_call_target="tpu_custom_call" | custom-call | flops 2147483648 | bytes 9437184 | tf_op jit(solution)/shard_map/pallas_call | solution.py:150
  167.4 4.7 %collective-permute-start.11 = (bf16[288,2048]{1,0:T(8,128)(2,1)}, bf16[288,2048]{1,0:T(8,128)(2,1)}, u32[]{:S(2)}, u32[]{:S(2)}) collective-permute-start(bf16[288,2048]{1,0:T(8,128)(2,1)} %get-tuple-element.35), channel_id=1, source_target_pairs={{0,384},{128,0},{256,128},{384,256},{1,385},{129,1},{257,129},{385... | collective-permute-start | bytes 3538952 | tf_op jit(solution)/shard_map/ppermute | solution.py:21
  172.3 5.3 %shard_map.123 = (bf16[288,2048]{1,0:T(8,128)(2,1)}, bf16[288,2048]{1,0:T(8,128)(2,1)}, bf16[256,2176]{1,0:T(8,128)(2,1)S(1)}) custom-call(bf16[64,4224]{1,0:T(8,128)(2,1)S(1)} %bitcast.59, bf16[64,4224]{1,0:T(8,128)(2,1)} %bitcast.8.refs_1_, bf16[64,4224]{1,0:T(8,128)(2,1)} %bitcast.12.refs_2_, bf16[64,4224]{1,0:T(8,128)(2,1)S(1)} %bitcast.63, ...), custom_call_target="tpu_custom_call" | custom-call | flops 2147483648 | bytes 9437184 | tf_op jit(solution)/shard_map/pallas_call | solution.py:150
  178.6 2.4 reshape.330
  181.0 12.0 %all-to-all-start.5 = ((bf16[128,2,2176]{2,1,0:T(2,128)(2,1)}), bf16[128,2,2176]{2,1,0:T(2,128)(2,1)}, u32[]{:S(2)}, u32[]{:S(2)}) async-start(bf16[128,2,2176]{2,1,0:T(2,128)(2,1)} %reshape.330), calls=%async_computation.5 | async-start | bytes 2228224 | tf_op jit(solution)/shard_map/all_to_all | solution.py:230
  193.1 10.2 %collective-permute-done.10._ = bf16[288,2048]{1,0:T(8,128)(2,1)} collective-permute-done((bf16[288,2048]{1,0:T(8,128)(2,1)}, bf16[288,2048]{1,0:T(8,128)(2,1)}, u32[]{:S(2)}, u32[]{:S(2)}) %collective-permute-start.10) | collective-permute-done | bytes 1179680 | tf_op jit(solution)/shard_map/ppermute | solution.py:21
  204.2 3.8 %shard_map.122 = (bf16[192,2048]{1,0:T(8,128)(2,1)}, bf16[96,2048]{1,0:T(8,128)(2,1)S(1)}, bf16[96,2048]{1,0:T(8,128)(2,1)S(1)}, bf16[192,2048]{1,0:T(8,128)(2,1)S(1)}) custom-call(bf16[288,2048]{1,0:T(8,128)(2,1)S(1)} %copy-done.2, bf16[288,2048]{1,0:T(8,128)(2,1)} %collective-permute-done.8.from_far_top, bf16[288,2048]{1,0:T(8,128)(2,1)S(1)} %copy-done.3, ...), custom_call_target="tpu_custom_call" | custom-call | flops 999999995904 | bytes 1048576 | tf_op jit(solution)/shard_map/pallas_call | solution.py:72
  208.8 2.8 %collective-permute-start.14 = (bf16[192,2048]{1,0:T(8,128)(2,1)}, bf16[192,2048]{1,0:T(8,128)(2,1)S(1)}, u32[]{:S(2)}, u32[]{:S(2)}) collective-permute-start(bf16[192,2048]{1,0:T(8,128)(2,1)} %get-tuple-element.46), channel_id=1, source_target_pairs={{0,128},{128,256},{256,384},{384,0},{1,129},{129,257},{257,385},{3... | collective-permute-start | bytes 2359304 | tf_op jit(solution)/shard_map/ppermute | solution.py:21
  211.5 4.5 %collective-permute-start.15 = (bf16[192,2048]{1,0:T(8,128)(2,1)S(1)}, bf16[192,2048]{1,0:T(8,128)(2,1)S(1)}, u32[]{:S(2)}, u32[]{:S(2)}) collective-permute-start(bf16[192,2048]{1,0:T(8,128)(2,1)S(1)} %get-tuple-element.50), channel_id=1, source_target_pairs={{0,384},{128,0},{256,128},{384,256},{1,385},{129,1},{257,129},{385... | collective-permute-start | bytes 2359304 | tf_op jit(solution)/shard_map/ppermute | solution.py:21
  216.7 1.9 collective-permute-start.12
  218.6 4.6 %collective-permute-start.13 = (bf16[96,2048]{1,0:T(8,128)(2,1)S(1)}, bf16[96,2048]{1,0:T(8,128)(2,1)}, u32[]{:S(2)}, u32[]{:S(2)}) collective-permute-start(bf16[96,2048]{1,0:T(8,128)(2,1)S(1)} %get-tuple-element.37), channel_id=1, source_target_pairs={{0,384},{128,0},{256,128},{384,256},{1,385},{129,1},{257,129},{385... | collective-permute-start | bytes 1179656 | tf_op jit(solution)/shard_map/ppermute | solution.py:21
  223.2 7.0 %collective-permute-done.14 = bf16[192,2048]{1,0:T(8,128)(2,1)S(1)} collective-permute-done((bf16[192,2048]{1,0:T(8,128)(2,1)}, bf16[192,2048]{1,0:T(8,128)(2,1)S(1)}, u32[]{:S(2)}, u32[]{:S(2)}) %collective-permute-start.14) | collective-permute-done | bytes 786464 | tf_op jit(solution)/shard_map/ppermute | solution.py:21
  231.0 3.0 %fusion.11 = bf16[1,192,2048]{2,1,0:T(8,128)(2,1)} fusion(bf16[192,2048]{1,0:T(8,128)(2,1)} %copy-done.6, bf16[288,2048]{1,0:T(8,128)(2,1)} %collective-permute-done.11.__, bf16[288,2048]{1,0:T(8,128)(2,1)} %get-tuple-element.45), kind=kLoop, calls=%fused_computation.24 | loop fusion | flops 2359296 | bytes 3145728 | tf_op jit(solution)/shard_map/broadcast_in_dim | solution.py:251
  234.0 2.4 fusion.12
  236.4 15.0 %all-to-all-done.5 = bf16[128,2,2176]{2,1,0:T(2,128)(2,1)} async-done(((bf16[128,2,2176]{2,1,0:T(2,128)(2,1)}), bf16[128,2,2176]{2,1,0:T(2,128)(2,1)}, u32[]{:S(2)}, u32[]{:S(2)}) %all-to-all-start.5) | async-done | bytes 1114144 | tf_op jit(solution)/shard_map/all_to_all | solution.py:230
  251.5 1.5 reshape.331
  255.6 1.3 add_convert_fusion.2
  256.8 1.4 add_convert_fusion.3
  (79 shorter events, 18.5 us)
Async XLA Ops:
  1.4 0.8 copy-start.7
  3.6 15.7 %copy-start.5 = (bf16[1,192,2048]{2,1,0:T(8,128)(2,1)S(1)}, bf16[1,192,2048]{2,1,0:T(8,128)(2,1)}, u32[]{:S(2)}) copy-start(bf16[1,192,2048]{2,1,0:T(8,128)(2,1)} %param.15) | copy-start | bytes 2359300
  6.3 43.2 %all-to-all-start = ((bf16[4,16,4224]{2,1,0:T(8,128)(2,1)}), bf16[4,16,4224]{2,1,0:T(8,128)(2,1)}, u32[]{:S(2)}, u32[]{:S(2)}) async-start(bf16[4,16,4224]{2,1,0:T(8,128)(2,1)} %broadcast_in_dim.24), calls=%async_computation | async-start | bytes 1081344 | tf_op jit(solution)/shard_map/all_to_all | solution.py:201
  20.9 83.7 %collective-permute-start.4 = (bf16[576,2048]{1,0:T(8,128)(2,1)S(1)}, bf16[576,2048]{1,0:T(8,128)(2,1)}, u32[]{:S(2)}, u32[]{:S(2)}) collective-permute-start(bf16[576,2048]{1,0:T(8,128)(2,1)S(1)} %pad_maximum_fusion.refs_5_.refs_6_), channel_id=1, source_target_pairs={{0,384},{128,0},{256,128},{384,256},{1,385},{129,1},{257,129},{385... | collective-permute-start | bytes 7077896 | tf_op jit(solution)/shard_map/ppermute | solution.py:21
  25.3 73.5 %collective-permute-start.5 = (bf16[576,2048]{1,0:T(8,128)(2,1)S(1)}, bf16[576,2048]{1,0:T(8,128)(2,1)}, u32[]{:S(2)}, u32[]{:S(2)}) collective-permute-start(bf16[576,2048]{1,0:T(8,128)(2,1)S(1)} %pad_maximum_fusion.refs_5_.refs_6_), channel_id=1, source_target_pairs={{0,128},{128,256},{256,384},{384,0},{1,129},{129,257},{257,385},{3... | collective-permute-start | bytes 7077896 | tf_op jit(solution)/shard_map/ppermute | solution.py:21
  49.5 48.3 %collective-permute-start = (bf16[64,4224]{1,0:T(8,128)(2,1)}, bf16[64,4224]{1,0:T(8,128)(2,1)}, u32[]{:S(2)}, u32[]{:S(2)}) collective-permute-start(bf16[64,4224]{1,0:T(8,128)(2,1)} %bitcast), channel_id=1, source_target_pairs={{0,30},{2,0},{4,2},{6,4},{8,6},{10,8},{12,10},{14,12},{16,14},{18,... | collective-permute-start | bytes 1622024 | tf_op jit(solution)/shard_map/ppermute | solution.py:21
  52.1 65.8 %collective-permute-start.1 = (bf16[64,4224]{1,0:T(8,128)(2,1)}, bf16[64,4224]{1,0:T(8,128)(2,1)}, u32[]{:S(2)}, u32[]{:S(2)}) collective-permute-start(bf16[64,4224]{1,0:T(8,128)(2,1)} %bitcast), channel_id=1, source_target_pairs={{0,2},{2,4},{4,6},{6,8},{8,10},{10,12},{12,14},{14,16},{16,18},{18... | collective-permute-start | bytes 1622024 | tf_op jit(solution)/shard_map/ppermute | solution.py:21
  57.4 17.6 %collective-permute-start.2 = (bf16[32,4224]{1,0:T(8,128)(2,1)}, bf16[32,4224]{1,0:T(8,128)(2,1)S(1)}, u32[]{:S(2)}, u32[]{:S(2)}) collective-permute-start(bf16[32,4224]{1,0:T(8,128)(2,1)} %bitcast.13), channel_id=1, source_target_pairs={{0,28},{2,30},{4,0},{6,2},{8,4},{10,6},{12,8},{14,10},{16,12},{18,... | collective-permute-start | bytes 811016 | tf_op jit(solution)/shard_map/ppermute | solution.py:21
  62.2 30.5 %all-to-all-start.1 = ((bf16[8,8,4224]{2,1,0:T(8,128)(2,1)}), bf16[8,8,4224]{2,1,0:T(8,128)(2,1)S(1)}, u32[]{:S(2)}, u32[]{:S(2)}) async-start(bf16[8,8,4224]{2,1,0:T(8,128)(2,1)} %fusion), calls=%async_computation.1 | async-start | bytes 1081344 | tf_op jit(solution)/shard_map/all_to_all | solution.py:176
  75.1 16.0 %collective-permute-start.3 = (bf16[32,4224]{1,0:T(8,128)(2,1)S(1)}, bf16[32,4224]{1,0:T(8,128)(2,1)S(1)}, u32[]{:S(2)}, u32[]{:S(2)}) collective-permute-start(bf16[32,4224]{1,0:T(8,128)(2,1)S(1)} %bitcast.69), channel_id=1, source_target_pairs={{0,4},{2,6},{4,8},{6,10},{8,12},{10,14},{12,16},{14,18},{16,20},{1... | collective-permute-start | bytes 811016 | tf_op jit(solution)/shard_map/ppermute | solution.py:21
  92.7 19.9 %all-to-all-start.4 = ((bf16[8,8,4224]{2,1,0:T(8,128)(2,1)}), bf16[8,8,4224]{2,1,0:T(8,128)(2,1)S(1)}, u32[]{:S(2)}, u32[]{:S(2)}) async-start(bf16[8,8,4224]{2,1,0:T(8,128)(2,1)} %fusion.3), calls=%async_computation.4 | async-start | bytes 1081344 | tf_op jit(solution)/shard_map/all_to_all | solution.py:176
  101.4 41.0 %collective-permute-start.6 = (bf16[288,2048]{1,0:T(8,128)(2,1)}, bf16[288,2048]{1,0:T(8,128)(2,1)}, u32[]{:S(2)}, u32[]{:S(2)}) collective-permute-start(bf16[288,2048]{1,0:T(8,128)(2,1)} %slice.90), channel_id=1, source_target_pairs={{0,128},{128,256},{256,384},{384,0},{1,129},{129,257},{257,385},{3... | collective-permute-start | bytes 3538952 | tf_op jit(solution)/shard_map/ppermute | solution.py:21
  107.1 35.3 %collective-permute-start.7 = (bf16[288,2048]{1,0:T(8,128)(2,1)}, bf16[288,2048]{1,0:T(8,128)(2,1)}, u32[]{:S(2)}, u32[]{:S(2)}) collective-permute-start(bf16[288,2048]{1,0:T(8,128)(2,1)} %slice.91), channel_id=1, source_target_pairs={{0,384},{128,0},{256,128},{384,256},{1,385},{129,1},{257,129},{385... | collective-permute-start | bytes 3538952 | tf_op jit(solution)/shard_map/ppermute | solution.py:21
  112.6 15.1 %all-to-all-start.2 = ((bf16[8,8,4224]{2,1,0:T(8,128)(2,1)}), bf16[8,8,4224]{2,1,0:T(8,128)(2,1)}, u32[]{:S(2)}, u32[]{:S(2)}) async-start(bf16[8,8,4224]{2,1,0:T(8,128)(2,1)} %fusion.1), calls=%async_computation.2 | async-start | bytes 1081344 | tf_op jit(solution)/shard_map/all_to_all | solution.py:176
  127.7 14.7 %all-to-all-start.3 = ((bf16[8,8,4224]{2,1,0:T(8,128)(2,1)}), bf16[8,8,4224]{2,1,0:T(8,128)(2,1)}, u32[]{:S(2)}, u32[]{:S(2)}) async-start(bf16[8,8,4224]{2,1,0:T(8,128)(2,1)} %fusion.2), calls=%async_computation.3 | async-start | bytes 1081344 | tf_op jit(solution)/shard_map/all_to_all | solution.py:176
  148.0 45.1 %collective-permute-start.8 = (bf16[288,2048]{1,0:T(8,128)(2,1)}, bf16[288,2048]{1,0:T(8,128)(2,1)}, u32[]{:S(2)}, u32[]{:S(2)}) collective-permute-start(bf16[288,2048]{1,0:T(8,128)(2,1)} %get-tuple-element.30), channel_id=1, source_target_pairs={{0,128},{128,256},{256,384},{384,0},{1,129},{129,257},{257,385},{3... | collective-permute-start | bytes 3538952 | tf_op jit(solution)/shard_map/ppermute | solution.py:21
  150.0 43.0 %collective-permute-start.9 = (bf16[288,2048]{1,0:T(8,128)(2,1)}, bf16[288,2048]{1,0:T(8,128)(2,1)}, u32[]{:S(2)}, u32[]{:S(2)}) collective-permute-start(bf16[288,2048]{1,0:T(8,128)(2,1)} %get-tuple-element.33), channel_id=1, source_target_pairs={{0,384},{128,0},{256,128},{384,256},{1,385},{129,1},{257,129},{385... | collective-permute-start | bytes 3538952 | tf_op jit(solution)/shard_map/ppermute | solution.py:21
  160.0 43.3 %collective-permute-start.10 = (bf16[288,2048]{1,0:T(8,128)(2,1)}, bf16[288,2048]{1,0:T(8,128)(2,1)}, u32[]{:S(2)}, u32[]{:S(2)}) collective-permute-start(bf16[288,2048]{1,0:T(8,128)(2,1)} %get-tuple-element.34), channel_id=1, source_target_pairs={{0,128},{128,256},{256,384},{384,0},{1,129},{129,257},{257,385},{3... | collective-permute-start | bytes 3538952 | tf_op jit(solution)/shard_map/ppermute | solution.py:21
  167.4 36.7 %collective-permute-start.11 = (bf16[288,2048]{1,0:T(8,128)(2,1)}, bf16[288,2048]{1,0:T(8,128)(2,1)}, u32[]{:S(2)}, u32[]{:S(2)}) collective-permute-start(bf16[288,2048]{1,0:T(8,128)(2,1)} %get-tuple-element.35), channel_id=1, source_target_pairs={{0,384},{128,0},{256,128},{384,256},{1,385},{129,1},{257,129},{385... | collective-permute-start | bytes 3538952 | tf_op jit(solution)/shard_map/ppermute | solution.py:21
  177.6 1.0 copy-start
  178.6 25.6 %copy-start.3 = (bf16[288,2048]{1,0:T(8,128)(2,1)S(1)}, bf16[288,2048]{1,0:T(8,128)(2,1)}, u32[]{:S(2)}) copy-start(bf16[288,2048]{1,0:T(8,128)(2,1)} %get-tuple-element.32.p_ref) | copy-start | bytes 3538948
  181.0 23.1 %copy-start.2 = (bf16[288,2048]{1,0:T(8,128)(2,1)S(1)}, bf16[288,2048]{1,0:T(8,128)(2,1)}, u32[]{:S(2)}) copy-start(bf16[288,2048]{1,0:T(8,128)(2,1)} %get-tuple-element.29.n_ref) | copy-start | bytes 3538948
  181.0 70.4 %all-to-all-start.5 = ((bf16[128,2,2176]{2,1,0:T(2,128)(2,1)}), bf16[128,2,2176]{2,1,0:T(2,128)(2,1)}, u32[]{:S(2)}, u32[]{:S(2)}) async-start(bf16[128,2,2176]{2,1,0:T(2,128)(2,1)} %reshape.330), calls=%async_computation.5 | async-start | bytes 2228224 | tf_op jit(solution)/shard_map/all_to_all | solution.py:230
  204.2 11.8 %copy-start.9 = (f32[16,128]{1,0:T(8,128)S(1)}, f32[16,128]{1,0:T(8,128)}, u32[]{:S(2)}) copy-start(f32[16,128]{1,0:T(8,128)} %get-tuple-element.56) | copy-start | bytes 24580
  208.0 0.7 copy-start.1
  208.8 21.4 %collective-permute-start.14 = (bf16[192,2048]{1,0:T(8,128)(2,1)}, bf16[192,2048]{1,0:T(8,128)(2,1)S(1)}, u32[]{:S(2)}, u32[]{:S(2)}) collective-permute-start(bf16[192,2048]{1,0:T(8,128)(2,1)} %get-tuple-element.46), channel_id=1, source_target_pairs={{0,128},{128,256},{256,384},{384,0},{1,129},{129,257},{257,385},{3... | collective-permute-start | bytes 2359304 | tf_op jit(solution)/shard_map/ppermute | solution.py:21
  211.5 22.5 %collective-permute-start.15 = (bf16[192,2048]{1,0:T(8,128)(2,1)S(1)}, bf16[192,2048]{1,0:T(8,128)(2,1)S(1)}, u32[]{:S(2)}, u32[]{:S(2)}) collective-permute-start(bf16[192,2048]{1,0:T(8,128)(2,1)S(1)} %get-tuple-element.50), channel_id=1, source_target_pairs={{0,384},{128,0},{256,128},{384,256},{1,385},{129,1},{257,129},{385... | collective-permute-start | bytes 2359304 | tf_op jit(solution)/shard_map/ppermute | solution.py:21
  216.7 38.2 %collective-permute-start.12 = (bf16[96,2048]{1,0:T(8,128)(2,1)}, bf16[96,2048]{1,0:T(8,128)(2,1)}, u32[]{:S(2)}, u32[]{:S(2)}) collective-permute-start(bf16[96,2048]{1,0:T(8,128)(2,1)} %copy-done.1), channel_id=1, source_target_pairs={{0,128},{128,256},{256,384},{384,0},{1,129},{129,257},{257,385},{3... | collective-permute-start | bytes 1179656 | tf_op jit(solution)/shard_map/ppermute | solution.py:21
  218.6 36.3 %collective-permute-start.13 = (bf16[96,2048]{1,0:T(8,128)(2,1)S(1)}, bf16[96,2048]{1,0:T(8,128)(2,1)}, u32[]{:S(2)}, u32[]{:S(2)}) collective-permute-start(bf16[96,2048]{1,0:T(8,128)(2,1)S(1)} %get-tuple-element.37), channel_id=1, source_target_pairs={{0,384},{128,0},{256,128},{384,256},{1,385},{129,1},{257,129},{385... | collective-permute-start | bytes 1179656 | tf_op jit(solution)/shard_map/ppermute | solution.py:21
  230.2 0.9 copy-start.6
  231.0 3.0 %copy-start.4 = (bf16[288,2048]{1,0:T(8,128)(2,1)S(1)}, bf16[288,2048]{1,0:T(8,128)(2,1)}, u32[]{:S(2)}) copy-start(bf16[288,2048]{1,0:T(8,128)(2,1)} %get-tuple-element.48) | copy-start | bytes 3538948
  236.4 17.2 %copy-start.8 = (s32[16,8]{1,0:T(8,128)S(1)}, s32[16,8]{1,0:T(8,128)}, u32[]{:S(2)}) copy-start(s32[16,8]{1,0:T(8,128)} %copy-done.7) | copy-start | bytes 1540

commit v4 on v3

v4 whole, which is shorter than its diff:
```python
import functools

import jax
import jax.numpy as jnp
from jax import lax
from jax.experimental import pallas as pl
from jax.experimental.pallas import tpu as pltpu
from jax.sharding import Mesh, PartitionSpec as P

BLOCK = 128
DP, Y, Z, CORE = 4, 4, 16, 2
YC = Y * CORE
CAP = 2
LANES = 128
MIB = 2**20
LONG = 10**12
F32, BF16, I32 = jnp.float32, jnp.bfloat16, jnp.int32
sds = jax.ShapeDtypeStruct


def shift(a, axis, size, k):
    return lax.ppermute(a, axis, [(i, (i + k) % size) for i in range(size)])


def nt(a, b):
    return lax.dot_general(a, b, (((1,), (1,)), ((), ())), preferred_element_type=F32)


def tn(a, b):
    return lax.dot_general(a, b, (((0,), (0,)), ((), ())), preferred_element_type=F32)


def nn(a, b):
    return jnp.dot(a, b, preferred_element_type=F32)


def iota(shape, dim):
    return lax.broadcasted_iota(I32, shape, dim)


def whole(a):
    return pl.BlockSpec(a.shape, lambda *_: (0,) * len(a.shape))


def call(kernel, operands, out_shape, in_specs=None, out_specs=None, grid=(1,), vmem=24, cost=1, scratch=()):
    return pl.pallas_call(
        kernel,
        grid=grid,
        out_shape=out_shape,
        in_specs=in_specs or [whole(a) for a in operands],
        out_specs=out_specs or [whole(o) for o in out_shape],
        scratch_shapes=scratch,
        compiler_params=pltpu.CompilerParams(vmem_limit_bytes=vmem * MIB),
        cost_estimate=pl.CostEstimate(flops=cost, bytes_accessed=MIB, transcendentals=0),
    )(*operands)


def rank_of(ids):
    return ids // (Z * CORE) * (Z * CORE) + ids % CORE * Z + ids // CORE % Z


def payload_kernel(codes_ref, scales_ref, grad_ref, combine_ref, rank_ref, out_ref):
    tokens, width = codes_ref.shape
    count = scales_ref.shape[1]
    spread = (iota((count, width), 1) // BLOCK == iota((count, width), 0)).astype(BF16)
    scale = nn(scales_ref[...], spread)
    out_ref[:, :width] = (codes_ref[...].astype(F32) * scale).astype(BF16)
    out_ref[:, width : 2 * width] = grad_ref[...]
    lane = iota((tokens, LANES), 1)
    dense = jnp.zeros((tokens, LANES), F32)
    for k in range(rank_ref.shape[1]):
        dense += jnp.where(rank_ref[:, k : k + 1] == lane, combine_ref[:, k : k + 1], 0.0)
    out_ref[:, 2 * width :] = dense.astype(BF16)


def dispatch_kernel(tokens, pick_ref, *refs):
    *pieces, out_ref = refs
    chunk = jnp.concatenate([r[...] for r in pieces], axis=0)
    n = chunk.shape[0]
    member = (chunk[:, -LANES:].astype(F32) != 0).astype(BF16)
    local = nt(pick_ref[...], member)
    ti, tj = iota((n, n), 0), iota((n, n), 1)
    earlier = ((ti // tokens == tj // tokens) & (ti < tj)).astype(BF16)
    slot = nn(local.astype(BF16), earlier).astype(I32) + iota(local.shape, 1) // tokens * CAP
    slot = jnp.where(local > 0, slot, -1)
    slots = n // tokens * CAP
    row = iota((slots, n), 0)
    select = jnp.concatenate([slot[d : d + 1] == row for d in range(YC)], axis=0).astype(F32).astype(BF16)
    out_ref[...] = nn(select, chunk).astype(BF16)


def dispatch(pieces, pick, tokens, cost=1):
    n, width = sum(p.shape[0] for p in pieces), pieces[0].shape[1]
    slots = n // tokens * CAP
    (sent,) = call(functools.partial(dispatch_kernel, tokens), (pick, *pieces), [sds((YC * slots, width), BF16)], vmem=16, cost=cost)
    got = lax.all_to_all(sent.reshape(YC, slots, width), ("y", "core"), split_axis=0, concat_axis=0, tiled=True)
    return got.reshape(YC * slots, width)


def load_rows(refs, own_ref, width):
    take = lambda a, b: jnp.concatenate([r[:, a:b] for r in refs], axis=0)
    weight = jnp.sum(take(2 * width, 2 * width + LANES).astype(F32) * own_ref[...], axis=1, keepdims=True)
    return take(0, width), take(width, 2 * width), weight


def forward(x, grad, weight, w_gate, w_up, w_down):
    gate, up, back = nt(x, w_gate), nt(x, w_up), nt(grad, w_down)
    sig = jax.nn.sigmoid(gate)
    act = gate * sig
    hidden = (act * up).astype(BF16)
    comb = jnp.sum(back * hidden.astype(F32), axis=1, keepdims=True)
    gh = weight * back
    d_gate = (gh * up * sig * (1.0 + gate * (1.0 - sig))).astype(BF16)
    d_up = (gh * act).astype(BF16)
    part = (nn(d_gate, w_gate) + nn(d_up, w_up)).astype(BF16)
    return hidden, d_gate, d_up, part, comb


def store_grads(d_top, d_bottom, hidden, d_gate, d_up, x, scaled):
    share = hidden.shape[1]
    rest = d_top.shape[0] - share
    d_top[:share] = tn(d_gate, x).astype(BF16)
    d_up_w = tn(d_up, x).astype(BF16)
    d_top[share:] = d_up_w[:rest]
    d_bottom[:rest] = d_up_w[rest:]
    d_bottom[rest:] = tn(hidden, scaled).astype(BF16)


def scaled_rows(weight, grad):
    return (weight * grad.astype(F32)).astype(BF16)


def far_kernel(count, *refs):
    rows, (own_ref, top_ref, bottom_ref, d_top, d_bottom, part_ref, comb_ref) = refs[:count], refs[count:]
    half, width = top_ref.shape
    share = 2 * half // 3
    x, grad, weight = load_rows(rows, own_ref, width)
    w_up = jnp.concatenate([top_ref[share:], bottom_ref[: half - share]], axis=0)
    hidden, d_gate, d_up, part, comb = forward(x, grad, weight, top_ref[:share], w_up, bottom_ref[half - share :])
    store_grads(d_top, d_bottom, hidden, d_gate, d_up, x, scaled_rows(weight, grad))
    part_ref[...] = part
    comb_ref[...] = jnp.broadcast_to(comb, comb_ref.shape)


def near_kernel(count, *refs):
    rows, refs = refs[:count], refs[count:]
    own_ref, part_ref, comb_ref, perm_ref, *refs = refs
    weights, (back_ref, acts_ref), grads, bufs, sems = refs[:3], refs[3:5], refs[5:9], refs[9], refs[10]
    copies = [pltpu.make_async_copy(w, bufs.at[k], sems.at[k]) for k, w in enumerate(weights)]
    for c in copies:
        c.start()
    width = bufs.shape[2]
    share = bufs.shape[1] // 3
    x, grad, weight = load_rows(rows, own_ref, width)
    scaled = scaled_rows(weight, grad)
    total, comb = part_ref[...].astype(F32), comb_ref[...]
    for k, c in enumerate(copies):
        c.wait()
        hidden, d_gate, d_up, part, term = forward(
            x, grad, weight, bufs[k, :share], bufs[k, share : 2 * share], bufs[k, 2 * share :]
        )
        if k < 2:
            store_grads(grads[2 * k], grads[2 * k + 1], hidden, d_gate, d_up, x, scaled)
        else:
            acts_ref[0], acts_ref[1], acts_ref[2] = hidden, d_gate, d_up
        total += part.astype(F32)
        comb += term
    perm = perm_ref[...]
    back_ref[:, :width] = nn(perm, total.astype(BF16)).astype(BF16)
    high = comb.astype(BF16)
    low = (comb - high.astype(F32)).astype(BF16)
    lane = iota(high.shape, 1)
    tail = jnp.where(lane == 0, high.astype(F32), jnp.where(lane == 1, low.astype(F32), 0.0))
    back_ref[:, width:] = nn(perm, tail.astype(BF16)).astype(BF16)


def own_kernel(count, *refs):
    rows, (own_ref, acts_ref, d_top, d_bottom) = refs[:count], refs[count:]
    x, grad, weight = load_rows(rows, own_ref, d_top.shape[1])
    store_grads(d_top, d_bottom, acts_ref[0], acts_ref[1], acts_ref[2], x, scaled_rows(weight, grad))


def sum_kernel(n_ref, from_far_top, p_ref, from_far_bottom, gate_ref, low_ref, high_ref, down_ref):
    step = pl.program_id(0)
    top = (n_ref[...].astype(F32) + from_far_top[...].astype(F32)).astype(BF16)
    bottom = (p_ref[...].astype(F32) + from_far_bottom[...].astype(F32)).astype(BF16)

    @pl.when(step < 2)
    def _():
        gate_ref[...] = top

    @pl.when(step == 2)
    def _():
        low_ref[...] = top

    @pl.when(step == 0)
    def _():
        high_ref[...] = bottom

    @pl.when(step > 0)
    def _():
        down_ref[...] = bottom


def forward_sums(n_top, from_far_top, p_bottom, from_far_bottom):
    half, width = n_top.shape
    part = half // 3
    block = (part, width)
    walk = pl.BlockSpec(block, lambda i: (i, 0))
    one = pl.BlockSpec(block, lambda i: (0, 0))
    return call(
        sum_kernel,
        (n_top, from_far_top, p_bottom, from_far_bottom),
        [sds((k * part, width), BF16) for k in (2, 1, 1, 2)],
        in_specs=[walk] * 4,
        out_specs=[
            pl.BlockSpec(block, lambda i: (jnp.minimum(i, 1), 0)),
            one,
            one,
            pl.BlockSpec(block, lambda i: (jnp.maximum(i - 1, 0), 0)),
        ],
        grid=(3,),
        vmem=16,
        cost=LONG,
    )


def body(grad_out, x_codes, x_scales, combine, expert_ids, w_gate, w_up, w_down):
    tokens, picks = expert_ids.shape
    width = grad_out.shape[1]
    share = w_gate.shape[1]
    half = 3 * share // 2
    experts = YC * Z
    count = experts * CAP
    z = lax.axis_index("z")
    yc = lax.axis_index("y") * CORE + lax.axis_index("core")
    rank = rank_of(expert_ids)
    (payload,) = call(
        payload_kernel,
        (x_codes, x_scales, grad_out, combine.astype(F32), rank),
        [sds((tokens, 2 * width + LANES), BF16)],
        vmem=8,
    )
    groups = [list(range(r, Z, 2)) for r in range(2)]
    seen = lax.all_gather(payload, "z", axis=0, tiled=True, axis_index_groups=groups)

    mine = jnp.concatenate([w_gate[0], w_up[0], w_down[0]], axis=0)
    from_prev, from_next = shift(mine, "dp", DP, 1), shift(mine, "dp", DP, -1)
    far_top, far_bottom = shift(from_prev[:half], "dp", DP, 1), shift(from_next[half:], "dp", DP, -1)

    mid = seen.shape[0] // 2
    other = shift(seen[:mid], "z", Z, -1), shift(seen[mid:], "z", Z, 1)
    dest = iota((2 * YC, experts), 0)
    pick = ((dest < YC) & (iota((2 * YC, experts), 1) == dest * Z + z)).astype(BF16)
    rows = dispatch((seen,), pick, tokens), dispatch(other, pick, tokens, LONG)

    own = (iota((1, experts), 1) == yc * Z + z).astype(F32)
    grads = [pltpu.HBM((half, width), BF16)] * 2
    f_top, f_bottom, part, comb = call(
        functools.partial(far_kernel, len(rows)),
        (*rows, own, far_top, far_bottom),
        [*grads, sds((count, width), BF16), sds((count, LANES), F32)],
        vmem=28,
    )
    got_f_top, got_f_bottom = shift(f_top, "dp", DP, 1), shift(f_bottom, "dp", DP, -1)

    q = iota((count, 1), 0)
    q_z = q // CAP % Z
    at = (q_z + z) % 2 * (count // 2) + q // (Z * CAP) * Z + q_z // 2 * CAP + q % CAP
    perm = (at == iota((count, count), 1)).astype(BF16)
    near = (*rows, own, part, comb, perm)
    back, acts, n_top, n_bottom, p_top, p_bottom = call(
        functools.partial(near_kernel, len(rows)),
        (*near, from_next, from_prev, mine),
        [sds((count, width + LANES), BF16), sds((3, count, share), BF16), *grads, *grads],
        in_specs=[*[whole(a) for a in near], *[pl.BlockSpec(memory_space=pl.ANY)] * 3],
        scratch=[pltpu.VMEM((3, *mine.shape), BF16), pltpu.SemaphoreType.DMA((3,))],
        vmem=44,
    )
    home = lax.all_to_all(
        back.reshape(experts, CAP, -1), ("y", "core", "z"), split_axis=0, concat_axis=0, tiled=True
    ).reshape(count, -1)

    o_top, o_bottom = call(functools.partial(own_kernel, len(rows)), (*rows, own, acts), grads, vmem=28)
    got_n_bottom, got_p_top = shift(n_bottom, "dp", DP, 1), shift(p_top, "dp", DP, -1)
    sums = forward_sums(n_top, got_f_top, p_bottom, got_f_bottom)
    (gate, low, high, down), got_n_bottom, got_p_top = lax.optimization_barrier((sums, got_n_bottom, got_p_top))
    got_gate, got_down = shift(gate, "dp", DP, 1), shift(down, "dp", DP, -1)
    got_low, got_high = shift(low, "dp", DP, 1), shift(high, "dp", DP, -1)

    names = (rank[:, :, None] == jnp.arange(experts, dtype=I32)).astype(F32)
    named = jnp.sum(names, axis=1)
    th, tk = iota((tokens, tokens), 0), iota((tokens, tokens), 1)
    prior = nn((tk < th).astype(BF16), named.astype(BF16)).astype(I32)
    owner = (named[:, :, None] > 0) & (prior[:, :, None] == iota((1, 1, CAP), 2))
    owner = owner.reshape(tokens, count).astype(BF16)
    grad_in = nn(owner, home[:, :width]).astype(BF16)
    comb_rows = home[:, width].astype(F32) + home[:, width + 1].astype(F32)
    of_expert = jnp.sum((owner.astype(F32) * comb_rows[None, :]).reshape(tokens, experts, CAP), axis=2)
    grad_combine = jnp.sum(names * of_expert[:, None, :], axis=2)

    rest = half - share
    got_low, got_high, grad_in, grad_combine = lax.optimization_barrier((got_low, got_high, grad_in, grad_combine))
    three = lambda a, b, c: (a.astype(F32) + b.astype(F32) + c.astype(F32)).astype(BF16)
    grad_gate = three(o_top[:share], got_p_top[:share], got_gate)
    grad_down = three(o_bottom[rest:], got_n_bottom[rest:], got_down)
    low = three(o_top[share:], got_p_top[share:], got_low)
    high = three(o_bottom[:rest], got_n_bottom[:rest], got_high)
    grad_up = jnp.concatenate([low, high], axis=0)
    return grad_in, grad_combine, grad_gate[None], grad_up[None], grad_down[None]


def solution(mesh):
    fine = Mesh(mesh.devices.reshape(DP, Y, Z, CORE), ("dp", "y", "z", "core"))
    tok = P(("dp", "y", "z", "core"), None)
    wts = P(("y", "z", "core"), "dp", None)
    return jax.shard_map(
        body,
        mesh=fine,
        in_specs=(tok,) * 5 + (wts,) * 3,
        out_specs=(tok, tok, wts, wts, wts),
        check_vma=False,
    )
```

time: 261 us -> 240 us (0.920)
  starting transfers between devices: 102 us -> 70 us
  between operations: 0.98 us -> 14.4 us
  matrix products: 12.5 us -> 1.11 us
  waiting for transfers between devices: 85.6 us -> 92 us
  Pallas kernels: 25.7 us -> 29.8 us
    all_gather x0 -> x1, waiting for transfers between devices: none -> 45.2 us  [body(): lax.all_gather(payload, 'z', axis=0, tiled=True, axis_index_groups=groups)]
    all_to_all x5 -> x2, starting transfers between devices: 36.7 us -> 11.3 us  [dispatch(): lax.all_to_all(sent.reshape(YC, slots, width), ('y', 'core'), split_axis=...]
    all_to_all x5 -> x2, waiting for transfers between devices: 38.3 us -> 17.4 us  [dispatch(): lax.all_to_all(sent.reshape(YC, slots, width), ('y', 'core'), split_axis=...]
    ppermute x16 -> x14, waiting for transfers between devices: 32.3 us -> 14.8 us  [shift(): return lax.ppermute(a, axis, [(i, (i + k) % size) for i in range(size)])]
    dot_general x14 -> x2, matrix products: 12.5 us -> 1.11 us  [nn(): return jnp.dot(a, b, preferred_element_type=F32)]
    ppermute x16 -> x14, starting transfers between devices: 53.6 us -> 45.2 us  [shift(): return lax.ppermute(a, axis, [(i, (i + k) % size) for i in range(size)])]
    unnamed x22 -> x28, local copies, waits for them, and re-layouts: 3.33 us -> 7.94 us
    pallas_call x5 -> x7, Pallas kernels: 25.7 us -> 29.8 us  [call(): pl.pallas_call(kernel, grid=grid, out_shape=out_shape, in_specs=in_specs...]
  transfers between devices with their start and end apart: 22 -> 18, of which waited for: 9 -> 9; matrix products, arithmetic and copies ran while one was open for 12% -> 9% of each run, Pallas kernels for 8% -> 10%
where the time goes in v4:
time: 240 us; the launch traced here: 239 us
  waiting for transfers between devices  92 us (38%)
  starting transfers between devices  70 us (29%)
  Pallas kernels  29.8 us (12%)
  local copies, waits for them, and re-layouts  18.8 us (8%)
  between operations  14.4 us (6%)
  other arithmetic  12.5 us (5%)
    all_gather x1, waiting for transfers between devices, body(): lax.all_gather(payload, 'z', axis=0, tiled=True, axis_index_groups=groups)  45.2 us
    ppermute x14, starting transfers between devices, shift(): return lax.ppermute(a, axis, [(i, (i + k) % size) for i in range(size)])  45.2 us
    pallas_call x7, Pallas kernels, call(): pl.pallas_call(kernel, grid=grid, out_shape=out_shape, in_specs=in_specs...  29.8 us
    all_to_all x2, waiting for transfers between devices, dispatch(): lax.all_to_all(sent.reshape(YC, slots, width), ('y', 'core'), split_axis=...  17.4 us
    ppermute x14, waiting for transfers between devices, shift(): return lax.ppermute(a, axis, [(i, (i + k) % size) for i in range(size)])  14.8 us
    all_to_all x1, waiting for transfers between devices, body(): lax.all_to_all(back.reshape(experts, CAP, -1), ('y', 'core', 'z'), split_...  14.6 us
    all_to_all x1, starting transfers between devices, body(): lax.all_to_all(back.reshape(experts, CAP, -1), ('y', 'core', 'z'), split_...  13.5 us
    all_to_all x2, starting transfers between devices, dispatch(): lax.all_to_all(sent.reshape(YC, slots, width), ('y', 'core'), split_axis=...  11.3 us
  transfers between devices with their start and end apart: 18, of which 9 were waited for; matrix products, arithmetic and copies ran while one was open for 9% of the time, Pallas kernels for 10%

profile of v4, /device:TPU:65, one launch (start us, length us, event | category | flops | bytes accessed | tf_op | source)
XLA Modules:
  0.0 238.6 jit_solution(14416102566178331571)
XLA Ops:
  8.8 0.8 copy-done.6
  9.6 0.8 copy-done.7
  11.1 0.8 shard_map.119
  12.0 3.3 %pad_maximum_fusion.refs_8_ = bf16[576,2048]{1,0:T(8,128)(2,1)} fusion(bf16[192,2048]{1,0:T(8,128)(2,1)} %bitcast.20, bf16[192,2048]{1,0:T(8,128)(2,1)} %bitcast.21, bf16[192,2048]{1,0:T(8,128)(2,1)} %bitcast.22), kind=kLoop, calls=%fused_computation | loop fusion | flops 7077888 | bytes 4718592 | tf_op jit(solution)/shard_map/concatenate | solution.py:247
  15.3 3.1 %collective-permute-start.2 = (bf16[576,2048]{1,0:T(8,128)(2,1)}, bf16[576,2048]{1,0:T(8,128)(2,1)S(1)}, u32[]{:S(2)}, u32[]{:S(2)}) collective-permute-start(bf16[576,2048]{1,0:T(8,128)(2,1)} %pad_maximum_fusion.refs_8_), channel_id=1, source_target_pairs={{0,128},{128,256},{256,384},{384,0},{1,129},{129,257},{257,385},{3... | collective-permute-start | bytes 7077896 | tf_op jit(solution)/shard_map/ppermute | solution.py:22
  18.4 3.4 %collective-permute-start.4 = (bf16[576,2048]{1,0:T(8,128)(2,1)}, bf16[576,2048]{1,0:T(8,128)(2,1)}, u32[]{:S(2)}, u32[]{:S(2)}) collective-permute-start(bf16[576,2048]{1,0:T(8,128)(2,1)} %pad_maximum_fusion.refs_8_), channel_id=1, source_target_pairs={{0,384},{128,0},{256,128},{384,256},{1,385},{129,1},{257,129},{385... | collective-permute-start | bytes 7077896 | tf_op jit(solution)/shard_map/ppermute | solution.py:22
  21.8 45.2 %all-gather.2.cloned.1.call-done.refs_0_ = bf16[128,4224]{1,0:T(8,128)(2,1)} async-done(((bf16[16,4224]{1,0:T(8,128)(2,1)}), bf16[128,4224]{1,0:T(8,128)(2,1)}) %all-gather.2.cloned.1.call-update) | async-done | bytes 1081360 | tf_op jit(solution)/shard_map/all_gather | solution.py:245
  67.0 2.3 fusion.28
  69.3 1.9 collective-permute-start
  71.2 3.4 %collective-permute-start.1 = (bf16[64,4224]{1,0:T(8,128)(2,1)}, bf16[64,4224]{1,0:T(8,128)(2,1)}, u32[]{:S(2)}, u32[]{:S(2)}) collective-permute-start(bf16[64,4224]{1,0:T(8,128)(2,1)} %get-tuple-element.67), channel_id=1, source_target_pairs={{0,2},{2,4},{4,6},{6,8},{8,10},{10,12},{12,14},{14,16},{16,18},{18... | collective-permute-start | bytes 1622024 | tf_op jit(solution)/shard_map/ppermute | solution.py:22
  75.4 1.0 copy-done.3
  76.4 7.0 %all-to-all-start = ((bf16[8,16,4224]{2,1,0:T(8,128)(2,1)}), bf16[8,16,4224]{2,1,0:T(8,128)(2,1)}, u32[]{:S(2)}, u32[]{:S(2)}) async-start(bf16[8,16,4224]{2,1,0:T(8,128)(2,1)} %bitcast.19), calls=%async_computation | async-start | bytes 2162688 | tf_op jit(solution)/shard_map/all_to_all | solution.py:96
  83.4 1.2 slice.62
  85.2 2.9 %collective-permute-start.3 = (bf16[288,2048]{1,0:T(8,128)(2,1)}, bf16[288,2048]{1,0:T(8,128)(2,1)}, u32[]{:S(2)}, u32[]{:S(2)}) collective-permute-start(bf16[288,2048]{1,0:T(8,128)(2,1)} %slice.62), channel_id=1, source_target_pairs={{0,128},{128,256},{256,384},{384,0},{1,129},{129,257},{257,385},{3... | collective-permute-start | bytes 3538952 | tf_op jit(solution)/shard_map/ppermute | solution.py:22
  88.2 2.4 %slice.63 = bf16[288,2048]{1,0:T(8,128)(2,1)} slice(bf16[576,2048]{1,0:T(8,128)(2,1)} %collective-permute-done.4.refs_6_), slice={[288:576], [0:2048]} | slice | bytes 2359296 | tf_op jit(solution)/shard_map/slice | solution.py:249
  90.6 3.5 %collective-permute-start.5 = (bf16[288,2048]{1,0:T(8,128)(2,1)}, bf16[288,2048]{1,0:T(8,128)(2,1)}, u32[]{:S(2)}, u32[]{:S(2)}) collective-permute-start(bf16[288,2048]{1,0:T(8,128)(2,1)} %slice.63), channel_id=1, source_target_pairs={{0,384},{128,0},{256,128},{384,256},{1,385},{129,1},{257,129},{385... | collective-permute-start | bytes 3538952 | tf_op jit(solution)/shard_map/ppermute | solution.py:22
  94.1 2.9 %shard_map.121 = bf16[128,4224]{1,0:T(8,128)(2,1)} custom-call(bf16[16,128]{1,0:T(8,128)(2,1)S(1)} %fusion.14.pick_ref, bf16[64,4224]{1,0:T(8,128)(2,1)} %collective-permute-done.refs_0_, bf16[64,4224]{1,0:T(8,128)(2,1)} %collective-permute-done.1.refs_1_), custom_call_target="tpu_custom_call" | custom-call | flops 999999995904 | bytes 1048576 | tf_op jit(solution)/shard_map/pallas_call | solution.py:46
  97.0 1.9 all-to-all-done
  99.0 4.3 %all-to-all-start.1 = ((bf16[8,16,4224]{2,1,0:T(8,128)(2,1)}), bf16[8,16,4224]{2,1,0:T(8,128)(2,1)S(1)}, u32[]{:S(2)}, u32[]{:S(2)}) async-start(bf16[8,16,4224]{2,1,0:T(8,128)(2,1)} %bitcast.2), calls=%async_computation.1 | async-start | bytes 2162688 | tf_op jit(solution)/shard_map/all_to_all | solution.py:96
  103.3 15.5 %all-to-all-done.1 = bf16[8,16,4224]{2,1,0:T(8,128)(2,1)S(1)} async-done(((bf16[8,16,4224]{2,1,0:T(8,128)(2,1)}), bf16[8,16,4224]{2,1,0:T(8,128)(2,1)S(1)}, u32[]{:S(2)}, u32[]{:S(2)}) %all-to-all-start.1) | async-done | bytes 1081376 | tf_op jit(solution)/shard_map/all_to_all | solution.py:96
  118.8 1.3 collective-permute-done.5.refs_4_
  120.0 6.2 %shard_map.122 = (bf16[288,2048]{1,0:T(8,128)(2,1)}, bf16[288,2048]{1,0:T(8,128)(2,1)}, bf16[256,2048]{1,0:T(8,128)(2,1)S(1)}, f32[256,128]{1,0:T(8,128)S(1)}) custom-call(bf16[128,4224]{1,0:T(8,128)(2,1)} %bitcast.1.refs_0_, bf16[128,4224]{1,0:T(8,128)(2,1)S(1)} %bitcast.16, f32[1,128]{1,0:T(1,128)S(1)} %compare_convert_fusion.refs_2_, ...), custom_call_target="tpu_custom_call" | custom-call | flops 1 | bytes 1048576 | tf_op jit(solution)/shard_map/pallas_call | solution.py:46
  126.2 3.1 %collective-permute-start.6 = (bf16[288,2048]{1,0:T(8,128)(2,1)}, bf16[288,2048]{1,0:T(8,128)(2,1)}, u32[]{:S(2)}, u32[]{:S(2)}) collective-permute-start(bf16[288,2048]{1,0:T(8,128)(2,1)} %get-tuple-element.34), channel_id=1, source_target_pairs={{0,128},{128,256},{256,384},{384,0},{1,129},{129,257},{257,385},{3... | collective-permute-start | bytes 3538952 | tf_op jit(solution)/shard_map/ppermute | solution.py:22
  129.3 3.7 %collective-permute-start.7 = (bf16[288,2048]{1,0:T(8,128)(2,1)}, bf16[288,2048]{1,0:T(8,128)(2,1)}, u32[]{:S(2)}, u32[]{:S(2)}) collective-permute-start(bf16[288,2048]{1,0:T(8,128)(2,1)} %get-tuple-element.36), channel_id=1, source_target_pairs={{0,384},{128,0},{256,128},{384,256},{1,385},{129,1},{257,129},{385... | collective-permute-start | bytes 3538952 | tf_op jit(solution)/shard_map/ppermute | solution.py:22
  133.2 12.1 %shard_map.123 = (bf16[256,2176]{1,0:T(8,128)(2,1)S(1)}, bf16[3,256,192]{2,1,0:T(8,128)(2,1)S(1)}, bf16[288,2048]{1,0:T(8,128)(2,1)}, bf16[288,2048]{1,0:T(8,128...) custom-call(bf16[128,4224]{1,0:T(8,128)(2,1)} %bitcast.1.refs_0_, bf16[128,4224]{1,0:T(8,128)(2,1)S(1)} %bitcast.17, ...), custom_call_target="tpu_custom_call" | custom-call | flops 1 | bytes 1048576 | tf_op jit(solution)/shard_map/pallas_call | solution.py:46
  145.4 1.9 collective-permute-start.8
  147.3 4.6 %collective-permute-start.9 = (bf16[288,2048]{1,0:T(8,128)(2,1)}, bf16[288,2048]{1,0:T(8,128)(2,1)}, u32[]{:S(2)}, u32[]{:S(2)}) collective-permute-start(bf16[288,2048]{1,0:T(8,128)(2,1)} %get-tuple-element.42), channel_id=1, source_target_pairs={{0,384},{128,0},{256,128},{384,256},{1,385},{129,1},{257,129},{385... | collective-permute-start | bytes 3538952 | tf_op jit(solution)/shard_map/ppermute | solution.py:22
  151.9 1.3 reshape.243
  153.1 13.5 %all-to-all-start.2 = ((bf16[128,2,2176]{2,1,0:T(2,128)(2,1)}), bf16[128,2,2176]{2,1,0:T(2,128)(2,1)}, u32[]{:S(2)}, u32[]{:S(2)}) async-start(bf16[128,2,2176]{2,1,0:T(2,128)(2,1)} %reshape.243), calls=%async_computation.2 | async-start | bytes 2228224 | tf_op jit(solution)/shard_map/all_to_all | solution.py:280
  166.7 1.3 copy-done.9
  167.9 1.3 copy-done.10
  169.2 3.8 %shard_map.124 = (bf16[192,2048]{1,0:T(8,128)(2,1)S(1)}, bf16[96,2048]{1,0:T(8,128)(2,1)}, bf16[96,2048]{1,0:T(8,128)(2,1)}, bf16[192,2048]{1,0:T(8,128)(2,1)S(1)}) custom-call(bf16[288,2048]{1,0:T(8,128)(2,1)S(1)} %copy-done.9, bf16[288,2048]{1,0:T(8,128)(2,1)} %collective-permute-done.6.from_far_top, bf16[288,2048]{1,0:T(8,128)(2,1)S(1)} %copy-done.10, ...), custom_call_target="tpu_custom_call" | custom-call | flops 999999995904 | bytes 1048576 | tf_op jit(solution)/shard_map/pallas_call | solution.py:46
  173.0 8.7 %collective-permute-done.8 = bf16[288,2048]{1,0:T(8,128)(2,1)} collective-permute-done((bf16[288,2048]{1,0:T(8,128)(2,1)}, bf16[288,2048]{1,0:T(8,128)(2,1)}, u32[]{:S(2)}, u32[]{:S(2)}) %collective-permute-start.8) | collective-permute-done | bytes 1179680 | tf_op jit(solution)/shard_map/ppermute | solution.py:22
  181.7 1.2 collective-permute-done.9
  182.9 5.0 %collective-permute-start.13 = (bf16[192,2048]{1,0:T(8,128)(2,1)S(1)}, bf16[192,2048]{1,0:T(8,128)(2,1)}, u32[]{:S(2)}, u32[]{:S(2)}) collective-permute-start(bf16[192,2048]{1,0:T(8,128)(2,1)S(1)} %get-tuple-element.56), channel_id=1, source_target_pairs={{0,384},{128,0},{256,128},{384,256},{1,385},{129,1},{257,129},{385... | collective-permute-start | bytes 2359304 | tf_op jit(solution)/shard_map/ppermute | solution.py:22
  188.0 1.9 collective-permute-start.12
  191.2 3.3 %shard_map.125 = (bf16[288,2048]{1,0:T(8,128)(2,1)}, bf16[288,2048]{1,0:T(8,128)(2,1)}) custom-call(bf16[128,4224]{1,0:T(8,128)(2,1)} %bitcast.1.refs_0_, bf16[128,4224]{1,0:T(8,128)(2,1)S(1)} %bitcast.18, f32[1,128]{1,0:T(1,128)S(1)} %compare_convert_fusion.refs_2_, bf16[3,256,192]{2,1,0:T(8,128)(2,1)S(1)} %get-tuple-element.48.refs_3_), custom_call_target="tpu_custom_call" | custom-call | flops 1 | bytes 1048576 | tf_op jit(solution)/shard_map/pallas_call | solution.py:46
  194.5 1.9 collective-permute-start.10
  196.4 4.8 %collective-permute-start.11 = (bf16[96,2048]{1,0:T(8,128)(2,1)}, bf16[96,2048]{1,0:T(8,128)(2,1)S(1)}, u32[]{:S(2)}, u32[]{:S(2)}) collective-permute-start(bf16[96,2048]{1,0:T(8,128)(2,1)} %get-tuple-element.44), channel_id=1, source_target_pairs={{0,384},{128,0},{256,128},{384,256},{1,385},{129,1},{257,129},{385... | collective-permute-start | bytes 1179656 | tf_op jit(solution)/shard_map/ppermute | solution.py:22
  201.2 1.4 collective-permute-done.13
  202.6 3.0 %fusion.2 = bf16[1,192,2048]{2,1,0:T(8,128)(2,1)} fusion(bf16[192,2048]{1,0:T(8,128)(2,1)} %collective-permute-done.13, bf16[288,2048]{1,0:T(8,128)(2,1)} %collective-permute-done.8, bf16[288,2048]{1,0:T(8,128)(2,1)} %get-tuple-element.53), kind=kLoop, calls=%fused_computation.7 | loop fusion | flops 2359296 | bytes 3145728 | tf_op jit(solution)/shard_map/broadcast_in_dim | solution.py:310
  205.6 2.3 collective-permute-done.12
  207.8 2.6 %fusion.1 = bf16[1,192,2048]{2,1,0:T(8,128)(2,1)} fusion(bf16[192,2048]{1,0:T(8,128)(2,1)} %collective-permute-done.12, bf16[288,2048]{1,0:T(8,128)(2,1)} %collective-permute-done.9, bf16[288,2048]{1,0:T(8,128)(2,1)S(1)} %copy-done.11), kind=kLoop, calls=%fused_computation.6 | loop fusion | flops 2359296 | bytes 3145728 | tf_op jit(solution)/shard_map/broadcast_in_dim | solution.py:310
  210.5 14.6 %all-to-all-done.2 = bf16[128,2,2176]{2,1,0:T(2,128)(2,1)} async-done(((bf16[128,2,2176]{2,1,0:T(2,128)(2,1)}), bf16[128,2,2176]{2,1,0:T(2,128)(2,1)}, u32[]{:S(2)}, u32[]{:S(2)}) %all-to-all-start.2) | async-done | bytes 1114144 | tf_op jit(solution)/shard_map/all_to_all | solution.py:280
  225.1 1.5 reshape.244
  227.5 1.0 convolution_convert_fusion
  229.2 1.6 add_convert_fusion.2
  230.8 1.0 maximum_bitcast_fusion
  (58 shorter events, 6.7 us)
Async XLA Ops:
  7.2 59.8 %all-gather.2.cloned.1.call-start = ((), (), s32[]{:S(2)}) async-start(), calls=%async_computation.3 | async-start | bytes 1216512 | tf_op jit(solution)/shard_map/all_gather | solution.py:245
  8.0 4.0 %copy-start.4 = (s32[16,8]{1,0:T(8,128)}, s32[16,8]{1,0:T(8,128)S(1)}, u32[]{:S(2)}) copy-start(s32[16,8]{1,0:T(8,128)S(1)} %fusion.10.rank_ref) | copy-start | bytes 1540
  8.8 0.8 copy-start.6
  9.6 0.8 copy-start.7
  10.4 0.7 copy-start.8
  15.3 68.2 %collective-permute-start.2 = (bf16[576,2048]{1,0:T(8,128)(2,1)}, bf16[576,2048]{1,0:T(8,128)(2,1)S(1)}, u32[]{:S(2)}, u32[]{:S(2)}) collective-permute-start(bf16[576,2048]{1,0:T(8,128)(2,1)} %pad_maximum_fusion.refs_8_), channel_id=1, source_target_pairs={{0,128},{128,256},{256,384},{384,0},{1,129},{129,257},{257,385},{3... | collective-permute-start | bytes 7077896 | tf_op jit(solution)/shard_map/ppermute | solution.py:22
  18.4 69.8 %collective-permute-start.4 = (bf16[576,2048]{1,0:T(8,128)(2,1)}, bf16[576,2048]{1,0:T(8,128)(2,1)}, u32[]{:S(2)}, u32[]{:S(2)}) collective-permute-start(bf16[576,2048]{1,0:T(8,128)(2,1)} %pad_maximum_fusion.refs_8_), channel_id=1, source_target_pairs={{0,384},{128,0},{256,128},{384,256},{1,385},{129,1},{257,129},{385... | collective-permute-start | bytes 7077896 | tf_op jit(solution)/shard_map/ppermute | solution.py:22
  66.9 7.8 %copy-start.2 = (bf16[128,4224]{1,0:T(8,128)(2,1)S(1)}, bf16[128,4224]{1,0:T(8,128)(2,1)}, u32[]{:S(2)}) copy-start(bf16[128,4224]{1,0:T(8,128)(2,1)} %all-gather.2.cloned.1.call-done.refs_0_) | copy-start | bytes 3244036
  69.3 24.8 %collective-permute-start = (bf16[64,4224]{1,0:T(8,128)(2,1)}, bf16[64,4224]{1,0:T(8,128)(2,1)}, u32[]{:S(2)}, u32[]{:S(2)}) collective-permute-start(bf16[64,4224]{1,0:T(8,128)(2,1)} %get-tuple-element.68), channel_id=1, source_target_pairs={{0,30},{2,0},{4,2},{6,4},{8,6},{10,8},{12,10},{14,12},{16,14},{18,... | collective-permute-start | bytes 1622024 | tf_op jit(solution)/shard_map/ppermute | solution.py:22
  71.2 22.9 %collective-permute-start.1 = (bf16[64,4224]{1,0:T(8,128)(2,1)}, bf16[64,4224]{1,0:T(8,128)(2,1)}, u32[]{:S(2)}, u32[]{:S(2)}) collective-permute-start(bf16[64,4224]{1,0:T(8,128)(2,1)} %get-tuple-element.67), channel_id=1, source_target_pairs={{0,2},{2,4},{4,6},{6,8},{8,10},{10,12},{12,14},{14,16},{16,18},{18... | collective-permute-start | bytes 1622024 | tf_op jit(solution)/shard_map/ppermute | solution.py:22
  75.4 1.0 copy-start.3
  76.4 22.6 %all-to-all-start = ((bf16[8,16,4224]{2,1,0:T(8,128)(2,1)}), bf16[8,16,4224]{2,1,0:T(8,128)(2,1)}, u32[]{:S(2)}, u32[]{:S(2)}) async-start(bf16[8,16,4224]{2,1,0:T(8,128)(2,1)} %bitcast.19), calls=%async_computation | async-start | bytes 2162688 | tf_op jit(solution)/shard_map/all_to_all | solution.py:96
  83.4 1.8 copy-start
  85.2 33.6 %collective-permute-start.3 = (bf16[288,2048]{1,0:T(8,128)(2,1)}, bf16[288,2048]{1,0:T(8,128)(2,1)}, u32[]{:S(2)}, u32[]{:S(2)}) collective-permute-start(bf16[288,2048]{1,0:T(8,128)(2,1)} %slice.62), channel_id=1, source_target_pairs={{0,128},{128,256},{256,384},{384,0},{1,129},{129,257},{257,385},{3... | collective-permute-start | bytes 3538952 | tf_op jit(solution)/shard_map/ppermute | solution.py:22
  90.6 29.5 %collective-permute-start.5 = (bf16[288,2048]{1,0:T(8,128)(2,1)}, bf16[288,2048]{1,0:T(8,128)(2,1)}, u32[]{:S(2)}, u32[]{:S(2)}) collective-permute-start(bf16[288,2048]{1,0:T(8,128)(2,1)} %slice.63), channel_id=1, source_target_pairs={{0,384},{128,0},{256,128},{384,256},{1,385},{129,1},{257,129},{385... | collective-permute-start | bytes 3538952 | tf_op jit(solution)/shard_map/ppermute | solution.py:22
  99.0 19.8 %all-to-all-start.1 = ((bf16[8,16,4224]{2,1,0:T(8,128)(2,1)}), bf16[8,16,4224]{2,1,0:T(8,128)(2,1)S(1)}, u32[]{:S(2)}, u32[]{:S(2)}) async-start(bf16[8,16,4224]{2,1,0:T(8,128)(2,1)} %bitcast.2), calls=%async_computation.1 | async-start | bytes 2162688 | tf_op jit(solution)/shard_map/all_to_all | solution.py:96
  120.0 13.2 %copy-start.1 = (bf16[576,2048]{1,0:T(8,128)(2,1)S(1)}, bf16[576,2048]{1,0:T(8,128)(2,1)}, u32[]{:S(2)}) copy-start(bf16[576,2048]{1,0:T(8,128)(2,1)} %copy-done) | copy-start | bytes 7077892
  126.2 40.4 %collective-permute-start.6 = (bf16[288,2048]{1,0:T(8,128)(2,1)}, bf16[288,2048]{1,0:T(8,128)(2,1)}, u32[]{:S(2)}, u32[]{:S(2)}) collective-permute-start(bf16[288,2048]{1,0:T(8,128)(2,1)} %get-tuple-element.34), channel_id=1, source_target_pairs={{0,128},{128,256},{256,384},{384,0},{1,129},{129,257},{257,385},{3... | collective-permute-start | bytes 3538952 | tf_op jit(solution)/shard_map/ppermute | solution.py:22
  129.3 37.3 %collective-permute-start.7 = (bf16[288,2048]{1,0:T(8,128)(2,1)}, bf16[288,2048]{1,0:T(8,128)(2,1)}, u32[]{:S(2)}, u32[]{:S(2)}) collective-permute-start(bf16[288,2048]{1,0:T(8,128)(2,1)} %get-tuple-element.36), channel_id=1, source_target_pairs={{0,384},{128,0},{256,128},{384,256},{1,385},{129,1},{257,129},{385... | collective-permute-start | bytes 3538952 | tf_op jit(solution)/shard_map/ppermute | solution.py:22
  145.4 36.3 %collective-permute-start.8 = (bf16[288,2048]{1,0:T(8,128)(2,1)}, bf16[288,2048]{1,0:T(8,128)(2,1)}, u32[]{:S(2)}, u32[]{:S(2)}) collective-permute-start(bf16[288,2048]{1,0:T(8,128)(2,1)} %get-tuple-element.41), channel_id=1, source_target_pairs={{0,128},{128,256},{256,384},{384,0},{1,129},{129,257},{257,385},{3... | collective-permute-start | bytes 3538952 | tf_op jit(solution)/shard_map/ppermute | solution.py:22
  147.3 35.6 %collective-permute-start.9 = (bf16[288,2048]{1,0:T(8,128)(2,1)}, bf16[288,2048]{1,0:T(8,128)(2,1)}, u32[]{:S(2)}, u32[]{:S(2)}) collective-permute-start(bf16[288,2048]{1,0:T(8,128)(2,1)} %get-tuple-element.42), channel_id=1, source_target_pairs={{0,384},{128,0},{256,128},{384,256},{1,385},{129,1},{257,129},{385... | collective-permute-start | bytes 3538952 | tf_op jit(solution)/shard_map/ppermute | solution.py:22
  153.1 71.9 %all-to-all-start.2 = ((bf16[128,2,2176]{2,1,0:T(2,128)(2,1)}), bf16[128,2,2176]{2,1,0:T(2,128)(2,1)}, u32[]{:S(2)}, u32[]{:S(2)}) async-start(bf16[128,2,2176]{2,1,0:T(2,128)(2,1)} %reshape.243), calls=%async_computation.2 | async-start | bytes 2228224 | tf_op jit(solution)/shard_map/all_to_all | solution.py:280
  166.6 1.3 copy-start.9
  167.9 1.3 copy-start.10
  169.2 18.7 %copy-start.5 = (s32[16,8]{1,0:T(8,128)S(1)}, s32[16,8]{1,0:T(8,128)}, u32[]{:S(2)}) copy-start(s32[16,8]{1,0:T(8,128)} %copy-done.4) | copy-start | bytes 1540
  182.9 19.7 %collective-permute-start.13 = (bf16[192,2048]{1,0:T(8,128)(2,1)S(1)}, bf16[192,2048]{1,0:T(8,128)(2,1)}, u32[]{:S(2)}, u32[]{:S(2)}) collective-permute-start(bf16[192,2048]{1,0:T(8,128)(2,1)S(1)} %get-tuple-element.56), channel_id=1, source_target_pairs={{0,384},{128,0},{256,128},{384,256},{1,385},{129,1},{257,129},{385... | collective-permute-start | bytes 2359304 | tf_op jit(solution)/shard_map/ppermute | solution.py:22
  188.0 19.8 %collective-permute-start.12 = (bf16[192,2048]{1,0:T(8,128)(2,1)S(1)}, bf16[192,2048]{1,0:T(8,128)(2,1)}, u32[]{:S(2)}, u32[]{:S(2)}) collective-permute-start(bf16[192,2048]{1,0:T(8,128)(2,1)S(1)} %get-tuple-element.51), channel_id=1, source_target_pairs={{0,128},{128,256},{256,384},{384,0},{1,129},{129,257},{257,385},{3... | collective-permute-start | bytes 2359304 | tf_op jit(solution)/shard_map/ppermute | solution.py:22
  194.5 34.0 %collective-permute-start.10 = (bf16[96,2048]{1,0:T(8,128)(2,1)}, bf16[96,2048]{1,0:T(8,128)(2,1)S(1)}, u32[]{:S(2)}, u32[]{:S(2)}) collective-permute-start(bf16[96,2048]{1,0:T(8,128)(2,1)} %get-tuple-element.43), channel_id=1, source_target_pairs={{0,128},{128,256},{256,384},{384,0},{1,129},{129,257},{257,385},{3... | collective-permute-start | bytes 1179656 | tf_op jit(solution)/shard_map/ppermute | solution.py:22
  196.4 32.1 %collective-permute-start.11 = (bf16[96,2048]{1,0:T(8,128)(2,1)}, bf16[96,2048]{1,0:T(8,128)(2,1)S(1)}, u32[]{:S(2)}, u32[]{:S(2)}) collective-permute-start(bf16[96,2048]{1,0:T(8,128)(2,1)} %get-tuple-element.44), channel_id=1, source_target_pairs={{0,384},{128,0},{256,128},{384,256},{1,385},{129,1},{257,129},{385... | collective-permute-start | bytes 1179656 | tf_op jit(solution)/shard_map/ppermute | solution.py:22
  202.6 5.3 %copy-start.11 = (bf16[288,2048]{1,0:T(8,128)(2,1)S(1)}, bf16[288,2048]{1,0:T(8,128)(2,1)}, u32[]{:S(2)}) copy-start(bf16[288,2048]{1,0:T(8,128)(2,1)} %get-tuple-element.49) | copy-start | bytes 3538948
  210.5 17.0 %copy-start.12 = (pred[16,256]{0,1:T(32,128)(4,1)S(1)}, pred[16,256]{0,1:T(32,128)(4,1)}, u32[]{:S(2)}) copy-start(pred[16,256]{0,1:T(32,128)(4,1)} %and.134) | copy-start | bytes 12292
Sparse Core Ops, SparseCore 0:
  12.1 54.8 all-gather.1

commit v5 on v4

v5 whole, which is shorter than its diff:
```python
import functools

import jax
import jax.numpy as jnp
from jax import lax
from jax.experimental import pallas as pl
from jax.experimental.pallas import tpu as pltpu
from jax.sharding import Mesh, PartitionSpec as P

BLOCK = 128
DP, Y, Z, CORE = 4, 4, 16, 2
YC = Y * CORE
CAP = 2
LANES = 128
MIB = 2**20
LONG = 10**12
MEDIUM = 3 * 10**10
F32, BF16, I32 = jnp.float32, jnp.bfloat16, jnp.int32
sds = jax.ShapeDtypeStruct


def shift(a, axis, size, k):
    return lax.ppermute(a, axis, [(i, (i + k) % size) for i in range(size)])


def nt(a, b):
    return lax.dot_general(a, b, (((1,), (1,)), ((), ())), preferred_element_type=F32)


def tn(a, b):
    return lax.dot_general(a, b, (((0,), (0,)), ((), ())), preferred_element_type=F32)


def nn(a, b):
    return jnp.dot(a, b, preferred_element_type=F32)


def iota(shape, dim):
    return lax.broadcasted_iota(I32, shape, dim)


def whole(a):
    return pl.BlockSpec(a.shape, lambda *_: (0,) * len(a.shape))


def call(kernel, operands, out_shape, in_specs=None, out_specs=None, grid=(1,), vmem=24, cost=1, scratch=()):
    return pl.pallas_call(
        kernel,
        grid=grid,
        out_shape=out_shape,
        in_specs=in_specs or [whole(a) for a in operands],
        out_specs=out_specs or [whole(o) for o in out_shape],
        scratch_shapes=scratch,
        compiler_params=pltpu.CompilerParams(vmem_limit_bytes=vmem * MIB),
        cost_estimate=pl.CostEstimate(flops=cost, bytes_accessed=MIB, transcendentals=0),
    )(*operands)


def move_kernel(plan, count, *refs):
    sources, targets, sems = refs[:count], refs[count:-1], refs[-1]
    copies = [
        pltpu.make_async_copy(sources[i].at[pl.ds(a, n)], targets[o].at[pl.ds(b, n)], sems.at[k])
        for k, (i, a, n, o, b) in enumerate(plan)
    ]
    for c in copies:
        c.start()
    for c in copies:
        c.wait()


def move(arrays, plan, out_rows):
    width = arrays[0].shape[1]
    return pl.pallas_call(
        functools.partial(move_kernel, plan, len(arrays)),
        out_shape=[pltpu.HBM((n, width), BF16) for n in out_rows],
        in_specs=[pl.BlockSpec(memory_space=pl.ANY)] * len(arrays),
        out_specs=[pl.BlockSpec(memory_space=pl.ANY)] * len(out_rows),
        scratch_shapes=[pltpu.SemaphoreType.DMA((len(plan),))],
        compiler_params=pltpu.CompilerParams(vmem_limit_bytes=2 * MIB),
    )(*arrays)


def rank_of(ids):
    return ids // (Z * CORE) * (Z * CORE) + ids % CORE * Z + ids // CORE % Z


def payload_kernel(codes_ref, scales_ref, grad_ref, combine_ref, rank_ref, out_ref):
    tokens, width = codes_ref.shape
    count = scales_ref.shape[1]
    spread = (iota((count, width), 1) // BLOCK == iota((count, width), 0)).astype(BF16)
    scale = nn(scales_ref[...], spread)
    out_ref[:, :width] = (codes_ref[...].astype(F32) * scale).astype(BF16)
    out_ref[:, width : 2 * width] = grad_ref[...]
    lane = iota((tokens, LANES), 1)
    dense = jnp.zeros((tokens, LANES), F32)
    for k in range(rank_ref.shape[1]):
        dense += jnp.where(rank_ref[:, k : k + 1] == lane, combine_ref[:, k : k + 1], 0.0)
    out_ref[:, 2 * width :] = dense.astype(BF16)


def dispatch_kernel(tokens, pick_ref, *refs):
    *pieces, out_ref = refs
    chunk = jnp.concatenate([r[...] for r in pieces], axis=0)
    n = chunk.shape[0]
    member = (chunk[:, -LANES:].astype(F32) != 0).astype(BF16)
    local = nt(pick_ref[...], member)
    ti, tj = iota((n, n), 0), iota((n, n), 1)
    earlier = ((ti // tokens == tj // tokens) & (ti < tj)).astype(BF16)
    slot = nn(local.astype(BF16), earlier).astype(I32) + iota(local.shape, 1) // tokens * CAP
    slot = jnp.where(local > 0, slot, -1)
    slots = n // tokens * CAP
    row = iota((slots, n), 0)
    select = jnp.concatenate([slot[d : d + 1] == row for d in range(YC)], axis=0).astype(F32).astype(BF16)
    out_ref[...] = nn(select, chunk).astype(BF16)


def dispatch(pieces, pick, tokens, cost=1):
    n, width = sum(p.shape[0] for p in pieces), pieces[0].shape[1]
    slots = n // tokens * CAP
    (sent,) = call(functools.partial(dispatch_kernel, tokens), (pick, *pieces), [sds((YC * slots, width), BF16)], vmem=16, cost=cost)
    got = lax.all_to_all(sent.reshape(YC, slots, width), ("y", "core"), split_axis=0, concat_axis=0, tiled=True)
    return got.reshape(YC * slots, width)


def forward_kernel(count, own_ref, perm_ref, *refs):
    rows, refs = refs[:count], refs[count:]
    weights, (back_ref, *acts_refs, bufs, sems) = refs[:5], refs[5:]
    half = bufs.shape[1] // 2
    copies = [[pltpu.make_async_copy(weights[k], bufs.at[k], sems.at[k])] for k in range(3)]
    copies.append(
        [pltpu.make_async_copy(weights[3 + k], bufs.at[3, pl.ds(k * half, half)], sems.at[3 + k]) for k in range(2)]
    )
    for c in sum(copies, []):
        c.start()
    width = bufs.shape[2]
    share = bufs.shape[1] // 3
    take = lambda a, b: jnp.concatenate([r[:, a:b] for r in rows], axis=0)
    x, grad = take(0, width), take(width, 2 * width)
    n = x.shape[0]
    weight = nt(own_ref[...], take(2 * width, 2 * width + LANES))[:1]
    total, comb = jnp.zeros((n, width), F32), jnp.zeros((1, n), F32)
    for k in range(4):
        for c in copies[k]:
            c.wait()
        both = nt(bufs[k, : 2 * share], x)
        back = nt(bufs[k, 2 * share :], grad)
        gate, up = both[:share], both[share:]
        sig = jax.nn.sigmoid(gate)
        act = gate * sig
        hidden = (act * up).astype(BF16)
        comb += jnp.sum(back * hidden.astype(F32), axis=0, keepdims=True)
        gh = weight * back
        d_gate = gh * up * sig * (1.0 + gate * (1.0 - sig))
        d_both = jnp.concatenate([d_gate, gh * act], axis=0).astype(BF16)
        acts_refs[k][: 2 * share] = d_both
        acts_refs[k][2 * share :] = hidden
        total += tn(d_both, bufs[k, : 2 * share]).astype(BF16).astype(F32)
    perm = perm_ref[...]
    back_ref[:, :width] = nn(perm, total.astype(BF16)).astype(BF16)
    high = comb.astype(BF16).astype(F32)
    line = iota((LANES, n), 0)
    tail = jnp.where(line == 0, high, jnp.where(line == 1, comb - high, 0.0)).astype(BF16)
    back_ref[:, width:] = nt(perm, tail).astype(BF16)


def grads_kernel(planes_ref, own_ref, *refs):
    parts, chunks, (gate_ref, up_ref, down_ref, acts_ref) = refs[:DP], refs[DP:-4], refs[-4:]
    share = gate_ref.shape[0]
    count = len(chunks) // 3
    part = parts[0].shape[1] // count

    @pl.when(pl.program_id(0) == 0)
    def _():
        for k in range(DP):
            for c in range(count):
                at = pl.multiple_of((c * DP + planes_ref[k]) * part, part)
                acts_ref[:, pl.ds(at, part)] = parts[k][:, c * part : (c + 1) * part]

    both, down = 0.0, 0.0
    for c in range(count):
        x_ref, grad_ref, tail_ref = chunks[3 * c : 3 * c + 3]
        at = slice(c * DP * part, (c + 1) * DP * part)
        weight = jnp.sum(tail_ref[...].astype(F32) * own_ref[...], axis=1, keepdims=True)
        scaled = (weight * grad_ref[...].astype(F32)).astype(BF16)
        both += nn(acts_ref[: 2 * share, at], x_ref[...])
        down += nn(acts_ref[2 * share :, at], scaled)
    gate_ref[...] = both[:share].astype(BF16)
    up_ref[...] = both[share:].astype(BF16)
    down_ref[...] = down.astype(BF16)


def weight_grads(planes, own, acts, chunks, share, width, tile=512):
    chunks = [pltpu.with_memory_space_constraint(c, pltpu.HBM) for c in chunks]
    operands = [planes, own, *acts]
    specs = [pl.BlockSpec(memory_space=pltpu.SMEM), whole(own), *[whole(a) for a in acts]]
    for c in chunks:
        n = c.shape[0]
        operands += [c] * 3
        specs += [
            pl.BlockSpec((n, tile), lambda j: (0, j)),
            pl.BlockSpec((n, tile), lambda j: (0, width // tile + j)),
            pl.BlockSpec((n, LANES), lambda j: (0, 2 * width // LANES)),
        ]
    return call(
        grads_kernel,
        operands,
        [sds((share, width), BF16)] * 3,
        in_specs=specs,
        out_specs=[pl.BlockSpec((share, tile), lambda j: (0, j))] * 3,
        grid=(width // tile,),
        scratch=[pltpu.VMEM((3 * share, DP * acts[0].shape[1]), BF16)],
        vmem=28,
    )


def home_kernel(home_ref, rank_ref, grad_ref, comb_ref):
    tokens, picks = rank_ref.shape
    width = grad_ref.shape[1]
    count = home_ref.shape[0]
    experts = count // CAP
    lane = iota((tokens, experts), 1)
    named = jnp.zeros((tokens, experts), F32)
    for k in range(picks):
        named += (rank_ref[:, k : k + 1] == lane).astype(F32)
    prior = nn((iota((tokens, tokens), 1) < iota((tokens, tokens), 0)).astype(BF16), named.astype(BF16))
    spread = (iota((experts, count), 1) // CAP == iota((experts, count), 0)).astype(BF16)
    slot = iota((tokens, count), 1)
    here = nn(named.astype(BF16), spread) > 0
    owner = (here & (nn(prior.astype(BF16), spread).astype(I32) == slot % CAP)).astype(F32)
    grad_ref[...] = nn(owner.astype(BF16), home_ref[:, :width]).astype(BF16)
    pair = (iota((tokens, LANES), 1) < 2).astype(BF16)
    value = owner * nt(pair, home_ref[:, width:])
    for k in range(picks):
        mine = jnp.where(rank_ref[:, k : k + 1] == slot // CAP, value, 0.0)
        comb_ref[:, k : k + 1] = jnp.sum(mine, axis=1, keepdims=True)


def body(grad_out, x_codes, x_scales, combine, expert_ids, w_gate, w_up, w_down):
    tokens, picks = expert_ids.shape
    width = grad_out.shape[1]
    share = w_gate.shape[1]
    experts = YC * Z
    count = experts * CAP
    z = lax.axis_index("z")
    yc = lax.axis_index("y") * CORE + lax.axis_index("core")
    rank = rank_of(expert_ids)
    (payload,) = call(
        payload_kernel,
        (x_codes, x_scales, grad_out, combine.astype(F32), rank),
        [sds((tokens, 2 * width + LANES), BF16)],
        vmem=8,
    )
    groups = [list(range(r, Z, 2)) for r in range(2)]
    seen = lax.all_gather(payload, "z", axis=0, tiled=True, axis_index_groups=groups)

    half = 3 * share // 2
    plan = [(k, 0, share, 0, k * share) for k in range(3)]
    (mine,) = move((w_gate[0], w_up[0], w_down[0]), plan, [3 * share])
    from_prev, from_next = shift(mine, "dp", DP, 1), shift(mine, "dp", DP, -1)
    top, bottom = move((from_prev, from_next), [(0, 0, half, 0, 0), (1, half, half, 1, 0)], [half] * 2)
    far = shift(top, "dp", DP, 1), shift(bottom, "dp", DP, -1)

    mid = seen.shape[0] // 2
    low, high = move((seen,), [(0, 0, mid, 0, 0), (0, mid, mid, 1, 0)], [mid] * 2)
    other = shift(low, "z", Z, -1), shift(high, "z", Z, 1)
    dest = iota((2 * YC, experts), 0)
    pick = ((dest < YC) & (iota((2 * YC, experts), 1) == dest * Z + z)).astype(BF16)
    rows = dispatch((seen,), pick, tokens), dispatch(other, pick, tokens, LONG)
    planes = [lax.all_gather(r, "dp", axis=0, tiled=True) for r in rows]

    own = (iota((16, experts), 1) == yc * Z + z).astype(F32)
    q = iota((count, 1), 0)
    q_z = q // CAP % Z
    at = (q_z + z) % 2 * (count // 2) + q // (Z * CAP) * Z + q_z // 2 * CAP + q % CAP
    perm = (at == iota((count, count), 1)).astype(BF16)
    weights = (mine, from_next, from_prev, *far)
    small = (own.astype(BF16), perm, *rows)
    back, a_own, a_next, a_prev, a_far = call(
        functools.partial(forward_kernel, len(rows)),
        (*small, *weights),
        [sds((count, width + LANES), BF16), *[sds((3 * share, count), BF16)] * DP],
        in_specs=[*[whole(a) for a in small], *[pl.BlockSpec(memory_space=pl.ANY)] * 5],
        scratch=[pltpu.VMEM((DP, 3 * share, width), BF16), pltpu.SemaphoreType.DMA((5,))],
        vmem=36,
        cost=MEDIUM,
    )
    home = lax.all_to_all(
        back.reshape(experts, CAP, -1), ("y", "core", "z"), split_axis=0, concat_axis=0, tiled=True
    ).reshape(count, -1)
    acts = a_own, shift(a_next, "dp", DP, 1), shift(a_prev, "dp", DP, -1), shift(a_far, "dp", DP, 2)
    origins = (lax.axis_index("dp") + jnp.array([0, 3, 1, 2], I32)) % DP
    grad_in, grad_combine = call(
        home_kernel, (home, rank), [sds((tokens, width), BF16), sds((tokens, picks), F32)], vmem=8
    )
    grad_gate, grad_up, grad_down = weight_grads(origins, own[:1], acts, planes, share, width)
    return grad_in, grad_combine, grad_gate[None], grad_up[None], grad_down[None]


def solution(mesh):
    fine = Mesh(mesh.devices.reshape(DP, Y, Z, CORE), ("dp", "y", "z", "core"))
    tok = P(("dp", "y", "z", "core"), None)
    wts = P(("y", "z", "core"), "dp", None)
    return jax.shard_map(
        body,
        mesh=fine,
        in_specs=(tok,) * 5 + (wts,) * 3,
        out_specs=(tok, tok, wts, wts, wts),
        check_vma=False,
    )
```

time: 240 us -> 298 us (1.24)
  the two profiles are of different devices: /device:TPU:65 before, /device:TPU:6 now
where the time goes in v5:
time: 298 us; the launch traced here: 295 us
  waiting for transfers between devices  119 us (40%)
  Pallas kernels  95.8 us (32%)
  starting transfers between devices  48.5 us (16%)
  local copies, waits for them, and re-layouts  16.9 us (6%)
  between operations  14.1 us (5%)
    pallas_call x3, Pallas kernels, move(): pl.pallas_call(functools.partial(move_kernel, plan, len(arrays)), out_sha...  75 us
    all_to_all x1, waiting for transfers between devices, body(): lax.all_to_all(back.reshape(experts, CAP, -1), ('y', 'core', 'z'), split_...  47.3 us
    all_gather x1, waiting for transfers between devices, body(): lax.all_gather(payload, 'z', axis=0, tiled=True, axis_index_groups=groups)  43 us
    ppermute x9, starting transfers between devices, shift(): return lax.ppermute(a, axis, [(i, (i + k) % size) for i in range(size)])  29.1 us
    pallas_call x6, Pallas kernels, call(): pl.pallas_call(kernel, grid=grid, out_shape=out_shape, in_specs=in_specs...  20.8 us
    all_to_all x2, waiting for transfers between devices, dispatch(): lax.all_to_all(sent.reshape(YC, slots, width), ('y', 'core'), split_axis=...  16.1 us
    unnamed x34, local copies, waits for them, and re-layouts  13.4 us
    ppermute x9, waiting for transfers between devices, shift(): return lax.ppermute(a, axis, [(i, (i + k) % size) for i in range(size)])  12.6 us
  transfers between devices with their start and end apart: 15, of which 5 were waited for; matrix products, arithmetic and copies ran while one was open for 1% of the time, Pallas kernels for 30%

profile of v5, /device:TPU:6, one launch (start us, length us, event | category | flops | bytes accessed | tf_op | source)
XLA Modules:
  0.0 294.6 jit_solution(10879668320549127102)
XLA Ops:
  7.2 0.0 all-gather.4.cloned.1.call-start
  7.2 0.8 copy.20
  8.0 0.8 copy.24.combine_ref
  8.8 0.8 copy-done.12
  9.6 0.8 copy-done.13
  10.4 0.7 copy-done.14
  11.1 0.8 shard_map.128
  12.0 1.1 copy-done.7
  13.1 1.1 copy-done.8
  14.2 1.1 copy-done.9
  15.4 1.4 shard_map.132.refs_2_
  16.8 2.7 collective-permute-start.2
  19.5 6.9 %collective-permute-start.3 = (bf16[576,2048]{1,0:T(8,128)(2,1)}, bf16[576,2048]{1,0:T(8,128)(2,1)}, u32[]{:S(2)}, u32[]{:S(2)}) collective-permute-start(bf16[576,2048]{1,0:T(8,128)(2,1)} %shard_map.132.refs_2_), channel_id=1, source_target_pairs={{0,128},{128,256},{256,384},{384,0},{1,129},{129,257},{257,385},{3... | collective-permute-start | bytes 7077896 | tf_op jit(solution)/shard_map/ppermute | solution.py:23
  26.5 0.1 fusion.8.pick_ref
  26.6 43.0 %all-gather.4.cloned.1.call-done.refs_0_ = bf16[128,4224]{1,0:T(8,128)(2,1)} async-done(((bf16[16,4224]{1,0:T(8,128)(2,1)}), bf16[128,4224]{1,0:T(8,128)(2,1)}) %all-gather.4.cloned.1.call-update) | async-done | bytes 1081360 | tf_op jit(solution)/shard_map/all_gather | solution.py:254
  69.6 1.2 copy-done.4
  70.8 1.7 shard_map.129
  72.5 4.4 %all-to-all-start = ((bf16[8,16,4224]{2,1,0:T(8,128)(2,1)}), bf16[8,16,4224]{2,1,0:T(8,128)(2,1)S(1)}, u32[]{:S(2)}, u32[]{:S(2)}) async-start(bf16[8,16,4224]{2,1,0:T(8,128)(2,1)} %bitcast), calls=%async_computation | async-start | bytes 2162688 | tf_op jit(solution)/shard_map/all_to_all | solution.py:121
  77.0 0.0 all-gather.6.cloned.1.call-start
  77.0 1.0 shard_map.130
  78.0 2.3 collective-permute-start
  80.3 3.5 %collective-permute-start.1 = (bf16[64,4224]{1,0:T(8,128)(2,1)}, bf16[64,4224]{1,0:T(8,128)(2,1)S(1)}, u32[]{:S(2)}, u32[]{:S(2)}) collective-permute-start(bf16[64,4224]{1,0:T(8,128)(2,1)} %get-tuple-element.20), channel_id=1, source_target_pairs={{0,2},{2,4},{4,6},{6,8},{8,10},{10,12},{12,14},{14,16},{16,18},{18... | collective-permute-start | bytes 1622024 | tf_op jit(solution)/shard_map/ppermute | solution.py:23
  83.9 72.6 %shard_map.133 = (bf16[288,2048]{1,0:T(8,128)(2,1)}, bf16[288,2048]{1,0:T(8,128)(2,1)}) custom-call(bf16[576,2048]{1,0:T(8,128)(2,1)} %collective-permute-done.3.refs_0_.refs_4_, bf16[576,2048]{1,0:T(8,128)(2,1)} %collective-permute-done.2.refs_1_.refs_3_), custom_call_target="tpu_custom_call" | custom-call | tf_op jit(solution)/shard_map/pallas_call | solution.py:73
  156.5 2.5 collective-permute-start.4
  159.0 3.4 %collective-permute-start.5 = (bf16[288,2048]{1,0:T(8,128)(2,1)}, bf16[288,2048]{1,0:T(8,128)(2,1)}, u32[]{:S(2)}, u32[]{:S(2)}) collective-permute-start(bf16[288,2048]{1,0:T(8,128)(2,1)} %get-tuple-element.22), channel_id=1, source_target_pairs={{0,384},{128,0},{256,128},{384,256},{1,385},{129,1},{257,129},{385... | collective-permute-start | bytes 3538952 | tf_op jit(solution)/shard_map/ppermute | solution.py:23
  162.4 1.0 copy-done
  163.4 1.7 shard_map.131
  165.1 4.9 %all-to-all-start.1 = ((bf16[8,16,4224]{2,1,0:T(8,128)(2,1)}), bf16[8,16,4224]{2,1,0:T(8,128)(2,1)S(1)}, u32[]{:S(2)}, u32[]{:S(2)}) async-start(bf16[8,16,4224]{2,1,0:T(8,128)(2,1)} %bitcast.2), calls=%async_computation.1 | async-start | bytes 2162688 | tf_op jit(solution)/shard_map/all_to_all | solution.py:121
  170.0 0.0 all-gather.8.cloned.1.call-start
  170.1 0.1 fusion.perm_ref
  170.2 16.1 %all-to-all-done.1 = bf16[8,16,4224]{2,1,0:T(8,128)(2,1)S(1)} async-done(((bf16[8,16,4224]{2,1,0:T(8,128)(2,1)}), bf16[8,16,4224]{2,1,0:T(8,128)(2,1)S(1)}, u32[]{:S(2)}, u32[]{:S(2)}) %all-to-all-start.1) | async-done | bytes 1081376 | tf_op jit(solution)/shard_map/all_to_all | solution.py:121
  186.3 1.0 copy-done.2
  187.4 6.0 %collective-permute-done.4.refs_5_ = bf16[288,2048]{1,0:T(8,128)(2,1)} collective-permute-done((bf16[288,2048]{1,0:T(8,128)(2,1)}, bf16[288,2048]{1,0:T(8,128)(2,1)}, u32[]{:S(2)}, u32[]{:S(2)}) %collective-permute-start.4) | collective-permute-done | bytes 1179680 | tf_op jit(solution)/shard_map/ppermute | solution.py:23
  193.4 6.5 %collective-permute-done.5.refs_6_ = bf16[288,2048]{1,0:T(8,128)(2,1)} collective-permute-done((bf16[288,2048]{1,0:T(8,128)(2,1)}, bf16[288,2048]{1,0:T(8,128)(2,1)}, u32[]{:S(2)}, u32[]{:S(2)}) %collective-permute-start.5) | collective-permute-done | bytes 1179680 | tf_op jit(solution)/shard_map/ppermute | solution.py:23
  199.9 1.3 copy-done.3
  201.2 1.7 copy-done.6
  202.8 8.5 %shard_map.134 = (bf16[256,2176]{1,0:T(8,128)(2,1)S(1)}, bf16[576,256]{1,0:T(8,128)(2,1)S(1)}, bf16[576,256]{1,0:T(8,128)(2,1)S(1)}, bf16[576,256]{1,0:T(8,128)(2,1)S(1)}, bf16[576,256]{1,0:T(8,128)(2,1)S(1)}) custom-call(bf16[16,128]{1,0:T(8,128)(2,1)S(1)} %iota.42.own_ref, bf16[256,256]{1,0:T(8,128)(2,1)S(1)} %fusion.perm_ref, ...), custom_call_target="tpu_custom_call" | custom-call | flops 30000001024 | bytes 1048576 | tf_op jit(solution)/shard_map/pallas_call | solution.py:47
  211.4 1.3 reshape.203
  212.6 9.9 %all-to-all-start.2 = ((bf16[128,2,2176]{2,1,0:T(2,128)(2,1)}), bf16[128,2,2176]{2,1,0:T(2,128)(2,1)}, u32[]{:S(2)}, u32[]{:S(2)}) async-start(bf16[128,2,2176]{2,1,0:T(2,128)(2,1)} %reshape.203), calls=%async_computation.2 | async-start | bytes 2228224 | tf_op jit(solution)/shard_map/all_to_all | solution.py:287
  222.6 1.9 collective-permute-start.6
  224.5 3.9 %collective-permute-start.7 = (bf16[576,256]{1,0:T(8,128)(2,1)S(1)}, bf16[576,256]{1,0:T(8,128)(2,1)S(1)}, u32[]{:S(2)}, u32[]{:S(2)}) collective-permute-start(bf16[576,256]{1,0:T(8,128)(2,1)S(1)} %get-tuple-element.28), channel_id=1, source_target_pairs={{0,384},{128,0},{256,128},{384,256},{1,385},{129,1},{257,129},{385... | collective-permute-start | bytes 884744 | tf_op jit(solution)/shard_map/ppermute | solution.py:23
  228.4 1.9 collective-permute-start.8
  230.4 47.3 %all-to-all-done.2 = bf16[128,2,2176]{2,1,0:T(2,128)(2,1)} async-done(((bf16[128,2,2176]{2,1,0:T(2,128)(2,1)}), bf16[128,2,2176]{2,1,0:T(2,128)(2,1)}, u32[]{:S(2)}, u32[]{:S(2)}) %all-to-all-start.2) | async-done | bytes 1114144 | tf_op jit(solution)/shard_map/all_to_all | solution.py:287
  277.7 1.5 reshape.204.home_ref
  279.2 1.2 shard_map.135
  280.4 0.7 copy.25
  281.1 0.0 all-gather.6.cloned.1.call-done.refs_4_.refs_5_.refs_6_
  281.1 6.9 %shard_map.136 = (bf16[192,2048]{1,0:T(8,128)(2,1)}, bf16[192,2048]{1,0:T(8,128)(2,1)}, bf16[192,2048]{1,0:T(8,128)(2,1)}) custom-call(s32[4]{0:T(128)S(1)} %and_select_fusion.planes_ref, f32[1,128]{1,0:T(1,128)S(1)} %compare_convert_fusion.own_ref, bf16[576,256]{1,0:T(8,128)(2,1)S(1)} %get-tuple-element.26.refs_0_, ...), custom_call_target="tpu_custom_call" | custom-call | flops 1 | bytes 1048576 | tf_op jit(solution)/shard_map/pallas_call | solution.py:47
  (41 shorter events, 0.2 us)
Async XLA Ops:
  7.2 62.4 %all-gather.4.cloned.1.call-start = ((), (), s32[]{:S(2)}) async-start(), calls=%async_computation.3 | async-start | bytes 1216512 | tf_op jit(solution)/shard_map/all_gather | solution.py:254
  8.0 8.8 %copy-start.10 = (s32[16,8]{1,0:T(8,128)}, s32[16,8]{1,0:T(8,128)S(1)}, u32[]{:S(2)}) copy-start(s32[16,8]{1,0:T(8,128)S(1)} %fusion.4.rank_ref) | copy-start | bytes 1540
  8.8 0.8 copy-start.12
  9.6 0.8 copy-start.13
  10.4 0.7 copy-start.14
  12.0 1.1 copy-start.7
  13.1 1.1 copy-start.8
  14.2 1.1 copy-start.9
  16.8 67.1 %collective-permute-start.2 = (bf16[576,2048]{1,0:T(8,128)(2,1)}, bf16[576,2048]{1,0:T(8,128)(2,1)}, u32[]{:S(2)}, u32[]{:S(2)}) collective-permute-start(bf16[576,2048]{1,0:T(8,128)(2,1)} %shard_map.132.refs_2_), channel_id=1, source_target_pairs={{0,384},{128,0},{256,128},{384,256},{1,385},{129,1},{257,129},{385... | collective-permute-start | bytes 7077896 | tf_op jit(solution)/shard_map/ppermute | solution.py:23
  19.5 64.3 %collective-permute-start.3 = (bf16[576,2048]{1,0:T(8,128)(2,1)}, bf16[576,2048]{1,0:T(8,128)(2,1)}, u32[]{:S(2)}, u32[]{:S(2)}) collective-permute-start(bf16[576,2048]{1,0:T(8,128)(2,1)} %shard_map.132.refs_2_), channel_id=1, source_target_pairs={{0,128},{128,256},{256,384},{384,0},{1,129},{129,257},{257,385},{3... | collective-permute-start | bytes 7077896 | tf_op jit(solution)/shard_map/ppermute | solution.py:23
  69.6 1.2 copy-start.4
  72.5 4.5 %copy-start.5 = (bf16[128,4224]{1,0:T(8,128)(2,1)S(1)}, bf16[128,4224]{1,0:T(8,128)(2,1)}, u32[]{:S(2)}) copy-start(bf16[128,4224]{1,0:T(8,128)(2,1)} %all-gather.4.cloned.1.call-done.refs_0_) | copy-start | bytes 3244036
  72.5 89.8 %all-to-all-start = ((bf16[8,16,4224]{2,1,0:T(8,128)(2,1)}), bf16[8,16,4224]{2,1,0:T(8,128)(2,1)S(1)}, u32[]{:S(2)}, u32[]{:S(2)}) async-start(bf16[8,16,4224]{2,1,0:T(8,128)(2,1)} %bitcast), calls=%async_computation | async-start | bytes 2162688 | tf_op jit(solution)/shard_map/all_to_all | solution.py:121
  77.0 204.1 %all-gather.6.cloned.1.call-start = ((), (), s32[]{:S(2)}) async-start(), calls=%async_computation.4 | async-start | bytes 5406720 | tf_op jit(solution)/shard_map/all_gather | solution.py:269
  78.0 85.4 %collective-permute-start = (bf16[64,4224]{1,0:T(8,128)(2,1)}, bf16[64,4224]{1,0:T(8,128)(2,1)S(1)}, u32[]{:S(2)}, u32[]{:S(2)}) collective-permute-start(bf16[64,4224]{1,0:T(8,128)(2,1)} %get-tuple-element.19), channel_id=1, source_target_pairs={{0,30},{2,0},{4,2},{6,4},{8,6},{10,8},{12,10},{14,12},{16,14},{18,... | collective-permute-start | bytes 1622024 | tf_op jit(solution)/shard_map/ppermute | solution.py:23
  80.3 83.0 %collective-permute-start.1 = (bf16[64,4224]{1,0:T(8,128)(2,1)}, bf16[64,4224]{1,0:T(8,128)(2,1)S(1)}, u32[]{:S(2)}, u32[]{:S(2)}) collective-permute-start(bf16[64,4224]{1,0:T(8,128)(2,1)} %get-tuple-element.20), channel_id=1, source_target_pairs={{0,2},{2,4},{4,6},{6,8},{8,10},{10,12},{12,14},{14,16},{16,18},{18... | collective-permute-start | bytes 1622024 | tf_op jit(solution)/shard_map/ppermute | solution.py:23
  156.5 36.9 %collective-permute-start.4 = (bf16[288,2048]{1,0:T(8,128)(2,1)}, bf16[288,2048]{1,0:T(8,128)(2,1)}, u32[]{:S(2)}, u32[]{:S(2)}) collective-permute-start(bf16[288,2048]{1,0:T(8,128)(2,1)} %get-tuple-element.21), channel_id=1, source_target_pairs={{0,128},{128,256},{256,384},{384,0},{1,129},{129,257},{257,385},{3... | collective-permute-start | bytes 3538952 | tf_op jit(solution)/shard_map/ppermute | solution.py:23
  159.0 41.0 %collective-permute-start.5 = (bf16[288,2048]{1,0:T(8,128)(2,1)}, bf16[288,2048]{1,0:T(8,128)(2,1)}, u32[]{:S(2)}, u32[]{:S(2)}) collective-permute-start(bf16[288,2048]{1,0:T(8,128)(2,1)} %get-tuple-element.22), channel_id=1, source_target_pairs={{0,384},{128,0},{256,128},{384,256},{1,385},{129,1},{257,129},{385... | collective-permute-start | bytes 3538952 | tf_op jit(solution)/shard_map/ppermute | solution.py:23
  162.4 1.0 copy-start
  165.1 34.8 %copy-start.1 = (bf16[8,16,4224]{2,1,0:T(8,128)(2,1)S(1)}, bf16[8,16,4224]{2,1,0:T(8,128)(2,1)}, u32[]{:S(2)}) copy-start(bf16[8,16,4224]{2,1,0:T(8,128)(2,1)} %copy-done) | copy-start | bytes 3244036
  165.1 21.2 %all-to-all-start.1 = ((bf16[8,16,4224]{2,1,0:T(8,128)(2,1)}), bf16[8,16,4224]{2,1,0:T(8,128)(2,1)S(1)}, u32[]{:S(2)}, u32[]{:S(2)}) async-start(bf16[8,16,4224]{2,1,0:T(8,128)(2,1)} %bitcast.2), calls=%async_computation.1 | async-start | bytes 2162688 | tf_op jit(solution)/shard_map/all_to_all | solution.py:121
  170.0 111.2 %all-gather.8.cloned.1.call-start = ((), (), s32[]{:S(2)}) async-start(), calls=%async_computation.5 | async-start | bytes 5406720 | tf_op jit(solution)/shard_map/all_gather | solution.py:269
  186.3 1.0 copy-start.2
  199.9 1.3 copy-start.3
  201.2 1.7 copy-start.6
  212.6 17.7 %copy-start.15 = (s32[4]{0:T(128)S(1)}, s32[4]{0:T(128)}, u32[]{:S(2)}) copy-start(s32[4]{0:T(128)} %constant.138.clone) | copy-start | bytes 52
  212.6 65.1 %all-to-all-start.2 = ((bf16[128,2,2176]{2,1,0:T(2,128)(2,1)}), bf16[128,2,2176]{2,1,0:T(2,128)(2,1)}, u32[]{:S(2)}, u32[]{:S(2)}) async-start(bf16[128,2,2176]{2,1,0:T(2,128)(2,1)} %reshape.203), calls=%async_computation.2 | async-start | bytes 2228224 | tf_op jit(solution)/shard_map/all_to_all | solution.py:287
  222.6 56.7 %copy-start.11 = (s32[16,8]{1,0:T(8,128)S(1)}, s32[16,8]{1,0:T(8,128)}, u32[]{:S(2)}) copy-start(s32[16,8]{1,0:T(8,128)} %copy-done.10) | copy-start | bytes 1540
  222.6 58.5 %collective-permute-start.6 = (bf16[576,256]{1,0:T(8,128)(2,1)S(1)}, bf16[576,256]{1,0:T(8,128)(2,1)S(1)}, u32[]{:S(2)}, u32[]{:S(2)}) collective-permute-start(bf16[576,256]{1,0:T(8,128)(2,1)S(1)} %get-tuple-element.27), channel_id=1, source_target_pairs={{0,128},{128,256},{256,384},{384,0},{1,129},{129,257},{257,385},{3... | collective-permute-start | bytes 884744 | tf_op jit(solution)/shard_map/ppermute | solution.py:23
  224.5 56.6 %collective-permute-start.7 = (bf16[576,256]{1,0:T(8,128)(2,1)S(1)}, bf16[576,256]{1,0:T(8,128)(2,1)S(1)}, u32[]{:S(2)}, u32[]{:S(2)}) collective-permute-start(bf16[576,256]{1,0:T(8,128)(2,1)S(1)} %get-tuple-element.28), channel_id=1, source_target_pairs={{0,384},{128,0},{256,128},{384,256},{1,385},{129,1},{257,129},{385... | collective-permute-start | bytes 884744 | tf_op jit(solution)/shard_map/ppermute | solution.py:23
  228.4 52.7 %collective-permute-start.8 = (bf16[576,256]{1,0:T(8,128)(2,1)S(1)}, bf16[576,256]{1,0:T(8,128)(2,1)S(1)}, u32[]{:S(2)}, u32[]{:S(2)}) collective-permute-start(bf16[576,256]{1,0:T(8,128)(2,1)S(1)} %get-tuple-element.29), channel_id=1, source_target_pairs={{0,256},{128,384},{256,0},{384,128},{1,257},{129,385},{257,1},{385... | collective-permute-start | bytes 884744 | tf_op jit(solution)/shard_map/ppermute | solution.py:23
Sparse Core Ops, SparseCore 0:
  12.1 57.4 all-gather.3
  163.5 61.3 all-gather.5
  227.0 51.7 all-gather.7

commit v6 on v5

--- a/solution.py
+++ b/solution.py
@@ -14,7 +14,6 @@
 LANES = 128
 MIB = 2**20
 LONG = 10**12
-MEDIUM = 3 * 10**10
 F32, BF16, I32 = jnp.float32, jnp.bfloat16, jnp.int32
 sds = jax.ShapeDtypeStruct
 
@@ -56,28 +55,41 @@
     )(*operands)
 
 
+def in_hbm(arrays):
+    return [pltpu.with_memory_space_constraint(a, pltpu.HBM) for a in arrays]
+
+
 def move_kernel(plan, count, *refs):
-    sources, targets, sems = refs[:count], refs[count:-1], refs[-1]
-    copies = [
-        pltpu.make_async_copy(sources[i].at[pl.ds(a, n)], targets[o].at[pl.ds(b, n)], sems.at[k])
-        for k, (i, a, n, o, b) in enumerate(plan)
+    sources, targets, buf, sems = refs[:count], refs[count:-2], refs[-2], refs[-1]
+    starts = [sum(p[2] for p in plan[:k]) for k in range(len(plan))]
+    loads = [
+        pltpu.make_async_copy(sources[i].at[pl.ds(a, n)], buf.at[pl.ds(s, n)], sems.at[k])
+        for k, (s, (i, a, n, o, b)) in enumerate(zip(starts, plan))
     ]
-    for c in copies:
+    stores = [
+        pltpu.make_async_copy(buf.at[pl.ds(s, n)], targets[o].at[pl.ds(b, n)], sems.at[len(plan) + k])
+        for k, (s, (i, a, n, o, b)) in enumerate(zip(starts, plan))
+    ]
+    for c in loads:
         c.start()
-    for c in copies:
+    for load, store in zip(loads, stores):
+        load.wait()
+        store.start()
+    for c in stores:
         c.wait()
 
 
-def move(arrays, plan, out_rows):
+def move(arrays, plan, out_rows, cost=1):
     width = arrays[0].shape[1]
     return pl.pallas_call(
         functools.partial(move_kernel, plan, len(arrays)),
         out_shape=[pltpu.HBM((n, width), BF16) for n in out_rows],
         in_specs=[pl.BlockSpec(memory_space=pl.ANY)] * len(arrays),
         out_specs=[pl.BlockSpec(memory_space=pl.ANY)] * len(out_rows),
-        scratch_shapes=[pltpu.SemaphoreType.DMA((len(plan),))],
-        compiler_params=pltpu.CompilerParams(vmem_limit_bytes=2 * MIB),
-    )(*arrays)
+        scratch_shapes=[pltpu.VMEM((sum(p[2] for p in plan), width), BF16), pltpu.SemaphoreType.DMA((2 * len(plan),))],
+        compiler_params=pltpu.CompilerParams(vmem_limit_bytes=6 * MIB),
+        cost_estimate=pl.CostEstimate(flops=cost, bytes_accessed=MIB, transcendentals=0),
+    )(*in_hbm(arrays))
 
 
 def rank_of(ids):
@@ -91,11 +103,12 @@
     scale = nn(scales_ref[...], spread)
     out_ref[:, :width] = (codes_ref[...].astype(F32) * scale).astype(BF16)
     out_ref[:, width : 2 * width] = grad_ref[...]
-    lane = iota((tokens, LANES), 1)
-    dense = jnp.zeros((tokens, LANES), F32)
-    for k in range(rank_ref.shape[1]):
-        dense += jnp.where(rank_ref[:, k : k + 1] == lane, combine_ref[:, k : k + 1], 0.0)
-    out_ref[:, 2 * width :] = dense.astype(BF16)
+    expert = iota((LANES, tokens), 0)
+    dense = jnp.zeros((LANES, tokens), F32)
+    for k in range(rank_ref.shape[0]):
+        dense += jnp.where(rank_ref[k : k + 1] == expert, combine_ref[k : k + 1], 0.0)
+    turn = (iota((LANES, LANES), 0) == iota((LANES, LANES), 1)).astype(BF16)
+    out_ref[:, 2 * width :] = tn(dense.astype(BF16), turn).astype(BF16)
 
 
 def dispatch_kernel(tokens, pick_ref, *refs):
@@ -116,10 +129,14 @@
 
 def dispatch(pieces, pick, tokens, cost=1):
     n, width = sum(p.shape[0] for p in pieces), pieces[0].shape[1]
-    slots = n // tokens * CAP
-    (sent,) = call(functools.partial(dispatch_kernel, tokens), (pick, *pieces), [sds((YC * slots, width), BF16)], vmem=16, cost=cost)
-    got = lax.all_to_all(sent.reshape(YC, slots, width), ("y", "core"), split_axis=0, concat_axis=0, tiled=True)
-    return got.reshape(YC * slots, width)
+    out = sds((YC * (n // tokens * CAP), width), BF16)
+    (sent,) = call(functools.partial(dispatch_kernel, tokens), (pick, *in_hbm(pieces)), [out], vmem=16, cost=cost)
+    return sent
+
+
+def to_experts(sent):
+    got = lax.all_to_all(sent.reshape(YC, -1, sent.shape[1]), ("y", "core"), split_axis=0, concat_axis=0, tiled=True)
+    return got.reshape(sent.shape)
 
 
 def forward_kernel(count, own_ref, perm_ref, *refs):
@@ -164,38 +181,36 @@
 
 
 def grads_kernel(planes_ref, own_ref, *refs):
-    parts, chunks, (gate_ref, up_ref, down_ref, acts_ref) = refs[:DP], refs[DP:-4], refs[-4:]
+    parts, tiles, (gate_ref, up_ref, down_ref, acts_ref) = refs[:DP], refs[DP:-4], refs[-4:]
     share = gate_ref.shape[0]
-    count = len(chunks) // 3
-    part = parts[0].shape[1] // count
+    part = parts[0].shape[1] // 2
 
     @pl.when(pl.program_id(0) == 0)
     def _():
         for k in range(DP):
-            for c in range(count):
-                at = pl.multiple_of((c * DP + planes_ref[k]) * part, part)
-                acts_ref[:, pl.ds(at, part)] = parts[k][:, c * part : (c + 1) * part]
+            at = pl.multiple_of(planes_ref[k] * part, part)
+            acts_ref[:, pl.ds(at, part)] = parts[k][:, :part]
+            acts_ref[:, (DP + k) * part : (DP + k + 1) * part] = parts[k][:, part:]
 
     both, down = 0.0, 0.0
-    for c in range(count):
-        x_ref, grad_ref, tail_ref = chunks[3 * c : 3 * c + 3]
+    for c, chunk in enumerate((tiles[:3], tiles[3:])):
+        x, grad, tail = (jnp.concatenate([r[...] for r in chunk[k::3]], axis=0) for k in range(3))
         at = slice(c * DP * part, (c + 1) * DP * part)
-        weight = jnp.sum(tail_ref[...].astype(F32) * own_ref[...], axis=1, keepdims=True)
-        scaled = (weight * grad_ref[...].astype(F32)).astype(BF16)
-        both += nn(acts_ref[: 2 * share, at], x_ref[...])
+        weight = jnp.sum(tail.astype(F32) * own_ref[...], axis=1, keepdims=True)
+        scaled = (weight * grad.astype(F32)).astype(BF16)
+        both += nn(acts_ref[: 2 * share, at], x)
         down += nn(acts_ref[2 * share :, at], scaled)
     gate_ref[...] = both[:share].astype(BF16)
     up_ref[...] = both[share:].astype(BF16)
     down_ref[...] = down.astype(BF16)
 
 
-def weight_grads(planes, own, acts, chunks, share, width, tile=512):
-    chunks = [pltpu.with_memory_space_constraint(c, pltpu.HBM) for c in chunks]
+def weight_grads(planes, own, acts, arrays, share, width, tile=512):
     operands = [planes, own, *acts]
     specs = [pl.BlockSpec(memory_space=pltpu.SMEM), whole(own), *[whole(a) for a in acts]]
-    for c in chunks:
-        n = c.shape[0]
-        operands += [c] * 3
+    for a in in_hbm(arrays):
+        n = a.shape[0]
+        operands += [a] * 3
         specs += [
             pl.BlockSpec((n, tile), lambda j: (0, j)),
             pl.BlockSpec((n, tile), lambda j: (0, width // tile + j)),
@@ -243,10 +258,9 @@
     count = experts * CAP
     z = lax.axis_index("z")
     yc = lax.axis_index("y") * CORE + lax.axis_index("core")
-    rank = rank_of(expert_ids)
     (payload,) = call(
         payload_kernel,
-        (x_codes, x_scales, grad_out, combine.astype(F32), rank),
+        (*in_hbm((x_codes, x_scales, grad_out)), combine.T.astype(F32), rank_of(expert_ids.T)),
         [sds((tokens, 2 * width + LANES), BF16)],
         vmem=8,
     )
@@ -265,34 +279,41 @@
     other = shift(low, "z", Z, -1), shift(high, "z", Z, 1)
     dest = iota((2 * YC, experts), 0)
     pick = ((dest < YC) & (iota((2 * YC, experts), 1) == dest * Z + z)).astype(BF16)
-    rows = dispatch((seen,), pick, tokens), dispatch(other, pick, tokens, LONG)
-    planes = [lax.all_gather(r, "dp", axis=0, tiled=True) for r in rows]
-
+    first = to_experts(dispatch((seen,), pick, tokens))
+    early = first
+    gathered = lax.all_gather(early, "dp", axis=0, tiled=True)
+    second = to_experts(dispatch(other, pick, tokens, LONG))
+    rows = first, second
+    prev_rows, next_rows = shift(second, "dp", DP, 1), shift(second, "dp", DP, -1)
     own = (iota((16, experts), 1) == yc * Z + z).astype(F32)
     q = iota((count, 1), 0)
     q_z = q // CAP % Z
     at = (q_z + z) % 2 * (count // 2) + q // (Z * CAP) * Z + q_z // 2 * CAP + q % CAP
     perm = (at == iota((count, count), 1)).astype(BF16)
-    weights = (mine, from_next, from_prev, *far)
-    small = (own.astype(BF16), perm, *rows)
+    weights = in_hbm((mine, from_next, from_prev, *far))
+    small = (own.astype(BF16), perm, *in_hbm(rows))
     back, a_own, a_next, a_prev, a_far = call(
         functools.partial(forward_kernel, len(rows)),
         (*small, *weights),
-        [sds((count, width + LANES), BF16), *[sds((3 * share, count), BF16)] * DP],
+        [sds((count, width + LANES), BF16), *[pltpu.HBM((3 * share, count), BF16)] * DP],
         in_specs=[*[whole(a) for a in small], *[pl.BlockSpec(memory_space=pl.ANY)] * 5],
         scratch=[pltpu.VMEM((DP, 3 * share, width), BF16), pltpu.SemaphoreType.DMA((5,))],
         vmem=36,
-        cost=MEDIUM,
+        cost=LONG,
     )
     home = lax.all_to_all(
         back.reshape(experts, CAP, -1), ("y", "core", "z"), split_axis=0, concat_axis=0, tiled=True
     ).reshape(count, -1)
     acts = a_own, shift(a_next, "dp", DP, 1), shift(a_prev, "dp", DP, -1), shift(a_far, "dp", DP, 2)
+    mid = second.shape[0] // 2
+    low, high = move((prev_rows, next_rows), [(0, 0, mid, 0, 0), (1, mid, mid, 1, 0)], [mid] * 2, LONG)
+    far_rows = shift(low, "dp", DP, 1), shift(high, "dp", DP, -1)
     origins = (lax.axis_index("dp") + jnp.array([0, 3, 1, 2], I32)) % DP
+    grads = weight_grads(origins, own[:1], acts, (gathered, second, prev_rows, next_rows, *far_rows), share, width)
+    home, (grad_gate, grad_up, grad_down) = lax.optimization_barrier((home, grads))
     grad_in, grad_combine = call(
-        home_kernel, (home, rank), [sds((tokens, width), BF16), sds((tokens, picks), F32)], vmem=8
-    )
-    grad_gate, grad_up, grad_down = weight_grads(origins, own[:1], acts, planes, share, width)
+        home_kernel, (home, rank_of(expert_ids)), [sds((tokens, width), BF16), sds((tokens, picks), F32)], vmem=8
+    )
     return grad_in, grad_combine, grad_gate[None], grad_up[None], grad_down[None]
 
 

time: 298 us -> 228 us (0.77)
  Pallas kernels: 95.8 us -> 36.7 us
  waiting for transfers between devices: 119 us -> 102 us
  starting transfers between devices: 48.5 us -> 64.9 us
  local copies, waits for them, and re-layouts: 16.9 us -> 8.03 us
    pallas_call x3 -> x4, Pallas kernels: 75 us -> 9.48 us  [move(): pl.pallas_call(functools.partial(move_kernel, plan, len(arrays)), out_sha...]
    all_to_all x1, waiting for transfers between devices: 47.3 us -> 10.6 us  [body(): lax.all_to_all(back.reshape(experts, CAP, -1), ('y', 'core', 'z'), split_...]
    ppermute x9 -> x13, starting transfers between devices: 29.1 us -> 46.2 us  [shift(): return lax.ppermute(a, axis, [(i, (i + k) % size) for i in range(size)])]
    ppermute x9 -> x13, waiting for transfers between devices: 12.6 us -> 28.2 us  [shift(): return lax.ppermute(a, axis, [(i, (i + k) % size) for i in range(size)])]
    unnamed x34 -> x20, local copies, waits for them, and re-layouts: 13.4 us -> 5.27 us
    pallas_call x6, Pallas kernels: 20.8 us -> 27.2 us  [call(): pl.pallas_call(kernel, grid=grid, out_shape=out_shape, in_specs=in_specs...]
  transfers between devices with their start and end apart: 15 -> 18, of which waited for: 5 -> 7; matrix products, arithmetic and copies ran while one was open for 1% -> 2% of each run, Pallas kernels for 30% -> 12%
where the time goes in v6:
time: 228 us; the launch traced here: 227 us
  waiting for transfers between devices  102 us (45%)
  starting transfers between devices  64.9 us (28%)
  Pallas kernels  36.7 us (16%)
  between operations  14.4 us (6%)
  local copies, waits for them, and re-layouts  8.03 us (4%)
    ppermute x13, starting transfers between devices, shift(): return lax.ppermute(a, axis, [(i, (i + k) % size) for i in range(size)])  46.2 us
    all_gather x1, waiting for transfers between devices, body(): lax.all_gather(payload, 'z', axis=0, tiled=True, axis_index_groups=groups)  45.5 us
    ppermute x13, waiting for transfers between devices, shift(): return lax.ppermute(a, axis, [(i, (i + k) % size) for i in range(size)])  28.2 us
    pallas_call x6, Pallas kernels, call(): pl.pallas_call(kernel, grid=grid, out_shape=out_shape, in_specs=in_specs...  27.2 us
    all_to_all x2, waiting for transfers between devices, to_experts(): lax.all_to_all(sent.reshape(YC, -1, sent.shape[1]), ('y', 'core'), split_...  17.4 us
    all_to_all x1, waiting for transfers between devices, body(): lax.all_to_all(back.reshape(experts, CAP, -1), ('y', 'core', 'z'), split_...  10.6 us
    all_to_all x1, starting transfers between devices, body(): lax.all_to_all(back.reshape(experts, CAP, -1), ('y', 'core', 'z'), split_...  10 us
    pallas_call x4, Pallas kernels, move(): pl.pallas_call(functools.partial(move_kernel, plan, len(arrays)), out_sha...  9.48 us
  transfers between devices with their start and end apart: 18, of which 7 were waited for; matrix products, arithmetic and copies ran while one was open for 2% of the time, Pallas kernels for 12%

profile of v6, /device:TPU:6, one launch (start us, length us, event | category | flops | bytes accessed | tf_op | source)
XLA Modules:
  0.0 227.4 jit_solution(463431466607395845)
XLA Ops:
  7.2 0.0 all-gather.3.cloned.1.call-start
  7.2 0.7 convert_bitcast_fusion.combine_ref
  7.9 0.7 fusion.14.rank_ref
  8.6 1.8 shard_map.128
  10.4 2.6 %shard_map.132.refs_2_ = bf16[576,2048]{1,0:T(8,128)(2,1)} custom-call(bf16[192,2048]{1,0:T(8,128)(2,1)} %bitcast.34, bf16[192,2048]{1,0:T(8,128)(2,1)} %bitcast.35, bf16[192,2048]{1,0:T(8,128)(2,1)} %bitcast.36), custom_call_target="tpu_custom_call" | custom-call | flops 1 | bytes 1048576 | tf_op jit(solution)/shard_map/pallas_call | solution.py:84
  13.0 2.7 %collective-permute-start.2 = (bf16[576,2048]{1,0:T(8,128)(2,1)}, bf16[576,2048]{1,0:T(8,128)(2,1)S(1)}, u32[]{:S(2)}, u32[]{:S(2)}) collective-permute-start(bf16[576,2048]{1,0:T(8,128)(2,1)} %shard_map.132.refs_2_), channel_id=1, source_target_pairs={{0,384},{128,0},{256,128},{384,256},{1,385},{129,1},{257,129},{385... | collective-permute-start | bytes 7077896 | tf_op jit(solution)/shard_map/ppermute | solution.py:22
  15.8 6.9 %collective-permute-start.3 = (bf16[576,2048]{1,0:T(8,128)(2,1)}, bf16[576,2048]{1,0:T(8,128)(2,1)}, u32[]{:S(2)}, u32[]{:S(2)}) collective-permute-start(bf16[576,2048]{1,0:T(8,128)(2,1)} %shard_map.132.refs_2_), channel_id=1, source_target_pairs={{0,128},{128,256},{256,384},{384,0},{1,129},{129,257},{257,385},{3... | collective-permute-start | bytes 7077896 | tf_op jit(solution)/shard_map/ppermute | solution.py:22
  22.7 45.5 %all-gather.3.cloned.1.call-done.refs_0_ = bf16[128,4224]{1,0:T(8,128)(2,1)} async-done(((bf16[16,4224]{1,0:T(8,128)(2,1)}), bf16[128,4224]{1,0:T(8,128)(2,1)}) %all-gather.3.cloned.1.call-update) | async-done | bytes 1081360 | tf_op jit(solution)/shard_map/all_gather | solution.py:268
  68.2 2.1 shard_map.130
  70.2 2.1 collective-permute-start
  72.3 3.8 %collective-permute-start.1 = (bf16[64,4224]{1,0:T(8,128)(2,1)}, bf16[64,4224]{1,0:T(8,128)(2,1)S(1)}, u32[]{:S(2)}, u32[]{:S(2)}) collective-permute-start(bf16[64,4224]{1,0:T(8,128)(2,1)} %get-tuple-element.26), channel_id=1, source_target_pairs={{0,2},{2,4},{4,6},{6,8},{8,10},{10,12},{12,14},{14,16},{16,18},{18... | collective-permute-start | bytes 1622024 | tf_op jit(solution)/shard_map/ppermute | solution.py:22
  76.1 0.1 fusion.8.pick_ref
  76.2 2.9 %shard_map.129 = bf16[128,4224]{1,0:T(8,128)(2,1)} custom-call(bf16[16,128]{1,0:T(8,128)(2,1)S(1)} %fusion.8.pick_ref, bf16[128,4224]{1,0:T(8,128)(2,1)} %all-gather.3.cloned.1.call-done.refs_0_), custom_call_target="tpu_custom_call" | custom-call | flops 1 | bytes 1048576 | tf_op jit(solution)/shard_map/pallas_call | solution.py:46
  79.1 4.3 %all-to-all-start = ((bf16[8,16,4224]{2,1,0:T(8,128)(2,1)}), bf16[8,16,4224]{2,1,0:T(8,128)(2,1)}, u32[]{:S(2)}, u32[]{:S(2)}) async-start(bf16[8,16,4224]{2,1,0:T(8,128)(2,1)} %bitcast.2), calls=%async_computation | async-start | bytes 2162688 | tf_op jit(solution)/shard_map/all_to_all | solution.py:138
  83.5 1.4 copy-done.3
  84.8 2.7 %shard_map.133 = (bf16[288,2048]{1,0:T(8,128)(2,1)}, bf16[288,2048]{1,0:T(8,128)(2,1)}) custom-call(bf16[576,2048]{1,0:T(8,128)(2,1)} %collective-permute-done.3.refs_0_.refs_4_, bf16[576,2048]{1,0:T(8,128)(2,1)} %copy-done.3), custom_call_target="tpu_custom_call" | custom-call | flops 1 | bytes 1048576 | tf_op jit(solution)/shard_map/pallas_call | solution.py:84
  87.5 2.4 %collective-permute-start.4 = (bf16[288,2048]{1,0:T(8,128)(2,1)}, bf16[288,2048]{1,0:T(8,128)(2,1)}, u32[]{:S(2)}, u32[]{:S(2)}) collective-permute-start(bf16[288,2048]{1,0:T(8,128)(2,1)} %get-tuple-element.27), channel_id=1, source_target_pairs={{0,128},{128,256},{256,384},{384,0},{1,129},{129,257},{257,385},{3... | collective-permute-start | bytes 3538952 | tf_op jit(solution)/shard_map/ppermute | solution.py:22
  90.0 3.4 %collective-permute-start.5 = (bf16[288,2048]{1,0:T(8,128)(2,1)}, bf16[288,2048]{1,0:T(8,128)(2,1)}, u32[]{:S(2)}, u32[]{:S(2)}) collective-permute-start(bf16[288,2048]{1,0:T(8,128)(2,1)} %get-tuple-element.28), channel_id=1, source_target_pairs={{0,384},{128,0},{256,128},{384,256},{1,385},{129,1},{257,129},{385... | collective-permute-start | bytes 3538952 | tf_op jit(solution)/shard_map/ppermute | solution.py:22
  93.4 0.8 copy-done.6
  94.2 0.8 copy-done.7
  95.0 2.9 %shard_map.131 = bf16[128,4224]{1,0:T(8,128)(2,1)} custom-call(bf16[16,128]{1,0:T(8,128)(2,1)S(1)} %fusion.8.pick_ref, bf16[64,4224]{1,0:T(8,128)(2,1)} %copy-done.6, bf16[64,4224]{1,0:T(8,128)(2,1)} %copy-done.7), custom_call_target="tpu_custom_call" | custom-call | flops 999999995904 | bytes 1048576 | tf_op jit(solution)/shard_map/pallas_call | solution.py:46
  97.9 1.9 all-to-all-done
  99.9 4.2 %all-to-all-start.1 = ((bf16[8,16,4224]{2,1,0:T(8,128)(2,1)}), bf16[8,16,4224]{2,1,0:T(8,128)(2,1)}, u32[]{:S(2)}, u32[]{:S(2)}) async-start(bf16[8,16,4224]{2,1,0:T(8,128)(2,1)} %bitcast.4), calls=%async_computation.1 | async-start | bytes 2162688 | tf_op jit(solution)/shard_map/all_to_all | solution.py:138
  104.1 0.0 all-gather.5.cloned.1.call-start
  104.2 0.7 copy.14
  104.9 0.1 fusion.perm_ref
  105.0 15.4 %all-to-all-done.1 = bf16[8,16,4224]{2,1,0:T(8,128)(2,1)} async-done(((bf16[8,16,4224]{2,1,0:T(8,128)(2,1)}), bf16[8,16,4224]{2,1,0:T(8,128)(2,1)}, u32[]{:S(2)}, u32[]{:S(2)}) %all-to-all-start.1) | async-done | bytes 1081376 | tf_op jit(solution)/shard_map/all_to_all | solution.py:138
  120.4 2.8 %collective-permute-start.10 = (bf16[128,4224]{1,0:T(8,128)(2,1)}, bf16[128,4224]{1,0:T(8,128)(2,1)}, u32[]{:S(2)}, u32[]{:S(2)}) collective-permute-start(bf16[128,4224]{1,0:T(8,128)(2,1)} %bitcast.5.refs_1_.refs_7_.refs_8_.refs_9_), channel_id=1, source_target_pairs={{0,384},{128,0},{256,128},{384,256},{1,385},{129,1},{257,129},{385... | collective-permute-start | bytes 3244040 | tf_op jit(solution)/shard_map/ppermute | solution.py:22
  123.2 4.3 %collective-permute-start.9 = (bf16[128,4224]{1,0:T(8,128)(2,1)}, bf16[128,4224]{1,0:T(8,128)(2,1)}, u32[]{:S(2)}, u32[]{:S(2)}) collective-permute-start(bf16[128,4224]{1,0:T(8,128)(2,1)} %bitcast.5.refs_1_.refs_7_.refs_8_.refs_9_), channel_id=1, source_target_pairs={{0,128},{128,256},{256,384},{384,0},{1,129},{129,257},{257,385},{3... | collective-permute-start | bytes 3244040 | tf_op jit(solution)/shard_map/ppermute | solution.py:22
  127.5 11.5 %shard_map.134 = (bf16[256,2176]{1,0:T(8,128)(2,1)S(1)}, bf16[576,256]{1,0:T(8,128)(2,1)}, bf16[576,256]{1,0:T(8,128)(2,1)}, bf16[576,256]{1,0:T(8,128)(2,1)}, bf16[576,256]{1,0:T(8,128)(2,1)}) custom-call(bf16[16,128]{1,0:T(8,128)(2,1)S(1)} %iota.42.own_ref, bf16[256,256]{1,0:T(8,128)(2,1)S(1)} %fusion.perm_ref, bf16[128,4224]{1,0:T(8,128)(2,1)} %bitcast.3.refs_0_, ...), custom_call_target="tpu_custom_call" | custom-call | flops 999999995904 | bytes 1048576 | tf_op jit(solution)/shard_map/pallas_call | solution.py:46
  139.0 1.3 reshape.203
  140.2 10.0 %all-to-all-start.2 = ((bf16[128,2,2176]{2,1,0:T(2,128)(2,1)}), bf16[128,2,2176]{2,1,0:T(2,128)(2,1)}, u32[]{:S(2)}, u32[]{:S(2)}) async-start(bf16[128,2,2176]{2,1,0:T(2,128)(2,1)} %reshape.203), calls=%async_computation.2 | async-start | bytes 2228224 | tf_op jit(solution)/shard_map/all_to_all | solution.py:304
  150.3 22.9 %collective-permute-done.10.refs_1_.refs_13_.refs_14_.refs_15_ = bf16[128,4224]{1,0:T(8,128)(2,1)} collective-permute-done((bf16[128,4224]{1,0:T(8,128)(2,1)}, bf16[128,4224]{1,0:T(8,128)(2,1)}, u32[]{:S(2)}, u32[]{:S(2)}) %collective-permute-start.10) | collective-permute-done | bytes 1081376 | tf_op jit(solution)/shard_map/ppermute | solution.py:22
  173.2 1.5 collective-permute-done.9.refs_0_.refs_10_.refs_11_.refs_12_
  174.7 2.1 shard_map.135
  176.8 5.5 %collective-permute-start.11 = (bf16[64,4224]{1,0:T(8,128)(2,1)}, bf16[64,4224]{1,0:T(8,128)(2,1)S(1)}, u32[]{:S(2)}, u32[]{:S(2)}) collective-permute-start(bf16[64,4224]{1,0:T(8,128)(2,1)} %get-tuple-element.34), channel_id=1, source_target_pairs={{0,128},{128,256},{256,384},{384,0},{1,129},{129,257},{257,385},{3... | collective-permute-start | bytes 1622024 | tf_op jit(solution)/shard_map/ppermute | solution.py:22
  182.3 1.9 collective-permute-start.12
  184.3 5.1 %collective-permute-start.6 = (bf16[576,256]{1,0:T(8,128)(2,1)}, bf16[576,256]{1,0:T(8,128)(2,1)S(1)}, u32[]{:S(2)}, u32[]{:S(2)}) collective-permute-start(bf16[576,256]{1,0:T(8,128)(2,1)} %get-tuple-element.31), channel_id=1, source_target_pairs={{0,128},{128,256},{256,384},{384,0},{1,129},{129,257},{257,385},{3... | collective-permute-start | bytes 884744 | tf_op jit(solution)/shard_map/ppermute | solution.py:22
  189.4 1.9 collective-permute-start.7
  191.4 3.4 %collective-permute-start.8 = (bf16[576,256]{1,0:T(8,128)(2,1)}, bf16[576,256]{1,0:T(8,128)(2,1)S(1)}, u32[]{:S(2)}, u32[]{:S(2)}) collective-permute-start(bf16[576,256]{1,0:T(8,128)(2,1)} %get-tuple-element.33), channel_id=1, source_target_pairs={{0,256},{128,384},{256,0},{384,128},{1,257},{129,385},{257,1},{385... | collective-permute-start | bytes 884744 | tf_op jit(solution)/shard_map/ppermute | solution.py:22
  194.8 10.6 %all-to-all-done.2 = bf16[128,2,2176]{2,1,0:T(2,128)(2,1)} async-done(((bf16[128,2,2176]{2,1,0:T(2,128)(2,1)}), bf16[128,2,2176]{2,1,0:T(2,128)(2,1)}, u32[]{:S(2)}, u32[]{:S(2)}) %all-to-all-start.2) | async-done | bytes 1114144 | tf_op jit(solution)/shard_map/all_to_all | solution.py:304
  205.4 1.5 reshape.204.home_ref
  206.9 3.7 %collective-permute-done.7.refs_2_ = bf16[576,256]{1,0:T(8,128)(2,1)S(1)} collective-permute-done((bf16[576,256]{1,0:T(8,128)(2,1)}, bf16[576,256]{1,0:T(8,128)(2,1)S(1)}, u32[]{:S(2)}, u32[]{:S(2)}) %collective-permute-start.7) | collective-permute-done | bytes 294944 | tf_op jit(solution)/shard_map/ppermute | solution.py:22
  210.8 0.8 copy-done.1
  211.5 0.2 copy-done.2
  211.7 7.0 %shard_map.136 = (bf16[192,2048]{1,0:T(8,128)(2,1)}, bf16[192,2048]{1,0:T(8,128)(2,1)}, bf16[192,2048]{1,0:T(8,128)(2,1)}) custom-call(s32[4]{0:T(128)S(1)} %and_select_fusion.planes_ref, f32[1,128]{1,0:T(1,128)S(1)} %compare_convert_fusion.own_ref, bf16[576,256]{1,0:T(8,128)(2,1)S(1)} %copy-done, bf16[576,256]{1,0:T(8,128)(2,1)S(1)} %collective-permute-done.6.refs_1_, ...), custom_call_target="tpu_custom_call" | custom-call | flops 1 | bytes 1048576 | tf_op jit(solution)/shard_map/pallas_call | solution.py:46
  218.7 1.2 shard_map.137
  219.9 0.7 copy.18
  (34 shorter events, 0.2 us)
Async XLA Ops:
  7.2 61.0 %all-gather.3.cloned.1.call-start = ((), (), s32[]{:S(2)}) async-start(), calls=%async_computation.3 | async-start | bytes 1216512 | tf_op jit(solution)/shard_map/all_gather | solution.py:268
  13.0 70.4 %collective-permute-start.2 = (bf16[576,2048]{1,0:T(8,128)(2,1)}, bf16[576,2048]{1,0:T(8,128)(2,1)S(1)}, u32[]{:S(2)}, u32[]{:S(2)}) collective-permute-start(bf16[576,2048]{1,0:T(8,128)(2,1)} %shard_map.132.refs_2_), channel_id=1, source_target_pairs={{0,384},{128,0},{256,128},{384,256},{1,385},{129,1},{257,129},{385... | collective-permute-start | bytes 7077896 | tf_op jit(solution)/shard_map/ppermute | solution.py:22
  15.8 67.7 %collective-permute-start.3 = (bf16[576,2048]{1,0:T(8,128)(2,1)}, bf16[576,2048]{1,0:T(8,128)(2,1)}, u32[]{:S(2)}, u32[]{:S(2)}) collective-permute-start(bf16[576,2048]{1,0:T(8,128)(2,1)} %shard_map.132.refs_2_), channel_id=1, source_target_pairs={{0,128},{128,256},{256,384},{384,0},{1,129},{129,257},{257,385},{3... | collective-permute-start | bytes 7077896 | tf_op jit(solution)/shard_map/ppermute | solution.py:22
  70.2 23.2 %collective-permute-start = (bf16[64,4224]{1,0:T(8,128)(2,1)}, bf16[64,4224]{1,0:T(8,128)(2,1)S(1)}, u32[]{:S(2)}, u32[]{:S(2)}) collective-permute-start(bf16[64,4224]{1,0:T(8,128)(2,1)} %get-tuple-element.25), channel_id=1, source_target_pairs={{0,30},{2,0},{4,2},{6,4},{8,6},{10,8},{12,10},{14,12},{16,14},{18,... | collective-permute-start | bytes 1622024 | tf_op jit(solution)/shard_map/ppermute | solution.py:22
  72.3 21.1 %collective-permute-start.1 = (bf16[64,4224]{1,0:T(8,128)(2,1)}, bf16[64,4224]{1,0:T(8,128)(2,1)S(1)}, u32[]{:S(2)}, u32[]{:S(2)}) collective-permute-start(bf16[64,4224]{1,0:T(8,128)(2,1)} %get-tuple-element.26), channel_id=1, source_target_pairs={{0,2},{2,4},{4,6},{6,8},{8,10},{10,12},{12,14},{14,16},{16,18},{18... | collective-permute-start | bytes 1622024 | tf_op jit(solution)/shard_map/ppermute | solution.py:22
  79.1 20.7 %all-to-all-start = ((bf16[8,16,4224]{2,1,0:T(8,128)(2,1)}), bf16[8,16,4224]{2,1,0:T(8,128)(2,1)}, u32[]{:S(2)}, u32[]{:S(2)}) async-start(bf16[8,16,4224]{2,1,0:T(8,128)(2,1)} %bitcast.2), calls=%async_computation | async-start | bytes 2162688 | tf_op jit(solution)/shard_map/all_to_all | solution.py:138
  83.4 1.4 copy-start.3
  87.5 39.9 %collective-permute-start.4 = (bf16[288,2048]{1,0:T(8,128)(2,1)}, bf16[288,2048]{1,0:T(8,128)(2,1)}, u32[]{:S(2)}, u32[]{:S(2)}) collective-permute-start(bf16[288,2048]{1,0:T(8,128)(2,1)} %get-tuple-element.27), channel_id=1, source_target_pairs={{0,128},{128,256},{256,384},{384,0},{1,129},{129,257},{257,385},{3... | collective-permute-start | bytes 3538952 | tf_op jit(solution)/shard_map/ppermute | solution.py:22
  90.0 37.5 %collective-permute-start.5 = (bf16[288,2048]{1,0:T(8,128)(2,1)}, bf16[288,2048]{1,0:T(8,128)(2,1)}, u32[]{:S(2)}, u32[]{:S(2)}) collective-permute-start(bf16[288,2048]{1,0:T(8,128)(2,1)} %get-tuple-element.28), channel_id=1, source_target_pairs={{0,384},{128,0},{256,128},{384,256},{1,385},{129,1},{257,129},{385... | collective-permute-start | bytes 3538952 | tf_op jit(solution)/shard_map/ppermute | solution.py:22
  93.4 0.8 copy-start.6
  94.2 0.8 copy-start.7
  97.9 6.2 %copy-start.5 = (s32[16,8]{0,1:T(8,128)S(1)}, s32[16,8]{0,1:T(8,128)}, u32[]{:S(2)}) copy-start(s32[16,8]{0,1:T(8,128)} %param.13) | copy-start | bytes 1540
  99.9 20.6 %all-to-all-start.1 = ((bf16[8,16,4224]{2,1,0:T(8,128)(2,1)}), bf16[8,16,4224]{2,1,0:T(8,128)(2,1)}, u32[]{:S(2)}, u32[]{:S(2)}) async-start(bf16[8,16,4224]{2,1,0:T(8,128)(2,1)} %bitcast.4), calls=%async_computation.1 | async-start | bytes 2162688 | tf_op jit(solution)/shard_map/all_to_all | solution.py:138
  104.1 106.6 %all-gather.5.cloned.1.call-start = ((), (), s32[]{:S(2)}) async-start(), calls=%async_computation.4 | async-start | bytes 5406720 | tf_op jit(solution)/shard_map/all_gather | solution.py:284
  120.4 52.8 %collective-permute-start.10 = (bf16[128,4224]{1,0:T(8,128)(2,1)}, bf16[128,4224]{1,0:T(8,128)(2,1)}, u32[]{:S(2)}, u32[]{:S(2)}) collective-permute-start(bf16[128,4224]{1,0:T(8,128)(2,1)} %bitcast.5.refs_1_.refs_7_.refs_8_.refs_9_), channel_id=1, source_target_pairs={{0,384},{128,0},{256,128},{384,256},{1,385},{129,1},{257,129},{385... | collective-permute-start | bytes 3244040 | tf_op jit(solution)/shard_map/ppermute | solution.py:22
  123.2 51.5 %collective-permute-start.9 = (bf16[128,4224]{1,0:T(8,128)(2,1)}, bf16[128,4224]{1,0:T(8,128)(2,1)}, u32[]{:S(2)}, u32[]{:S(2)}) collective-permute-start(bf16[128,4224]{1,0:T(8,128)(2,1)} %bitcast.5.refs_1_.refs_7_.refs_8_.refs_9_), channel_id=1, source_target_pairs={{0,128},{128,256},{256,384},{384,0},{1,129},{129,257},{257,385},{3... | collective-permute-start | bytes 3244040 | tf_op jit(solution)/shard_map/ppermute | solution.py:22
  140.2 65.2 %all-to-all-start.2 = ((bf16[128,2,2176]{2,1,0:T(2,128)(2,1)}), bf16[128,2,2176]{2,1,0:T(2,128)(2,1)}, u32[]{:S(2)}, u32[]{:S(2)}) async-start(bf16[128,2,2176]{2,1,0:T(2,128)(2,1)} %reshape.203), calls=%async_computation.2 | async-start | bytes 2228224 | tf_op jit(solution)/shard_map/all_to_all | solution.py:304
  174.7 9.5 %copy-start.8 = (s32[4]{0:T(128)S(1)}, s32[4]{0:T(128)}, u32[]{:S(2)}) copy-start(s32[4]{0:T(128)} %constant.169.clone) | copy-start | bytes 52
  174.7 20.0 %copy-start.4 = (s32[16,8]{1,0:T(8,128)S(1)}, s32[16,8]{1,0:T(8,128)}, u32[]{:S(2)}) copy-start(s32[16,8]{1,0:T(8,128)} %copy.14) | copy-start | bytes 1540
  176.8 33.9 %collective-permute-start.11 = (bf16[64,4224]{1,0:T(8,128)(2,1)}, bf16[64,4224]{1,0:T(8,128)(2,1)S(1)}, u32[]{:S(2)}, u32[]{:S(2)}) collective-permute-start(bf16[64,4224]{1,0:T(8,128)(2,1)} %get-tuple-element.34), channel_id=1, source_target_pairs={{0,128},{128,256},{256,384},{384,0},{1,129},{129,257},{257,385},{3... | collective-permute-start | bytes 1622024 | tf_op jit(solution)/shard_map/ppermute | solution.py:22
  182.3 28.4 %collective-permute-start.12 = (bf16[64,4224]{1,0:T(8,128)(2,1)}, bf16[64,4224]{1,0:T(8,128)(2,1)S(1)}, u32[]{:S(2)}, u32[]{:S(2)}) collective-permute-start(bf16[64,4224]{1,0:T(8,128)(2,1)} %get-tuple-element.35), channel_id=1, source_target_pairs={{0,384},{128,0},{256,128},{384,256},{1,385},{129,1},{257,129},{385... | collective-permute-start | bytes 1622024 | tf_op jit(solution)/shard_map/ppermute | solution.py:22
  184.3 22.7 %collective-permute-start.6 = (bf16[576,256]{1,0:T(8,128)(2,1)}, bf16[576,256]{1,0:T(8,128)(2,1)S(1)}, u32[]{:S(2)}, u32[]{:S(2)}) collective-permute-start(bf16[576,256]{1,0:T(8,128)(2,1)} %get-tuple-element.31), channel_id=1, source_target_pairs={{0,128},{128,256},{256,384},{384,0},{1,129},{129,257},{257,385},{3... | collective-permute-start | bytes 884744 | tf_op jit(solution)/shard_map/ppermute | solution.py:22
  189.4 21.3 %collective-permute-start.7 = (bf16[576,256]{1,0:T(8,128)(2,1)}, bf16[576,256]{1,0:T(8,128)(2,1)S(1)}, u32[]{:S(2)}, u32[]{:S(2)}) collective-permute-start(bf16[576,256]{1,0:T(8,128)(2,1)} %get-tuple-element.32), channel_id=1, source_target_pairs={{0,384},{128,0},{256,128},{384,256},{1,385},{129,1},{257,129},{385... | collective-permute-start | bytes 884744 | tf_op jit(solution)/shard_map/ppermute | solution.py:22
  191.4 19.3 %collective-permute-start.8 = (bf16[576,256]{1,0:T(8,128)(2,1)}, bf16[576,256]{1,0:T(8,128)(2,1)S(1)}, u32[]{:S(2)}, u32[]{:S(2)}) collective-permute-start(bf16[576,256]{1,0:T(8,128)(2,1)} %get-tuple-element.33), channel_id=1, source_target_pairs={{0,256},{128,384},{256,0},{384,128},{1,257},{129,385},{257,1},{385... | collective-permute-start | bytes 884744 | tf_op jit(solution)/shard_map/ppermute | solution.py:22
  194.8 16.9 %copy-start = (bf16[576,256]{1,0:T(8,128)(2,1)S(1)}, bf16[576,256]{1,0:T(8,128)(2,1)}, u32[]{:S(2)}) copy-start(bf16[576,256]{1,0:T(8,128)(2,1)} %get-tuple-element.30.refs_0_) | copy-start | bytes 884740
  210.7 0.8 copy-start.1
  210.7 1.0 copy-start.2
Sparse Core Ops, SparseCore 0:
  10.7 57.4 all-gather.2
  107.1 74.8 all-gather.4

commit v7 on v6

--- a/solution.py
+++ b/solution.py
@@ -11,6 +11,7 @@
 DP, Y, Z, CORE = 4, 4, 16, 2
 YC = Y * CORE
 CAP = 2
+STRIDE = 4
 LANES = 128
 MIB = 2**20
 LONG = 10**12
@@ -90,6 +91,18 @@
         compiler_params=pltpu.CompilerParams(vmem_limit_bytes=6 * MIB),
         cost_estimate=pl.CostEstimate(flops=cost, bytes_accessed=MIB, transcendentals=0),
     )(*in_hbm(arrays))
+
+
+def relay(arrays):
+    return pl.pallas_call(
+        lambda *refs: None,
+        out_shape=[pltpu.HBM(a.shape, a.dtype) for a in arrays],
+        in_specs=[pl.BlockSpec(memory_space=pl.ANY)] * len(arrays),
+        out_specs=[pl.BlockSpec(memory_space=pl.ANY)] * len(arrays),
+        input_output_aliases={k: k for k in range(len(arrays))},
+        compiler_params=pltpu.CompilerParams(vmem_limit_bytes=MIB),
+        cost_estimate=pl.CostEstimate(flops=LONG, bytes_accessed=MIB, transcendentals=0),
+    )(*arrays)
 
 
 def rank_of(ids):
@@ -180,34 +193,28 @@
     back_ref[:, width:] = nt(perm, tail).astype(BF16)
 
 
-def grads_kernel(planes_ref, own_ref, *refs):
-    parts, tiles, (gate_ref, up_ref, down_ref, acts_ref) = refs[:DP], refs[DP:-4], refs[-4:]
+def grads_kernel(own_ref, *refs):
+    parts, tiles, (gate_ref, up_ref, down_ref) = refs[:DP], refs[DP:-3], refs[-3:]
     share = gate_ref.shape[0]
     part = parts[0].shape[1] // 2
-
-    @pl.when(pl.program_id(0) == 0)
-    def _():
-        for k in range(DP):
-            at = pl.multiple_of(planes_ref[k] * part, part)
-            acts_ref[:, pl.ds(at, part)] = parts[k][:, :part]
-            acts_ref[:, (DP + k) * part : (DP + k + 1) * part] = parts[k][:, part:]
-
     both, down = 0.0, 0.0
-    for c, chunk in enumerate((tiles[:3], tiles[3:])):
-        x, grad, tail = (jnp.concatenate([r[...] for r in chunk[k::3]], axis=0) for k in range(3))
-        at = slice(c * DP * part, (c + 1) * DP * part)
+    for c in range(2):
+        x, grad, tail = (
+            jnp.concatenate([r[...] for r in tiles[3 * DP * c + k : 3 * DP * (c + 1) : 3]], axis=0) for k in range(3)
+        )
+        acts = jnp.concatenate([p[:, c * part : (c + 1) * part] for p in parts], axis=1)
         weight = jnp.sum(tail.astype(F32) * own_ref[...], axis=1, keepdims=True)
         scaled = (weight * grad.astype(F32)).astype(BF16)
-        both += nn(acts_ref[: 2 * share, at], x)
-        down += nn(acts_ref[2 * share :, at], scaled)
+        both += nn(acts[: 2 * share], x)
+        down += nn(acts[2 * share :], scaled)
     gate_ref[...] = both[:share].astype(BF16)
     up_ref[...] = both[share:].astype(BF16)
     down_ref[...] = down.astype(BF16)
 
 
-def weight_grads(planes, own, acts, arrays, share, width, tile=512):
-    operands = [planes, own, *acts]
-    specs = [pl.BlockSpec(memory_space=pltpu.SMEM), whole(own), *[whole(a) for a in acts]]
+def weight_grads(own, acts, arrays, share, width, tile=512):
+    operands = [own, *acts]
+    specs = [whole(own), *[whole(a) for a in acts]]
     for a in in_hbm(arrays):
         n = a.shape[0]
         operands += [a] * 3
@@ -223,7 +230,6 @@
         in_specs=specs,
         out_specs=[pl.BlockSpec((share, tile), lambda j: (0, j))] * 3,
         grid=(width // tile,),
-        scratch=[pltpu.VMEM((3 * share, DP * acts[0].shape[1]), BF16)],
         vmem=28,
     )
 
@@ -264,7 +270,7 @@
         [sds((tokens, 2 * width + LANES), BF16)],
         vmem=8,
     )
-    groups = [list(range(r, Z, 2)) for r in range(2)]
+    groups = [list(range(r, Z, STRIDE)) for r in range(STRIDE)]
     seen = lax.all_gather(payload, "z", axis=0, tiled=True, axis_index_groups=groups)
 
     half = 3 * share // 2
@@ -272,23 +278,27 @@
     (mine,) = move((w_gate[0], w_up[0], w_down[0]), plan, [3 * share])
     from_prev, from_next = shift(mine, "dp", DP, 1), shift(mine, "dp", DP, -1)
     top, bottom = move((from_prev, from_next), [(0, 0, half, 0, 0), (1, half, half, 1, 0)], [half] * 2)
+    ahead, behind = shift(seen, "z", Z, -1), shift(seen, "z", Z, 1)
+    across = lax.ppermute(seen, "z", [((i + 2 - i % 2 * 4) % Z, i) for i in range(Z)])
+    behind, across, top, bottom = lax.optimization_barrier((behind, across, top, bottom))
     far = shift(top, "dp", DP, 1), shift(bottom, "dp", DP, -1)
-
-    mid = seen.shape[0] // 2
-    low, high = move((seen,), [(0, 0, mid, 0, 0), (0, mid, mid, 1, 0)], [mid] * 2)
-    other = shift(low, "z", Z, -1), shift(high, "z", Z, 1)
     dest = iota((2 * YC, experts), 0)
     pick = ((dest < YC) & (iota((2 * YC, experts), 1) == dest * Z + z)).astype(BF16)
-    first = to_experts(dispatch((seen,), pick, tokens))
-    early = first
-    gathered = lax.all_gather(early, "dp", axis=0, tiled=True)
-    second = to_experts(dispatch(other, pick, tokens, LONG))
+    first = to_experts(dispatch((seen, ahead), pick, tokens))
+    second = to_experts(dispatch((behind, across), pick, tokens, LONG))
     rows = first, second
-    prev_rows, next_rows = shift(second, "dp", DP, 1), shift(second, "dp", DP, -1)
+    first_prev, first_next = shift(first, "dp", DP, 1), shift(first, "dp", DP, -1)
+    second_prev, second_next = shift(second, "dp", DP, 1), shift(second, "dp", DP, -1)
+    first_prev, first_next, second_prev, second_next = relay((first_prev, first_next, second_prev, second_next))
+    first_far, second_far = shift(first_prev, "dp", DP, 1), shift(second_next, "dp", DP, -1)
+    planes = first, first_prev, first_next, first_far, second, second_prev, second_next, second_far
+
     own = (iota((16, experts), 1) == yc * Z + z).astype(F32)
     q = iota((count, 1), 0)
     q_z = q // CAP % Z
-    at = (q_z + z) % 2 * (count // 2) + q // (Z * CAP) * Z + q_z // 2 * CAP + q % CAP
+    kind = (q_z - z + Z) % STRIDE
+    place = jnp.where(kind < 2, kind * STRIDE, jnp.where(kind == 3, Z // 2, Z // 2 + STRIDE)) + q_z // STRIDE
+    at = place // (Z // 2) * (count // 2) + q // (Z * CAP) * Z + place % (Z // 2) * CAP + q % CAP
     perm = (at == iota((count, count), 1)).astype(BF16)
     weights = in_hbm((mine, from_next, from_prev, *far))
     small = (own.astype(BF16), perm, *in_hbm(rows))
@@ -305,11 +315,7 @@
         back.reshape(experts, CAP, -1), ("y", "core", "z"), split_axis=0, concat_axis=0, tiled=True
     ).reshape(count, -1)
     acts = a_own, shift(a_next, "dp", DP, 1), shift(a_prev, "dp", DP, -1), shift(a_far, "dp", DP, 2)
-    mid = second.shape[0] // 2
-    low, high = move((prev_rows, next_rows), [(0, 0, mid, 0, 0), (1, mid, mid, 1, 0)], [mid] * 2, LONG)
-    far_rows = shift(low, "dp", DP, 1), shift(high, "dp", DP, -1)
-    origins = (lax.axis_index("dp") + jnp.array([0, 3, 1, 2], I32)) % DP
-    grads = weight_grads(origins, own[:1], acts, (gathered, second, prev_rows, next_rows, *far_rows), share, width)
+    grads = weight_grads(own[:1], acts, planes, share, width)
     home, (grad_gate, grad_up, grad_down) = lax.optimization_barrier((home, grads))
     grad_in, grad_combine = call(
         home_kernel, (home, rank_of(expert_ids)), [sds((tokens, width), BF16), sds((tokens, picks), F32)], vmem=8

time: 228 us -> 218 us (0.956)
  blocking collectives: 0 us -> 28.3 us
  waiting for transfers between devices: 102 us -> 77.3 us
  between operations: 14.4 us -> 1.09 us
  starting transfers between devices: 64.9 us -> 70.6 us
  Pallas kernels: 36.7 us -> 31.5 us
    all_gather x2 -> x0, waiting for transfers between devices: 45.5 us -> none  [the longest x1 45.5 us: body(): lax.all_gather(payload, 'z', axis=0, tiled=True, axis_index_groups=groups)]
    ppermute x13 -> x15, waiting for transfers between devices: 28.2 us -> 63.7 us  [shift(): return lax.ppermute(a, axis, [(i, (i + k) % size) for i in range(size)])]
    all_gather x0 -> x1, blocking collectives: none -> 28.3 us  [body(): lax.all_gather(payload, 'z', axis=0, tiled=True, axis_index_groups=groups)]
    all_to_all x1, waiting for transfers between devices: 10.6 us -> 0.01 us  [body(): lax.all_to_all(back.reshape(experts, CAP, -1), ('y', 'core', 'z'), split_...]
    ppermute x0 -> x1, starting transfers between devices: none -> 4.19 us  [body(): lax.ppermute(seen, 'z', [((i + 2 - i % 2 * 4) % Z, i) for i in range(Z)])]
    pallas_call x4 -> x2, Pallas kernels: 9.48 us -> 5.32 us  [move(): pl.pallas_call(functools.partial(move_kernel, plan, len(arrays)), out_sha...]
    all_to_all x2, waiting for transfers between devices: 17.4 us -> 13.7 us  [to_experts(): lax.all_to_all(sent.reshape(YC, -1, sent.shape[1]), ('y', 'core'), split_...]
    ppermute x13 -> x15, starting transfers between devices: 46.2 us -> 47.7 us  [shift(): return lax.ppermute(a, axis, [(i, (i + k) % size) for i in range(size)])]
  transfers between devices with their start and end apart: 18 -> 19, of which waited for: 7 -> 7; matrix products, arithmetic and copies ran while one was open for 2% -> 1% of each run, Pallas kernels for 12% -> 13%
where the time goes in v7:
time: 218 us; the launch traced here: 216 us
  waiting for transfers between devices  77.3 us (35%)
  starting transfers between devices  70.6 us (32%)
  Pallas kernels  31.5 us (14%)
  blocking collectives  28.3 us (13%)
  local copies, waits for them, and re-layouts  7.1 us (3%)
    ppermute x15, waiting for transfers between devices, shift(): return lax.ppermute(a, axis, [(i, (i + k) % size) for i in range(size)])  63.7 us
    ppermute x15, starting transfers between devices, shift(): return lax.ppermute(a, axis, [(i, (i + k) % size) for i in range(size)])  47.7 us
    all_gather x1, blocking collectives, body(): lax.all_gather(payload, 'z', axis=0, tiled=True, axis_index_groups=groups)  28.3 us
    pallas_call x6, Pallas kernels, call(): pl.pallas_call(kernel, grid=grid, out_shape=out_shape, in_specs=in_specs...  26.2 us
    all_to_all x2, waiting for transfers between devices, to_experts(): lax.all_to_all(sent.reshape(YC, -1, sent.shape[1]), ('y', 'core'), split_...  13.7 us
    all_to_all x1, starting transfers between devices, body(): lax.all_to_all(back.reshape(experts, CAP, -1), ('y', 'core', 'z'), split_...  10.1 us
    all_to_all x2, starting transfers between devices, to_experts(): lax.all_to_all(sent.reshape(YC, -1, sent.shape[1]), ('y', 'core'), split_...  8.52 us
    pallas_call x2, Pallas kernels, move(): pl.pallas_call(functools.partial(move_kernel, plan, len(arrays)), out_sha...  5.32 us
  transfers between devices with their start and end apart: 19, of which 7 were waited for; matrix products, arithmetic and copies ran while one was open for 1% of the time, Pallas kernels for 13%

profile of v7, /device:TPU:6, one launch (start us, length us, event | category | flops | bytes accessed | tf_op | source)
XLA Modules:
  0.0 216.2 jit_solution(340193482799220418)
XLA Ops:
  0.6 0.0 copy-start.6
  0.7 2.6 %shard_map.121.refs_2_ = bf16[576,2048]{1,0:T(8,128)(2,1)} custom-call(bf16[192,2048]{1,0:T(8,128)(2,1)} %bitcast.34, bf16[192,2048]{1,0:T(8,128)(2,1)} %bitcast.35, bf16[192,2048]{1,0:T(8,128)(2,1)} %bitcast.36), custom_call_target="tpu_custom_call" | custom-call | flops 1 | bytes 1048576 | tf_op jit(solution)/shard_map/pallas_call | solution.py:85
  3.3 7.8 %collective-permute-start.3 = (bf16[576,2048]{1,0:T(8,128)(2,1)}, bf16[576,2048]{1,0:T(8,128)(2,1)S(1)}, u32[]{:S(2)}, u32[]{:S(2)}) collective-permute-start(bf16[576,2048]{1,0:T(8,128)(2,1)} %shard_map.121.refs_2_), channel_id=1, source_target_pairs={{0,128},{128,256},{256,384},{384,0},{1,129},{129,257},{257,385},{3... | collective-permute-start | bytes 7077896 | tf_op jit(solution)/shard_map/ppermute | solution.py:23
  11.0 1.9 collective-permute-start.4
  13.0 1.1 shard_map.119
  14.1 28.3 %all_gather.3.refs_0_ = bf16[64,4224]{1,0:T(8,128)(2,1)S(1)} all-gather(bf16[16,4224]{1,0:T(8,128)(2,1)S(1)} %shard_map.119), channel_id=1, replica_groups={{0,8,16,24},{2,10,18,26},{4,12,20,28},{6,14,22,30},{1,9,17,25},{3,11,19..., dimensions={0}, use_global_device_ids=true | all-gather | bytes 675840 | tf_op jit(solution)/shard_map/all_gather | solution.py:274
  42.5 4.2 %collective-permute-start = (bf16[64,4224]{1,0:T(8,128)(2,1)S(1)}, bf16[64,4224]{1,0:T(8,128)(2,1)S(1)}, u32[]{:S(2)}, u32[]{:S(2)}) collective-permute-start(bf16[64,4224]{1,0:T(8,128)(2,1)S(1)} %all_gather.3.refs_0_), channel_id=1, source_target_pairs={{0,30},{2,0},{4,2},{6,4},{8,6},{10,8},{12,10},{14,12},{16,14},{18,... | collective-permute-start | bytes 1622024 | tf_op jit(solution)/shard_map/ppermute | solution.py:23
  46.7 1.9 collective-permute-start.1
  48.6 4.2 %collective-permute-start.2 = (bf16[64,4224]{1,0:T(8,128)(2,1)S(1)}, bf16[64,4224]{1,0:T(8,128)(2,1)}, u32[]{:S(2)}, u32[]{:S(2)}) collective-permute-start(bf16[64,4224]{1,0:T(8,128)(2,1)S(1)} %all_gather.3.refs_0_), channel_id=1, source_target_pairs={{4,0},{30,2},{8,4},{2,6},{12,8},{6,10},{16,12},{10,14},{20,16},{14... | collective-permute-start | bytes 1622024 | tf_op jit(solution)/shard_map/ppermute | solution.py:282
  52.8 0.1 fusion.8.pick_ref
  52.9 15.0 %collective-permute-done.refs_1_ = bf16[64,4224]{1,0:T(8,128)(2,1)S(1)} collective-permute-done((bf16[64,4224]{1,0:T(8,128)(2,1)S(1)}, bf16[64,4224]{1,0:T(8,128)(2,1)S(1)}, u32[]{:S(2)}, u32[]{:S(2)}) %collective-permute-start) | collective-permute-done | bytes 540704 | tf_op jit(solution)/shard_map/ppermute | solution.py:23
  67.9 0.8 copy-done.5
  68.7 2.9 %shard_map.120 = bf16[128,4224]{1,0:T(8,128)(2,1)} custom-call(bf16[16,128]{1,0:T(8,128)(2,1)S(1)} %fusion.8.pick_ref, bf16[64,4224]{1,0:T(8,128)(2,1)} %copy-done.4, bf16[64,4224]{1,0:T(8,128)(2,1)} %copy-done.5), custom_call_target="tpu_custom_call" | custom-call | flops 1 | bytes 1048576 | tf_op jit(solution)/shard_map/pallas_call | solution.py:47
  71.6 4.3 %all-to-all-start = ((bf16[8,16,4224]{2,1,0:T(8,128)(2,1)}), bf16[8,16,4224]{2,1,0:T(8,128)(2,1)}, u32[]{:S(2)}, u32[]{:S(2)}) async-start(bf16[8,16,4224]{2,1,0:T(8,128)(2,1)} %bitcast.2), calls=%async_computation | async-start | bytes 2162688 | tf_op jit(solution)/shard_map/all_to_all | solution.py:151
  75.9 0.0 collective-permute-done.3.refs_0_.refs_4_
  75.9 1.4 copy-done.3
  77.3 2.7 %shard_map.122 = (bf16[288,2048]{1,0:T(8,128)(2,1)}, bf16[288,2048]{1,0:T(8,128)(2,1)}) custom-call(bf16[576,2048]{1,0:T(8,128)(2,1)} %copy-done.3, bf16[576,2048]{1,0:T(8,128)(2,1)} %collective-permute-done.4.refs_1_.refs_3_), custom_call_target="tpu_custom_call" | custom-call | flops 1 | bytes 1048576 | tf_op jit(solution)/shard_map/pallas_call | solution.py:85
  80.1 3.7 %collective-permute-start.5 = (bf16[288,2048]{1,0:T(8,128)(2,1)}, bf16[288,2048]{1,0:T(8,128)(2,1)}, u32[]{:S(2)}, u32[]{:S(2)}) collective-permute-start(bf16[288,2048]{1,0:T(8,128)(2,1)} %get-tuple-element.33), channel_id=1, source_target_pairs={{0,128},{128,256},{256,384},{384,0},{1,129},{129,257},{257,385},{3... | collective-permute-start | bytes 3538952 | tf_op jit(solution)/shard_map/ppermute | solution.py:23
  83.7 2.2 %collective-permute-start.6 = (bf16[288,2048]{1,0:T(8,128)(2,1)}, bf16[288,2048]{1,0:T(8,128)(2,1)}, u32[]{:S(2)}, u32[]{:S(2)}) collective-permute-start(bf16[288,2048]{1,0:T(8,128)(2,1)} %get-tuple-element.34), channel_id=1, source_target_pairs={{0,384},{128,0},{256,128},{384,256},{1,385},{129,1},{257,129},{385... | collective-permute-start | bytes 3538952 | tf_op jit(solution)/shard_map/ppermute | solution.py:23
  85.9 2.9 %shard_map.123 = bf16[128,4224]{1,0:T(8,128)(2,1)} custom-call(bf16[16,128]{1,0:T(8,128)(2,1)S(1)} %fusion.8.pick_ref, bf16[64,4224]{1,0:T(8,128)(2,1)} %collective-permute-done.1.refs_0_, bf16[64,4224]{1,0:T(8,128)(2,1)} %collective-permute-done.2.refs_1_), custom_call_target="tpu_custom_call" | custom-call | flops 999999995904 | bytes 1048576 | tf_op jit(solution)/shard_map/pallas_call | solution.py:47
  88.8 3.4 %all-to-all-done = bf16[8,16,4224]{2,1,0:T(8,128)(2,1)} async-done(((bf16[8,16,4224]{2,1,0:T(8,128)(2,1)}), bf16[8,16,4224]{2,1,0:T(8,128)(2,1)}, u32[]{:S(2)}, u32[]{:S(2)}) %all-to-all-start) | async-done | bytes 1081376 | tf_op jit(solution)/shard_map/all_to_all | solution.py:151
  92.2 4.2 %all-to-all-start.1 = ((bf16[8,16,4224]{2,1,0:T(8,128)(2,1)}), bf16[8,16,4224]{2,1,0:T(8,128)(2,1)}, u32[]{:S(2)}, u32[]{:S(2)}) async-start(bf16[8,16,4224]{2,1,0:T(8,128)(2,1)} %bitcast.7), calls=%async_computation.1 | async-start | bytes 2162688 | tf_op jit(solution)/shard_map/all_to_all | solution.py:151
  96.5 0.1 fusion.perm_ref
  96.6 3.7 %collective-permute-start.10 = (bf16[128,4224]{1,0:T(8,128)(2,1)}, bf16[128,4224]{1,0:T(8,128)(2,1)}, u32[]{:S(2)}, u32[]{:S(2)}) collective-permute-start(bf16[128,4224]{1,0:T(8,128)(2,1)} %bitcast.3.refs_0_.refs_4_.refs_5_.refs_6_), channel_id=1, source_target_pairs={{0,128},{128,256},{256,384},{384,0},{1,129},{129,257},{257,385},{3... | collective-permute-start | bytes 3244040 | tf_op jit(solution)/shard_map/ppermute | solution.py:23
  100.4 2.1 collective-permute-start.11
  102.5 10.3 %all-to-all-done.1 = bf16[8,16,4224]{2,1,0:T(8,128)(2,1)} async-done(((bf16[8,16,4224]{2,1,0:T(8,128)(2,1)}), bf16[8,16,4224]{2,1,0:T(8,128)(2,1)}, u32[]{:S(2)}, u32[]{:S(2)}) %all-to-all-start.1) | async-done | bytes 1081376 | tf_op jit(solution)/shard_map/all_to_all | solution.py:151
  112.8 3.7 %collective-permute-start.12 = (bf16[128,4224]{1,0:T(8,128)(2,1)}, bf16[128,4224]{1,0:T(8,128)(2,1)}, u32[]{:S(2)}, u32[]{:S(2)}) collective-permute-start(bf16[128,4224]{1,0:T(8,128)(2,1)} %bitcast.8.refs_1_.refs_16_.refs_17_.refs_18_), channel_id=1, source_target_pairs={{0,128},{128,256},{256,384},{384,0},{1,129},{129,257},{257,385},{3... | collective-permute-start | bytes 3244040 | tf_op jit(solution)/shard_map/ppermute | solution.py:23
  116.5 2.1 collective-permute-start.13
  118.7 11.4 %shard_map.124 = (bf16[256,2176]{1,0:T(8,128)(2,1)S(1)}, bf16[576,256]{1,0:T(8,128)(2,1)}, bf16[576,256]{1,0:T(8,128)(2,1)}, bf16[576,256]{1,0:T(8,128)(2,1)}, bf16[576,256]{1,0:T(8,128)(2,1)}) custom-call(bf16[16,128]{1,0:T(8,128)(2,1)S(1)} %iota.42.own_ref, bf16[256,256]{1,0:T(8,128)(2,1)S(1)} %fusion.perm_ref, ...), custom_call_target="tpu_custom_call" | custom-call | flops 999999995904 | bytes 1048576 | tf_op jit(solution)/shard_map/pallas_call | solution.py:47
  130.1 1.3 reshape.267
  131.4 10.1 %all-to-all-start.2 = ((bf16[128,2,2176]{2,1,0:T(2,128)(2,1)}), bf16[128,2,2176]{2,1,0:T(2,128)(2,1)}, u32[]{:S(2)}, u32[]{:S(2)}) async-start(bf16[128,2,2176]{2,1,0:T(2,128)(2,1)} %reshape.267), calls=%async_computation.2 | async-start | bytes 2228224 | tf_op jit(solution)/shard_map/all_to_all | solution.py:314
  141.6 15.4 %collective-permute-done.12.refs_2_ = bf16[128,4224]{1,0:T(8,128)(2,1)} collective-permute-done((bf16[128,4224]{1,0:T(8,128)(2,1)}, bf16[128,4224]{1,0:T(8,128)(2,1)}, u32[]{:S(2)}, u32[]{:S(2)}) %collective-permute-start.12) | collective-permute-done | bytes 1081376 | tf_op jit(solution)/shard_map/ppermute | solution.py:23
  156.9 4.7 %collective-permute-done.13.refs_3_ = bf16[128,4224]{1,0:T(8,128)(2,1)} collective-permute-done((bf16[128,4224]{1,0:T(8,128)(2,1)}, bf16[128,4224]{1,0:T(8,128)(2,1)}, u32[]{:S(2)}, u32[]{:S(2)}) %collective-permute-start.13) | collective-permute-done | bytes 1081376 | tf_op jit(solution)/shard_map/ppermute | solution.py:23
  161.6 0.0 copy-start
  161.6 2.1 collective-permute-start.14
  163.7 3.9 %collective-permute-start.15 = (bf16[128,4224]{1,0:T(8,128)(2,1)}, bf16[128,4224]{1,0:T(8,128)(2,1)S(1)}, u32[]{:S(2)}, u32[]{:S(2)}) collective-permute-start(bf16[128,4224]{1,0:T(8,128)(2,1)} %get-tuple-element.43.refs_22_.refs_23_.refs_24_), channel_id=1, source_target_pairs={{0,384},{128,0},{256,128},{384,256},{1,385},{129,1},{257,129},{385... | collective-permute-start | bytes 3244040 | tf_op jit(solution)/shard_map/ppermute | solution.py:23
  167.6 0.1 copy.17
  167.7 3.1 %collective-permute-start.7 = (bf16[576,256]{1,0:T(8,128)(2,1)S(1)}, bf16[576,256]{1,0:T(8,128)(2,1)S(1)}, u32[]{:S(2)}, u32[]{:S(2)}) collective-permute-start(bf16[576,256]{1,0:T(8,128)(2,1)S(1)} %copy-done.11), channel_id=1, source_target_pairs={{0,128},{128,256},{256,384},{384,0},{1,129},{129,257},{257,385},{3... | collective-permute-start | bytes 884744 | tf_op jit(solution)/shard_map/ppermute | solution.py:23
  170.8 2.7 %collective-permute-start.8 = (bf16[576,256]{1,0:T(8,128)(2,1)S(1)}, bf16[576,256]{1,0:T(8,128)(2,1)S(1)}, u32[]{:S(2)}, u32[]{:S(2)}) collective-permute-start(bf16[576,256]{1,0:T(8,128)(2,1)S(1)} %copy-done.10), channel_id=1, source_target_pairs={{0,384},{128,0},{256,128},{384,256},{1,385},{129,1},{257,129},{385... | collective-permute-start | bytes 884744 | tf_op jit(solution)/shard_map/ppermute | solution.py:23
  173.6 2.6 %collective-permute-start.9 = (bf16[576,256]{1,0:T(8,128)(2,1)S(1)}, bf16[576,256]{1,0:T(8,128)(2,1)S(1)}, u32[]{:S(2)}, u32[]{:S(2)}) collective-permute-start(bf16[576,256]{1,0:T(8,128)(2,1)S(1)} %copy-done.9), channel_id=1, source_target_pairs={{0,256},{128,384},{256,0},{384,128},{1,257},{129,385},{257,1},{385... | collective-permute-start | bytes 884744 | tf_op jit(solution)/shard_map/ppermute | solution.py:23
  176.2 20.8 %collective-permute-done.7.refs_1_ = bf16[576,256]{1,0:T(8,128)(2,1)S(1)} collective-permute-done((bf16[576,256]{1,0:T(8,128)(2,1)S(1)}, bf16[576,256]{1,0:T(8,128)(2,1)S(1)}, u32[]{:S(2)}, u32[]{:S(2)}) %collective-permute-start.7) | collective-permute-done | bytes 294944 | tf_op jit(solution)/shard_map/ppermute | solution.py:23
  197.0 7.8 %collective-permute-done.8.refs_2_ = bf16[576,256]{1,0:T(8,128)(2,1)S(1)} collective-permute-done((bf16[576,256]{1,0:T(8,128)(2,1)S(1)}, bf16[576,256]{1,0:T(8,128)(2,1)S(1)}, u32[]{:S(2)}, u32[]{:S(2)}) %collective-permute-start.8) | collective-permute-done | bytes 294944 | tf_op jit(solution)/shard_map/ppermute | solution.py:23
  204.8 1.0 copy-done.1
  205.8 0.4 copy-done.2
  206.2 6.7 %shard_map.126 = (bf16[192,2048]{1,0:T(8,128)(2,1)}, bf16[192,2048]{1,0:T(8,128)(2,1)}, bf16[192,2048]{1,0:T(8,128)(2,1)}) custom-call(f32[1,128]{1,0:T(1,128)S(1)} %compare_convert_fusion.own_ref, bf16[576,256]{1,0:T(8,128)(2,1)S(1)} %copy-done, bf16[576,256]{1,0:T(8,128)(2,1)S(1)} %collective-permute-done.7.refs_1_, ...), custom_call_target="tpu_custom_call" | custom-call | flops 1 | bytes 1048576 | tf_op jit(solution)/shard_map/pallas_call | solution.py:47
  212.9 1.5 reshape.268.home_ref
  214.4 1.2 shard_map.127
  215.6 0.7 copy.21
  (39 shorter events, 0.2 us)
Async XLA Ops:
  0.6 12.3 %copy-start.8 = (bf16[16,8]{0,1:T(8,128)(2,1)S(1)}, bf16[16,8]{0,1:T(8,128)(2,1)}, u32[]{:S(2)}) copy-start(bf16[16,8]{0,1:T(8,128)(2,1)} %param.11) | copy-start | bytes 772
  0.6 12.4 %copy-start.6 = (s32[16,8]{0,1:T(8,128)S(1)}, s32[16,8]{0,1:T(8,128)}, u32[]{:S(2)}) copy-start(s32[16,8]{0,1:T(8,128)} %param.12) | copy-start | bytes 1540
  3.3 72.6 %collective-permute-start.3 = (bf16[576,2048]{1,0:T(8,128)(2,1)}, bf16[576,2048]{1,0:T(8,128)(2,1)S(1)}, u32[]{:S(2)}, u32[]{:S(2)}) collective-permute-start(bf16[576,2048]{1,0:T(8,128)(2,1)} %shard_map.121.refs_2_), channel_id=1, source_target_pairs={{0,128},{128,256},{256,384},{384,0},{1,129},{129,257},{257,385},{3... | collective-permute-start | bytes 7077896 | tf_op jit(solution)/shard_map/ppermute | solution.py:23
  11.0 64.8 %collective-permute-start.4 = (bf16[576,2048]{1,0:T(8,128)(2,1)}, bf16[576,2048]{1,0:T(8,128)(2,1)}, u32[]{:S(2)}, u32[]{:S(2)}) collective-permute-start(bf16[576,2048]{1,0:T(8,128)(2,1)} %shard_map.121.refs_2_), channel_id=1, source_target_pairs={{0,384},{128,0},{256,128},{384,256},{1,385},{129,1},{257,129},{385... | collective-permute-start | bytes 7077896 | tf_op jit(solution)/shard_map/ppermute | solution.py:23
  42.5 25.4 %copy-start.4 = (bf16[64,4224]{1,0:T(8,128)(2,1)}, bf16[64,4224]{1,0:T(8,128)(2,1)S(1)}, u32[]{:S(2)}) copy-start(bf16[64,4224]{1,0:T(8,128)(2,1)S(1)} %all_gather.3.refs_0_) | copy-start | bytes 1622020
  42.5 25.4 %collective-permute-start = (bf16[64,4224]{1,0:T(8,128)(2,1)S(1)}, bf16[64,4224]{1,0:T(8,128)(2,1)S(1)}, u32[]{:S(2)}, u32[]{:S(2)}) collective-permute-start(bf16[64,4224]{1,0:T(8,128)(2,1)S(1)} %all_gather.3.refs_0_), channel_id=1, source_target_pairs={{0,30},{2,0},{4,2},{6,4},{8,6},{10,8},{12,10},{14,12},{16,14},{18,... | collective-permute-start | bytes 1622024 | tf_op jit(solution)/shard_map/ppermute | solution.py:23
  46.7 33.4 %collective-permute-start.1 = (bf16[64,4224]{1,0:T(8,128)(2,1)S(1)}, bf16[64,4224]{1,0:T(8,128)(2,1)}, u32[]{:S(2)}, u32[]{:S(2)}) collective-permute-start(bf16[64,4224]{1,0:T(8,128)(2,1)S(1)} %all_gather.3.refs_0_), channel_id=1, source_target_pairs={{0,2},{2,4},{4,6},{6,8},{8,10},{10,12},{12,14},{14,16},{16,18},{18... | collective-permute-start | bytes 1622024 | tf_op jit(solution)/shard_map/ppermute | solution.py:23
  48.6 31.4 %collective-permute-start.2 = (bf16[64,4224]{1,0:T(8,128)(2,1)S(1)}, bf16[64,4224]{1,0:T(8,128)(2,1)}, u32[]{:S(2)}, u32[]{:S(2)}) collective-permute-start(bf16[64,4224]{1,0:T(8,128)(2,1)S(1)} %all_gather.3.refs_0_), channel_id=1, source_target_pairs={{4,0},{30,2},{8,4},{2,6},{12,8},{6,10},{16,12},{10,14},{20,16},{14... | collective-permute-start | bytes 1622024 | tf_op jit(solution)/shard_map/ppermute | solution.py:282
  67.9 0.8 copy-start.5
  71.6 20.6 %all-to-all-start = ((bf16[8,16,4224]{2,1,0:T(8,128)(2,1)}), bf16[8,16,4224]{2,1,0:T(8,128)(2,1)}, u32[]{:S(2)}, u32[]{:S(2)}) async-start(bf16[8,16,4224]{2,1,0:T(8,128)(2,1)} %bitcast.2), calls=%async_computation | async-start | bytes 2162688 | tf_op jit(solution)/shard_map/all_to_all | solution.py:151
  75.9 1.5 copy-start.3
  80.1 36.5 %collective-permute-start.5 = (bf16[288,2048]{1,0:T(8,128)(2,1)}, bf16[288,2048]{1,0:T(8,128)(2,1)}, u32[]{:S(2)}, u32[]{:S(2)}) collective-permute-start(bf16[288,2048]{1,0:T(8,128)(2,1)} %get-tuple-element.33), channel_id=1, source_target_pairs={{0,128},{128,256},{256,384},{384,0},{1,129},{129,257},{257,385},{3... | collective-permute-start | bytes 3538952 | tf_op jit(solution)/shard_map/ppermute | solution.py:23
  83.7 34.9 %collective-permute-start.6 = (bf16[288,2048]{1,0:T(8,128)(2,1)}, bf16[288,2048]{1,0:T(8,128)(2,1)}, u32[]{:S(2)}, u32[]{:S(2)}) collective-permute-start(bf16[288,2048]{1,0:T(8,128)(2,1)} %get-tuple-element.34), channel_id=1, source_target_pairs={{0,384},{128,0},{256,128},{384,256},{1,385},{129,1},{257,129},{385... | collective-permute-start | bytes 3538952 | tf_op jit(solution)/shard_map/ppermute | solution.py:23
  92.2 20.6 %all-to-all-start.1 = ((bf16[8,16,4224]{2,1,0:T(8,128)(2,1)}), bf16[8,16,4224]{2,1,0:T(8,128)(2,1)}, u32[]{:S(2)}, u32[]{:S(2)}) async-start(bf16[8,16,4224]{2,1,0:T(8,128)(2,1)} %bitcast.7), calls=%async_computation.1 | async-start | bytes 2162688 | tf_op jit(solution)/shard_map/all_to_all | solution.py:151
  96.6 44.9 %collective-permute-start.10 = (bf16[128,4224]{1,0:T(8,128)(2,1)}, bf16[128,4224]{1,0:T(8,128)(2,1)}, u32[]{:S(2)}, u32[]{:S(2)}) collective-permute-start(bf16[128,4224]{1,0:T(8,128)(2,1)} %bitcast.3.refs_0_.refs_4_.refs_5_.refs_6_), channel_id=1, source_target_pairs={{0,128},{128,256},{256,384},{384,0},{1,129},{129,257},{257,385},{3... | collective-permute-start | bytes 3244040 | tf_op jit(solution)/shard_map/ppermute | solution.py:23
  100.4 41.2 %collective-permute-start.11 = (bf16[128,4224]{1,0:T(8,128)(2,1)}, bf16[128,4224]{1,0:T(8,128)(2,1)}, u32[]{:S(2)}, u32[]{:S(2)}) collective-permute-start(bf16[128,4224]{1,0:T(8,128)(2,1)} %bitcast.3.refs_0_.refs_4_.refs_5_.refs_6_), channel_id=1, source_target_pairs={{0,384},{128,0},{256,128},{384,256},{1,385},{129,1},{257,129},{385... | collective-permute-start | bytes 3244040 | tf_op jit(solution)/shard_map/ppermute | solution.py:23
  112.8 44.1 %collective-permute-start.12 = (bf16[128,4224]{1,0:T(8,128)(2,1)}, bf16[128,4224]{1,0:T(8,128)(2,1)}, u32[]{:S(2)}, u32[]{:S(2)}) collective-permute-start(bf16[128,4224]{1,0:T(8,128)(2,1)} %bitcast.8.refs_1_.refs_16_.refs_17_.refs_18_), channel_id=1, source_target_pairs={{0,128},{128,256},{256,384},{384,0},{1,129},{129,257},{257,385},{3... | collective-permute-start | bytes 3244040 | tf_op jit(solution)/shard_map/ppermute | solution.py:23
  116.5 45.1 %collective-permute-start.13 = (bf16[128,4224]{1,0:T(8,128)(2,1)}, bf16[128,4224]{1,0:T(8,128)(2,1)}, u32[]{:S(2)}, u32[]{:S(2)}) collective-permute-start(bf16[128,4224]{1,0:T(8,128)(2,1)} %bitcast.8.refs_1_.refs_16_.refs_17_.refs_18_), channel_id=1, source_target_pairs={{0,384},{128,0},{256,128},{384,256},{1,385},{129,1},{257,129},{385... | collective-permute-start | bytes 3244040 | tf_op jit(solution)/shard_map/ppermute | solution.py:23
  131.4 81.5 %all-to-all-start.2 = ((bf16[128,2,2176]{2,1,0:T(2,128)(2,1)}), bf16[128,2,2176]{2,1,0:T(2,128)(2,1)}, u32[]{:S(2)}, u32[]{:S(2)}) async-start(bf16[128,2,2176]{2,1,0:T(2,128)(2,1)} %reshape.267), calls=%async_computation.2 | async-start | bytes 2228224 | tf_op jit(solution)/shard_map/all_to_all | solution.py:314
  161.6 6.0 %copy-start.7 = (s32[16,8]{0,1:T(8,128)S(1)}, s32[16,8]{0,1:T(8,128)}, u32[]{:S(2)}) copy-start(s32[16,8]{0,1:T(8,128)} %param.12) | copy-start | bytes 1540
  161.6 6.1 %copy-start.11 = (bf16[576,256]{1,0:T(8,128)(2,1)S(1)}, bf16[576,256]{1,0:T(8,128)(2,1)}, u32[]{:S(2)}) copy-start(bf16[576,256]{1,0:T(8,128)(2,1)} %get-tuple-element.37) | copy-start | bytes 884740
  161.6 9.2 %copy-start.10 = (bf16[576,256]{1,0:T(8,128)(2,1)S(1)}, bf16[576,256]{1,0:T(8,128)(2,1)}, u32[]{:S(2)}) copy-start(bf16[576,256]{1,0:T(8,128)(2,1)} %get-tuple-element.38) | copy-start | bytes 884740
  161.6 12.0 %copy-start.9 = (bf16[576,256]{1,0:T(8,128)(2,1)S(1)}, bf16[576,256]{1,0:T(8,128)(2,1)}, u32[]{:S(2)}) copy-start(bf16[576,256]{1,0:T(8,128)(2,1)} %get-tuple-element.39) | copy-start | bytes 884740
  161.6 44.6 %copy-start = (bf16[576,256]{1,0:T(8,128)(2,1)S(1)}, bf16[576,256]{1,0:T(8,128)(2,1)}, u32[]{:S(2)}) copy-start(bf16[576,256]{1,0:T(8,128)(2,1)} %get-tuple-element.36.refs_0_) | copy-start | bytes 884740
  161.6 43.2 %collective-permute-start.14 = (bf16[128,4224]{1,0:T(8,128)(2,1)}, bf16[128,4224]{1,0:T(8,128)(2,1)S(1)}, u32[]{:S(2)}, u32[]{:S(2)}) collective-permute-start(bf16[128,4224]{1,0:T(8,128)(2,1)} %get-tuple-element.40.refs_7_.refs_8_.refs_9_), channel_id=1, source_target_pairs={{0,128},{128,256},{256,384},{384,0},{1,129},{129,257},{257,385},{3... | collective-permute-start | bytes 3244040 | tf_op jit(solution)/shard_map/ppermute | solution.py:23
  163.7 41.1 %collective-permute-start.15 = (bf16[128,4224]{1,0:T(8,128)(2,1)}, bf16[128,4224]{1,0:T(8,128)(2,1)S(1)}, u32[]{:S(2)}, u32[]{:S(2)}) collective-permute-start(bf16[128,4224]{1,0:T(8,128)(2,1)} %get-tuple-element.43.refs_22_.refs_23_.refs_24_), channel_id=1, source_target_pairs={{0,384},{128,0},{256,128},{384,256},{1,385},{129,1},{257,129},{385... | collective-permute-start | bytes 3244040 | tf_op jit(solution)/shard_map/ppermute | solution.py:23
  167.7 29.3 %collective-permute-start.7 = (bf16[576,256]{1,0:T(8,128)(2,1)S(1)}, bf16[576,256]{1,0:T(8,128)(2,1)S(1)}, u32[]{:S(2)}, u32[]{:S(2)}) collective-permute-start(bf16[576,256]{1,0:T(8,128)(2,1)S(1)} %copy-done.11), channel_id=1, source_target_pairs={{0,128},{128,256},{256,384},{384,0},{1,129},{129,257},{257,385},{3... | collective-permute-start | bytes 884744 | tf_op jit(solution)/shard_map/ppermute | solution.py:23
  170.8 34.0 %collective-permute-start.8 = (bf16[576,256]{1,0:T(8,128)(2,1)S(1)}, bf16[576,256]{1,0:T(8,128)(2,1)S(1)}, u32[]{:S(2)}, u32[]{:S(2)}) collective-permute-start(bf16[576,256]{1,0:T(8,128)(2,1)S(1)} %copy-done.10), channel_id=1, source_target_pairs={{0,384},{128,0},{256,128},{384,256},{1,385},{129,1},{257,129},{385... | collective-permute-start | bytes 884744 | tf_op jit(solution)/shard_map/ppermute | solution.py:23
  173.6 31.2 %collective-permute-start.9 = (bf16[576,256]{1,0:T(8,128)(2,1)S(1)}, bf16[576,256]{1,0:T(8,128)(2,1)S(1)}, u32[]{:S(2)}, u32[]{:S(2)}) collective-permute-start(bf16[576,256]{1,0:T(8,128)(2,1)S(1)} %copy-done.9), channel_id=1, source_target_pairs={{0,256},{128,384},{256,0},{384,128},{1,257},{129,385},{257,1},{385... | collective-permute-start | bytes 884744 | tf_op jit(solution)/shard_map/ppermute | solution.py:23
  204.8 1.0 copy-start.1
  204.8 1.3 copy-start.2

commit v8 on v7

--- a/solution.py
+++ b/solution.py
@@ -279,6 +279,7 @@
     from_prev, from_next = shift(mine, "dp", DP, 1), shift(mine, "dp", DP, -1)
     top, bottom = move((from_prev, from_next), [(0, 0, half, 0, 0), (1, half, half, 1, 0)], [half] * 2)
     ahead, behind = shift(seen, "z", Z, -1), shift(seen, "z", Z, 1)
+    seen, ahead = lax.optimization_barrier((seen, ahead))
     across = lax.ppermute(seen, "z", [((i + 2 - i % 2 * 4) % Z, i) for i in range(Z)])
     behind, across, top, bottom = lax.optimization_barrier((behind, across, top, bottom))
     far = shift(top, "dp", DP, 1), shift(bottom, "dp", DP, -1)
@@ -315,11 +316,11 @@
         back.reshape(experts, CAP, -1), ("y", "core", "z"), split_axis=0, concat_axis=0, tiled=True
     ).reshape(count, -1)
     acts = a_own, shift(a_next, "dp", DP, 1), shift(a_prev, "dp", DP, -1), shift(a_far, "dp", DP, 2)
-    grads = weight_grads(own[:1], acts, planes, share, width)
-    home, (grad_gate, grad_up, grad_down) = lax.optimization_barrier((home, grads))
     grad_in, grad_combine = call(
         home_kernel, (home, rank_of(expert_ids)), [sds((tokens, width), BF16), sds((tokens, picks), F32)], vmem=8
     )
+    own, grad_in, grad_combine = lax.optimization_barrier((own, grad_in, grad_combine))
+    grad_gate, grad_up, grad_down = weight_grads(own[:1], acts, planes, share, width)
     return grad_in, grad_combine, grad_gate[None], grad_up[None], grad_down[None]
 
 

time: 218 us -> 206 us (0.945)
  waiting for transfers between devices: 77.3 us -> 66 us
    ppermute x15, waiting for transfers between devices: 63.7 us -> 30.9 us  [shift(): return lax.ppermute(a, axis, [(i, (i + k) % size) for i in range(size)])]
    all_to_all x1, waiting for transfers between devices: 0.01 us -> 21.4 us  [body(): lax.all_to_all(back.reshape(experts, CAP, -1), ('y', 'core', 'z'), split_...]
  transfers between devices with their start and end apart: 19 -> 19, of which waited for: 7 -> 7; matrix products, arithmetic and copies ran while one was open for 1% -> 2% of each run, Pallas kernels for 13% -> 11%
where the time goes in v8:
time: 206 us; the launch traced here: 204 us
  starting transfers between devices  70.9 us (34%)
  waiting for transfers between devices  66 us (32%)
  Pallas kernels  31.5 us (15%)
  blocking collectives  28.3 us (14%)
  local copies, waits for them, and re-layouts  5.95 us (3%)
    ppermute x15, starting transfers between devices, shift(): return lax.ppermute(a, axis, [(i, (i + k) % size) for i in range(size)])  47.7 us
    ppermute x15, waiting for transfers between devices, shift(): return lax.ppermute(a, axis, [(i, (i + k) % size) for i in range(size)])  30.9 us
    all_gather x1, blocking collectives, body(): lax.all_gather(payload, 'z', axis=0, tiled=True, axis_index_groups=groups)  28.3 us
    pallas_call x6, Pallas kernels, call(): pl.pallas_call(kernel, grid=grid, out_shape=out_shape, in_specs=in_specs...  26.2 us
    all_to_all x1, waiting for transfers between devices, body(): lax.all_to_all(back.reshape(experts, CAP, -1), ('y', 'core', 'z'), split_...  21.4 us
    all_to_all x2, waiting for transfers between devices, to_experts(): lax.all_to_all(sent.reshape(YC, -1, sent.shape[1]), ('y', 'core'), split_...  13.8 us
    all_to_all x1, starting transfers between devices, body(): lax.all_to_all(back.reshape(experts, CAP, -1), ('y', 'core', 'z'), split_...  10.8 us
    all_to_all x2, starting transfers between devices, to_experts(): lax.all_to_all(sent.reshape(YC, -1, sent.shape[1]), ('y', 'core'), split_...  8.72 us
  transfers between devices with their start and end apart: 19, of which 7 were waited for; matrix products, arithmetic and copies ran while one was open for 2% of the time, Pallas kernels for 11%

profile of v8, /device:TPU:6, one launch (start us, length us, event | category | flops | bytes accessed | tf_op | source)
XLA Modules:
  0.0 203.9 jit_solution(16702829070110224868)
XLA Ops:
  0.6 0.0 copy-start.5
  0.7 2.6 %shard_map.121.refs_2_ = bf16[576,2048]{1,0:T(8,128)(2,1)} custom-call(bf16[192,2048]{1,0:T(8,128)(2,1)} %bitcast.34, bf16[192,2048]{1,0:T(8,128)(2,1)} %bitcast.35, bf16[192,2048]{1,0:T(8,128)(2,1)} %bitcast.36), custom_call_target="tpu_custom_call" | custom-call | flops 1 | bytes 1048576 | tf_op jit(solution)/shard_map/pallas_call | solution.py:85
  3.3 7.8 %collective-permute-start.3 = (bf16[576,2048]{1,0:T(8,128)(2,1)}, bf16[576,2048]{1,0:T(8,128)(2,1)S(1)}, u32[]{:S(2)}, u32[]{:S(2)}) collective-permute-start(bf16[576,2048]{1,0:T(8,128)(2,1)} %shard_map.121.refs_2_), channel_id=1, source_target_pairs={{0,128},{128,256},{256,384},{384,0},{1,129},{129,257},{257,385},{3... | collective-permute-start | bytes 7077896 | tf_op jit(solution)/shard_map/ppermute | solution.py:23
  11.0 1.9 collective-permute-start.4
  13.0 1.1 shard_map.119
  14.1 28.3 %all_gather.3.refs_0_ = bf16[64,4224]{1,0:T(8,128)(2,1)S(1)} all-gather(bf16[16,4224]{1,0:T(8,128)(2,1)S(1)} %shard_map.119), channel_id=1, replica_groups={{0,8,16,24},{2,10,18,26},{4,12,20,28},{6,14,22,30},{1,9,17,25},{3,11,19..., dimensions={0}, use_global_device_ids=true | all-gather | bytes 675840 | tf_op jit(solution)/shard_map/all_gather | solution.py:274
  42.5 4.2 %collective-permute-start = (bf16[64,4224]{1,0:T(8,128)(2,1)S(1)}, bf16[64,4224]{1,0:T(8,128)(2,1)S(1)}, u32[]{:S(2)}, u32[]{:S(2)}) collective-permute-start(bf16[64,4224]{1,0:T(8,128)(2,1)S(1)} %all_gather.3.refs_0_), channel_id=1, source_target_pairs={{0,30},{2,0},{4,2},{6,4},{8,6},{10,8},{12,10},{14,12},{16,14},{18,... | collective-permute-start | bytes 1622024 | tf_op jit(solution)/shard_map/ppermute | solution.py:23
  46.7 1.9 collective-permute-start.1
  48.6 7.7 %collective-permute-done.refs_1_ = bf16[64,4224]{1,0:T(8,128)(2,1)S(1)} collective-permute-done((bf16[64,4224]{1,0:T(8,128)(2,1)S(1)}, bf16[64,4224]{1,0:T(8,128)(2,1)S(1)}, u32[]{:S(2)}, u32[]{:S(2)}) %collective-permute-start) | collective-permute-done | bytes 540704 | tf_op jit(solution)/shard_map/ppermute | solution.py:23
  56.3 3.6 %collective-permute-start.2 = (bf16[64,4224]{1,0:T(8,128)(2,1)S(1)}, bf16[64,4224]{1,0:T(8,128)(2,1)}, u32[]{:S(2)}, u32[]{:S(2)}) collective-permute-start(bf16[64,4224]{1,0:T(8,128)(2,1)S(1)} %all_gather.3.refs_0_), channel_id=1, source_target_pairs={{4,0},{30,2},{8,4},{2,6},{12,8},{6,10},{16,12},{10,14},{20,16},{14... | collective-permute-start | bytes 1622024 | tf_op jit(solution)/shard_map/ppermute | solution.py:283
  60.0 0.1 fusion.8.pick_ref
  60.0 2.9 %shard_map.120 = bf16[128,4224]{1,0:T(8,128)(2,1)} custom-call(bf16[16,128]{1,0:T(8,128)(2,1)S(1)} %fusion.8.pick_ref, bf16[64,4224]{1,0:T(8,128)(2,1)} %copy-done.3, bf16[64,4224]{1,0:T(8,128)(2,1)} %copy-done.4), custom_call_target="tpu_custom_call" | custom-call | flops 1 | bytes 1048576 | tf_op jit(solution)/shard_map/pallas_call | solution.py:47
  62.9 4.5 %all-to-all-start = ((bf16[8,16,4224]{2,1,0:T(8,128)(2,1)}), bf16[8,16,4224]{2,1,0:T(8,128)(2,1)}, u32[]{:S(2)}, u32[]{:S(2)}) async-start(bf16[8,16,4224]{2,1,0:T(8,128)(2,1)} %bitcast.2), calls=%async_computation | async-start | bytes 2162688 | tf_op jit(solution)/shard_map/all_to_all | solution.py:151
  67.4 0.0 collective-permute-done.4.refs_1_.refs_3_
  67.4 1.4 copy-done.2
  68.9 2.7 %shard_map.122 = (bf16[288,2048]{1,0:T(8,128)(2,1)}, bf16[288,2048]{1,0:T(8,128)(2,1)}) custom-call(bf16[576,2048]{1,0:T(8,128)(2,1)} %copy-done.2, bf16[576,2048]{1,0:T(8,128)(2,1)} %collective-permute-done.4.refs_1_.refs_3_), custom_call_target="tpu_custom_call" | custom-call | flops 1 | bytes 1048576 | tf_op jit(solution)/shard_map/pallas_call | solution.py:85
  71.6 0.0 collective-permute-done.2.refs_1_
  71.6 3.6 %collective-permute-start.5 = (bf16[288,2048]{1,0:T(8,128)(2,1)}, bf16[288,2048]{1,0:T(8,128)(2,1)}, u32[]{:S(2)}, u32[]{:S(2)}) collective-permute-start(bf16[288,2048]{1,0:T(8,128)(2,1)} %get-tuple-element.36), channel_id=1, source_target_pairs={{0,128},{128,256},{256,384},{384,0},{1,129},{129,257},{257,385},{3... | collective-permute-start | bytes 3538952 | tf_op jit(solution)/shard_map/ppermute | solution.py:23
  75.2 2.2 %collective-permute-start.6 = (bf16[288,2048]{1,0:T(8,128)(2,1)}, bf16[288,2048]{1,0:T(8,128)(2,1)}, u32[]{:S(2)}, u32[]{:S(2)}) collective-permute-start(bf16[288,2048]{1,0:T(8,128)(2,1)} %get-tuple-element.37), channel_id=1, source_target_pairs={{0,384},{128,0},{256,128},{384,256},{1,385},{129,1},{257,129},{385... | collective-permute-start | bytes 3538952 | tf_op jit(solution)/shard_map/ppermute | solution.py:23
  77.5 2.9 %shard_map.123 = bf16[128,4224]{1,0:T(8,128)(2,1)} custom-call(bf16[16,128]{1,0:T(8,128)(2,1)S(1)} %fusion.8.pick_ref, bf16[64,4224]{1,0:T(8,128)(2,1)} %collective-permute-done.1.refs_0_, bf16[64,4224]{1,0:T(8,128)(2,1)} %collective-permute-done.2.refs_1_), custom_call_target="tpu_custom_call" | custom-call | flops 999999995904 | bytes 1048576 | tf_op jit(solution)/shard_map/pallas_call | solution.py:47
  80.3 3.5 %all-to-all-done = bf16[8,16,4224]{2,1,0:T(8,128)(2,1)} async-done(((bf16[8,16,4224]{2,1,0:T(8,128)(2,1)}), bf16[8,16,4224]{2,1,0:T(8,128)(2,1)}, u32[]{:S(2)}, u32[]{:S(2)}) %all-to-all-start) | async-done | bytes 1081376 | tf_op jit(solution)/shard_map/all_to_all | solution.py:151
  83.8 4.2 %all-to-all-start.1 = ((bf16[8,16,4224]{2,1,0:T(8,128)(2,1)}), bf16[8,16,4224]{2,1,0:T(8,128)(2,1)}, u32[]{:S(2)}, u32[]{:S(2)}) async-start(bf16[8,16,4224]{2,1,0:T(8,128)(2,1)} %bitcast.7), calls=%async_computation.1 | async-start | bytes 2162688 | tf_op jit(solution)/shard_map/all_to_all | solution.py:151
  88.1 0.1 fusion.perm_ref
  88.2 3.6 %collective-permute-start.10 = (bf16[128,4224]{1,0:T(8,128)(2,1)}, bf16[128,4224]{1,0:T(8,128)(2,1)}, u32[]{:S(2)}, u32[]{:S(2)}) collective-permute-start(bf16[128,4224]{1,0:T(8,128)(2,1)} %bitcast.3.refs_0_.refs_4_.refs_5_.refs_6_), channel_id=1, source_target_pairs={{0,128},{128,256},{256,384},{384,0},{1,129},{129,257},{257,385},{3... | collective-permute-start | bytes 3244040 | tf_op jit(solution)/shard_map/ppermute | solution.py:23
  91.9 2.2 %collective-permute-start.11 = (bf16[128,4224]{1,0:T(8,128)(2,1)}, bf16[128,4224]{1,0:T(8,128)(2,1)}, u32[]{:S(2)}, u32[]{:S(2)}) collective-permute-start(bf16[128,4224]{1,0:T(8,128)(2,1)} %bitcast.3.refs_0_.refs_4_.refs_5_.refs_6_), channel_id=1, source_target_pairs={{0,384},{128,0},{256,128},{384,256},{1,385},{129,1},{257,129},{385... | collective-permute-start | bytes 3244040 | tf_op jit(solution)/shard_map/ppermute | solution.py:23
  94.1 10.3 %all-to-all-done.1 = bf16[8,16,4224]{2,1,0:T(8,128)(2,1)} async-done(((bf16[8,16,4224]{2,1,0:T(8,128)(2,1)}), bf16[8,16,4224]{2,1,0:T(8,128)(2,1)}, u32[]{:S(2)}, u32[]{:S(2)}) %all-to-all-start.1) | async-done | bytes 1081376 | tf_op jit(solution)/shard_map/all_to_all | solution.py:151
  104.4 3.6 %collective-permute-start.12 = (bf16[128,4224]{1,0:T(8,128)(2,1)}, bf16[128,4224]{1,0:T(8,128)(2,1)}, u32[]{:S(2)}, u32[]{:S(2)}) collective-permute-start(bf16[128,4224]{1,0:T(8,128)(2,1)} %bitcast.8.refs_1_.refs_16_.refs_17_.refs_18_), channel_id=1, source_target_pairs={{0,128},{128,256},{256,384},{384,0},{1,129},{129,257},{257,385},{3... | collective-permute-start | bytes 3244040 | tf_op jit(solution)/shard_map/ppermute | solution.py:23
  108.0 2.2 %collective-permute-start.13 = (bf16[128,4224]{1,0:T(8,128)(2,1)}, bf16[128,4224]{1,0:T(8,128)(2,1)}, u32[]{:S(2)}, u32[]{:S(2)}) collective-permute-start(bf16[128,4224]{1,0:T(8,128)(2,1)} %bitcast.8.refs_1_.refs_16_.refs_17_.refs_18_), channel_id=1, source_target_pairs={{0,384},{128,0},{256,128},{384,256},{1,385},{129,1},{257,129},{385... | collective-permute-start | bytes 3244040 | tf_op jit(solution)/shard_map/ppermute | solution.py:23
  110.3 0.0 collective-permute-done.6.refs_6_
  110.3 11.4 %shard_map.124 = (bf16[256,2176]{1,0:T(8,128)(2,1)S(1)}, bf16[576,256]{1,0:T(8,128)(2,1)}, bf16[576,256]{1,0:T(8,128)(2,1)}, bf16[576,256]{1,0:T(8,128)(2,1)}, bf16[576,256]{1,0:T(8,128)(2,1)}) custom-call(bf16[16,128]{1,0:T(8,128)(2,1)S(1)} %iota.42.own_ref, bf16[256,256]{1,0:T(8,128)(2,1)S(1)} %fusion.perm_ref, ...), custom_call_target="tpu_custom_call" | custom-call | flops 999999995904 | bytes 1048576 | tf_op jit(solution)/shard_map/pallas_call | solution.py:47
  121.7 1.3 reshape.259
  123.0 10.8 %all-to-all-start.2 = ((bf16[128,2,2176]{2,1,0:T(2,128)(2,1)}), bf16[128,2,2176]{2,1,0:T(2,128)(2,1)}, u32[]{:S(2)}, u32[]{:S(2)}) async-start(bf16[128,2,2176]{2,1,0:T(2,128)(2,1)} %reshape.259), calls=%async_computation.2 | async-start | bytes 2228224 | tf_op jit(solution)/shard_map/all_to_all | solution.py:315
  133.8 14.7 %collective-permute-done.12.refs_2_ = bf16[128,4224]{1,0:T(8,128)(2,1)} collective-permute-done((bf16[128,4224]{1,0:T(8,128)(2,1)}, bf16[128,4224]{1,0:T(8,128)(2,1)}, u32[]{:S(2)}, u32[]{:S(2)}) %collective-permute-start.12) | collective-permute-done | bytes 1081376 | tf_op jit(solution)/shard_map/ppermute | solution.py:23
  148.5 4.5 %collective-permute-done.13.refs_3_ = bf16[128,4224]{1,0:T(8,128)(2,1)} collective-permute-done((bf16[128,4224]{1,0:T(8,128)(2,1)}, bf16[128,4224]{1,0:T(8,128)(2,1)}, u32[]{:S(2)}, u32[]{:S(2)}) %collective-permute-start.13) | collective-permute-done | bytes 1081376 | tf_op jit(solution)/shard_map/ppermute | solution.py:23
  153.1 2.0 %collective-permute-start.14 = (bf16[128,4224]{1,0:T(8,128)(2,1)}, bf16[128,4224]{1,0:T(8,128)(2,1)S(1)}, u32[]{:S(2)}, u32[]{:S(2)}) collective-permute-start(bf16[128,4224]{1,0:T(8,128)(2,1)} %get-tuple-element.48.refs_7_.refs_8_.refs_9_), channel_id=1, source_target_pairs={{0,128},{128,256},{256,384},{384,0},{1,129},{129,257},{257,385},{3... | collective-permute-start | bytes 3244040 | tf_op jit(solution)/shard_map/ppermute | solution.py:23
  155.1 3.9 %collective-permute-start.15 = (bf16[128,4224]{1,0:T(8,128)(2,1)}, bf16[128,4224]{1,0:T(8,128)(2,1)}, u32[]{:S(2)}, u32[]{:S(2)}) collective-permute-start(bf16[128,4224]{1,0:T(8,128)(2,1)} %get-tuple-element.51.refs_22_.refs_23_.refs_24_), channel_id=1, source_target_pairs={{0,384},{128,0},{256,128},{384,256},{1,385},{129,1},{257,129},{385... | collective-permute-start | bytes 3244040 | tf_op jit(solution)/shard_map/ppermute | solution.py:23
  159.1 0.1 copy.17
  159.1 3.1 %collective-permute-start.7 = (bf16[576,256]{1,0:T(8,128)(2,1)}, bf16[576,256]{1,0:T(8,128)(2,1)S(1)}, u32[]{:S(2)}, u32[]{:S(2)}) collective-permute-start(bf16[576,256]{1,0:T(8,128)(2,1)} %get-tuple-element.45), channel_id=1, source_target_pairs={{0,128},{128,256},{256,384},{384,0},{1,129},{129,257},{257,385},{3... | collective-permute-start | bytes 884744 | tf_op jit(solution)/shard_map/ppermute | solution.py:23
  162.3 2.7 %collective-permute-start.8 = (bf16[576,256]{1,0:T(8,128)(2,1)}, bf16[576,256]{1,0:T(8,128)(2,1)S(1)}, u32[]{:S(2)}, u32[]{:S(2)}) collective-permute-start(bf16[576,256]{1,0:T(8,128)(2,1)} %get-tuple-element.46), channel_id=1, source_target_pairs={{0,384},{128,0},{256,128},{384,256},{1,385},{129,1},{257,129},{385... | collective-permute-start | bytes 884744 | tf_op jit(solution)/shard_map/ppermute | solution.py:23
  165.0 2.6 %collective-permute-start.9 = (bf16[576,256]{1,0:T(8,128)(2,1)}, bf16[576,256]{1,0:T(8,128)(2,1)S(1)}, u32[]{:S(2)}, u32[]{:S(2)}) collective-permute-start(bf16[576,256]{1,0:T(8,128)(2,1)} %get-tuple-element.47), channel_id=1, source_target_pairs={{0,256},{128,384},{256,0},{384,128},{1,257},{129,385},{257,1},{385... | collective-permute-start | bytes 884744 | tf_op jit(solution)/shard_map/ppermute | solution.py:23
  167.6 21.4 %all-to-all-done.2 = bf16[128,2,2176]{2,1,0:T(2,128)(2,1)} async-done(((bf16[128,2,2176]{2,1,0:T(2,128)(2,1)}), bf16[128,2,2176]{2,1,0:T(2,128)(2,1)}, u32[]{:S(2)}, u32[]{:S(2)}) %all-to-all-start.2) | async-done | bytes 1114144 | tf_op jit(solution)/shard_map/all_to_all | solution.py:315
  189.0 1.5 reshape.260.home_ref
  190.5 0.0 copy-start
  190.5 1.2 shard_map.125
  191.7 0.7 copy.21
  192.4 3.9 %collective-permute-done.8.refs_2_ = bf16[576,256]{1,0:T(8,128)(2,1)S(1)} collective-permute-done((bf16[576,256]{1,0:T(8,128)(2,1)}, bf16[576,256]{1,0:T(8,128)(2,1)S(1)}, u32[]{:S(2)}, u32[]{:S(2)}) %collective-permute-start.8) | collective-permute-done | bytes 294944 | tf_op jit(solution)/shard_map/ppermute | solution.py:23
  196.3 1.0 copy-done.1
  197.2 6.7 %shard_map.127 = (bf16[192,2048]{1,0:T(8,128)(2,1)}, bf16[192,2048]{1,0:T(8,128)(2,1)}, bf16[192,2048]{1,0:T(8,128)(2,1)}) custom-call(f32[1,128]{1,0:T(1,128)S(1)} %slice.3.own_ref, bf16[576,256]{1,0:T(8,128)(2,1)S(1)} %copy-done, bf16[576,256]{1,0:T(8,128)(2,1)S(1)} %collective-permute-done.7.refs_1_, bf16[576,256]{1,0:T(8,128)(2,1)S(1)} %collective-permute-done.8.refs_2_, ...), custom_call_target="tpu_custom_call" | custom-call | flops 1 | bytes 1048576 | tf_op jit(solution)/shard_map/pallas_call | solution.py:47
  (33 shorter events, 0.1 us)
Async XLA Ops:
  0.6 12.3 %copy-start.7 = (bf16[16,8]{0,1:T(8,128)(2,1)S(1)}, bf16[16,8]{0,1:T(8,128)(2,1)}, u32[]{:S(2)}) copy-start(bf16[16,8]{0,1:T(8,128)(2,1)} %param.11) | copy-start | bytes 772
  0.6 12.4 %copy-start.5 = (s32[16,8]{0,1:T(8,128)S(1)}, s32[16,8]{0,1:T(8,128)}, u32[]{:S(2)}) copy-start(s32[16,8]{0,1:T(8,128)} %param.12) | copy-start | bytes 1540
  3.3 64.1 %collective-permute-start.3 = (bf16[576,2048]{1,0:T(8,128)(2,1)}, bf16[576,2048]{1,0:T(8,128)(2,1)S(1)}, u32[]{:S(2)}, u32[]{:S(2)}) collective-permute-start(bf16[576,2048]{1,0:T(8,128)(2,1)} %shard_map.121.refs_2_), channel_id=1, source_target_pairs={{0,128},{128,256},{256,384},{384,0},{1,129},{129,257},{257,385},{3... | collective-permute-start | bytes 7077896 | tf_op jit(solution)/shard_map/ppermute | solution.py:23
  11.0 56.4 %collective-permute-start.4 = (bf16[576,2048]{1,0:T(8,128)(2,1)}, bf16[576,2048]{1,0:T(8,128)(2,1)}, u32[]{:S(2)}, u32[]{:S(2)}) collective-permute-start(bf16[576,2048]{1,0:T(8,128)(2,1)} %shard_map.121.refs_2_), channel_id=1, source_target_pairs={{0,384},{128,0},{256,128},{384,256},{1,385},{129,1},{257,129},{385... | collective-permute-start | bytes 7077896 | tf_op jit(solution)/shard_map/ppermute | solution.py:23
  42.5 17.6 %copy-start.3 = (bf16[64,4224]{1,0:T(8,128)(2,1)}, bf16[64,4224]{1,0:T(8,128)(2,1)S(1)}, u32[]{:S(2)}) copy-start(bf16[64,4224]{1,0:T(8,128)(2,1)S(1)} %all_gather.3.refs_0_) | copy-start | bytes 1622020
  42.5 13.9 %collective-permute-start = (bf16[64,4224]{1,0:T(8,128)(2,1)S(1)}, bf16[64,4224]{1,0:T(8,128)(2,1)S(1)}, u32[]{:S(2)}, u32[]{:S(2)}) collective-permute-start(bf16[64,4224]{1,0:T(8,128)(2,1)S(1)} %all_gather.3.refs_0_), channel_id=1, source_target_pairs={{0,30},{2,0},{4,2},{6,4},{8,6},{10,8},{12,10},{14,12},{16,14},{18,... | collective-permute-start | bytes 1622024 | tf_op jit(solution)/shard_map/ppermute | solution.py:23
  46.7 24.9 %collective-permute-start.1 = (bf16[64,4224]{1,0:T(8,128)(2,1)S(1)}, bf16[64,4224]{1,0:T(8,128)(2,1)}, u32[]{:S(2)}, u32[]{:S(2)}) collective-permute-start(bf16[64,4224]{1,0:T(8,128)(2,1)S(1)} %all_gather.3.refs_0_), channel_id=1, source_target_pairs={{0,2},{2,4},{4,6},{6,8},{8,10},{10,12},{12,14},{14,16},{16,18},{18... | collective-permute-start | bytes 1622024 | tf_op jit(solution)/shard_map/ppermute | solution.py:23
  56.3 3.7 %copy-start.4 = (bf16[64,4224]{1,0:T(8,128)(2,1)}, bf16[64,4224]{1,0:T(8,128)(2,1)S(1)}, u32[]{:S(2)}) copy-start(bf16[64,4224]{1,0:T(8,128)(2,1)S(1)} %collective-permute-done.refs_1_) | copy-start | bytes 1622020
  56.3 15.3 %collective-permute-start.2 = (bf16[64,4224]{1,0:T(8,128)(2,1)S(1)}, bf16[64,4224]{1,0:T(8,128)(2,1)}, u32[]{:S(2)}, u32[]{:S(2)}) collective-permute-start(bf16[64,4224]{1,0:T(8,128)(2,1)S(1)} %all_gather.3.refs_0_), channel_id=1, source_target_pairs={{4,0},{30,2},{8,4},{2,6},{12,8},{6,10},{16,12},{10,14},{20,16},{14... | collective-permute-start | bytes 1622024 | tf_op jit(solution)/shard_map/ppermute | solution.py:283
  62.9 20.9 %all-to-all-start = ((bf16[8,16,4224]{2,1,0:T(8,128)(2,1)}), bf16[8,16,4224]{2,1,0:T(8,128)(2,1)}, u32[]{:S(2)}, u32[]{:S(2)}) async-start(bf16[8,16,4224]{2,1,0:T(8,128)(2,1)} %bitcast.2), calls=%async_computation | async-start | bytes 2162688 | tf_op jit(solution)/shard_map/all_to_all | solution.py:151
  67.4 1.5 copy-start.2
  71.6 36.4 %collective-permute-start.5 = (bf16[288,2048]{1,0:T(8,128)(2,1)}, bf16[288,2048]{1,0:T(8,128)(2,1)}, u32[]{:S(2)}, u32[]{:S(2)}) collective-permute-start(bf16[288,2048]{1,0:T(8,128)(2,1)} %get-tuple-element.36), channel_id=1, source_target_pairs={{0,128},{128,256},{256,384},{384,0},{1,129},{129,257},{257,385},{3... | collective-permute-start | bytes 3538952 | tf_op jit(solution)/shard_map/ppermute | solution.py:23
  75.2 35.1 %collective-permute-start.6 = (bf16[288,2048]{1,0:T(8,128)(2,1)}, bf16[288,2048]{1,0:T(8,128)(2,1)}, u32[]{:S(2)}, u32[]{:S(2)}) collective-permute-start(bf16[288,2048]{1,0:T(8,128)(2,1)} %get-tuple-element.37), channel_id=1, source_target_pairs={{0,384},{128,0},{256,128},{384,256},{1,385},{129,1},{257,129},{385... | collective-permute-start | bytes 3538952 | tf_op jit(solution)/shard_map/ppermute | solution.py:23
  83.8 20.6 %all-to-all-start.1 = ((bf16[8,16,4224]{2,1,0:T(8,128)(2,1)}), bf16[8,16,4224]{2,1,0:T(8,128)(2,1)}, u32[]{:S(2)}, u32[]{:S(2)}) async-start(bf16[8,16,4224]{2,1,0:T(8,128)(2,1)} %bitcast.7), calls=%async_computation.1 | async-start | bytes 2162688 | tf_op jit(solution)/shard_map/all_to_all | solution.py:151
  88.2 45.6 %collective-permute-start.10 = (bf16[128,4224]{1,0:T(8,128)(2,1)}, bf16[128,4224]{1,0:T(8,128)(2,1)}, u32[]{:S(2)}, u32[]{:S(2)}) collective-permute-start(bf16[128,4224]{1,0:T(8,128)(2,1)} %bitcast.3.refs_0_.refs_4_.refs_5_.refs_6_), channel_id=1, source_target_pairs={{0,128},{128,256},{256,384},{384,0},{1,129},{129,257},{257,385},{3... | collective-permute-start | bytes 3244040 | tf_op jit(solution)/shard_map/ppermute | solution.py:23
  91.9 42.0 %collective-permute-start.11 = (bf16[128,4224]{1,0:T(8,128)(2,1)}, bf16[128,4224]{1,0:T(8,128)(2,1)}, u32[]{:S(2)}, u32[]{:S(2)}) collective-permute-start(bf16[128,4224]{1,0:T(8,128)(2,1)} %bitcast.3.refs_0_.refs_4_.refs_5_.refs_6_), channel_id=1, source_target_pairs={{0,384},{128,0},{256,128},{384,256},{1,385},{129,1},{257,129},{385... | collective-permute-start | bytes 3244040 | tf_op jit(solution)/shard_map/ppermute | solution.py:23
  104.4 44.1 %collective-permute-start.12 = (bf16[128,4224]{1,0:T(8,128)(2,1)}, bf16[128,4224]{1,0:T(8,128)(2,1)}, u32[]{:S(2)}, u32[]{:S(2)}) collective-permute-start(bf16[128,4224]{1,0:T(8,128)(2,1)} %bitcast.8.refs_1_.refs_16_.refs_17_.refs_18_), channel_id=1, source_target_pairs={{0,128},{128,256},{256,384},{384,0},{1,129},{129,257},{257,385},{3... | collective-permute-start | bytes 3244040 | tf_op jit(solution)/shard_map/ppermute | solution.py:23
  108.0 45.1 %collective-permute-start.13 = (bf16[128,4224]{1,0:T(8,128)(2,1)}, bf16[128,4224]{1,0:T(8,128)(2,1)}, u32[]{:S(2)}, u32[]{:S(2)}) collective-permute-start(bf16[128,4224]{1,0:T(8,128)(2,1)} %bitcast.8.refs_1_.refs_16_.refs_17_.refs_18_), channel_id=1, source_target_pairs={{0,384},{128,0},{256,128},{384,256},{1,385},{129,1},{257,129},{385... | collective-permute-start | bytes 3244040 | tf_op jit(solution)/shard_map/ppermute | solution.py:23
  123.0 66.0 %all-to-all-start.2 = ((bf16[128,2,2176]{2,1,0:T(2,128)(2,1)}), bf16[128,2,2176]{2,1,0:T(2,128)(2,1)}, u32[]{:S(2)}, u32[]{:S(2)}) async-start(bf16[128,2,2176]{2,1,0:T(2,128)(2,1)} %reshape.259), calls=%async_computation.2 | async-start | bytes 2228224 | tf_op jit(solution)/shard_map/all_to_all | solution.py:315
  153.1 6.0 %copy-start.6 = (s32[16,8]{0,1:T(8,128)S(1)}, s32[16,8]{0,1:T(8,128)}, u32[]{:S(2)}) copy-start(s32[16,8]{0,1:T(8,128)} %param.12) | copy-start | bytes 1540
  153.1 43.2 %collective-permute-start.14 = (bf16[128,4224]{1,0:T(8,128)(2,1)}, bf16[128,4224]{1,0:T(8,128)(2,1)S(1)}, u32[]{:S(2)}, u32[]{:S(2)}) collective-permute-start(bf16[128,4224]{1,0:T(8,128)(2,1)} %get-tuple-element.48.refs_7_.refs_8_.refs_9_), channel_id=1, source_target_pairs={{0,128},{128,256},{256,384},{384,0},{1,129},{129,257},{257,385},{3... | collective-permute-start | bytes 3244040 | tf_op jit(solution)/shard_map/ppermute | solution.py:23
  155.1 41.1 %collective-permute-start.15 = (bf16[128,4224]{1,0:T(8,128)(2,1)}, bf16[128,4224]{1,0:T(8,128)(2,1)}, u32[]{:S(2)}, u32[]{:S(2)}) collective-permute-start(bf16[128,4224]{1,0:T(8,128)(2,1)} %get-tuple-element.51.refs_22_.refs_23_.refs_24_), channel_id=1, source_target_pairs={{0,384},{128,0},{256,128},{384,256},{1,385},{129,1},{257,129},{385... | collective-permute-start | bytes 3244040 | tf_op jit(solution)/shard_map/ppermute | solution.py:23
  159.1 33.2 %collective-permute-start.7 = (bf16[576,256]{1,0:T(8,128)(2,1)}, bf16[576,256]{1,0:T(8,128)(2,1)S(1)}, u32[]{:S(2)}, u32[]{:S(2)}) collective-permute-start(bf16[576,256]{1,0:T(8,128)(2,1)} %get-tuple-element.45), channel_id=1, source_target_pairs={{0,128},{128,256},{256,384},{384,0},{1,129},{129,257},{257,385},{3... | collective-permute-start | bytes 884744 | tf_op jit(solution)/shard_map/ppermute | solution.py:23
  162.3 34.0 %collective-permute-start.8 = (bf16[576,256]{1,0:T(8,128)(2,1)}, bf16[576,256]{1,0:T(8,128)(2,1)S(1)}, u32[]{:S(2)}, u32[]{:S(2)}) collective-permute-start(bf16[576,256]{1,0:T(8,128)(2,1)} %get-tuple-element.46), channel_id=1, source_target_pairs={{0,384},{128,0},{256,128},{384,256},{1,385},{129,1},{257,129},{385... | collective-permute-start | bytes 884744 | tf_op jit(solution)/shard_map/ppermute | solution.py:23
  165.0 31.3 %collective-permute-start.9 = (bf16[576,256]{1,0:T(8,128)(2,1)}, bf16[576,256]{1,0:T(8,128)(2,1)S(1)}, u32[]{:S(2)}, u32[]{:S(2)}) collective-permute-start(bf16[576,256]{1,0:T(8,128)(2,1)} %get-tuple-element.47), channel_id=1, source_target_pairs={{0,256},{128,384},{256,0},{384,128},{1,257},{129,385},{257,1},{385... | collective-permute-start | bytes 884744 | tf_op jit(solution)/shard_map/ppermute | solution.py:23
  190.5 6.8 %copy-start = (bf16[576,256]{1,0:T(8,128)(2,1)S(1)}, bf16[576,256]{1,0:T(8,128)(2,1)}, u32[]{:S(2)}) copy-start(bf16[576,256]{1,0:T(8,128)(2,1)} %get-tuple-element.44.refs_0_) | copy-start | bytes 884740
  196.2 1.0 copy-start.1

commit v9 on v8

--- a/solution.py
+++ b/solution.py
@@ -184,7 +184,7 @@
         d_both = jnp.concatenate([d_gate, gh * act], axis=0).astype(BF16)
         acts_refs[k][: 2 * share] = d_both
         acts_refs[k][2 * share :] = hidden
-        total += tn(d_both, bufs[k, : 2 * share]).astype(BF16).astype(F32)
+        total += tn(d_both, bufs[k, : 2 * share])
     perm = perm_ref[...]
     back_ref[:, :width] = nn(perm, total.astype(BF16)).astype(BF16)
     high = comb.astype(BF16).astype(F32)
@@ -193,26 +193,33 @@
     back_ref[:, width:] = nt(perm, tail).astype(BF16)
 
 
-def grads_kernel(own_ref, *refs):
-    parts, tiles, (gate_ref, up_ref, down_ref) = refs[:DP], refs[DP:-3], refs[-3:]
-    share = gate_ref.shape[0]
+def grads_kernel(count, last, own_ref, *refs):
+    parts, tiles, refs = refs[:count], refs[count : 7 * count], refs[7 * count :]
     part = parts[0].shape[1] // 2
-    both, down = 0.0, 0.0
+    both_share = 2 * (parts[0].shape[0] // 3)
+    both, down = (refs[0][:both_share], refs[0][both_share:]) if last else (0.0, 0.0)
     for c in range(2):
         x, grad, tail = (
-            jnp.concatenate([r[...] for r in tiles[3 * DP * c + k : 3 * DP * (c + 1) : 3]], axis=0) for k in range(3)
+            jnp.concatenate([r[...] for r in tiles[3 * count * c + k : 3 * count * (c + 1) : 3]], axis=0) for k in range(3)
         )
         acts = jnp.concatenate([p[:, c * part : (c + 1) * part] for p in parts], axis=1)
         weight = jnp.sum(tail.astype(F32) * own_ref[...], axis=1, keepdims=True)
         scaled = (weight * grad.astype(F32)).astype(BF16)
-        both += nn(acts[: 2 * share], x)
-        down += nn(acts[2 * share :], scaled)
-    gate_ref[...] = both[:share].astype(BF16)
-    up_ref[...] = both[share:].astype(BF16)
-    down_ref[...] = down.astype(BF16)
-
-
-def weight_grads(own, acts, arrays, share, width, tile=512):
+        both += nn(acts[:both_share], x)
+        down += nn(acts[both_share:], scaled)
+    if last:
+        gate_ref, up_ref, down_ref = refs[1:]
+        gate_ref[...] = both[: both_share // 2].astype(BF16)
+        up_ref[...] = both[both_share // 2 :].astype(BF16)
+        down_ref[...] = down.astype(BF16)
+    else:
+        refs[0][:both_share] = both
+        refs[0][both_share:] = down
+
+
+def weight_grads(own, acts, arrays, before=(), tile=512):
+    rows = acts[0].shape[0]
+    width = (arrays[0].shape[1] - LANES) // 2
     operands = [own, *acts]
     specs = [whole(own), *[whole(a) for a in acts]]
     for a in in_hbm(arrays):
@@ -223,14 +230,19 @@
             pl.BlockSpec((n, tile), lambda j: (0, width // tile + j)),
             pl.BlockSpec((n, LANES), lambda j: (0, 2 * width // LANES)),
         ]
+    for a in before:
+        operands.append(a)
+        specs.append(pl.BlockSpec((rows, tile), lambda j: (0, j)))
+    out = [sds((rows // 3, width), BF16)] * 3 if before else [pltpu.HBM((rows, width), F32)]
     return call(
-        grads_kernel,
+        functools.partial(grads_kernel, len(acts), bool(before)),
         operands,
-        [sds((share, width), BF16)] * 3,
+        out,
         in_specs=specs,
-        out_specs=[pl.BlockSpec((share, tile), lambda j: (0, j))] * 3,
+        out_specs=[pl.BlockSpec((o.shape[0], tile), lambda j: (0, j)) for o in out],
         grid=(width // tile,),
         vmem=28,
+        cost=1 if before else LONG,
     )
 
 
@@ -292,7 +304,7 @@
     second_prev, second_next = shift(second, "dp", DP, 1), shift(second, "dp", DP, -1)
     first_prev, first_next, second_prev, second_next = relay((first_prev, first_next, second_prev, second_next))
     first_far, second_far = shift(first_prev, "dp", DP, 1), shift(second_next, "dp", DP, -1)
-    planes = first, first_prev, first_next, first_far, second, second_prev, second_next, second_far
+    near = first, first_prev, first_next, second, second_prev, second_next
 
     own = (iota((16, experts), 1) == yc * Z + z).astype(F32)
     q = iota((count, 1), 0)
@@ -315,12 +327,14 @@
     home = lax.all_to_all(
         back.reshape(experts, CAP, -1), ("y", "core", "z"), split_axis=0, concat_axis=0, tiled=True
     ).reshape(count, -1)
-    acts = a_own, shift(a_next, "dp", DP, 1), shift(a_prev, "dp", DP, -1), shift(a_far, "dp", DP, 2)
+    *near_acts, far_acts = a_own, shift(a_next, "dp", DP, 1), shift(a_prev, "dp", DP, -1), shift(a_far, "dp", DP, 2)
+    sums = weight_grads(own[:1], near_acts, near)
+    home, sums = lax.optimization_barrier((home, sums))
     grad_in, grad_combine = call(
         home_kernel, (home, rank_of(expert_ids)), [sds((tokens, width), BF16), sds((tokens, picks), F32)], vmem=8
     )
     own, grad_in, grad_combine = lax.optimization_barrier((own, grad_in, grad_combine))
-    grad_gate, grad_up, grad_down = weight_grads(own[:1], acts, planes, share, width)
+    grad_gate, grad_up, grad_down = weight_grads(own[:1], [far_acts], (first_far, second_far), sums)
     return grad_in, grad_combine, grad_gate[None], grad_up[None], grad_down[None]
 
 

time: 206 us -> 205 us (level)
  the two profiles are of different devices: /device:TPU:6 before, /device:TPU:65 now
where the time goes in v9:
time: 205 us; the launch traced here: 204 us
  starting transfers between devices  79.3 us (39%)
  waiting for transfers between devices  51.7 us (25%)
  Pallas kernels  36.6 us (18%)
  blocking collectives  26.9 us (13%)
  local copies, waits for them, and re-layouts  7.29 us (4%)
    ppermute x15, starting transfers between devices, shift(): return lax.ppermute(a, axis, [(i, (i + k) % size) for i in range(size)])  48 us
    pallas_call x7, Pallas kernels, call(): pl.pallas_call(kernel, grid=grid, out_shape=out_shape, in_specs=in_specs...  31.3 us
    all_gather x1, blocking collectives, body(): lax.all_gather(payload, 'z', axis=0, tiled=True, axis_index_groups=groups)  26.9 us
    all_to_all x1, waiting for transfers between devices, body(): lax.all_to_all(back.reshape(experts, CAP, -1), ('y', 'core', 'z'), split_...  24 us
    ppermute x15, waiting for transfers between devices, shift(): return lax.ppermute(a, axis, [(i, (i + k) % size) for i in range(size)])  17.5 us
    all_to_all x2, starting transfers between devices, to_experts(): lax.all_to_all(sent.reshape(YC, -1, sent.shape[1]), ('y', 'core'), split_...  14.1 us
    all_to_all x1, starting transfers between devices, body(): lax.all_to_all(back.reshape(experts, CAP, -1), ('y', 'core', 'z'), split_...  12.2 us
    all_to_all x2, waiting for transfers between devices, to_experts(): lax.all_to_all(sent.reshape(YC, -1, sent.shape[1]), ('y', 'core'), split_...  10.2 us
  transfers between devices with their start and end apart: 19, of which 7 were waited for; matrix products, arithmetic and copies ran while one was open for 2% of the time, Pallas kernels for 14%

profile of v9, /device:TPU:65, one launch (start us, length us, event | category | flops | bytes accessed | tf_op | source)
XLA Modules:
  0.0 203.6 jit_solution(2409002125837619266)
XLA Ops:
  0.6 0.0 copy-start.5
  0.7 2.6 %shard_map.121.refs_2_ = bf16[576,2048]{1,0:T(8,128)(2,1)} custom-call(bf16[192,2048]{1,0:T(8,128)(2,1)} %bitcast.34, bf16[192,2048]{1,0:T(8,128)(2,1)} %bitcast.35, bf16[192,2048]{1,0:T(8,128)(2,1)} %bitcast.36), custom_call_target="tpu_custom_call" | custom-call | flops 1 | bytes 1048576 | tf_op jit(solution)/shard_map/pallas_call | solution.py:85
  3.3 3.1 %collective-permute-start.3 = (bf16[576,2048]{1,0:T(8,128)(2,1)}, bf16[576,2048]{1,0:T(8,128)(2,1)S(1)}, u32[]{:S(2)}, u32[]{:S(2)}) collective-permute-start(bf16[576,2048]{1,0:T(8,128)(2,1)} %shard_map.121.refs_2_), channel_id=1, source_target_pairs={{0,128},{128,256},{256,384},{384,0},{1,129},{129,257},{257,385},{3... | collective-permute-start | bytes 7077896 | tf_op jit(solution)/shard_map/ppermute | solution.py:23
  6.4 3.4 %collective-permute-start.4 = (bf16[576,2048]{1,0:T(8,128)(2,1)}, bf16[576,2048]{1,0:T(8,128)(2,1)}, u32[]{:S(2)}, u32[]{:S(2)}) collective-permute-start(bf16[576,2048]{1,0:T(8,128)(2,1)} %shard_map.121.refs_2_), channel_id=1, source_target_pairs={{0,384},{128,0},{256,128},{384,256},{1,385},{129,1},{257,129},{385... | collective-permute-start | bytes 7077896 | tf_op jit(solution)/shard_map/ppermute | solution.py:23
  9.8 1.1 shard_map.119
  10.9 26.9 %all_gather.3.refs_0_ = bf16[64,4224]{1,0:T(8,128)(2,1)S(1)} all-gather(bf16[16,4224]{1,0:T(8,128)(2,1)S(1)} %shard_map.119), channel_id=1, replica_groups={{0,8,16,24},{2,10,18,26},{4,12,20,28},{6,14,22,30},{1,9,17,25},{3,11,19..., dimensions={0}, use_global_device_ids=true | all-gather | bytes 675840 | tf_op jit(solution)/shard_map/all_gather | solution.py:286
  37.8 3.7 %collective-permute-start = (bf16[64,4224]{1,0:T(8,128)(2,1)S(1)}, bf16[64,4224]{1,0:T(8,128)(2,1)S(1)}, u32[]{:S(2)}, u32[]{:S(2)}) collective-permute-start(bf16[64,4224]{1,0:T(8,128)(2,1)S(1)} %all_gather.3.refs_0_), channel_id=1, source_target_pairs={{0,30},{2,0},{4,2},{6,4},{8,6},{10,8},{12,10},{14,12},{16,14},{18,... | collective-permute-start | bytes 1622024 | tf_op jit(solution)/shard_map/ppermute | solution.py:23
  41.5 2.6 %collective-permute-start.1 = (bf16[64,4224]{1,0:T(8,128)(2,1)S(1)}, bf16[64,4224]{1,0:T(8,128)(2,1)}, u32[]{:S(2)}, u32[]{:S(2)}) collective-permute-start(bf16[64,4224]{1,0:T(8,128)(2,1)S(1)} %all_gather.3.refs_0_), channel_id=1, source_target_pairs={{0,2},{2,4},{4,6},{6,8},{8,10},{10,12},{12,14},{14,16},{16,18},{18... | collective-permute-start | bytes 1622024 | tf_op jit(solution)/shard_map/ppermute | solution.py:23
  44.1 6.1 %collective-permute-done.refs_1_ = bf16[64,4224]{1,0:T(8,128)(2,1)S(1)} collective-permute-done((bf16[64,4224]{1,0:T(8,128)(2,1)S(1)}, bf16[64,4224]{1,0:T(8,128)(2,1)S(1)}, u32[]{:S(2)}, u32[]{:S(2)}) %collective-permute-start) | collective-permute-done | bytes 540704 | tf_op jit(solution)/shard_map/ppermute | solution.py:23
  50.3 4.9 %collective-permute-start.2 = (bf16[64,4224]{1,0:T(8,128)(2,1)S(1)}, bf16[64,4224]{1,0:T(8,128)(2,1)}, u32[]{:S(2)}, u32[]{:S(2)}) collective-permute-start(bf16[64,4224]{1,0:T(8,128)(2,1)S(1)} %all_gather.3.refs_0_), channel_id=1, source_target_pairs={{4,0},{30,2},{8,4},{2,6},{12,8},{6,10},{16,12},{10,14},{20,16},{14... | collective-permute-start | bytes 1622024 | tf_op jit(solution)/shard_map/ppermute | solution.py:295
  55.3 0.1 fusion.8.pick_ref
  55.3 2.9 %shard_map.120 = bf16[128,4224]{1,0:T(8,128)(2,1)} custom-call(bf16[16,128]{1,0:T(8,128)(2,1)S(1)} %fusion.8.pick_ref, bf16[64,4224]{1,0:T(8,128)(2,1)} %copy-done.3, bf16[64,4224]{1,0:T(8,128)(2,1)} %copy-done.4), custom_call_target="tpu_custom_call" | custom-call | flops 1 | bytes 1048576 | tf_op jit(solution)/shard_map/pallas_call | solution.py:47
  58.2 9.0 %all-to-all-start = ((bf16[8,16,4224]{2,1,0:T(8,128)(2,1)}), bf16[8,16,4224]{2,1,0:T(8,128)(2,1)}, u32[]{:S(2)}, u32[]{:S(2)}) async-start(bf16[8,16,4224]{2,1,0:T(8,128)(2,1)} %bitcast.2), calls=%async_computation | async-start | bytes 2162688 | tf_op jit(solution)/shard_map/all_to_all | solution.py:151
  67.3 1.4 copy-done.2
  68.7 2.7 %shard_map.122 = (bf16[288,2048]{1,0:T(8,128)(2,1)}, bf16[288,2048]{1,0:T(8,128)(2,1)}) custom-call(bf16[576,2048]{1,0:T(8,128)(2,1)} %copy-done.2, bf16[576,2048]{1,0:T(8,128)(2,1)} %collective-permute-done.4.refs_1_.refs_3_), custom_call_target="tpu_custom_call" | custom-call | flops 1 | bytes 1048576 | tf_op jit(solution)/shard_map/pallas_call | solution.py:85
  71.4 0.0 collective-permute-done.1.refs_0_
  71.4 1.9 collective-permute-start.5
  73.4 4.6 %collective-permute-start.6 = (bf16[288,2048]{1,0:T(8,128)(2,1)}, bf16[288,2048]{1,0:T(8,128)(2,1)}, u32[]{:S(2)}, u32[]{:S(2)}) collective-permute-start(bf16[288,2048]{1,0:T(8,128)(2,1)} %get-tuple-element.39), channel_id=1, source_target_pairs={{0,384},{128,0},{256,128},{384,256},{1,385},{129,1},{257,129},{385... | collective-permute-start | bytes 3538952 | tf_op jit(solution)/shard_map/ppermute | solution.py:23
  78.0 2.9 %shard_map.123 = bf16[128,4224]{1,0:T(8,128)(2,1)} custom-call(bf16[16,128]{1,0:T(8,128)(2,1)S(1)} %fusion.8.pick_ref, bf16[64,4224]{1,0:T(8,128)(2,1)} %collective-permute-done.1.refs_0_, bf16[64,4224]{1,0:T(8,128)(2,1)} %collective-permute-done.2.refs_1_), custom_call_target="tpu_custom_call" | custom-call | flops 999999995904 | bytes 1048576 | tf_op jit(solution)/shard_map/pallas_call | solution.py:47
  80.9 1.9 all-to-all-done
  82.8 5.1 %all-to-all-start.1 = ((bf16[8,16,4224]{2,1,0:T(8,128)(2,1)}), bf16[8,16,4224]{2,1,0:T(8,128)(2,1)}, u32[]{:S(2)}, u32[]{:S(2)}) async-start(bf16[8,16,4224]{2,1,0:T(8,128)(2,1)} %bitcast.7), calls=%async_computation.1 | async-start | bytes 2162688 | tf_op jit(solution)/shard_map/all_to_all | solution.py:151
  87.9 0.1 copy.17
  88.0 0.5 compare_convert_fusion.1
  88.6 0.1 fusion.perm_ref
  88.7 1.9 collective-permute-start.9
  90.6 4.6 %collective-permute-start.10 = (bf16[128,4224]{1,0:T(8,128)(2,1)}, bf16[128,4224]{1,0:T(8,128)(2,1)}, u32[]{:S(2)}, u32[]{:S(2)}) collective-permute-start(bf16[128,4224]{1,0:T(8,128)(2,1)} %bitcast.3.refs_0_.refs_3_.refs_4_.refs_5_), channel_id=1, source_target_pairs={{0,384},{128,0},{256,128},{384,256},{1,385},{129,1},{257,129},{385... | collective-permute-start | bytes 3244040 | tf_op jit(solution)/shard_map/ppermute | solution.py:23
  95.2 8.3 %all-to-all-done.1 = bf16[8,16,4224]{2,1,0:T(8,128)(2,1)} async-done(((bf16[8,16,4224]{2,1,0:T(8,128)(2,1)}), bf16[8,16,4224]{2,1,0:T(8,128)(2,1)}, u32[]{:S(2)}, u32[]{:S(2)}) %all-to-all-start.1) | async-done | bytes 1081376 | tf_op jit(solution)/shard_map/all_to_all | solution.py:151
  103.5 1.9 collective-permute-start.11
  105.4 4.6 %collective-permute-start.12 = (bf16[128,4224]{1,0:T(8,128)(2,1)}, bf16[128,4224]{1,0:T(8,128)(2,1)}, u32[]{:S(2)}, u32[]{:S(2)}) collective-permute-start(bf16[128,4224]{1,0:T(8,128)(2,1)} %bitcast.8.refs_1_.refs_12_.refs_13_.refs_14_), channel_id=1, source_target_pairs={{0,384},{128,0},{256,128},{384,256},{1,385},{129,1},{257,129},{385... | collective-permute-start | bytes 3244040 | tf_op jit(solution)/shard_map/ppermute | solution.py:23
  110.0 11.3 %shard_map.124 = (bf16[256,2176]{1,0:T(8,128)(2,1)S(1)}, bf16[576,256]{1,0:T(8,128)(2,1)}, bf16[576,256]{1,0:T(8,128)(2,1)}, bf16[576,256]{1,0:T(8,128)(2,1)}, bf16[576,256]{1,0:T(8,128)(2,1)}) custom-call(bf16[16,128]{1,0:T(8,128)(2,1)S(1)} %iota.45.own_ref, bf16[256,256]{1,0:T(8,128)(2,1)S(1)} %fusion.perm_ref, ...), custom_call_target="tpu_custom_call" | custom-call | flops 999999995904 | bytes 1048576 | tf_op jit(solution)/shard_map/pallas_call | solution.py:47
  121.3 1.3 reshape.267
  122.5 12.2 %all-to-all-start.2 = ((bf16[128,2,2176]{2,1,0:T(2,128)(2,1)}), bf16[128,2,2176]{2,1,0:T(2,128)(2,1)}, u32[]{:S(2)}, u32[]{:S(2)}) async-start(bf16[128,2,2176]{2,1,0:T(2,128)(2,1)} %reshape.267), calls=%async_computation.2 | async-start | bytes 2228224 | tf_op jit(solution)/shard_map/all_to_all | solution.py:327
  134.8 1.9 collective-permute-start.7
  136.7 4.6 %collective-permute-start.8 = (bf16[576,256]{1,0:T(8,128)(2,1)}, bf16[576,256]{1,0:T(8,128)(2,1)}, u32[]{:S(2)}, u32[]{:S(2)}) collective-permute-start(bf16[576,256]{1,0:T(8,128)(2,1)} %get-tuple-element.43), channel_id=1, source_target_pairs={{0,384},{128,0},{256,128},{384,256},{1,385},{129,1},{257,129},{385... | collective-permute-start | bytes 884744 | tf_op jit(solution)/shard_map/ppermute | solution.py:23
  141.3 1.9 collective-permute-start.13
  143.2 5.6 %collective-permute-done.11.refs_2_ = bf16[128,4224]{1,0:T(8,128)(2,1)} collective-permute-done((bf16[128,4224]{1,0:T(8,128)(2,1)}, bf16[128,4224]{1,0:T(8,128)(2,1)}, u32[]{:S(2)}, u32[]{:S(2)}) %collective-permute-start.11) | collective-permute-done | bytes 1081376 | tf_op jit(solution)/shard_map/ppermute | solution.py:23
  148.8 0.9 collective-permute-done.12.refs_3_
  149.7 2.5 %collective-permute-start.14 = (bf16[128,4224]{1,0:T(8,128)(2,1)}, bf16[128,4224]{1,0:T(8,128)(2,1)}, u32[]{:S(2)}, u32[]{:S(2)}) collective-permute-start(bf16[128,4224]{1,0:T(8,128)(2,1)} %get-tuple-element.44.refs_6_.refs_7_.refs_8_), channel_id=1, source_target_pairs={{0,128},{128,256},{256,384},{384,0},{1,129},{129,257},{257,385},{3... | collective-permute-start | bytes 3244040 | tf_op jit(solution)/shard_map/ppermute | solution.py:23
  152.1 4.9 %collective-permute-start.15 = (bf16[128,4224]{1,0:T(8,128)(2,1)}, bf16[128,4224]{1,0:T(8,128)(2,1)}, u32[]{:S(2)}, u32[]{:S(2)}) collective-permute-start(bf16[128,4224]{1,0:T(8,128)(2,1)} %get-tuple-element.47.refs_18_.refs_19_.refs_20_), channel_id=1, source_target_pairs={{0,384},{128,0},{256,128},{384,256},{1,385},{129,1},{257,129},{385... | collective-permute-start | bytes 3244040 | tf_op jit(solution)/shard_map/ppermute | solution.py:23
  157.1 4.9 %collective-permute-done.8.refs_2_ = bf16[576,256]{1,0:T(8,128)(2,1)} collective-permute-done((bf16[576,256]{1,0:T(8,128)(2,1)}, bf16[576,256]{1,0:T(8,128)(2,1)}, u32[]{:S(2)}, u32[]{:S(2)}) %collective-permute-start.8) | collective-permute-done | bytes 294944 | tf_op jit(solution)/shard_map/ppermute | solution.py:23
  162.0 7.3 %shard_map.126.refs_7_ = f32[576,2048]{1,0:T(8,128)} custom-call(f32[1,128]{1,0:T(1,128)S(1)} %compare_convert_fusion.own_ref, bf16[576,256]{1,0:T(8,128)(2,1)S(1)} %copy-done.1, bf16[576,256]{1,0:T(8,128)(2,1)} %collective-permute-done.7.refs_1_, bf16[576,256]{1,0:T(8,128)(2,1)} %collective-permute-done.8.refs_2_, ...), custom_call_target="tpu_custom_call" | custom-call | flops 999999995904 | bytes 1048576 | tf_op jit(solution)/shard_map/pallas_call | solution.py:47
  169.3 24.0 %all-to-all-done.2 = bf16[128,2,2176]{2,1,0:T(2,128)(2,1)} async-done(((bf16[128,2,2176]{2,1,0:T(2,128)(2,1)}), bf16[128,2,2176]{2,1,0:T(2,128)(2,1)}, u32[]{:S(2)}, u32[]{:S(2)}) %all-to-all-start.2) | async-done | bytes 1114144 | tf_op jit(solution)/shard_map/all_to_all | solution.py:327
  193.2 1.5 reshape.268.home_ref
  194.7 0.0 copy-start.8
  194.7 1.2 shard_map.127
  195.9 0.7 copy.21
  196.6 2.3 %copy-done = f32[576,2048]{1,0:T(8,128)S(1)} copy-done((f32[576,2048]{1,0:T(8,128)S(1)}, f32[576,2048]{1,0:T(8,128)}, u32[]{:S(2)}) %copy-start) | copy-done | bytes 4718616
  198.9 4.7 %shard_map.128 = (bf16[192,2048]{1,0:T(8,128)(2,1)}, bf16[192,2048]{1,0:T(8,128)(2,1)}, bf16[192,2048]{1,0:T(8,128)(2,1)}) custom-call(f32[1,128]{1,0:T(1,128)S(1)} %slice.4.own_ref, bf16[576,256]{1,0:T(8,128)(2,1)} %collective-permute-done.13.refs_0_, bf16[128,4224]{1,0:T(8,128)(2,1)} %collective-permute-done.14.refs_1_.refs_2_.refs_3_, ...), custom_call_target="tpu_custom_call" | custom-call | flops 1 | bytes 1048576 | tf_op jit(solution)/shard_map/pallas_call | solution.py:47
  (37 shorter events, 0.2 us)
Async XLA Ops:
  0.6 9.2 %copy-start.7 = (bf16[16,8]{0,1:T(8,128)(2,1)S(1)}, bf16[16,8]{0,1:T(8,128)(2,1)}, u32[]{:S(2)}) copy-start(bf16[16,8]{0,1:T(8,128)(2,1)} %param.11) | copy-start | bytes 772
  0.6 9.2 %copy-start.5 = (s32[16,8]{0,1:T(8,128)S(1)}, s32[16,8]{0,1:T(8,128)}, u32[]{:S(2)}) copy-start(s32[16,8]{0,1:T(8,128)} %param.12) | copy-start | bytes 1540
  3.3 64.0 %collective-permute-start.3 = (bf16[576,2048]{1,0:T(8,128)(2,1)}, bf16[576,2048]{1,0:T(8,128)(2,1)S(1)}, u32[]{:S(2)}, u32[]{:S(2)}) collective-permute-start(bf16[576,2048]{1,0:T(8,128)(2,1)} %shard_map.121.refs_2_), channel_id=1, source_target_pairs={{0,128},{128,256},{256,384},{384,0},{1,129},{129,257},{257,385},{3... | collective-permute-start | bytes 7077896 | tf_op jit(solution)/shard_map/ppermute | solution.py:23
  6.4 60.9 %collective-permute-start.4 = (bf16[576,2048]{1,0:T(8,128)(2,1)}, bf16[576,2048]{1,0:T(8,128)(2,1)}, u32[]{:S(2)}, u32[]{:S(2)}) collective-permute-start(bf16[576,2048]{1,0:T(8,128)(2,1)} %shard_map.121.refs_2_), channel_id=1, source_target_pairs={{0,384},{128,0},{256,128},{384,256},{1,385},{129,1},{257,129},{385... | collective-permute-start | bytes 7077896 | tf_op jit(solution)/shard_map/ppermute | solution.py:23
  37.8 17.5 %copy-start.3 = (bf16[64,4224]{1,0:T(8,128)(2,1)}, bf16[64,4224]{1,0:T(8,128)(2,1)S(1)}, u32[]{:S(2)}) copy-start(bf16[64,4224]{1,0:T(8,128)(2,1)S(1)} %all_gather.3.refs_0_) | copy-start | bytes 1622020
  37.8 12.4 %collective-permute-start = (bf16[64,4224]{1,0:T(8,128)(2,1)S(1)}, bf16[64,4224]{1,0:T(8,128)(2,1)S(1)}, u32[]{:S(2)}, u32[]{:S(2)}) collective-permute-start(bf16[64,4224]{1,0:T(8,128)(2,1)S(1)} %all_gather.3.refs_0_), channel_id=1, source_target_pairs={{0,30},{2,0},{4,2},{6,4},{8,6},{10,8},{12,10},{14,12},{16,14},{18,... | collective-permute-start | bytes 1622024 | tf_op jit(solution)/shard_map/ppermute | solution.py:23
  41.5 29.9 %collective-permute-start.1 = (bf16[64,4224]{1,0:T(8,128)(2,1)S(1)}, bf16[64,4224]{1,0:T(8,128)(2,1)}, u32[]{:S(2)}, u32[]{:S(2)}) collective-permute-start(bf16[64,4224]{1,0:T(8,128)(2,1)S(1)} %all_gather.3.refs_0_), channel_id=1, source_target_pairs={{0,2},{2,4},{4,6},{6,8},{8,10},{10,12},{12,14},{14,16},{16,18},{18... | collective-permute-start | bytes 1622024 | tf_op jit(solution)/shard_map/ppermute | solution.py:23
  50.3 5.1 %copy-start.4 = (bf16[64,4224]{1,0:T(8,128)(2,1)}, bf16[64,4224]{1,0:T(8,128)(2,1)S(1)}, u32[]{:S(2)}) copy-start(bf16[64,4224]{1,0:T(8,128)(2,1)S(1)} %collective-permute-done.refs_1_) | copy-start | bytes 1622020
  50.3 21.2 %collective-permute-start.2 = (bf16[64,4224]{1,0:T(8,128)(2,1)S(1)}, bf16[64,4224]{1,0:T(8,128)(2,1)}, u32[]{:S(2)}, u32[]{:S(2)}) collective-permute-start(bf16[64,4224]{1,0:T(8,128)(2,1)S(1)} %all_gather.3.refs_0_), channel_id=1, source_target_pairs={{4,0},{30,2},{8,4},{2,6},{12,8},{6,10},{16,12},{10,14},{20,16},{14... | collective-permute-start | bytes 1622024 | tf_op jit(solution)/shard_map/ppermute | solution.py:295
  58.2 24.6 %all-to-all-start = ((bf16[8,16,4224]{2,1,0:T(8,128)(2,1)}), bf16[8,16,4224]{2,1,0:T(8,128)(2,1)}, u32[]{:S(2)}, u32[]{:S(2)}) async-start(bf16[8,16,4224]{2,1,0:T(8,128)(2,1)} %bitcast.2), calls=%async_computation | async-start | bytes 2162688 | tf_op jit(solution)/shard_map/all_to_all | solution.py:151
  67.3 1.5 copy-start.2
  71.4 34.0 %collective-permute-start.5 = (bf16[288,2048]{1,0:T(8,128)(2,1)}, bf16[288,2048]{1,0:T(8,128)(2,1)}, u32[]{:S(2)}, u32[]{:S(2)}) collective-permute-start(bf16[288,2048]{1,0:T(8,128)(2,1)} %get-tuple-element.38), channel_id=1, source_target_pairs={{0,128},{128,256},{256,384},{384,0},{1,129},{129,257},{257,385},{3... | collective-permute-start | bytes 3538952 | tf_op jit(solution)/shard_map/ppermute | solution.py:23
  73.4 36.6 %collective-permute-start.6 = (bf16[288,2048]{1,0:T(8,128)(2,1)}, bf16[288,2048]{1,0:T(8,128)(2,1)}, u32[]{:S(2)}, u32[]{:S(2)}) collective-permute-start(bf16[288,2048]{1,0:T(8,128)(2,1)} %get-tuple-element.39), channel_id=1, source_target_pairs={{0,384},{128,0},{256,128},{384,256},{1,385},{129,1},{257,129},{385... | collective-permute-start | bytes 3538952 | tf_op jit(solution)/shard_map/ppermute | solution.py:23
  82.8 5.1 %copy-start.6 = (s32[16,8]{0,1:T(8,128)S(1)}, s32[16,8]{0,1:T(8,128)}, u32[]{:S(2)}) copy-start(s32[16,8]{0,1:T(8,128)} %param.12) | copy-start | bytes 1540
  82.8 20.7 %all-to-all-start.1 = ((bf16[8,16,4224]{2,1,0:T(8,128)(2,1)}), bf16[8,16,4224]{2,1,0:T(8,128)(2,1)}, u32[]{:S(2)}, u32[]{:S(2)}) async-start(bf16[8,16,4224]{2,1,0:T(8,128)(2,1)} %bitcast.7), calls=%async_computation.1 | async-start | bytes 2162688 | tf_op jit(solution)/shard_map/all_to_all | solution.py:151
  88.7 48.0 %collective-permute-start.9 = (bf16[128,4224]{1,0:T(8,128)(2,1)}, bf16[128,4224]{1,0:T(8,128)(2,1)}, u32[]{:S(2)}, u32[]{:S(2)}) collective-permute-start(bf16[128,4224]{1,0:T(8,128)(2,1)} %bitcast.3.refs_0_.refs_3_.refs_4_.refs_5_), channel_id=1, source_target_pairs={{0,128},{128,256},{256,384},{384,0},{1,129},{129,257},{257,385},{3... | collective-permute-start | bytes 3244040 | tf_op jit(solution)/shard_map/ppermute | solution.py:23
  90.6 50.7 %collective-permute-start.10 = (bf16[128,4224]{1,0:T(8,128)(2,1)}, bf16[128,4224]{1,0:T(8,128)(2,1)}, u32[]{:S(2)}, u32[]{:S(2)}) collective-permute-start(bf16[128,4224]{1,0:T(8,128)(2,1)} %bitcast.3.refs_0_.refs_3_.refs_4_.refs_5_), channel_id=1, source_target_pairs={{0,384},{128,0},{256,128},{384,256},{1,385},{129,1},{257,129},{385... | collective-permute-start | bytes 3244040 | tf_op jit(solution)/shard_map/ppermute | solution.py:23
  103.5 45.3 %collective-permute-start.11 = (bf16[128,4224]{1,0:T(8,128)(2,1)}, bf16[128,4224]{1,0:T(8,128)(2,1)}, u32[]{:S(2)}, u32[]{:S(2)}) collective-permute-start(bf16[128,4224]{1,0:T(8,128)(2,1)} %bitcast.8.refs_1_.refs_12_.refs_13_.refs_14_), channel_id=1, source_target_pairs={{0,128},{128,256},{256,384},{384,0},{1,129},{129,257},{257,385},{3... | collective-permute-start | bytes 3244040 | tf_op jit(solution)/shard_map/ppermute | solution.py:23
  105.4 44.2 %collective-permute-start.12 = (bf16[128,4224]{1,0:T(8,128)(2,1)}, bf16[128,4224]{1,0:T(8,128)(2,1)}, u32[]{:S(2)}, u32[]{:S(2)}) collective-permute-start(bf16[128,4224]{1,0:T(8,128)(2,1)} %bitcast.8.refs_1_.refs_12_.refs_13_.refs_14_), channel_id=1, source_target_pairs={{0,384},{128,0},{256,128},{384,256},{1,385},{129,1},{257,129},{385... | collective-permute-start | bytes 3244040 | tf_op jit(solution)/shard_map/ppermute | solution.py:23
  122.5 70.7 %all-to-all-start.2 = ((bf16[128,2,2176]{2,1,0:T(2,128)(2,1)}), bf16[128,2,2176]{2,1,0:T(2,128)(2,1)}, u32[]{:S(2)}, u32[]{:S(2)}) async-start(bf16[128,2,2176]{2,1,0:T(2,128)(2,1)} %reshape.267), calls=%async_computation.2 | async-start | bytes 2228224 | tf_op jit(solution)/shard_map/all_to_all | solution.py:327
  134.8 22.3 %collective-permute-start.7 = (bf16[576,256]{1,0:T(8,128)(2,1)}, bf16[576,256]{1,0:T(8,128)(2,1)}, u32[]{:S(2)}, u32[]{:S(2)}) collective-permute-start(bf16[576,256]{1,0:T(8,128)(2,1)} %get-tuple-element.42), channel_id=1, source_target_pairs={{0,128},{128,256},{256,384},{384,0},{1,129},{129,257},{257,385},{3... | collective-permute-start | bytes 884744 | tf_op jit(solution)/shard_map/ppermute | solution.py:23
  136.7 25.3 %collective-permute-start.8 = (bf16[576,256]{1,0:T(8,128)(2,1)}, bf16[576,256]{1,0:T(8,128)(2,1)}, u32[]{:S(2)}, u32[]{:S(2)}) collective-permute-start(bf16[576,256]{1,0:T(8,128)(2,1)} %get-tuple-element.43), channel_id=1, source_target_pairs={{0,384},{128,0},{256,128},{384,256},{1,385},{129,1},{257,129},{385... | collective-permute-start | bytes 884744 | tf_op jit(solution)/shard_map/ppermute | solution.py:23
  141.3 55.3 %collective-permute-start.13 = (bf16[576,256]{1,0:T(8,128)(2,1)}, bf16[576,256]{1,0:T(8,128)(2,1)}, u32[]{:S(2)}, u32[]{:S(2)}) collective-permute-start(bf16[576,256]{1,0:T(8,128)(2,1)} %get-tuple-element.54), channel_id=1, source_target_pairs={{0,256},{128,384},{256,0},{384,128},{1,257},{129,385},{257,1},{385... | collective-permute-start | bytes 884744 | tf_op jit(solution)/shard_map/ppermute | solution.py:23
  149.7 12.3 %copy-start.1 = (bf16[576,256]{1,0:T(8,128)(2,1)S(1)}, bf16[576,256]{1,0:T(8,128)(2,1)}, u32[]{:S(2)}) copy-start(bf16[576,256]{1,0:T(8,128)(2,1)} %get-tuple-element.41.refs_0_) | copy-start | bytes 884740
  149.7 46.9 %collective-permute-start.14 = (bf16[128,4224]{1,0:T(8,128)(2,1)}, bf16[128,4224]{1,0:T(8,128)(2,1)}, u32[]{:S(2)}, u32[]{:S(2)}) collective-permute-start(bf16[128,4224]{1,0:T(8,128)(2,1)} %get-tuple-element.44.refs_6_.refs_7_.refs_8_), channel_id=1, source_target_pairs={{0,128},{128,256},{256,384},{384,0},{1,129},{129,257},{257,385},{3... | collective-permute-start | bytes 3244040 | tf_op jit(solution)/shard_map/ppermute | solution.py:23
  152.1 44.5 %collective-permute-start.15 = (bf16[128,4224]{1,0:T(8,128)(2,1)}, bf16[128,4224]{1,0:T(8,128)(2,1)}, u32[]{:S(2)}, u32[]{:S(2)}) collective-permute-start(bf16[128,4224]{1,0:T(8,128)(2,1)} %get-tuple-element.47.refs_18_.refs_19_.refs_20_), channel_id=1, source_target_pairs={{0,384},{128,0},{256,128},{384,256},{1,385},{129,1},{257,129},{385... | collective-permute-start | bytes 3244040 | tf_op jit(solution)/shard_map/ppermute | solution.py:23
  194.7 1.2 copy-start.8
  196.6 2.3 %copy-start = (f32[576,2048]{1,0:T(8,128)S(1)}, f32[576,2048]{1,0:T(8,128)}, u32[]{:S(2)}) copy-start(f32[576,2048]{1,0:T(8,128)} %shard_map.126.refs_7_) | copy-start | bytes 14155780

commit v10 on v9

--- a/solution.py
+++ b/solution.py
@@ -247,25 +247,25 @@
 
 
 def home_kernel(home_ref, rank_ref, grad_ref, comb_ref):
-    tokens, picks = rank_ref.shape
+    picks, tokens = rank_ref.shape
     width = grad_ref.shape[1]
     count = home_ref.shape[0]
     experts = count // CAP
-    lane = iota((tokens, experts), 1)
-    named = jnp.zeros((tokens, experts), F32)
+    expert = iota((experts, tokens), 0)
+    named = jnp.zeros((experts, tokens), F32)
     for k in range(picks):
-        named += (rank_ref[:, k : k + 1] == lane).astype(F32)
-    prior = nn((iota((tokens, tokens), 1) < iota((tokens, tokens), 0)).astype(BF16), named.astype(BF16))
-    spread = (iota((experts, count), 1) // CAP == iota((experts, count), 0)).astype(BF16)
-    slot = iota((tokens, count), 1)
-    here = nn(named.astype(BF16), spread) > 0
-    owner = (here & (nn(prior.astype(BF16), spread).astype(I32) == slot % CAP)).astype(F32)
-    grad_ref[...] = nn(owner.astype(BF16), home_ref[:, :width]).astype(BF16)
-    pair = (iota((tokens, LANES), 1) < 2).astype(BF16)
-    value = owner * nt(pair, home_ref[:, width:])
+        named += (rank_ref[k : k + 1] == expert).astype(F32)
+    prior = nn(named.astype(BF16), (iota((tokens, tokens), 0) < iota((tokens, tokens), 1)).astype(BF16))
+    spread = (iota((count, experts), 0) // CAP == iota((count, experts), 1)).astype(BF16)
+    slot = iota((count, tokens), 0)
+    here = nn(spread, named.astype(BF16)) > 0
+    owner = (here & (nn(spread, prior.astype(BF16)).astype(I32) == slot % CAP)).astype(F32)
+    grad_ref[...] = tn(owner.astype(BF16), home_ref[:, :width]).astype(BF16)
+    tail = home_ref[:, width:].astype(F32)
+    value = owner * jnp.sum(jnp.where(iota(tail.shape, 1) < 2, tail, 0.0), axis=1, keepdims=True)
     for k in range(picks):
-        mine = jnp.where(rank_ref[:, k : k + 1] == slot // CAP, value, 0.0)
-        comb_ref[:, k : k + 1] = jnp.sum(mine, axis=1, keepdims=True)
+        mine = jnp.where(rank_ref[k : k + 1] == slot // CAP, value, 0.0)
+        comb_ref[k : k + 1] = jnp.sum(mine, axis=0, keepdims=True)
 
 
 def body(grad_out, x_codes, x_scales, combine, expert_ids, w_gate, w_up, w_down):
@@ -329,12 +329,12 @@
     ).reshape(count, -1)
     *near_acts, far_acts = a_own, shift(a_next, "dp", DP, 1), shift(a_prev, "dp", DP, -1), shift(a_far, "dp", DP, 2)
     sums = weight_grads(own[:1], near_acts, near)
-    home, sums = lax.optimization_barrier((home, sums))
+    grad_gate, grad_up, grad_down = weight_grads(own[:1], [far_acts], (first_far, second_far), in_hbm(sums))
+    home, grad_gate, grad_up, grad_down = lax.optimization_barrier((home, grad_gate, grad_up, grad_down))
     grad_in, grad_combine = call(
-        home_kernel, (home, rank_of(expert_ids)), [sds((tokens, width), BF16), sds((tokens, picks), F32)], vmem=8
-    )
-    own, grad_in, grad_combine = lax.optimization_barrier((own, grad_in, grad_combine))
-    grad_gate, grad_up, grad_down = weight_grads(own[:1], [far_acts], (first_far, second_far), sums)
+        home_kernel, (home, rank_of(expert_ids.T)), [sds((tokens, width), BF16), sds((picks, tokens), F32)], vmem=8
+    )
+    grad_combine = grad_combine.T
     return grad_in, grad_combine, grad_gate[None], grad_up[None], grad_down[None]
 
 

time: 205 us -> 200 us (0.976)
  the two profiles are of different devices: /device:TPU:65 before, /device:TPU:6 now
where the time goes in v10:
time: 200 us; the launch traced here: 198 us
  starting transfers between devices  72.6 us (36%)
  waiting for transfers between devices  54.3 us (27%)
  Pallas kernels  37.7 us (19%)
  blocking collectives  28.4 us (14%)
  local copies, waits for them, and re-layouts  4.24 us (2%)
    ppermute x15, starting transfers between devices, shift(): return lax.ppermute(a, axis, [(i, (i + k) % size) for i in range(size)])  49.6 us
    ppermute x15, waiting for transfers between devices, shift(): return lax.ppermute(a, axis, [(i, (i + k) % size) for i in range(size)])  40.5 us
    pallas_call x7, Pallas kernels, call(): pl.pallas_call(kernel, grid=grid, out_shape=out_shape, in_specs=in_specs...  32.4 us
    all_gather x1, blocking collectives, body(): lax.all_gather(payload, 'z', axis=0, tiled=True, axis_index_groups=groups)  28.4 us
    all_to_all x2, waiting for transfers between devices, to_experts(): lax.all_to_all(sent.reshape(YC, -1, sent.shape[1]), ('y', 'core'), split_...  13.8 us
    all_to_all x1, starting transfers between devices, body(): lax.all_to_all(back.reshape(experts, CAP, -1), ('y', 'core', 'z'), split_...  10.5 us
    all_to_all x2, starting transfers between devices, to_experts(): lax.all_to_all(sent.reshape(YC, -1, sent.shape[1]), ('y', 'core'), split_...  8.73 us
    pallas_call x2, Pallas kernels, move(): pl.pallas_call(functools.partial(move_kernel, plan, len(arrays)), out_sha...  5.31 us
  transfers between devices with their start and end apart: 19, of which 7 were waited for; matrix products, arithmetic and copies ran while one was open for 1% of the time, Pallas kernels for 17%

profile of v10, /device:TPU:6, one launch (start us, length us, event | category | flops | bytes accessed | tf_op | source)
XLA Modules:
  0.0 198.5 jit_solution(8207218982158254207)
XLA Ops:
  0.7 2.6 %shard_map.121.refs_2_ = bf16[576,2048]{1,0:T(8,128)(2,1)} custom-call(bf16[192,2048]{1,0:T(8,128)(2,1)} %bitcast.35, bf16[192,2048]{1,0:T(8,128)(2,1)} %bitcast.36, bf16[192,2048]{1,0:T(8,128)(2,1)} %bitcast.37), custom_call_target="tpu_custom_call" | custom-call | flops 1 | bytes 1048576 | tf_op jit(solution)/shard_map/pallas_call | solution.py:85
  3.3 7.8 %collective-permute-start.3 = (bf16[576,2048]{1,0:T(8,128)(2,1)}, bf16[576,2048]{1,0:T(8,128)(2,1)S(1)}, u32[]{:S(2)}, u32[]{:S(2)}) collective-permute-start(bf16[576,2048]{1,0:T(8,128)(2,1)} %shard_map.121.refs_2_), channel_id=1, source_target_pairs={{0,128},{128,256},{256,384},{384,0},{1,129},{129,257},{257,385},{3... | collective-permute-start | bytes 7077896 | tf_op jit(solution)/shard_map/ppermute | solution.py:23
  11.0 1.9 collective-permute-start.4
  13.0 0.0 copy-start
  13.0 1.1 shard_map.119
  14.2 28.4 %all_gather.3.refs_0_ = bf16[64,4224]{1,0:T(8,128)(2,1)S(1)} all-gather(bf16[16,4224]{1,0:T(8,128)(2,1)S(1)} %shard_map.119), channel_id=1, replica_groups={{0,8,16,24},{2,10,18,26},{4,12,20,28},{6,14,22,30},{1,9,17,25},{3,11,19..., dimensions={0}, use_global_device_ids=true | all-gather | bytes 675840 | tf_op jit(solution)/shard_map/all_gather | solution.py:286
  42.5 4.8 %collective-permute-start = (bf16[64,4224]{1,0:T(8,128)(2,1)S(1)}, bf16[64,4224]{1,0:T(8,128)(2,1)S(1)}, u32[]{:S(2)}, u32[]{:S(2)}) collective-permute-start(bf16[64,4224]{1,0:T(8,128)(2,1)S(1)} %all_gather.3.refs_0_), channel_id=1, source_target_pairs={{0,30},{2,0},{4,2},{6,4},{8,6},{10,8},{12,10},{14,12},{16,14},{18,... | collective-permute-start | bytes 1622024 | tf_op jit(solution)/shard_map/ppermute | solution.py:23
  47.3 1.9 collective-permute-start.1
  49.2 7.0 %collective-permute-done.refs_1_ = bf16[64,4224]{1,0:T(8,128)(2,1)S(1)} collective-permute-done((bf16[64,4224]{1,0:T(8,128)(2,1)S(1)}, bf16[64,4224]{1,0:T(8,128)(2,1)S(1)}, u32[]{:S(2)}, u32[]{:S(2)}) %collective-permute-start) | collective-permute-done | bytes 540704 | tf_op jit(solution)/shard_map/ppermute | solution.py:23
  56.2 3.7 %collective-permute-start.2 = (bf16[64,4224]{1,0:T(8,128)(2,1)S(1)}, bf16[64,4224]{1,0:T(8,128)(2,1)}, u32[]{:S(2)}, u32[]{:S(2)}) collective-permute-start(bf16[64,4224]{1,0:T(8,128)(2,1)S(1)} %all_gather.3.refs_0_), channel_id=1, source_target_pairs={{4,0},{30,2},{8,4},{2,6},{12,8},{6,10},{16,12},{10,14},{20,16},{14... | collective-permute-start | bytes 1622024 | tf_op jit(solution)/shard_map/ppermute | solution.py:295
  60.0 0.1 fusion.2.pick_ref
  60.1 2.9 %shard_map.120 = bf16[128,4224]{1,0:T(8,128)(2,1)} custom-call(bf16[16,128]{1,0:T(8,128)(2,1)S(1)} %fusion.2.pick_ref, bf16[64,4224]{1,0:T(8,128)(2,1)} %copy-done.4, bf16[64,4224]{1,0:T(8,128)(2,1)} %copy-done.5), custom_call_target="tpu_custom_call" | custom-call | flops 1 | bytes 1048576 | tf_op jit(solution)/shard_map/pallas_call | solution.py:47
  62.9 4.5 %all-to-all-start = ((bf16[8,16,4224]{2,1,0:T(8,128)(2,1)}), bf16[8,16,4224]{2,1,0:T(8,128)(2,1)}, u32[]{:S(2)}, u32[]{:S(2)}) async-start(bf16[8,16,4224]{2,1,0:T(8,128)(2,1)} %bitcast.2), calls=%async_computation | async-start | bytes 2162688 | tf_op jit(solution)/shard_map/all_to_all | solution.py:151
  67.4 0.0 collective-permute-done.3.refs_0_.refs_4_
  67.5 1.4 copy-done.3
  68.9 2.7 %shard_map.122 = (bf16[288,2048]{1,0:T(8,128)(2,1)}, bf16[288,2048]{1,0:T(8,128)(2,1)}) custom-call(bf16[576,2048]{1,0:T(8,128)(2,1)} %copy-done.3, bf16[576,2048]{1,0:T(8,128)(2,1)} %collective-permute-done.4.refs_1_.refs_3_), custom_call_target="tpu_custom_call" | custom-call | flops 1 | bytes 1048576 | tf_op jit(solution)/shard_map/pallas_call | solution.py:85
  71.6 0.0 collective-permute-done.1.refs_0_
  71.6 3.6 %collective-permute-start.5 = (bf16[288,2048]{1,0:T(8,128)(2,1)}, bf16[288,2048]{1,0:T(8,128)(2,1)}, u32[]{:S(2)}, u32[]{:S(2)}) collective-permute-start(bf16[288,2048]{1,0:T(8,128)(2,1)} %get-tuple-element.37), channel_id=1, source_target_pairs={{0,128},{128,256},{256,384},{384,0},{1,129},{129,257},{257,385},{3... | collective-permute-start | bytes 3538952 | tf_op jit(solution)/shard_map/ppermute | solution.py:23
  75.2 2.3 %collective-permute-start.6 = (bf16[288,2048]{1,0:T(8,128)(2,1)}, bf16[288,2048]{1,0:T(8,128)(2,1)}, u32[]{:S(2)}, u32[]{:S(2)}) collective-permute-start(bf16[288,2048]{1,0:T(8,128)(2,1)} %get-tuple-element.38), channel_id=1, source_target_pairs={{0,384},{128,0},{256,128},{384,256},{1,385},{129,1},{257,129},{385... | collective-permute-start | bytes 3538952 | tf_op jit(solution)/shard_map/ppermute | solution.py:23
  77.5 2.9 %shard_map.123 = bf16[128,4224]{1,0:T(8,128)(2,1)} custom-call(bf16[16,128]{1,0:T(8,128)(2,1)S(1)} %fusion.2.pick_ref, bf16[64,4224]{1,0:T(8,128)(2,1)} %collective-permute-done.1.refs_0_, bf16[64,4224]{1,0:T(8,128)(2,1)} %collective-permute-done.2.refs_1_), custom_call_target="tpu_custom_call" | custom-call | flops 999999995904 | bytes 1048576 | tf_op jit(solution)/shard_map/pallas_call | solution.py:47
  80.4 3.5 %all-to-all-done = bf16[8,16,4224]{2,1,0:T(8,128)(2,1)} async-done(((bf16[8,16,4224]{2,1,0:T(8,128)(2,1)}), bf16[8,16,4224]{2,1,0:T(8,128)(2,1)}, u32[]{:S(2)}, u32[]{:S(2)}) %all-to-all-start) | async-done | bytes 1081376 | tf_op jit(solution)/shard_map/all_to_all | solution.py:151
  83.9 4.2 %all-to-all-start.1 = ((bf16[8,16,4224]{2,1,0:T(8,128)(2,1)}), bf16[8,16,4224]{2,1,0:T(8,128)(2,1)}, u32[]{:S(2)}, u32[]{:S(2)}) async-start(bf16[8,16,4224]{2,1,0:T(8,128)(2,1)} %bitcast.7), calls=%async_computation.1 | async-start | bytes 2162688 | tf_op jit(solution)/shard_map/all_to_all | solution.py:151
  88.2 0.1 fusion.perm_ref
  88.3 3.6 %collective-permute-start.8 = (bf16[128,4224]{1,0:T(8,128)(2,1)}, bf16[128,4224]{1,0:T(8,128)(2,1)}, u32[]{:S(2)}, u32[]{:S(2)}) collective-permute-start(bf16[128,4224]{1,0:T(8,128)(2,1)} %bitcast.3.refs_0_.refs_3_.refs_4_.refs_5_), channel_id=1, source_target_pairs={{0,128},{128,256},{256,384},{384,0},{1,129},{129,257},{257,385},{3... | collective-permute-start | bytes 3244040 | tf_op jit(solution)/shard_map/ppermute | solution.py:23
  91.9 2.3 %collective-permute-start.9 = (bf16[128,4224]{1,0:T(8,128)(2,1)}, bf16[128,4224]{1,0:T(8,128)(2,1)}, u32[]{:S(2)}, u32[]{:S(2)}) collective-permute-start(bf16[128,4224]{1,0:T(8,128)(2,1)} %bitcast.3.refs_0_.refs_3_.refs_4_.refs_5_), channel_id=1, source_target_pairs={{0,384},{128,0},{256,128},{384,256},{1,385},{129,1},{257,129},{385... | collective-permute-start | bytes 3244040 | tf_op jit(solution)/shard_map/ppermute | solution.py:23
  94.1 10.3 %all-to-all-done.1 = bf16[8,16,4224]{2,1,0:T(8,128)(2,1)} async-done(((bf16[8,16,4224]{2,1,0:T(8,128)(2,1)}), bf16[8,16,4224]{2,1,0:T(8,128)(2,1)}, u32[]{:S(2)}, u32[]{:S(2)}) %all-to-all-start.1) | async-done | bytes 1081376 | tf_op jit(solution)/shard_map/all_to_all | solution.py:151
  104.4 3.6 %collective-permute-start.10 = (bf16[128,4224]{1,0:T(8,128)(2,1)}, bf16[128,4224]{1,0:T(8,128)(2,1)}, u32[]{:S(2)}, u32[]{:S(2)}) collective-permute-start(bf16[128,4224]{1,0:T(8,128)(2,1)} %bitcast.8.refs_1_.refs_12_.refs_13_.refs_14_), channel_id=1, source_target_pairs={{0,128},{128,256},{256,384},{384,0},{1,129},{129,257},{257,385},{3... | collective-permute-start | bytes 3244040 | tf_op jit(solution)/shard_map/ppermute | solution.py:23
  108.0 0.0 collective-permute-done.5.refs_5_
  108.0 2.3 %collective-permute-start.11 = (bf16[128,4224]{1,0:T(8,128)(2,1)}, bf16[128,4224]{1,0:T(8,128)(2,1)}, u32[]{:S(2)}, u32[]{:S(2)}) collective-permute-start(bf16[128,4224]{1,0:T(8,128)(2,1)} %bitcast.8.refs_1_.refs_12_.refs_13_.refs_14_), channel_id=1, source_target_pairs={{0,384},{128,0},{256,128},{384,256},{1,385},{129,1},{257,129},{385... | collective-permute-start | bytes 3244040 | tf_op jit(solution)/shard_map/ppermute | solution.py:23
  110.3 11.3 %shard_map.124 = (bf16[256,2176]{1,0:T(8,128)(2,1)S(1)}, bf16[576,256]{1,0:T(8,128)(2,1)}, bf16[576,256]{1,0:T(8,128)(2,1)}, bf16[576,256]{1,0:T(8,128)(2,1)}, bf16[576,256]{1,0:T(8,128)(2,1)}) custom-call(bf16[16,128]{1,0:T(8,128)(2,1)S(1)} %iota.42.own_ref, bf16[256,256]{1,0:T(8,128)(2,1)S(1)} %fusion.perm_ref, ...), custom_call_target="tpu_custom_call" | custom-call | flops 999999995904 | bytes 1048576 | tf_op jit(solution)/shard_map/pallas_call | solution.py:47
  121.6 1.3 reshape.267
  122.8 10.5 %all-to-all-start.2 = ((bf16[128,2,2176]{2,1,0:T(2,128)(2,1)}), bf16[128,2,2176]{2,1,0:T(2,128)(2,1)}, u32[]{:S(2)}, u32[]{:S(2)}) async-start(bf16[128,2,2176]{2,1,0:T(2,128)(2,1)} %reshape.267), calls=%async_computation.2 | async-start | bytes 2228224 | tf_op jit(solution)/shard_map/all_to_all | solution.py:327
  133.4 3.6 %collective-permute-start.7 = (bf16[576,256]{1,0:T(8,128)(2,1)}, bf16[576,256]{1,0:T(8,128)(2,1)}, u32[]{:S(2)}, u32[]{:S(2)}) collective-permute-start(bf16[576,256]{1,0:T(8,128)(2,1)} %get-tuple-element.40), channel_id=1, source_target_pairs={{0,256},{128,384},{256,0},{384,128},{1,257},{129,385},{257,1},{385... | collective-permute-start | bytes 884744 | tf_op jit(solution)/shard_map/ppermute | solution.py:23
  137.0 0.0 collective-permute-done.8.refs_0_
  137.0 3.6 %collective-permute-start.14 = (bf16[576,256]{1,0:T(8,128)(2,1)}, bf16[576,256]{1,0:T(8,128)(2,1)}, u32[]{:S(2)}, u32[]{:S(2)}) collective-permute-start(bf16[576,256]{1,0:T(8,128)(2,1)} %get-tuple-element.44), channel_id=1, source_target_pairs={{0,128},{128,256},{256,384},{384,0},{1,129},{129,257},{257,385},{3... | collective-permute-start | bytes 884744 | tf_op jit(solution)/shard_map/ppermute | solution.py:23
  140.6 0.0 collective-permute-done.9.refs_1_
  140.6 2.6 %collective-permute-start.15 = (bf16[576,256]{1,0:T(8,128)(2,1)}, bf16[576,256]{1,0:T(8,128)(2,1)}, u32[]{:S(2)}, u32[]{:S(2)}) collective-permute-start(bf16[576,256]{1,0:T(8,128)(2,1)} %get-tuple-element.45), channel_id=1, source_target_pairs={{0,384},{128,0},{256,128},{384,256},{1,385},{129,1},{257,129},{385... | collective-permute-start | bytes 884744 | tf_op jit(solution)/shard_map/ppermute | solution.py:23
  143.2 10.9 %collective-permute-done.10.refs_2_ = bf16[128,4224]{1,0:T(8,128)(2,1)} collective-permute-done((bf16[128,4224]{1,0:T(8,128)(2,1)}, bf16[128,4224]{1,0:T(8,128)(2,1)}, u32[]{:S(2)}, u32[]{:S(2)}) %collective-permute-start.10) | collective-permute-done | bytes 1081376 | tf_op jit(solution)/shard_map/ppermute | solution.py:23
  154.1 6.0 %collective-permute-done.11.refs_3_ = bf16[128,4224]{1,0:T(8,128)(2,1)} collective-permute-done((bf16[128,4224]{1,0:T(8,128)(2,1)}, bf16[128,4224]{1,0:T(8,128)(2,1)}, u32[]{:S(2)}, u32[]{:S(2)}) %collective-permute-start.11) | collective-permute-done | bytes 1081376 | tf_op jit(solution)/shard_map/ppermute | solution.py:23
  160.1 2.0 %collective-permute-start.12 = (bf16[128,4224]{1,0:T(8,128)(2,1)}, bf16[128,4224]{1,0:T(8,128)(2,1)}, u32[]{:S(2)}, u32[]{:S(2)}) collective-permute-start(bf16[128,4224]{1,0:T(8,128)(2,1)} %get-tuple-element.41.refs_6_.refs_7_.refs_8_), channel_id=1, source_target_pairs={{0,128},{128,256},{256,384},{384,0},{1,129},{129,257},{257,385},{3... | collective-permute-start | bytes 3244040 | tf_op jit(solution)/shard_map/ppermute | solution.py:23
  162.1 3.9 %collective-permute-start.13 = (bf16[128,4224]{1,0:T(8,128)(2,1)}, bf16[128,4224]{1,0:T(8,128)(2,1)}, u32[]{:S(2)}, u32[]{:S(2)}) collective-permute-start(bf16[128,4224]{1,0:T(8,128)(2,1)} %get-tuple-element.42.refs_18_.refs_19_.refs_20_), channel_id=1, source_target_pairs={{0,384},{128,0},{256,128},{384,256},{1,385},{129,1},{257,129},{385... | collective-permute-start | bytes 3244040 | tf_op jit(solution)/shard_map/ppermute | solution.py:23
  166.1 0.0 collective-permute-done.14.refs_1_
  166.1 7.3 %shard_map.126.refs_7_ = f32[576,2048]{1,0:T(8,128)} custom-call(f32[1,128]{1,0:T(1,128)S(1)} %compare_convert_fusion.own_ref, bf16[576,256]{1,0:T(8,128)(2,1)S(1)} %copy-done.2, bf16[576,256]{1,0:T(8,128)(2,1)} %collective-permute-done.14.refs_1_, bf16[576,256]{1,0:T(8,128)(2,1)} %collective-permute-done.15.refs_2_, ...), custom_call_target="tpu_custom_call" | custom-call | flops 999999995904 | bytes 1048576 | tf_op jit(solution)/shard_map/pallas_call | solution.py:47
  173.4 13.4 %collective-permute-done.12.refs_1_.refs_2_.refs_3_ = bf16[128,4224]{1,0:T(8,128)(2,1)} collective-permute-done((bf16[128,4224]{1,0:T(8,128)(2,1)}, bf16[128,4224]{1,0:T(8,128)(2,1)}, u32[]{:S(2)}, u32[]{:S(2)}) %collective-permute-start.12) | collective-permute-done | bytes 1081376 | tf_op jit(solution)/shard_map/ppermute | solution.py:23
  186.9 3.1 %collective-permute-done.13.refs_4_.refs_5_.refs_6_ = bf16[128,4224]{1,0:T(8,128)(2,1)} collective-permute-done((bf16[128,4224]{1,0:T(8,128)(2,1)}, bf16[128,4224]{1,0:T(8,128)(2,1)}, u32[]{:S(2)}, u32[]{:S(2)}) %collective-permute-start.13) | collective-permute-done | bytes 1081376 | tf_op jit(solution)/shard_map/ppermute | solution.py:23
  190.0 5.6 %shard_map.127 = (bf16[192,2048]{1,0:T(8,128)(2,1)}, bf16[192,2048]{1,0:T(8,128)(2,1)}, bf16[192,2048]{1,0:T(8,128)(2,1)}) custom-call(f32[1,128]{1,0:T(1,128)S(1)} %compare_convert_fusion.own_ref, bf16[576,256]{1,0:T(8,128)(2,1)} %collective-permute-done.7.refs_0_, bf16[128,4224]{1,0:T(8,128)(2,1)} %collective-permute-done.12.refs_1_.refs_2_.refs_3_, ...), custom_call_target="tpu_custom_call" | custom-call | flops 1 | bytes 1048576 | tf_op jit(solution)/shard_map/pallas_call | solution.py:47
  195.7 1.5 reshape.268.home_ref
  197.2 1.3 shard_map.128
  (29 shorter events, 0.1 us)
Async XLA Ops:
  0.6 12.3 %copy-start.7 = (bf16[16,8]{0,1:T(8,128)(2,1)S(1)}, bf16[16,8]{0,1:T(8,128)(2,1)}, u32[]{:S(2)}) copy-start(bf16[16,8]{0,1:T(8,128)(2,1)} %param.11) | copy-start | bytes 772
  0.6 12.4 %copy-start.6 = (s32[16,8]{0,1:T(8,128)S(1)}, s32[16,8]{0,1:T(8,128)}, u32[]{:S(2)}) copy-start(s32[16,8]{0,1:T(8,128)} %param.12) | copy-start | bytes 1540
  3.3 64.2 %collective-permute-start.3 = (bf16[576,2048]{1,0:T(8,128)(2,1)}, bf16[576,2048]{1,0:T(8,128)(2,1)S(1)}, u32[]{:S(2)}, u32[]{:S(2)}) collective-permute-start(bf16[576,2048]{1,0:T(8,128)(2,1)} %shard_map.121.refs_2_), channel_id=1, source_target_pairs={{0,128},{128,256},{256,384},{384,0},{1,129},{129,257},{257,385},{3... | collective-permute-start | bytes 7077896 | tf_op jit(solution)/shard_map/ppermute | solution.py:23
  11.0 56.4 %collective-permute-start.4 = (bf16[576,2048]{1,0:T(8,128)(2,1)}, bf16[576,2048]{1,0:T(8,128)(2,1)}, u32[]{:S(2)}, u32[]{:S(2)}) collective-permute-start(bf16[576,2048]{1,0:T(8,128)(2,1)} %shard_map.121.refs_2_), channel_id=1, source_target_pairs={{0,384},{128,0},{256,128},{384,256},{1,385},{129,1},{257,129},{385... | collective-permute-start | bytes 7077896 | tf_op jit(solution)/shard_map/ppermute | solution.py:23
  13.0 29.5 %copy-start = (s32[8,16]{1,0:T(8,128)}, s32[8,16]{1,0:T(8,128)S(1)}, u32[]{:S(2)}) copy-start(s32[8,16]{1,0:T(8,128)S(1)} %fusion.6.rank_ref) | copy-start | bytes 1540
  42.5 17.5 %copy-start.4 = (bf16[64,4224]{1,0:T(8,128)(2,1)}, bf16[64,4224]{1,0:T(8,128)(2,1)S(1)}, u32[]{:S(2)}) copy-start(bf16[64,4224]{1,0:T(8,128)(2,1)S(1)} %all_gather.3.refs_0_) | copy-start | bytes 1622020
  42.5 13.7 %collective-permute-start = (bf16[64,4224]{1,0:T(8,128)(2,1)S(1)}, bf16[64,4224]{1,0:T(8,128)(2,1)S(1)}, u32[]{:S(2)}, u32[]{:S(2)}) collective-permute-start(bf16[64,4224]{1,0:T(8,128)(2,1)S(1)} %all_gather.3.refs_0_), channel_id=1, source_target_pairs={{0,30},{2,0},{4,2},{6,4},{8,6},{10,8},{12,10},{14,12},{16,14},{18,... | collective-permute-start | bytes 1622024 | tf_op jit(solution)/shard_map/ppermute | solution.py:23
  47.3 24.3 %collective-permute-start.1 = (bf16[64,4224]{1,0:T(8,128)(2,1)S(1)}, bf16[64,4224]{1,0:T(8,128)(2,1)}, u32[]{:S(2)}, u32[]{:S(2)}) collective-permute-start(bf16[64,4224]{1,0:T(8,128)(2,1)S(1)} %all_gather.3.refs_0_), channel_id=1, source_target_pairs={{0,2},{2,4},{4,6},{6,8},{8,10},{10,12},{12,14},{14,16},{16,18},{18... | collective-permute-start | bytes 1622024 | tf_op jit(solution)/shard_map/ppermute | solution.py:23
  56.2 3.8 %copy-start.5 = (bf16[64,4224]{1,0:T(8,128)(2,1)}, bf16[64,4224]{1,0:T(8,128)(2,1)S(1)}, u32[]{:S(2)}) copy-start(bf16[64,4224]{1,0:T(8,128)(2,1)S(1)} %collective-permute-done.refs_1_) | copy-start | bytes 1622020
  56.2 15.4 %collective-permute-start.2 = (bf16[64,4224]{1,0:T(8,128)(2,1)S(1)}, bf16[64,4224]{1,0:T(8,128)(2,1)}, u32[]{:S(2)}, u32[]{:S(2)}) collective-permute-start(bf16[64,4224]{1,0:T(8,128)(2,1)S(1)} %all_gather.3.refs_0_), channel_id=1, source_target_pairs={{4,0},{30,2},{8,4},{2,6},{12,8},{6,10},{16,12},{10,14},{20,16},{14... | collective-permute-start | bytes 1622024 | tf_op jit(solution)/shard_map/ppermute | solution.py:295
  62.9 20.9 %all-to-all-start = ((bf16[8,16,4224]{2,1,0:T(8,128)(2,1)}), bf16[8,16,4224]{2,1,0:T(8,128)(2,1)}, u32[]{:S(2)}, u32[]{:S(2)}) async-start(bf16[8,16,4224]{2,1,0:T(8,128)(2,1)} %bitcast.2), calls=%async_computation | async-start | bytes 2162688 | tf_op jit(solution)/shard_map/all_to_all | solution.py:151
  67.4 1.5 copy-start.3
  71.6 36.4 %collective-permute-start.5 = (bf16[288,2048]{1,0:T(8,128)(2,1)}, bf16[288,2048]{1,0:T(8,128)(2,1)}, u32[]{:S(2)}, u32[]{:S(2)}) collective-permute-start(bf16[288,2048]{1,0:T(8,128)(2,1)} %get-tuple-element.37), channel_id=1, source_target_pairs={{0,128},{128,256},{256,384},{384,0},{1,129},{129,257},{257,385},{3... | collective-permute-start | bytes 3538952 | tf_op jit(solution)/shard_map/ppermute | solution.py:23
  75.2 35.1 %collective-permute-start.6 = (bf16[288,2048]{1,0:T(8,128)(2,1)}, bf16[288,2048]{1,0:T(8,128)(2,1)}, u32[]{:S(2)}, u32[]{:S(2)}) collective-permute-start(bf16[288,2048]{1,0:T(8,128)(2,1)} %get-tuple-element.38), channel_id=1, source_target_pairs={{0,384},{128,0},{256,128},{384,256},{1,385},{129,1},{257,129},{385... | collective-permute-start | bytes 3538952 | tf_op jit(solution)/shard_map/ppermute | solution.py:23
  83.9 20.6 %all-to-all-start.1 = ((bf16[8,16,4224]{2,1,0:T(8,128)(2,1)}), bf16[8,16,4224]{2,1,0:T(8,128)(2,1)}, u32[]{:S(2)}, u32[]{:S(2)}) async-start(bf16[8,16,4224]{2,1,0:T(8,128)(2,1)} %bitcast.7), calls=%async_computation.1 | async-start | bytes 2162688 | tf_op jit(solution)/shard_map/all_to_all | solution.py:151
  88.3 48.7 %collective-permute-start.8 = (bf16[128,4224]{1,0:T(8,128)(2,1)}, bf16[128,4224]{1,0:T(8,128)(2,1)}, u32[]{:S(2)}, u32[]{:S(2)}) collective-permute-start(bf16[128,4224]{1,0:T(8,128)(2,1)} %bitcast.3.refs_0_.refs_3_.refs_4_.refs_5_), channel_id=1, source_target_pairs={{0,128},{128,256},{256,384},{384,0},{1,129},{129,257},{257,385},{3... | collective-permute-start | bytes 3244040 | tf_op jit(solution)/shard_map/ppermute | solution.py:23
  91.9 48.7 %collective-permute-start.9 = (bf16[128,4224]{1,0:T(8,128)(2,1)}, bf16[128,4224]{1,0:T(8,128)(2,1)}, u32[]{:S(2)}, u32[]{:S(2)}) collective-permute-start(bf16[128,4224]{1,0:T(8,128)(2,1)} %bitcast.3.refs_0_.refs_3_.refs_4_.refs_5_), channel_id=1, source_target_pairs={{0,384},{128,0},{256,128},{384,256},{1,385},{129,1},{257,129},{385... | collective-permute-start | bytes 3244040 | tf_op jit(solution)/shard_map/ppermute | solution.py:23
  104.4 49.7 %collective-permute-start.10 = (bf16[128,4224]{1,0:T(8,128)(2,1)}, bf16[128,4224]{1,0:T(8,128)(2,1)}, u32[]{:S(2)}, u32[]{:S(2)}) collective-permute-start(bf16[128,4224]{1,0:T(8,128)(2,1)} %bitcast.8.refs_1_.refs_12_.refs_13_.refs_14_), channel_id=1, source_target_pairs={{0,128},{128,256},{256,384},{384,0},{1,129},{129,257},{257,385},{3... | collective-permute-start | bytes 3244040 | tf_op jit(solution)/shard_map/ppermute | solution.py:23
  108.0 52.1 %collective-permute-start.11 = (bf16[128,4224]{1,0:T(8,128)(2,1)}, bf16[128,4224]{1,0:T(8,128)(2,1)}, u32[]{:S(2)}, u32[]{:S(2)}) collective-permute-start(bf16[128,4224]{1,0:T(8,128)(2,1)} %bitcast.8.refs_1_.refs_12_.refs_13_.refs_14_), channel_id=1, source_target_pairs={{0,384},{128,0},{256,128},{384,256},{1,385},{129,1},{257,129},{385... | collective-permute-start | bytes 3244040 | tf_op jit(solution)/shard_map/ppermute | solution.py:23
  122.8 72.8 %all-to-all-start.2 = ((bf16[128,2,2176]{2,1,0:T(2,128)(2,1)}), bf16[128,2,2176]{2,1,0:T(2,128)(2,1)}, u32[]{:S(2)}, u32[]{:S(2)}) async-start(bf16[128,2,2176]{2,1,0:T(2,128)(2,1)} %reshape.267), calls=%async_computation.2 | async-start | bytes 2228224 | tf_op jit(solution)/shard_map/all_to_all | solution.py:327
  133.4 40.1 %collective-permute-start.7 = (bf16[576,256]{1,0:T(8,128)(2,1)}, bf16[576,256]{1,0:T(8,128)(2,1)}, u32[]{:S(2)}, u32[]{:S(2)}) collective-permute-start(bf16[576,256]{1,0:T(8,128)(2,1)} %get-tuple-element.40), channel_id=1, source_target_pairs={{0,256},{128,384},{256,0},{384,128},{1,257},{129,385},{257,1},{385... | collective-permute-start | bytes 884744 | tf_op jit(solution)/shard_map/ppermute | solution.py:23
  137.0 29.1 %collective-permute-start.14 = (bf16[576,256]{1,0:T(8,128)(2,1)}, bf16[576,256]{1,0:T(8,128)(2,1)}, u32[]{:S(2)}, u32[]{:S(2)}) collective-permute-start(bf16[576,256]{1,0:T(8,128)(2,1)} %get-tuple-element.44), channel_id=1, source_target_pairs={{0,128},{128,256},{256,384},{384,0},{1,129},{129,257},{257,385},{3... | collective-permute-start | bytes 884744 | tf_op jit(solution)/shard_map/ppermute | solution.py:23
  140.6 25.5 %collective-permute-start.15 = (bf16[576,256]{1,0:T(8,128)(2,1)}, bf16[576,256]{1,0:T(8,128)(2,1)}, u32[]{:S(2)}, u32[]{:S(2)}) collective-permute-start(bf16[576,256]{1,0:T(8,128)(2,1)} %get-tuple-element.45), channel_id=1, source_target_pairs={{0,384},{128,0},{256,128},{384,256},{1,385},{129,1},{257,129},{385... | collective-permute-start | bytes 884744 | tf_op jit(solution)/shard_map/ppermute | solution.py:23
  160.1 6.0 %copy-start.2 = (bf16[576,256]{1,0:T(8,128)(2,1)S(1)}, bf16[576,256]{1,0:T(8,128)(2,1)}, u32[]{:S(2)}) copy-start(bf16[576,256]{1,0:T(8,128)(2,1)} %get-tuple-element.43.refs_0_) | copy-start | bytes 884740
  160.1 26.8 %collective-permute-start.12 = (bf16[128,4224]{1,0:T(8,128)(2,1)}, bf16[128,4224]{1,0:T(8,128)(2,1)}, u32[]{:S(2)}, u32[]{:S(2)}) collective-permute-start(bf16[128,4224]{1,0:T(8,128)(2,1)} %get-tuple-element.41.refs_6_.refs_7_.refs_8_), channel_id=1, source_target_pairs={{0,128},{128,256},{256,384},{384,0},{1,129},{129,257},{257,385},{3... | collective-permute-start | bytes 3244040 | tf_op jit(solution)/shard_map/ppermute | solution.py:23
  162.1 27.9 %collective-permute-start.13 = (bf16[128,4224]{1,0:T(8,128)(2,1)}, bf16[128,4224]{1,0:T(8,128)(2,1)}, u32[]{:S(2)}, u32[]{:S(2)}) collective-permute-start(bf16[128,4224]{1,0:T(8,128)(2,1)} %get-tuple-element.42.refs_18_.refs_19_.refs_20_), channel_id=1, source_target_pairs={{0,384},{128,0},{256,128},{384,256},{1,385},{129,1},{257,129},{385... | collective-permute-start | bytes 3244040 | tf_op jit(solution)/shard_map/ppermute | solution.py:23
  195.7 1.5 copy-start.1

commit v11 on v10

--- a/solution.py
+++ b/solution.py
@@ -61,35 +61,27 @@
 
 
 def move_kernel(plan, count, *refs):
-    sources, targets, buf, sems = refs[:count], refs[count:-2], refs[-2], refs[-1]
-    starts = [sum(p[2] for p in plan[:k]) for k in range(len(plan))]
-    loads = [
-        pltpu.make_async_copy(sources[i].at[pl.ds(a, n)], buf.at[pl.ds(s, n)], sems.at[k])
-        for k, (s, (i, a, n, o, b)) in enumerate(zip(starts, plan))
+    sources, targets, sems = refs[:count], refs[count:-1], refs[-1]
+    copies = [
+        pltpu.make_async_copy(sources[i].at[pl.ds(a, n)], targets[o].at[pl.ds(b, n)], sems.at[k])
+        for k, (i, a, n, o, b) in enumerate(plan)
     ]
-    stores = [
-        pltpu.make_async_copy(buf.at[pl.ds(s, n)], targets[o].at[pl.ds(b, n)], sems.at[len(plan) + k])
-        for k, (s, (i, a, n, o, b)) in enumerate(zip(starts, plan))
-    ]
-    for c in loads:
+    for c in copies:
         c.start()
-    for load, store in zip(loads, stores):
-        load.wait()
-        store.start()
-    for c in stores:
+    for c in copies:
         c.wait()
 
 
-def move(arrays, plan, out_rows, cost=1):
+def move(arrays, plan, out_rows):
     width = arrays[0].shape[1]
     return pl.pallas_call(
         functools.partial(move_kernel, plan, len(arrays)),
-        out_shape=[pltpu.HBM((n, width), BF16) for n in out_rows],
+        out_shape=[sds((n, width), BF16) for n in out_rows],
         in_specs=[pl.BlockSpec(memory_space=pl.ANY)] * len(arrays),
-        out_specs=[pl.BlockSpec(memory_space=pl.ANY)] * len(out_rows),
-        scratch_shapes=[pltpu.VMEM((sum(p[2] for p in plan), width), BF16), pltpu.SemaphoreType.DMA((2 * len(plan),))],
+        out_specs=[pl.BlockSpec(memory_space=pltpu.VMEM)] * len(out_rows),
+        scratch_shapes=[pltpu.SemaphoreType.DMA((len(plan),))],
         compiler_params=pltpu.CompilerParams(vmem_limit_bytes=6 * MIB),
-        cost_estimate=pl.CostEstimate(flops=cost, bytes_accessed=MIB, transcendentals=0),
+        cost_estimate=pl.CostEstimate(flops=1, bytes_accessed=MIB, transcendentals=0),
     )(*in_hbm(arrays))
 
 
@@ -313,7 +305,7 @@
     place = jnp.where(kind < 2, kind * STRIDE, jnp.where(kind == 3, Z // 2, Z // 2 + STRIDE)) + q_z // STRIDE
     at = place // (Z // 2) * (count // 2) + q // (Z * CAP) * Z + place % (Z // 2) * CAP + q % CAP
     perm = (at == iota((count, count), 1)).astype(BF16)
-    weights = in_hbm((mine, from_next, from_prev, *far))
+    weights = (mine, *in_hbm((from_next, from_prev, *far)))
     small = (own.astype(BF16), perm, *in_hbm(rows))
     back, a_own, a_next, a_prev, a_far = call(
         functools.partial(forward_kernel, len(rows)),

time: 200 us -> 198 us (0.990)
  waiting for transfers between devices: 54.3 us -> 52.3 us
    ppermute x15, waiting for transfers between devices: 40.5 us -> 38.3 us  [shift(): return lax.ppermute(a, axis, [(i, (i + k) % size) for i in range(size)])]
where the time goes in v11:
time: 198 us; the launch traced here: 196 us
  starting transfers between devices  73.8 us (37%)
  waiting for transfers between devices  52.3 us (26%)
  Pallas kernels  36.2 us (18%)
  blocking collectives  28.3 us (14%)
  local copies, waits for them, and re-layouts  3.77 us (2%)
    ppermute x15, starting transfers between devices, shift(): return lax.ppermute(a, axis, [(i, (i + k) % size) for i in range(size)])  50.4 us
    ppermute x15, waiting for transfers between devices, shift(): return lax.ppermute(a, axis, [(i, (i + k) % size) for i in range(size)])  38.3 us
    pallas_call x7, Pallas kernels, call(): pl.pallas_call(kernel, grid=grid, out_shape=out_shape, in_specs=in_specs...  31.4 us
    all_gather x1, blocking collectives, body(): lax.all_gather(payload, 'z', axis=0, tiled=True, axis_index_groups=groups)  28.3 us
    all_to_all x2, waiting for transfers between devices, to_experts(): lax.all_to_all(sent.reshape(YC, -1, sent.shape[1]), ('y', 'core'), split_...  14.1 us
    all_to_all x1, starting transfers between devices, body(): lax.all_to_all(back.reshape(experts, CAP, -1), ('y', 'core', 'z'), split_...  10.8 us
    all_to_all x2, starting transfers between devices, to_experts(): lax.all_to_all(sent.reshape(YC, -1, sent.shape[1]), ('y', 'core'), split_...  8.69 us
    pallas_call x2, Pallas kernels, move(): pl.pallas_call(functools.partial(move_kernel, plan, len(arrays)), out_sha...  4.84 us
  transfers between devices with their start and end apart: 19, of which 7 were waited for; matrix products, arithmetic and copies ran while one was open for 1% of the time, Pallas kernels for 17%

profile of v11, /device:TPU:6, one launch (start us, length us, event | category | flops | bytes accessed | tf_op | source)
XLA Modules:
  0.0 196.4 jit_solution(14788279679855067983)
XLA Ops:
  0.7 1.6 shard_map.121.refs_2_
  2.3 7.8 %collective-permute-start.3 = (bf16[576,2048]{1,0:T(8,128)(2,1)S(1)}, bf16[576,2048]{1,0:T(8,128)(2,1)}, u32[]{:S(2)}, u32[]{:S(2)}) collective-permute-start(bf16[576,2048]{1,0:T(8,128)(2,1)S(1)} %shard_map.121.refs_2_), channel_id=1, source_target_pairs={{0,128},{128,256},{256,384},{384,0},{1,129},{129,257},{257,385},{3... | collective-permute-start | bytes 7077896 | tf_op jit(solution)/shard_map/ppermute | solution.py:23
  10.1 1.9 collective-permute-start.4
  12.1 0.0 copy-start.1
  12.1 1.1 shard_map.119
  13.2 28.3 %all_gather.3.refs_0_ = bf16[64,4224]{1,0:T(8,128)(2,1)S(1)} all-gather(bf16[16,4224]{1,0:T(8,128)(2,1)S(1)} %shard_map.119), channel_id=1, replica_groups={{0,8,16,24},{2,10,18,26},{4,12,20,28},{6,14,22,30},{1,9,17,25},{3,11,19..., dimensions={0}, use_global_device_ids=true | all-gather | bytes 675840 | tf_op jit(solution)/shard_map/all_gather | solution.py:278
  41.5 5.5 %collective-permute-start = (bf16[64,4224]{1,0:T(8,128)(2,1)S(1)}, bf16[64,4224]{1,0:T(8,128)(2,1)S(1)}, u32[]{:S(2)}, u32[]{:S(2)}) collective-permute-start(bf16[64,4224]{1,0:T(8,128)(2,1)S(1)} %all_gather.3.refs_0_), channel_id=1, source_target_pairs={{0,30},{2,0},{4,2},{6,4},{8,6},{10,8},{12,10},{14,12},{16,14},{18,... | collective-permute-start | bytes 1622024 | tf_op jit(solution)/shard_map/ppermute | solution.py:23
  47.0 1.9 collective-permute-start.1
  48.9 6.2 %collective-permute-done.refs_1_ = bf16[64,4224]{1,0:T(8,128)(2,1)S(1)} collective-permute-done((bf16[64,4224]{1,0:T(8,128)(2,1)S(1)}, bf16[64,4224]{1,0:T(8,128)(2,1)S(1)}, u32[]{:S(2)}, u32[]{:S(2)}) %collective-permute-start) | collective-permute-done | bytes 540704 | tf_op jit(solution)/shard_map/ppermute | solution.py:23
  55.1 3.9 %collective-permute-start.2 = (bf16[64,4224]{1,0:T(8,128)(2,1)S(1)}, bf16[64,4224]{1,0:T(8,128)(2,1)}, u32[]{:S(2)}, u32[]{:S(2)}) collective-permute-start(bf16[64,4224]{1,0:T(8,128)(2,1)S(1)} %all_gather.3.refs_0_), channel_id=1, source_target_pairs={{4,0},{30,2},{8,4},{2,6},{12,8},{6,10},{16,12},{10,14},{20,16},{14... | collective-permute-start | bytes 1622024 | tf_op jit(solution)/shard_map/ppermute | solution.py:287
  59.0 0.1 fusion.2.pick_ref
  59.1 2.9 %shard_map.120 = bf16[128,4224]{1,0:T(8,128)(2,1)} custom-call(bf16[16,128]{1,0:T(8,128)(2,1)S(1)} %fusion.2.pick_ref, bf16[64,4224]{1,0:T(8,128)(2,1)} %copy-done.4, bf16[64,4224]{1,0:T(8,128)(2,1)} %copy-done.5), custom_call_target="tpu_custom_call" | custom-call | flops 1 | bytes 1048576 | tf_op jit(solution)/shard_map/pallas_call | solution.py:47
  62.0 4.5 %all-to-all-start = ((bf16[8,16,4224]{2,1,0:T(8,128)(2,1)}), bf16[8,16,4224]{2,1,0:T(8,128)(2,1)}, u32[]{:S(2)}, u32[]{:S(2)}) async-start(bf16[8,16,4224]{2,1,0:T(8,128)(2,1)} %bitcast.2), calls=%async_computation | async-start | bytes 2162688 | tf_op jit(solution)/shard_map/all_to_all | solution.py:143
  66.5 0.0 collective-permute-done.3.refs_0_.refs_4_
  66.5 0.0 collective-permute-done.4.refs_1_.refs_3_
  66.5 3.2 %shard_map.122 = (bf16[288,2048]{1,0:T(8,128)(2,1)}, bf16[288,2048]{1,0:T(8,128)(2,1)}) custom-call(bf16[576,2048]{1,0:T(8,128)(2,1)} %collective-permute-done.3.refs_0_.refs_4_, bf16[576,2048]{1,0:T(8,128)(2,1)} %collective-permute-done.4.refs_1_.refs_3_), custom_call_target="tpu_custom_call" | custom-call | flops 1 | bytes 1048576 | tf_op jit(solution)/shard_map/pallas_call | solution.py:77
  69.7 0.0 collective-permute-done.1.refs_0_
  69.7 0.0 collective-permute-done.2.refs_1_
  69.7 3.5 %collective-permute-start.5 = (bf16[288,2048]{1,0:T(8,128)(2,1)}, bf16[288,2048]{1,0:T(8,128)(2,1)}, u32[]{:S(2)}, u32[]{:S(2)}) collective-permute-start(bf16[288,2048]{1,0:T(8,128)(2,1)} %get-tuple-element.37), channel_id=1, source_target_pairs={{0,128},{128,256},{256,384},{384,0},{1,129},{129,257},{257,385},{3... | collective-permute-start | bytes 3538952 | tf_op jit(solution)/shard_map/ppermute | solution.py:23
  73.2 2.3 %collective-permute-start.6 = (bf16[288,2048]{1,0:T(8,128)(2,1)}, bf16[288,2048]{1,0:T(8,128)(2,1)}, u32[]{:S(2)}, u32[]{:S(2)}) collective-permute-start(bf16[288,2048]{1,0:T(8,128)(2,1)} %get-tuple-element.38), channel_id=1, source_target_pairs={{0,384},{128,0},{256,128},{384,256},{1,385},{129,1},{257,129},{385... | collective-permute-start | bytes 3538952 | tf_op jit(solution)/shard_map/ppermute | solution.py:23
  75.6 2.9 %shard_map.123 = bf16[128,4224]{1,0:T(8,128)(2,1)} custom-call(bf16[16,128]{1,0:T(8,128)(2,1)S(1)} %fusion.2.pick_ref, bf16[64,4224]{1,0:T(8,128)(2,1)} %collective-permute-done.1.refs_0_, bf16[64,4224]{1,0:T(8,128)(2,1)} %collective-permute-done.2.refs_1_), custom_call_target="tpu_custom_call" | custom-call | flops 999999995904 | bytes 1048576 | tf_op jit(solution)/shard_map/pallas_call | solution.py:47
  78.5 4.4 %all-to-all-done = bf16[8,16,4224]{2,1,0:T(8,128)(2,1)} async-done(((bf16[8,16,4224]{2,1,0:T(8,128)(2,1)}), bf16[8,16,4224]{2,1,0:T(8,128)(2,1)}, u32[]{:S(2)}, u32[]{:S(2)}) %all-to-all-start) | async-done | bytes 1081376 | tf_op jit(solution)/shard_map/all_to_all | solution.py:143
  82.9 4.2 %all-to-all-start.1 = ((bf16[8,16,4224]{2,1,0:T(8,128)(2,1)}), bf16[8,16,4224]{2,1,0:T(8,128)(2,1)}, u32[]{:S(2)}, u32[]{:S(2)}) async-start(bf16[8,16,4224]{2,1,0:T(8,128)(2,1)} %bitcast.7), calls=%async_computation.1 | async-start | bytes 2162688 | tf_op jit(solution)/shard_map/all_to_all | solution.py:143
  87.2 0.8 fusion.perm_ref
  88.0 3.5 %collective-permute-start.8 = (bf16[128,4224]{1,0:T(8,128)(2,1)}, bf16[128,4224]{1,0:T(8,128)(2,1)}, u32[]{:S(2)}, u32[]{:S(2)}) collective-permute-start(bf16[128,4224]{1,0:T(8,128)(2,1)} %bitcast.3.refs_0_.refs_3_.refs_4_.refs_5_), channel_id=1, source_target_pairs={{0,128},{128,256},{256,384},{384,0},{1,129},{129,257},{257,385},{3... | collective-permute-start | bytes 3244040 | tf_op jit(solution)/shard_map/ppermute | solution.py:23
  91.5 2.3 %collective-permute-start.9 = (bf16[128,4224]{1,0:T(8,128)(2,1)}, bf16[128,4224]{1,0:T(8,128)(2,1)}, u32[]{:S(2)}, u32[]{:S(2)}) collective-permute-start(bf16[128,4224]{1,0:T(8,128)(2,1)} %bitcast.3.refs_0_.refs_3_.refs_4_.refs_5_), channel_id=1, source_target_pairs={{0,384},{128,0},{256,128},{384,256},{1,385},{129,1},{257,129},{385... | collective-permute-start | bytes 3244040 | tf_op jit(solution)/shard_map/ppermute | solution.py:23
  93.8 9.6 %all-to-all-done.1 = bf16[8,16,4224]{2,1,0:T(8,128)(2,1)} async-done(((bf16[8,16,4224]{2,1,0:T(8,128)(2,1)}), bf16[8,16,4224]{2,1,0:T(8,128)(2,1)}, u32[]{:S(2)}, u32[]{:S(2)}) %all-to-all-start.1) | async-done | bytes 1081376 | tf_op jit(solution)/shard_map/all_to_all | solution.py:143
  103.4 3.5 %collective-permute-start.10 = (bf16[128,4224]{1,0:T(8,128)(2,1)}, bf16[128,4224]{1,0:T(8,128)(2,1)}, u32[]{:S(2)}, u32[]{:S(2)}) collective-permute-start(bf16[128,4224]{1,0:T(8,128)(2,1)} %bitcast.8.refs_1_.refs_12_.refs_13_.refs_14_), channel_id=1, source_target_pairs={{0,128},{128,256},{256,384},{384,0},{1,129},{129,257},{257,385},{3... | collective-permute-start | bytes 3244040 | tf_op jit(solution)/shard_map/ppermute | solution.py:23
  107.0 2.3 %collective-permute-start.11 = (bf16[128,4224]{1,0:T(8,128)(2,1)}, bf16[128,4224]{1,0:T(8,128)(2,1)}, u32[]{:S(2)}, u32[]{:S(2)}) collective-permute-start(bf16[128,4224]{1,0:T(8,128)(2,1)} %bitcast.8.refs_1_.refs_12_.refs_13_.refs_14_), channel_id=1, source_target_pairs={{0,384},{128,0},{256,128},{384,256},{1,385},{129,1},{257,129},{385... | collective-permute-start | bytes 3244040 | tf_op jit(solution)/shard_map/ppermute | solution.py:23
  109.3 0.0 copy-start
  109.3 0.9 copy-done
  110.2 10.3 %shard_map.124 = (bf16[256,2176]{1,0:T(8,128)(2,1)S(1)}, bf16[576,256]{1,0:T(8,128)(2,1)}, bf16[576,256]{1,0:T(8,128)(2,1)}, bf16[576,256]{1,0:T(8,128)(2,1)}, bf16[576,256]{1,0:T(8,128)(2,1)}) custom-call(bf16[16,128]{1,0:T(8,128)(2,1)S(1)} %iota.42.own_ref, bf16[256,256]{1,0:T(8,128)(2,1)S(1)} %copy-done, ...), custom_call_target="tpu_custom_call" | custom-call | flops 999999995904 | bytes 1048576 | tf_op jit(solution)/shard_map/pallas_call | solution.py:47
  120.6 1.3 reshape.267
  121.9 10.8 %all-to-all-start.2 = ((bf16[128,2,2176]{2,1,0:T(2,128)(2,1)}), bf16[128,2,2176]{2,1,0:T(2,128)(2,1)}, u32[]{:S(2)}, u32[]{:S(2)}) async-start(bf16[128,2,2176]{2,1,0:T(2,128)(2,1)} %reshape.267), calls=%async_computation.2 | async-start | bytes 2228224 | tf_op jit(solution)/shard_map/all_to_all | solution.py:319
  132.7 3.4 %collective-permute-start.7 = (bf16[576,256]{1,0:T(8,128)(2,1)}, bf16[576,256]{1,0:T(8,128)(2,1)}, u32[]{:S(2)}, u32[]{:S(2)}) collective-permute-start(bf16[576,256]{1,0:T(8,128)(2,1)} %get-tuple-element.40), channel_id=1, source_target_pairs={{0,256},{128,384},{256,0},{384,128},{1,257},{129,385},{257,1},{385... | collective-permute-start | bytes 884744 | tf_op jit(solution)/shard_map/ppermute | solution.py:23
  136.1 3.9 %collective-permute-start.14 = (bf16[576,256]{1,0:T(8,128)(2,1)}, bf16[576,256]{1,0:T(8,128)(2,1)}, u32[]{:S(2)}, u32[]{:S(2)}) collective-permute-start(bf16[576,256]{1,0:T(8,128)(2,1)} %get-tuple-element.44), channel_id=1, source_target_pairs={{0,128},{128,256},{256,384},{384,0},{1,129},{129,257},{257,385},{3... | collective-permute-start | bytes 884744 | tf_op jit(solution)/shard_map/ppermute | solution.py:23
  140.1 2.5 %collective-permute-start.15 = (bf16[576,256]{1,0:T(8,128)(2,1)}, bf16[576,256]{1,0:T(8,128)(2,1)}, u32[]{:S(2)}, u32[]{:S(2)}) collective-permute-start(bf16[576,256]{1,0:T(8,128)(2,1)} %get-tuple-element.45), channel_id=1, source_target_pairs={{0,384},{128,0},{256,128},{384,256},{1,385},{129,1},{257,129},{385... | collective-permute-start | bytes 884744 | tf_op jit(solution)/shard_map/ppermute | solution.py:23
  142.6 9.5 %collective-permute-done.10.refs_2_ = bf16[128,4224]{1,0:T(8,128)(2,1)} collective-permute-done((bf16[128,4224]{1,0:T(8,128)(2,1)}, bf16[128,4224]{1,0:T(8,128)(2,1)}, u32[]{:S(2)}, u32[]{:S(2)}) %collective-permute-start.10) | collective-permute-done | bytes 1081376 | tf_op jit(solution)/shard_map/ppermute | solution.py:23
  152.1 6.0 %collective-permute-done.11.refs_3_ = bf16[128,4224]{1,0:T(8,128)(2,1)} collective-permute-done((bf16[128,4224]{1,0:T(8,128)(2,1)}, bf16[128,4224]{1,0:T(8,128)(2,1)}, u32[]{:S(2)}, u32[]{:S(2)}) %collective-permute-start.11) | collective-permute-done | bytes 1081376 | tf_op jit(solution)/shard_map/ppermute | solution.py:23
  158.1 2.0 %collective-permute-start.12 = (bf16[128,4224]{1,0:T(8,128)(2,1)}, bf16[128,4224]{1,0:T(8,128)(2,1)}, u32[]{:S(2)}, u32[]{:S(2)}) collective-permute-start(bf16[128,4224]{1,0:T(8,128)(2,1)} %get-tuple-element.41.refs_6_.refs_7_.refs_8_), channel_id=1, source_target_pairs={{0,128},{128,256},{256,384},{384,0},{1,129},{129,257},{257,385},{3... | collective-permute-start | bytes 3244040 | tf_op jit(solution)/shard_map/ppermute | solution.py:23
  160.2 3.9 %collective-permute-start.13 = (bf16[128,4224]{1,0:T(8,128)(2,1)}, bf16[128,4224]{1,0:T(8,128)(2,1)}, u32[]{:S(2)}, u32[]{:S(2)}) collective-permute-start(bf16[128,4224]{1,0:T(8,128)(2,1)} %get-tuple-element.42.refs_18_.refs_19_.refs_20_), channel_id=1, source_target_pairs={{0,384},{128,0},{256,128},{384,256},{1,385},{129,1},{257,129},{385... | collective-permute-start | bytes 3244040 | tf_op jit(solution)/shard_map/ppermute | solution.py:23
  164.1 0.0 collective-permute-done.15.refs_2_
  164.1 7.3 %shard_map.126.refs_7_ = f32[576,2048]{1,0:T(8,128)} custom-call(f32[1,128]{1,0:T(1,128)S(1)} %compare_convert_fusion.own_ref, bf16[576,256]{1,0:T(8,128)(2,1)S(1)} %copy-done.3, bf16[576,256]{1,0:T(8,128)(2,1)} %collective-permute-done.14.refs_1_, bf16[576,256]{1,0:T(8,128)(2,1)} %collective-permute-done.15.refs_2_, ...), custom_call_target="tpu_custom_call" | custom-call | flops 999999995904 | bytes 1048576 | tf_op jit(solution)/shard_map/pallas_call | solution.py:47
  171.5 13.4 %collective-permute-done.12.refs_1_.refs_2_.refs_3_ = bf16[128,4224]{1,0:T(8,128)(2,1)} collective-permute-done((bf16[128,4224]{1,0:T(8,128)(2,1)}, bf16[128,4224]{1,0:T(8,128)(2,1)}, u32[]{:S(2)}, u32[]{:S(2)}) %collective-permute-start.12) | collective-permute-done | bytes 1081376 | tf_op jit(solution)/shard_map/ppermute | solution.py:23
  184.9 3.1 %collective-permute-done.13.refs_4_.refs_5_.refs_6_ = bf16[128,4224]{1,0:T(8,128)(2,1)} collective-permute-done((bf16[128,4224]{1,0:T(8,128)(2,1)}, bf16[128,4224]{1,0:T(8,128)(2,1)}, u32[]{:S(2)}, u32[]{:S(2)}) %collective-permute-start.13) | collective-permute-done | bytes 1081376 | tf_op jit(solution)/shard_map/ppermute | solution.py:23
  188.0 5.6 %shard_map.127 = (bf16[192,2048]{1,0:T(8,128)(2,1)}, bf16[192,2048]{1,0:T(8,128)(2,1)}, bf16[192,2048]{1,0:T(8,128)(2,1)}) custom-call(f32[1,128]{1,0:T(1,128)S(1)} %compare_convert_fusion.own_ref, bf16[576,256]{1,0:T(8,128)(2,1)} %collective-permute-done.7.refs_0_, bf16[128,4224]{1,0:T(8,128)(2,1)} %collective-permute-done.12.refs_1_.refs_2_.refs_3_, ...), custom_call_target="tpu_custom_call" | custom-call | flops 1 | bytes 1048576 | tf_op jit(solution)/shard_map/pallas_call | solution.py:47
  193.6 1.5 reshape.268.home_ref
  195.1 1.3 shard_map.128
  (29 shorter events, 0.1 us)
Async XLA Ops:
  0.6 11.4 %copy-start.7 = (bf16[16,8]{0,1:T(8,128)(2,1)S(1)}, bf16[16,8]{0,1:T(8,128)(2,1)}, u32[]{:S(2)}) copy-start(bf16[16,8]{0,1:T(8,128)(2,1)} %param.11) | copy-start | bytes 772
  0.6 11.4 %copy-start.6 = (s32[16,8]{0,1:T(8,128)S(1)}, s32[16,8]{0,1:T(8,128)}, u32[]{:S(2)}) copy-start(s32[16,8]{0,1:T(8,128)} %param.12) | copy-start | bytes 1540
  2.3 64.2 %collective-permute-start.3 = (bf16[576,2048]{1,0:T(8,128)(2,1)S(1)}, bf16[576,2048]{1,0:T(8,128)(2,1)}, u32[]{:S(2)}, u32[]{:S(2)}) collective-permute-start(bf16[576,2048]{1,0:T(8,128)(2,1)S(1)} %shard_map.121.refs_2_), channel_id=1, source_target_pairs={{0,128},{128,256},{256,384},{384,0},{1,129},{129,257},{257,385},{3... | collective-permute-start | bytes 7077896 | tf_op jit(solution)/shard_map/ppermute | solution.py:23
  10.1 56.4 %collective-permute-start.4 = (bf16[576,2048]{1,0:T(8,128)(2,1)S(1)}, bf16[576,2048]{1,0:T(8,128)(2,1)}, u32[]{:S(2)}, u32[]{:S(2)}) collective-permute-start(bf16[576,2048]{1,0:T(8,128)(2,1)S(1)} %shard_map.121.refs_2_), channel_id=1, source_target_pairs={{0,384},{128,0},{256,128},{384,256},{1,385},{129,1},{257,129},{385... | collective-permute-start | bytes 7077896 | tf_op jit(solution)/shard_map/ppermute | solution.py:23
  12.1 29.5 %copy-start.1 = (s32[8,16]{1,0:T(8,128)}, s32[8,16]{1,0:T(8,128)S(1)}, u32[]{:S(2)}) copy-start(s32[8,16]{1,0:T(8,128)S(1)} %fusion.6.rank_ref) | copy-start | bytes 1540
  41.5 17.6 %copy-start.4 = (bf16[64,4224]{1,0:T(8,128)(2,1)}, bf16[64,4224]{1,0:T(8,128)(2,1)S(1)}, u32[]{:S(2)}) copy-start(bf16[64,4224]{1,0:T(8,128)(2,1)S(1)} %all_gather.3.refs_0_) | copy-start | bytes 1622020
  41.5 13.6 %collective-permute-start = (bf16[64,4224]{1,0:T(8,128)(2,1)S(1)}, bf16[64,4224]{1,0:T(8,128)(2,1)S(1)}, u32[]{:S(2)}, u32[]{:S(2)}) collective-permute-start(bf16[64,4224]{1,0:T(8,128)(2,1)S(1)} %all_gather.3.refs_0_), channel_id=1, source_target_pairs={{0,30},{2,0},{4,2},{6,4},{8,6},{10,8},{12,10},{14,12},{16,14},{18,... | collective-permute-start | bytes 1622024 | tf_op jit(solution)/shard_map/ppermute | solution.py:23
  47.0 22.7 %collective-permute-start.1 = (bf16[64,4224]{1,0:T(8,128)(2,1)S(1)}, bf16[64,4224]{1,0:T(8,128)(2,1)}, u32[]{:S(2)}, u32[]{:S(2)}) collective-permute-start(bf16[64,4224]{1,0:T(8,128)(2,1)S(1)} %all_gather.3.refs_0_), channel_id=1, source_target_pairs={{0,2},{2,4},{4,6},{6,8},{8,10},{10,12},{12,14},{14,16},{16,18},{18... | collective-permute-start | bytes 1622024 | tf_op jit(solution)/shard_map/ppermute | solution.py:23
  55.1 4.0 %copy-start.5 = (bf16[64,4224]{1,0:T(8,128)(2,1)}, bf16[64,4224]{1,0:T(8,128)(2,1)S(1)}, u32[]{:S(2)}) copy-start(bf16[64,4224]{1,0:T(8,128)(2,1)S(1)} %collective-permute-done.refs_1_) | copy-start | bytes 1622020
  55.1 14.6 %collective-permute-start.2 = (bf16[64,4224]{1,0:T(8,128)(2,1)S(1)}, bf16[64,4224]{1,0:T(8,128)(2,1)}, u32[]{:S(2)}, u32[]{:S(2)}) collective-permute-start(bf16[64,4224]{1,0:T(8,128)(2,1)S(1)} %all_gather.3.refs_0_), channel_id=1, source_target_pairs={{4,0},{30,2},{8,4},{2,6},{12,8},{6,10},{16,12},{10,14},{20,16},{14... | collective-permute-start | bytes 1622024 | tf_op jit(solution)/shard_map/ppermute | solution.py:287
  62.0 20.9 %all-to-all-start = ((bf16[8,16,4224]{2,1,0:T(8,128)(2,1)}), bf16[8,16,4224]{2,1,0:T(8,128)(2,1)}, u32[]{:S(2)}, u32[]{:S(2)}) async-start(bf16[8,16,4224]{2,1,0:T(8,128)(2,1)} %bitcast.2), calls=%async_computation | async-start | bytes 2162688 | tf_op jit(solution)/shard_map/all_to_all | solution.py:143
  69.7 37.3 %collective-permute-start.5 = (bf16[288,2048]{1,0:T(8,128)(2,1)}, bf16[288,2048]{1,0:T(8,128)(2,1)}, u32[]{:S(2)}, u32[]{:S(2)}) collective-permute-start(bf16[288,2048]{1,0:T(8,128)(2,1)} %get-tuple-element.37), channel_id=1, source_target_pairs={{0,128},{128,256},{256,384},{384,0},{1,129},{129,257},{257,385},{3... | collective-permute-start | bytes 3538952 | tf_op jit(solution)/shard_map/ppermute | solution.py:23
  73.2 36.1 %collective-permute-start.6 = (bf16[288,2048]{1,0:T(8,128)(2,1)}, bf16[288,2048]{1,0:T(8,128)(2,1)}, u32[]{:S(2)}, u32[]{:S(2)}) collective-permute-start(bf16[288,2048]{1,0:T(8,128)(2,1)} %get-tuple-element.38), channel_id=1, source_target_pairs={{0,384},{128,0},{256,128},{384,256},{1,385},{129,1},{257,129},{385... | collective-permute-start | bytes 3538952 | tf_op jit(solution)/shard_map/ppermute | solution.py:23
  82.9 20.6 %all-to-all-start.1 = ((bf16[8,16,4224]{2,1,0:T(8,128)(2,1)}), bf16[8,16,4224]{2,1,0:T(8,128)(2,1)}, u32[]{:S(2)}, u32[]{:S(2)}) async-start(bf16[8,16,4224]{2,1,0:T(8,128)(2,1)} %bitcast.7), calls=%async_computation.1 | async-start | bytes 2162688 | tf_op jit(solution)/shard_map/all_to_all | solution.py:143
  88.0 48.2 %collective-permute-start.8 = (bf16[128,4224]{1,0:T(8,128)(2,1)}, bf16[128,4224]{1,0:T(8,128)(2,1)}, u32[]{:S(2)}, u32[]{:S(2)}) collective-permute-start(bf16[128,4224]{1,0:T(8,128)(2,1)} %bitcast.3.refs_0_.refs_3_.refs_4_.refs_5_), channel_id=1, source_target_pairs={{0,128},{128,256},{256,384},{384,0},{1,129},{129,257},{257,385},{3... | collective-permute-start | bytes 3244040 | tf_op jit(solution)/shard_map/ppermute | solution.py:23
  91.5 48.6 %collective-permute-start.9 = (bf16[128,4224]{1,0:T(8,128)(2,1)}, bf16[128,4224]{1,0:T(8,128)(2,1)}, u32[]{:S(2)}, u32[]{:S(2)}) collective-permute-start(bf16[128,4224]{1,0:T(8,128)(2,1)} %bitcast.3.refs_0_.refs_3_.refs_4_.refs_5_), channel_id=1, source_target_pairs={{0,384},{128,0},{256,128},{384,256},{1,385},{129,1},{257,129},{385... | collective-permute-start | bytes 3244040 | tf_op jit(solution)/shard_map/ppermute | solution.py:23
  103.4 48.7 %collective-permute-start.10 = (bf16[128,4224]{1,0:T(8,128)(2,1)}, bf16[128,4224]{1,0:T(8,128)(2,1)}, u32[]{:S(2)}, u32[]{:S(2)}) collective-permute-start(bf16[128,4224]{1,0:T(8,128)(2,1)} %bitcast.8.refs_1_.refs_12_.refs_13_.refs_14_), channel_id=1, source_target_pairs={{0,128},{128,256},{256,384},{384,0},{1,129},{129,257},{257,385},{3... | collective-permute-start | bytes 3244040 | tf_op jit(solution)/shard_map/ppermute | solution.py:23
  107.0 51.1 %collective-permute-start.11 = (bf16[128,4224]{1,0:T(8,128)(2,1)}, bf16[128,4224]{1,0:T(8,128)(2,1)}, u32[]{:S(2)}, u32[]{:S(2)}) collective-permute-start(bf16[128,4224]{1,0:T(8,128)(2,1)} %bitcast.8.refs_1_.refs_12_.refs_13_.refs_14_), channel_id=1, source_target_pairs={{0,384},{128,0},{256,128},{384,256},{1,385},{129,1},{257,129},{385... | collective-permute-start | bytes 3244040 | tf_op jit(solution)/shard_map/ppermute | solution.py:23
  109.3 0.9 copy-start
  121.9 71.7 %all-to-all-start.2 = ((bf16[128,2,2176]{2,1,0:T(2,128)(2,1)}), bf16[128,2,2176]{2,1,0:T(2,128)(2,1)}, u32[]{:S(2)}, u32[]{:S(2)}) async-start(bf16[128,2,2176]{2,1,0:T(2,128)(2,1)} %reshape.267), calls=%async_computation.2 | async-start | bytes 2228224 | tf_op jit(solution)/shard_map/all_to_all | solution.py:319
  132.7 38.7 %collective-permute-start.7 = (bf16[576,256]{1,0:T(8,128)(2,1)}, bf16[576,256]{1,0:T(8,128)(2,1)}, u32[]{:S(2)}, u32[]{:S(2)}) collective-permute-start(bf16[576,256]{1,0:T(8,128)(2,1)} %get-tuple-element.40), channel_id=1, source_target_pairs={{0,256},{128,384},{256,0},{384,128},{1,257},{129,385},{257,1},{385... | collective-permute-start | bytes 884744 | tf_op jit(solution)/shard_map/ppermute | solution.py:23
  136.1 28.0 %collective-permute-start.14 = (bf16[576,256]{1,0:T(8,128)(2,1)}, bf16[576,256]{1,0:T(8,128)(2,1)}, u32[]{:S(2)}, u32[]{:S(2)}) collective-permute-start(bf16[576,256]{1,0:T(8,128)(2,1)} %get-tuple-element.44), channel_id=1, source_target_pairs={{0,128},{128,256},{256,384},{384,0},{1,129},{129,257},{257,385},{3... | collective-permute-start | bytes 884744 | tf_op jit(solution)/shard_map/ppermute | solution.py:23
  140.1 24.0 %collective-permute-start.15 = (bf16[576,256]{1,0:T(8,128)(2,1)}, bf16[576,256]{1,0:T(8,128)(2,1)}, u32[]{:S(2)}, u32[]{:S(2)}) collective-permute-start(bf16[576,256]{1,0:T(8,128)(2,1)} %get-tuple-element.45), channel_id=1, source_target_pairs={{0,384},{128,0},{256,128},{384,256},{1,385},{129,1},{257,129},{385... | collective-permute-start | bytes 884744 | tf_op jit(solution)/shard_map/ppermute | solution.py:23
  158.1 6.0 %copy-start.3 = (bf16[576,256]{1,0:T(8,128)(2,1)S(1)}, bf16[576,256]{1,0:T(8,128)(2,1)}, u32[]{:S(2)}) copy-start(bf16[576,256]{1,0:T(8,128)(2,1)} %get-tuple-element.43.refs_0_) | copy-start | bytes 884740
  158.1 26.7 %collective-permute-start.12 = (bf16[128,4224]{1,0:T(8,128)(2,1)}, bf16[128,4224]{1,0:T(8,128)(2,1)}, u32[]{:S(2)}, u32[]{:S(2)}) collective-permute-start(bf16[128,4224]{1,0:T(8,128)(2,1)} %get-tuple-element.41.refs_6_.refs_7_.refs_8_), channel_id=1, source_target_pairs={{0,128},{128,256},{256,384},{384,0},{1,129},{129,257},{257,385},{3... | collective-permute-start | bytes 3244040 | tf_op jit(solution)/shard_map/ppermute | solution.py:23
  160.2 27.8 %collective-permute-start.13 = (bf16[128,4224]{1,0:T(8,128)(2,1)}, bf16[128,4224]{1,0:T(8,128)(2,1)}, u32[]{:S(2)}, u32[]{:S(2)}) collective-permute-start(bf16[128,4224]{1,0:T(8,128)(2,1)} %get-tuple-element.42.refs_18_.refs_19_.refs_20_), channel_id=1, source_target_pairs={{0,384},{128,0},{256,128},{384,256},{1,385},{129,1},{257,129},{385... | collective-permute-start | bytes 3244040 | tf_op jit(solution)/shard_map/ppermute | solution.py:23
  193.6 1.5 copy-start.2

commit v12 on v11

--- a/solution.py
+++ b/solution.py
@@ -225,7 +225,7 @@
     for a in before:
         operands.append(a)
         specs.append(pl.BlockSpec((rows, tile), lambda j: (0, j)))
-    out = [sds((rows // 3, width), BF16)] * 3 if before else [pltpu.HBM((rows, width), F32)]
+    out = [sds((rows // 3, width), BF16)] * 3 if before else [sds((rows, width), F32)]
     return call(
         functools.partial(grads_kernel, len(acts), bool(before)),
         operands,
@@ -235,6 +235,33 @@
         grid=(width // tile,),
         vmem=28,
         cost=1 if before else LONG,
+    )
+
+
+def last_kernel(own_ref, acts_ref, first_ref, second_ref, sums_ref, gate_ref, up_ref, down_ref):
+    share, tile = gate_ref.shape
+    width = sums_ref.shape[1]
+    at = pl.multiple_of(pl.program_id(0) * tile, tile)
+    take = lambda a, n: jnp.concatenate([r[:, pl.ds(a, n)] for r in (first_ref, second_ref)], axis=0)
+    weight = jnp.sum(take(2 * width, LANES).astype(F32) * own_ref[...], axis=1, keepdims=True)
+    scaled = (weight * take(pl.multiple_of(width + at, tile), tile).astype(F32)).astype(BF16)
+    both = sums_ref[: 2 * share, pl.ds(at, tile)] + nn(acts_ref[: 2 * share], take(at, tile))
+    down = sums_ref[2 * share :, pl.ds(at, tile)] + nn(acts_ref[2 * share :], scaled)
+    gate_ref[...] = both[:share].astype(BF16)
+    up_ref[...] = both[share:].astype(BF16)
+    down_ref[...] = down.astype(BF16)
+
+
+def last_grads(own, acts, first, second, sums, tile=512):
+    rows, width = sums.shape
+    return call(
+        last_kernel,
+        (own, acts, first, second, sums),
+        [sds((rows // 3, width), BF16)] * 3,
+        in_specs=[pl.BlockSpec(memory_space=pltpu.VMEM)] * 5,
+        out_specs=[pl.BlockSpec((rows // 3, tile), lambda j: (0, j))] * 3,
+        grid=(width // tile,),
+        vmem=16,
     )
 
 
@@ -321,7 +348,7 @@
     ).reshape(count, -1)
     *near_acts, far_acts = a_own, shift(a_next, "dp", DP, 1), shift(a_prev, "dp", DP, -1), shift(a_far, "dp", DP, 2)
     sums = weight_grads(own[:1], near_acts, near)
-    grad_gate, grad_up, grad_down = weight_grads(own[:1], [far_acts], (first_far, second_far), in_hbm(sums))
+    grad_gate, grad_up, grad_down = last_grads(own[:1], far_acts, first_far, second_far, *sums)
     home, grad_gate, grad_up, grad_down = lax.optimization_barrier((home, grad_gate, grad_up, grad_down))
     grad_in, grad_combine = call(
         home_kernel, (home, rank_of(expert_ids.T)), [sds((tokens, width), BF16), sds((picks, tokens), F32)], vmem=8

time: 198 us -> 197 us (level)
  Pallas kernels: 36.2 us -> 33.3 us
    pallas_call x7, Pallas kernels: 31.4 us -> 28.5 us  [call(): pl.pallas_call(kernel, grid=grid, out_shape=out_shape, in_specs=in_specs...]
  transfers between devices with their start and end apart: 19 -> 19, of which waited for: 7 -> 7; matrix products, arithmetic and copies ran while one was open for 1% -> 1% of each run, Pallas kernels for 17% -> 16%
where the time goes in v12:
time: 197 us; the launch traced here: 195 us
  starting transfers between devices  73.8 us (37%)
  waiting for transfers between devices  53.8 us (27%)
  Pallas kernels  33.3 us (17%)
  blocking collectives  28.3 us (14%)
  local copies, waits for them, and re-layouts  3.71 us (2%)
    ppermute x15, starting transfers between devices, shift(): return lax.ppermute(a, axis, [(i, (i + k) % size) for i in range(size)])  50.4 us
    ppermute x15, waiting for transfers between devices, shift(): return lax.ppermute(a, axis, [(i, (i + k) % size) for i in range(size)])  39.6 us
    pallas_call x7, Pallas kernels, call(): pl.pallas_call(kernel, grid=grid, out_shape=out_shape, in_specs=in_specs...  28.5 us
    all_gather x1, blocking collectives, body(): lax.all_gather(payload, 'z', axis=0, tiled=True, axis_index_groups=groups)  28.3 us
    all_to_all x2, waiting for transfers between devices, to_experts(): lax.all_to_all(sent.reshape(YC, -1, sent.shape[1]), ('y', 'core'), split_...  14.1 us
    all_to_all x1, starting transfers between devices, body(): lax.all_to_all(back.reshape(experts, CAP, -1), ('y', 'core', 'z'), split_...  10.8 us
    all_to_all x2, starting transfers between devices, to_experts(): lax.all_to_all(sent.reshape(YC, -1, sent.shape[1]), ('y', 'core'), split_...  8.7 us
    pallas_call x2, Pallas kernels, move(): pl.pallas_call(functools.partial(move_kernel, plan, len(arrays)), out_sha...  4.78 us
  transfers between devices with their start and end apart: 19, of which 7 were waited for; matrix products, arithmetic and copies ran while one was open for 1% of the time, Pallas kernels for 16%

profile of v12, /device:TPU:6, one launch (start us, length us, event | category | flops | bytes accessed | tf_op | source)
XLA Modules:
  0.0 194.8 jit_solution(12782663847920481566)
XLA Ops:
  0.7 1.6 shard_map.121.refs_2_
  2.3 7.8 %collective-permute-start.3 = (bf16[576,2048]{1,0:T(8,128)(2,1)S(1)}, bf16[576,2048]{1,0:T(8,128)(2,1)}, u32[]{:S(2)}, u32[]{:S(2)}) collective-permute-start(bf16[576,2048]{1,0:T(8,128)(2,1)S(1)} %shard_map.121.refs_2_), channel_id=1, source_target_pairs={{0,128},{128,256},{256,384},{384,0},{1,129},{129,257},{257,385},{3... | collective-permute-start | bytes 7077896 | tf_op jit(solution)/shard_map/ppermute | solution.py:23
  10.1 1.9 collective-permute-start.4
  12.1 0.0 copy-start.1
  12.1 1.1 shard_map.119
  13.2 28.3 %all_gather.3.refs_0_ = bf16[64,4224]{1,0:T(8,128)(2,1)S(1)} all-gather(bf16[16,4224]{1,0:T(8,128)(2,1)S(1)} %shard_map.119), channel_id=1, replica_groups={{0,8,16,24},{2,10,18,26},{4,12,20,28},{6,14,22,30},{1,9,17,25},{3,11,19..., dimensions={0}, use_global_device_ids=true | all-gather | bytes 675840 | tf_op jit(solution)/shard_map/all_gather | solution.py:305
  41.5 5.5 %collective-permute-start = (bf16[64,4224]{1,0:T(8,128)(2,1)S(1)}, bf16[64,4224]{1,0:T(8,128)(2,1)S(1)}, u32[]{:S(2)}, u32[]{:S(2)}) collective-permute-start(bf16[64,4224]{1,0:T(8,128)(2,1)S(1)} %all_gather.3.refs_0_), channel_id=1, source_target_pairs={{0,30},{2,0},{4,2},{6,4},{8,6},{10,8},{12,10},{14,12},{16,14},{18,... | collective-permute-start | bytes 1622024 | tf_op jit(solution)/shard_map/ppermute | solution.py:23
  47.0 1.9 collective-permute-start.1
  48.9 6.2 %collective-permute-done.refs_1_ = bf16[64,4224]{1,0:T(8,128)(2,1)S(1)} collective-permute-done((bf16[64,4224]{1,0:T(8,128)(2,1)S(1)}, bf16[64,4224]{1,0:T(8,128)(2,1)S(1)}, u32[]{:S(2)}, u32[]{:S(2)}) %collective-permute-start) | collective-permute-done | bytes 540704 | tf_op jit(solution)/shard_map/ppermute | solution.py:23
  55.1 3.9 %collective-permute-start.2 = (bf16[64,4224]{1,0:T(8,128)(2,1)S(1)}, bf16[64,4224]{1,0:T(8,128)(2,1)}, u32[]{:S(2)}, u32[]{:S(2)}) collective-permute-start(bf16[64,4224]{1,0:T(8,128)(2,1)S(1)} %all_gather.3.refs_0_), channel_id=1, source_target_pairs={{4,0},{30,2},{8,4},{2,6},{12,8},{6,10},{16,12},{10,14},{20,16},{14... | collective-permute-start | bytes 1622024 | tf_op jit(solution)/shard_map/ppermute | solution.py:314
  59.0 0.1 fusion.2.pick_ref
  59.1 2.9 %shard_map.120 = bf16[128,4224]{1,0:T(8,128)(2,1)} custom-call(bf16[16,128]{1,0:T(8,128)(2,1)S(1)} %fusion.2.pick_ref, bf16[64,4224]{1,0:T(8,128)(2,1)} %copy-done.4, bf16[64,4224]{1,0:T(8,128)(2,1)} %copy-done.5), custom_call_target="tpu_custom_call" | custom-call | flops 1 | bytes 1048576 | tf_op jit(solution)/shard_map/pallas_call | solution.py:47
  62.0 4.5 %all-to-all-start = ((bf16[8,16,4224]{2,1,0:T(8,128)(2,1)}), bf16[8,16,4224]{2,1,0:T(8,128)(2,1)}, u32[]{:S(2)}, u32[]{:S(2)}) async-start(bf16[8,16,4224]{2,1,0:T(8,128)(2,1)} %bitcast.2), calls=%async_computation | async-start | bytes 2162688 | tf_op jit(solution)/shard_map/all_to_all | solution.py:143
  66.5 0.0 collective-permute-done.4.refs_1_.refs_3_
  66.5 3.1 %shard_map.122 = (bf16[288,2048]{1,0:T(8,128)(2,1)}, bf16[288,2048]{1,0:T(8,128)(2,1)}) custom-call(bf16[576,2048]{1,0:T(8,128)(2,1)} %collective-permute-done.3.refs_0_.refs_4_, bf16[576,2048]{1,0:T(8,128)(2,1)} %collective-permute-done.4.refs_1_.refs_3_), custom_call_target="tpu_custom_call" | custom-call | flops 1 | bytes 1048576 | tf_op jit(solution)/shard_map/pallas_call | solution.py:77
  69.6 0.0 collective-permute-done.2.refs_1_
  69.6 3.5 %collective-permute-start.5 = (bf16[288,2048]{1,0:T(8,128)(2,1)}, bf16[288,2048]{1,0:T(8,128)(2,1)}, u32[]{:S(2)}, u32[]{:S(2)}) collective-permute-start(bf16[288,2048]{1,0:T(8,128)(2,1)} %get-tuple-element.37), channel_id=1, source_target_pairs={{0,128},{128,256},{256,384},{384,0},{1,129},{129,257},{257,385},{3... | collective-permute-start | bytes 3538952 | tf_op jit(solution)/shard_map/ppermute | solution.py:23
  73.2 2.3 %collective-permute-start.6 = (bf16[288,2048]{1,0:T(8,128)(2,1)}, bf16[288,2048]{1,0:T(8,128)(2,1)}, u32[]{:S(2)}, u32[]{:S(2)}) collective-permute-start(bf16[288,2048]{1,0:T(8,128)(2,1)} %get-tuple-element.38), channel_id=1, source_target_pairs={{0,384},{128,0},{256,128},{384,256},{1,385},{129,1},{257,129},{385... | collective-permute-start | bytes 3538952 | tf_op jit(solution)/shard_map/ppermute | solution.py:23
  75.5 2.9 %shard_map.123 = bf16[128,4224]{1,0:T(8,128)(2,1)} custom-call(bf16[16,128]{1,0:T(8,128)(2,1)S(1)} %fusion.2.pick_ref, bf16[64,4224]{1,0:T(8,128)(2,1)} %collective-permute-done.1.refs_0_, bf16[64,4224]{1,0:T(8,128)(2,1)} %collective-permute-done.2.refs_1_), custom_call_target="tpu_custom_call" | custom-call | flops 999999995904 | bytes 1048576 | tf_op jit(solution)/shard_map/pallas_call | solution.py:47
  78.4 4.5 %all-to-all-done = bf16[8,16,4224]{2,1,0:T(8,128)(2,1)} async-done(((bf16[8,16,4224]{2,1,0:T(8,128)(2,1)}), bf16[8,16,4224]{2,1,0:T(8,128)(2,1)}, u32[]{:S(2)}, u32[]{:S(2)}) %all-to-all-start) | async-done | bytes 1081376 | tf_op jit(solution)/shard_map/all_to_all | solution.py:143
  82.9 4.2 %all-to-all-start.1 = ((bf16[8,16,4224]{2,1,0:T(8,128)(2,1)}), bf16[8,16,4224]{2,1,0:T(8,128)(2,1)}, u32[]{:S(2)}, u32[]{:S(2)}) async-start(bf16[8,16,4224]{2,1,0:T(8,128)(2,1)} %bitcast.7), calls=%async_computation.1 | async-start | bytes 2162688 | tf_op jit(solution)/shard_map/all_to_all | solution.py:143
  87.2 0.8 fusion.perm_ref
  88.0 3.5 %collective-permute-start.8 = (bf16[128,4224]{1,0:T(8,128)(2,1)}, bf16[128,4224]{1,0:T(8,128)(2,1)}, u32[]{:S(2)}, u32[]{:S(2)}) collective-permute-start(bf16[128,4224]{1,0:T(8,128)(2,1)} %bitcast.3.refs_0_.refs_3_.refs_4_.refs_5_), channel_id=1, source_target_pairs={{0,128},{128,256},{256,384},{384,0},{1,129},{129,257},{257,385},{3... | collective-permute-start | bytes 3244040 | tf_op jit(solution)/shard_map/ppermute | solution.py:23
  91.5 2.3 %collective-permute-start.9 = (bf16[128,4224]{1,0:T(8,128)(2,1)}, bf16[128,4224]{1,0:T(8,128)(2,1)}, u32[]{:S(2)}, u32[]{:S(2)}) collective-permute-start(bf16[128,4224]{1,0:T(8,128)(2,1)} %bitcast.3.refs_0_.refs_3_.refs_4_.refs_5_), channel_id=1, source_target_pairs={{0,384},{128,0},{256,128},{384,256},{1,385},{129,1},{257,129},{385... | collective-permute-start | bytes 3244040 | tf_op jit(solution)/shard_map/ppermute | solution.py:23
  93.8 9.6 %all-to-all-done.1 = bf16[8,16,4224]{2,1,0:T(8,128)(2,1)} async-done(((bf16[8,16,4224]{2,1,0:T(8,128)(2,1)}), bf16[8,16,4224]{2,1,0:T(8,128)(2,1)}, u32[]{:S(2)}, u32[]{:S(2)}) %all-to-all-start.1) | async-done | bytes 1081376 | tf_op jit(solution)/shard_map/all_to_all | solution.py:143
  103.4 3.5 %collective-permute-start.10 = (bf16[128,4224]{1,0:T(8,128)(2,1)}, bf16[128,4224]{1,0:T(8,128)(2,1)}, u32[]{:S(2)}, u32[]{:S(2)}) collective-permute-start(bf16[128,4224]{1,0:T(8,128)(2,1)} %bitcast.8.refs_1_.refs_12_.refs_13_.refs_14_), channel_id=1, source_target_pairs={{0,128},{128,256},{256,384},{384,0},{1,129},{129,257},{257,385},{3... | collective-permute-start | bytes 3244040 | tf_op jit(solution)/shard_map/ppermute | solution.py:23
  107.0 2.3 %collective-permute-start.11 = (bf16[128,4224]{1,0:T(8,128)(2,1)}, bf16[128,4224]{1,0:T(8,128)(2,1)}, u32[]{:S(2)}, u32[]{:S(2)}) collective-permute-start(bf16[128,4224]{1,0:T(8,128)(2,1)} %bitcast.8.refs_1_.refs_12_.refs_13_.refs_14_), channel_id=1, source_target_pairs={{0,384},{128,0},{256,128},{384,256},{1,385},{129,1},{257,129},{385... | collective-permute-start | bytes 3244040 | tf_op jit(solution)/shard_map/ppermute | solution.py:23
  109.3 0.0 copy-start
  109.3 0.9 copy-done
  110.2 10.3 %shard_map.124 = (bf16[256,2176]{1,0:T(8,128)(2,1)S(1)}, bf16[576,256]{1,0:T(8,128)(2,1)}, bf16[576,256]{1,0:T(8,128)(2,1)}, bf16[576,256]{1,0:T(8,128)(2,1)}, bf16[576,256]{1,0:T(8,128)(2,1)}) custom-call(bf16[16,128]{1,0:T(8,128)(2,1)S(1)} %iota.42.own_ref, bf16[256,256]{1,0:T(8,128)(2,1)S(1)} %copy-done, ...), custom_call_target="tpu_custom_call" | custom-call | flops 999999995904 | bytes 1048576 | tf_op jit(solution)/shard_map/pallas_call | solution.py:47
  120.5 1.3 reshape.267
  121.8 10.8 %all-to-all-start.2 = ((bf16[128,2,2176]{2,1,0:T(2,128)(2,1)}), bf16[128,2,2176]{2,1,0:T(2,128)(2,1)}, u32[]{:S(2)}, u32[]{:S(2)}) async-start(bf16[128,2,2176]{2,1,0:T(2,128)(2,1)} %reshape.267), calls=%async_computation.2 | async-start | bytes 2228224 | tf_op jit(solution)/shard_map/all_to_all | solution.py:346
  132.7 3.4 %collective-permute-start.7 = (bf16[576,256]{1,0:T(8,128)(2,1)}, bf16[576,256]{1,0:T(8,128)(2,1)}, u32[]{:S(2)}, u32[]{:S(2)}) collective-permute-start(bf16[576,256]{1,0:T(8,128)(2,1)} %get-tuple-element.40), channel_id=1, source_target_pairs={{0,256},{128,384},{256,0},{384,128},{1,257},{129,385},{257,1},{385... | collective-permute-start | bytes 884744 | tf_op jit(solution)/shard_map/ppermute | solution.py:23
  136.0 0.0 collective-permute-done.8.refs_0_
  136.0 4.0 %collective-permute-start.14 = (bf16[576,256]{1,0:T(8,128)(2,1)}, bf16[576,256]{1,0:T(8,128)(2,1)}, u32[]{:S(2)}, u32[]{:S(2)}) collective-permute-start(bf16[576,256]{1,0:T(8,128)(2,1)} %get-tuple-element.44), channel_id=1, source_target_pairs={{0,128},{128,256},{256,384},{384,0},{1,129},{129,257},{257,385},{3... | collective-permute-start | bytes 884744 | tf_op jit(solution)/shard_map/ppermute | solution.py:23
  140.0 0.0 collective-permute-done.9.refs_1_
  140.0 2.5 %collective-permute-start.15 = (bf16[576,256]{1,0:T(8,128)(2,1)}, bf16[576,256]{1,0:T(8,128)(2,1)}, u32[]{:S(2)}, u32[]{:S(2)}) collective-permute-start(bf16[576,256]{1,0:T(8,128)(2,1)} %get-tuple-element.45), channel_id=1, source_target_pairs={{0,384},{128,0},{256,128},{384,256},{1,385},{129,1},{257,129},{385... | collective-permute-start | bytes 884744 | tf_op jit(solution)/shard_map/ppermute | solution.py:23
  142.5 9.5 %collective-permute-done.10.refs_2_ = bf16[128,4224]{1,0:T(8,128)(2,1)} collective-permute-done((bf16[128,4224]{1,0:T(8,128)(2,1)}, bf16[128,4224]{1,0:T(8,128)(2,1)}, u32[]{:S(2)}, u32[]{:S(2)}) %collective-permute-start.10) | collective-permute-done | bytes 1081376 | tf_op jit(solution)/shard_map/ppermute | solution.py:23
  152.0 6.0 %collective-permute-done.11.refs_3_ = bf16[128,4224]{1,0:T(8,128)(2,1)} collective-permute-done((bf16[128,4224]{1,0:T(8,128)(2,1)}, bf16[128,4224]{1,0:T(8,128)(2,1)}, u32[]{:S(2)}, u32[]{:S(2)}) %collective-permute-start.11) | collective-permute-done | bytes 1081376 | tf_op jit(solution)/shard_map/ppermute | solution.py:23
  158.1 2.0 %collective-permute-start.12 = (bf16[128,4224]{1,0:T(8,128)(2,1)}, bf16[128,4224]{1,0:T(8,128)(2,1)}, u32[]{:S(2)}, u32[]{:S(2)}) collective-permute-start(bf16[128,4224]{1,0:T(8,128)(2,1)} %get-tuple-element.41.refs_6_.refs_7_.refs_8_), channel_id=1, source_target_pairs={{0,128},{128,256},{256,384},{384,0},{1,129},{129,257},{257,385},{3... | collective-permute-start | bytes 3244040 | tf_op jit(solution)/shard_map/ppermute | solution.py:23
  160.1 3.9 %collective-permute-start.13 = (bf16[128,4224]{1,0:T(8,128)(2,1)}, bf16[128,4224]{1,0:T(8,128)(2,1)}, u32[]{:S(2)}, u32[]{:S(2)}) collective-permute-start(bf16[128,4224]{1,0:T(8,128)(2,1)} %get-tuple-element.42.refs_18_.refs_19_.refs_20_), channel_id=1, source_target_pairs={{0,384},{128,0},{256,128},{384,256},{1,385},{129,1},{257,129},{385... | collective-permute-start | bytes 3244040 | tf_op jit(solution)/shard_map/ppermute | solution.py:23
  164.1 0.0 collective-permute-done.14.refs_1_
  164.1 6.0 %shard_map.126.sums_ref = f32[576,2048]{1,0:T(8,128)S(1)} custom-call(f32[1,128]{1,0:T(1,128)S(1)} %compare_convert_fusion.own_ref, bf16[576,256]{1,0:T(8,128)(2,1)S(1)} %copy-done.3, bf16[576,256]{1,0:T(8,128)(2,1)} %collective-permute-done.14.refs_1_, bf16[576,256]{1,0:T(8,128)(2,1)} %collective-permute-done.15.refs_2_, ...), custom_call_target="tpu_custom_call" | custom-call | flops 999999995904 | bytes 1048576 | tf_op jit(solution)/shard_map/pallas_call | solution.py:47
  170.1 14.7 %collective-permute-done.12.first_ref = bf16[128,4224]{1,0:T(8,128)(2,1)} collective-permute-done((bf16[128,4224]{1,0:T(8,128)(2,1)}, bf16[128,4224]{1,0:T(8,128)(2,1)}, u32[]{:S(2)}, u32[]{:S(2)}) %collective-permute-start.12) | collective-permute-done | bytes 1081376 | tf_op jit(solution)/shard_map/ppermute | solution.py:23
  184.8 3.1 %collective-permute-done.13.second_ref = bf16[128,4224]{1,0:T(8,128)(2,1)} collective-permute-done((bf16[128,4224]{1,0:T(8,128)(2,1)}, bf16[128,4224]{1,0:T(8,128)(2,1)}, u32[]{:S(2)}, u32[]{:S(2)}) %collective-permute-start.13) | collective-permute-done | bytes 1081376 | tf_op jit(solution)/shard_map/ppermute | solution.py:23
  187.9 4.1 %shard_map.127 = (bf16[192,2048]{1,0:T(8,128)(2,1)}, bf16[192,2048]{1,0:T(8,128)(2,1)}, bf16[192,2048]{1,0:T(8,128)(2,1)}) custom-call(f32[1,128]{1,0:T(1,128)S(1)} %compare_convert_fusion.own_ref, bf16[576,256]{1,0:T(8,128)(2,1)} %collective-permute-done.7.acts_ref, bf16[128,4224]{1,0:T(8,128)(2,1)} %collective-permute-done.12.first_ref, ...), custom_call_target="tpu_custom_call" | custom-call | flops 1 | bytes 1048576 | tf_op jit(solution)/shard_map/pallas_call | solution.py:47
  192.0 1.5 reshape.268.home_ref
  193.5 1.3 shard_map.128
  (29 shorter events, 0.1 us)
Async XLA Ops:
  0.6 11.4 %copy-start.7 = (bf16[16,8]{0,1:T(8,128)(2,1)S(1)}, bf16[16,8]{0,1:T(8,128)(2,1)}, u32[]{:S(2)}) copy-start(bf16[16,8]{0,1:T(8,128)(2,1)} %param.11) | copy-start | bytes 772
  0.6 11.4 %copy-start.6 = (s32[16,8]{0,1:T(8,128)S(1)}, s32[16,8]{0,1:T(8,128)}, u32[]{:S(2)}) copy-start(s32[16,8]{0,1:T(8,128)} %param.12) | copy-start | bytes 1540
  2.3 64.1 %collective-permute-start.3 = (bf16[576,2048]{1,0:T(8,128)(2,1)S(1)}, bf16[576,2048]{1,0:T(8,128)(2,1)}, u32[]{:S(2)}, u32[]{:S(2)}) collective-permute-start(bf16[576,2048]{1,0:T(8,128)(2,1)S(1)} %shard_map.121.refs_2_), channel_id=1, source_target_pairs={{0,128},{128,256},{256,384},{384,0},{1,129},{129,257},{257,385},{3... | collective-permute-start | bytes 7077896 | tf_op jit(solution)/shard_map/ppermute | solution.py:23
  10.1 56.4 %collective-permute-start.4 = (bf16[576,2048]{1,0:T(8,128)(2,1)S(1)}, bf16[576,2048]{1,0:T(8,128)(2,1)}, u32[]{:S(2)}, u32[]{:S(2)}) collective-permute-start(bf16[576,2048]{1,0:T(8,128)(2,1)S(1)} %shard_map.121.refs_2_), channel_id=1, source_target_pairs={{0,384},{128,0},{256,128},{384,256},{1,385},{129,1},{257,129},{385... | collective-permute-start | bytes 7077896 | tf_op jit(solution)/shard_map/ppermute | solution.py:23
  12.1 29.5 %copy-start.1 = (s32[8,16]{1,0:T(8,128)}, s32[8,16]{1,0:T(8,128)S(1)}, u32[]{:S(2)}) copy-start(s32[8,16]{1,0:T(8,128)S(1)} %fusion.6.rank_ref) | copy-start | bytes 1540
  41.5 17.6 %copy-start.4 = (bf16[64,4224]{1,0:T(8,128)(2,1)}, bf16[64,4224]{1,0:T(8,128)(2,1)S(1)}, u32[]{:S(2)}) copy-start(bf16[64,4224]{1,0:T(8,128)(2,1)S(1)} %all_gather.3.refs_0_) | copy-start | bytes 1622020
  41.5 13.6 %collective-permute-start = (bf16[64,4224]{1,0:T(8,128)(2,1)S(1)}, bf16[64,4224]{1,0:T(8,128)(2,1)S(1)}, u32[]{:S(2)}, u32[]{:S(2)}) collective-permute-start(bf16[64,4224]{1,0:T(8,128)(2,1)S(1)} %all_gather.3.refs_0_), channel_id=1, source_target_pairs={{0,30},{2,0},{4,2},{6,4},{8,6},{10,8},{12,10},{14,12},{16,14},{18,... | collective-permute-start | bytes 1622024 | tf_op jit(solution)/shard_map/ppermute | solution.py:23
  47.0 22.6 %collective-permute-start.1 = (bf16[64,4224]{1,0:T(8,128)(2,1)S(1)}, bf16[64,4224]{1,0:T(8,128)(2,1)}, u32[]{:S(2)}, u32[]{:S(2)}) collective-permute-start(bf16[64,4224]{1,0:T(8,128)(2,1)S(1)} %all_gather.3.refs_0_), channel_id=1, source_target_pairs={{0,2},{2,4},{4,6},{6,8},{8,10},{10,12},{12,14},{14,16},{16,18},{18... | collective-permute-start | bytes 1622024 | tf_op jit(solution)/shard_map/ppermute | solution.py:23
  55.1 4.0 %copy-start.5 = (bf16[64,4224]{1,0:T(8,128)(2,1)}, bf16[64,4224]{1,0:T(8,128)(2,1)S(1)}, u32[]{:S(2)}) copy-start(bf16[64,4224]{1,0:T(8,128)(2,1)S(1)} %collective-permute-done.refs_1_) | copy-start | bytes 1622020
  55.1 14.5 %collective-permute-start.2 = (bf16[64,4224]{1,0:T(8,128)(2,1)S(1)}, bf16[64,4224]{1,0:T(8,128)(2,1)}, u32[]{:S(2)}, u32[]{:S(2)}) collective-permute-start(bf16[64,4224]{1,0:T(8,128)(2,1)S(1)} %all_gather.3.refs_0_), channel_id=1, source_target_pairs={{4,0},{30,2},{8,4},{2,6},{12,8},{6,10},{16,12},{10,14},{20,16},{14... | collective-permute-start | bytes 1622024 | tf_op jit(solution)/shard_map/ppermute | solution.py:314
  62.0 20.9 %all-to-all-start = ((bf16[8,16,4224]{2,1,0:T(8,128)(2,1)}), bf16[8,16,4224]{2,1,0:T(8,128)(2,1)}, u32[]{:S(2)}, u32[]{:S(2)}) async-start(bf16[8,16,4224]{2,1,0:T(8,128)(2,1)} %bitcast.2), calls=%async_computation | async-start | bytes 2162688 | tf_op jit(solution)/shard_map/all_to_all | solution.py:143
  69.6 37.4 %collective-permute-start.5 = (bf16[288,2048]{1,0:T(8,128)(2,1)}, bf16[288,2048]{1,0:T(8,128)(2,1)}, u32[]{:S(2)}, u32[]{:S(2)}) collective-permute-start(bf16[288,2048]{1,0:T(8,128)(2,1)} %get-tuple-element.37), channel_id=1, source_target_pairs={{0,128},{128,256},{256,384},{384,0},{1,129},{129,257},{257,385},{3... | collective-permute-start | bytes 3538952 | tf_op jit(solution)/shard_map/ppermute | solution.py:23
  73.2 36.1 %collective-permute-start.6 = (bf16[288,2048]{1,0:T(8,128)(2,1)}, bf16[288,2048]{1,0:T(8,128)(2,1)}, u32[]{:S(2)}, u32[]{:S(2)}) collective-permute-start(bf16[288,2048]{1,0:T(8,128)(2,1)} %get-tuple-element.38), channel_id=1, source_target_pairs={{0,384},{128,0},{256,128},{384,256},{1,385},{129,1},{257,129},{385... | collective-permute-start | bytes 3538952 | tf_op jit(solution)/shard_map/ppermute | solution.py:23
  82.9 20.6 %all-to-all-start.1 = ((bf16[8,16,4224]{2,1,0:T(8,128)(2,1)}), bf16[8,16,4224]{2,1,0:T(8,128)(2,1)}, u32[]{:S(2)}, u32[]{:S(2)}) async-start(bf16[8,16,4224]{2,1,0:T(8,128)(2,1)} %bitcast.7), calls=%async_computation.1 | async-start | bytes 2162688 | tf_op jit(solution)/shard_map/all_to_all | solution.py:143
  88.0 48.1 %collective-permute-start.8 = (bf16[128,4224]{1,0:T(8,128)(2,1)}, bf16[128,4224]{1,0:T(8,128)(2,1)}, u32[]{:S(2)}, u32[]{:S(2)}) collective-permute-start(bf16[128,4224]{1,0:T(8,128)(2,1)} %bitcast.3.refs_0_.refs_3_.refs_4_.refs_5_), channel_id=1, source_target_pairs={{0,128},{128,256},{256,384},{384,0},{1,129},{129,257},{257,385},{3... | collective-permute-start | bytes 3244040 | tf_op jit(solution)/shard_map/ppermute | solution.py:23
  91.5 48.5 %collective-permute-start.9 = (bf16[128,4224]{1,0:T(8,128)(2,1)}, bf16[128,4224]{1,0:T(8,128)(2,1)}, u32[]{:S(2)}, u32[]{:S(2)}) collective-permute-start(bf16[128,4224]{1,0:T(8,128)(2,1)} %bitcast.3.refs_0_.refs_3_.refs_4_.refs_5_), channel_id=1, source_target_pairs={{0,384},{128,0},{256,128},{384,256},{1,385},{129,1},{257,129},{385... | collective-permute-start | bytes 3244040 | tf_op jit(solution)/shard_map/ppermute | solution.py:23
  103.4 48.6 %collective-permute-start.10 = (bf16[128,4224]{1,0:T(8,128)(2,1)}, bf16[128,4224]{1,0:T(8,128)(2,1)}, u32[]{:S(2)}, u32[]{:S(2)}) collective-permute-start(bf16[128,4224]{1,0:T(8,128)(2,1)} %bitcast.8.refs_1_.refs_12_.refs_13_.refs_14_), channel_id=1, source_target_pairs={{0,128},{128,256},{256,384},{384,0},{1,129},{129,257},{257,385},{3... | collective-permute-start | bytes 3244040 | tf_op jit(solution)/shard_map/ppermute | solution.py:23
  107.0 51.1 %collective-permute-start.11 = (bf16[128,4224]{1,0:T(8,128)(2,1)}, bf16[128,4224]{1,0:T(8,128)(2,1)}, u32[]{:S(2)}, u32[]{:S(2)}) collective-permute-start(bf16[128,4224]{1,0:T(8,128)(2,1)} %bitcast.8.refs_1_.refs_12_.refs_13_.refs_14_), channel_id=1, source_target_pairs={{0,384},{128,0},{256,128},{384,256},{1,385},{129,1},{257,129},{385... | collective-permute-start | bytes 3244040 | tf_op jit(solution)/shard_map/ppermute | solution.py:23
  109.3 0.9 copy-start
  121.8 70.2 %all-to-all-start.2 = ((bf16[128,2,2176]{2,1,0:T(2,128)(2,1)}), bf16[128,2,2176]{2,1,0:T(2,128)(2,1)}, u32[]{:S(2)}, u32[]{:S(2)}) async-start(bf16[128,2,2176]{2,1,0:T(2,128)(2,1)} %reshape.267), calls=%async_computation.2 | async-start | bytes 2228224 | tf_op jit(solution)/shard_map/all_to_all | solution.py:346
  132.7 37.4 %collective-permute-start.7 = (bf16[576,256]{1,0:T(8,128)(2,1)}, bf16[576,256]{1,0:T(8,128)(2,1)}, u32[]{:S(2)}, u32[]{:S(2)}) collective-permute-start(bf16[576,256]{1,0:T(8,128)(2,1)} %get-tuple-element.40), channel_id=1, source_target_pairs={{0,256},{128,384},{256,0},{384,128},{1,257},{129,385},{257,1},{385... | collective-permute-start | bytes 884744 | tf_op jit(solution)/shard_map/ppermute | solution.py:23
  136.0 28.0 %collective-permute-start.14 = (bf16[576,256]{1,0:T(8,128)(2,1)}, bf16[576,256]{1,0:T(8,128)(2,1)}, u32[]{:S(2)}, u32[]{:S(2)}) collective-permute-start(bf16[576,256]{1,0:T(8,128)(2,1)} %get-tuple-element.44), channel_id=1, source_target_pairs={{0,128},{128,256},{256,384},{384,0},{1,129},{129,257},{257,385},{3... | collective-permute-start | bytes 884744 | tf_op jit(solution)/shard_map/ppermute | solution.py:23
  140.0 24.0 %collective-permute-start.15 = (bf16[576,256]{1,0:T(8,128)(2,1)}, bf16[576,256]{1,0:T(8,128)(2,1)}, u32[]{:S(2)}, u32[]{:S(2)}) collective-permute-start(bf16[576,256]{1,0:T(8,128)(2,1)} %get-tuple-element.45), channel_id=1, source_target_pairs={{0,384},{128,0},{256,128},{384,256},{1,385},{129,1},{257,129},{385... | collective-permute-start | bytes 884744 | tf_op jit(solution)/shard_map/ppermute | solution.py:23
  158.1 6.0 %copy-start.3 = (bf16[576,256]{1,0:T(8,128)(2,1)S(1)}, bf16[576,256]{1,0:T(8,128)(2,1)}, u32[]{:S(2)}) copy-start(bf16[576,256]{1,0:T(8,128)(2,1)} %get-tuple-element.43.refs_0_) | copy-start | bytes 884740
  158.1 26.7 %collective-permute-start.12 = (bf16[128,4224]{1,0:T(8,128)(2,1)}, bf16[128,4224]{1,0:T(8,128)(2,1)}, u32[]{:S(2)}, u32[]{:S(2)}) collective-permute-start(bf16[128,4224]{1,0:T(8,128)(2,1)} %get-tuple-element.41.refs_6_.refs_7_.refs_8_), channel_id=1, source_target_pairs={{0,128},{128,256},{256,384},{384,0},{1,129},{129,257},{257,385},{3... | collective-permute-start | bytes 3244040 | tf_op jit(solution)/shard_map/ppermute | solution.py:23
  160.1 27.8 %collective-permute-start.13 = (bf16[128,4224]{1,0:T(8,128)(2,1)}, bf16[128,4224]{1,0:T(8,128)(2,1)}, u32[]{:S(2)}, u32[]{:S(2)}) collective-permute-start(bf16[128,4224]{1,0:T(8,128)(2,1)} %get-tuple-element.42.refs_18_.refs_19_.refs_20_), channel_id=1, source_target_pairs={{0,384},{128,0},{256,128},{384,256},{1,385},{129,1},{257,129},{385... | collective-permute-start | bytes 3244040 | tf_op jit(solution)/shard_map/ppermute | solution.py:23
  192.0 1.5 copy-start.2

commit v13 on v12

--- a/solution.py
+++ b/solution.py
@@ -338,7 +338,7 @@
         functools.partial(forward_kernel, len(rows)),
         (*small, *weights),
         [sds((count, width + LANES), BF16), *[pltpu.HBM((3 * share, count), BF16)] * DP],
-        in_specs=[*[whole(a) for a in small], *[pl.BlockSpec(memory_space=pl.ANY)] * 5],
+        in_specs=[*[whole(a) for a in small], pl.BlockSpec(memory_space=pltpu.VMEM), *[pl.BlockSpec(memory_space=pl.ANY)] * 4],
         scratch=[pltpu.VMEM((DP, 3 * share, width), BF16), pltpu.SemaphoreType.DMA((5,))],
         vmem=36,
         cost=LONG,

time: 197 us -> 197 us (level)
  no operation moved by 1% of the time
where the time goes in v13:
time: 197 us; the launch traced here: 195 us
  starting transfers between devices  73.8 us (37%)
  waiting for transfers between devices  53.8 us (27%)
  Pallas kernels  33.3 us (17%)
  blocking collectives  28.3 us (14%)
  local copies, waits for them, and re-layouts  3.71 us (2%)
    ppermute x15, starting transfers between devices, shift(): return lax.ppermute(a, axis, [(i, (i + k) % size) for i in range(size)])  50.4 us
    ppermute x15, waiting for transfers between devices, shift(): return lax.ppermute(a, axis, [(i, (i + k) % size) for i in range(size)])  39.6 us
    pallas_call x7, Pallas kernels, call(): pl.pallas_call(kernel, grid=grid, out_shape=out_shape, in_specs=in_specs...  28.5 us
    all_gather x1, blocking collectives, body(): lax.all_gather(payload, 'z', axis=0, tiled=True, axis_index_groups=groups)  28.3 us
    all_to_all x2, waiting for transfers between devices, to_experts(): lax.all_to_all(sent.reshape(YC, -1, sent.shape[1]), ('y', 'core'), split_...  14.1 us
    all_to_all x1, starting transfers between devices, body(): lax.all_to_all(back.reshape(experts, CAP, -1), ('y', 'core', 'z'), split_...  10.8 us
    all_to_all x2, starting transfers between devices, to_experts(): lax.all_to_all(sent.reshape(YC, -1, sent.shape[1]), ('y', 'core'), split_...  8.7 us
    pallas_call x2, Pallas kernels, move(): pl.pallas_call(functools.partial(move_kernel, plan, len(arrays)), out_sha...  4.78 us
  transfers between devices with their start and end apart: 19, of which 7 were waited for; matrix products, arithmetic and copies ran while one was open for 1% of the time, Pallas kernels for 16%

profile of v13, /device:TPU:6, one launch (start us, length us, event | category | flops | bytes accessed | tf_op | source)
XLA Modules:
  0.0 194.8 jit_solution(12782663847920481566)
XLA Ops:
  0.7 1.6 shard_map.121.refs_2_
  2.3 7.8 %collective-permute-start.3 = (bf16[576,2048]{1,0:T(8,128)(2,1)S(1)}, bf16[576,2048]{1,0:T(8,128)(2,1)}, u32[]{:S(2)}, u32[]{:S(2)}) collective-permute-start(bf16[576,2048]{1,0:T(8,128)(2,1)S(1)} %shard_map.121.refs_2_), channel_id=1, source_target_pairs={{0,128},{128,256},{256,384},{384,0},{1,129},{129,257},{257,385},{3... | collective-permute-start | bytes 7077896 | tf_op jit(solution)/shard_map/ppermute | solution.py:23
  10.1 1.9 collective-permute-start.4
  12.1 0.0 copy-start.1
  12.1 1.1 shard_map.119
  13.2 28.3 %all_gather.3.refs_0_ = bf16[64,4224]{1,0:T(8,128)(2,1)S(1)} all-gather(bf16[16,4224]{1,0:T(8,128)(2,1)S(1)} %shard_map.119), channel_id=1, replica_groups={{0,8,16,24},{2,10,18,26},{4,12,20,28},{6,14,22,30},{1,9,17,25},{3,11,19..., dimensions={0}, use_global_device_ids=true | all-gather | bytes 675840 | tf_op jit(solution)/shard_map/all_gather | solution.py:305
  41.5 5.5 %collective-permute-start = (bf16[64,4224]{1,0:T(8,128)(2,1)S(1)}, bf16[64,4224]{1,0:T(8,128)(2,1)S(1)}, u32[]{:S(2)}, u32[]{:S(2)}) collective-permute-start(bf16[64,4224]{1,0:T(8,128)(2,1)S(1)} %all_gather.3.refs_0_), channel_id=1, source_target_pairs={{0,30},{2,0},{4,2},{6,4},{8,6},{10,8},{12,10},{14,12},{16,14},{18,... | collective-permute-start | bytes 1622024 | tf_op jit(solution)/shard_map/ppermute | solution.py:23
  47.0 1.9 collective-permute-start.1
  48.9 6.2 %collective-permute-done.refs_1_ = bf16[64,4224]{1,0:T(8,128)(2,1)S(1)} collective-permute-done((bf16[64,4224]{1,0:T(8,128)(2,1)S(1)}, bf16[64,4224]{1,0:T(8,128)(2,1)S(1)}, u32[]{:S(2)}, u32[]{:S(2)}) %collective-permute-start) | collective-permute-done | bytes 540704 | tf_op jit(solution)/shard_map/ppermute | solution.py:23
  55.1 3.9 %collective-permute-start.2 = (bf16[64,4224]{1,0:T(8,128)(2,1)S(1)}, bf16[64,4224]{1,0:T(8,128)(2,1)}, u32[]{:S(2)}, u32[]{:S(2)}) collective-permute-start(bf16[64,4224]{1,0:T(8,128)(2,1)S(1)} %all_gather.3.refs_0_), channel_id=1, source_target_pairs={{4,0},{30,2},{8,4},{2,6},{12,8},{6,10},{16,12},{10,14},{20,16},{14... | collective-permute-start | bytes 1622024 | tf_op jit(solution)/shard_map/ppermute | solution.py:314
  59.0 0.1 fusion.2.pick_ref
  59.1 2.9 %shard_map.120 = bf16[128,4224]{1,0:T(8,128)(2,1)} custom-call(bf16[16,128]{1,0:T(8,128)(2,1)S(1)} %fusion.2.pick_ref, bf16[64,4224]{1,0:T(8,128)(2,1)} %copy-done.4, bf16[64,4224]{1,0:T(8,128)(2,1)} %copy-done.5), custom_call_target="tpu_custom_call" | custom-call | flops 1 | bytes 1048576 | tf_op jit(solution)/shard_map/pallas_call | solution.py:47
  62.0 4.5 %all-to-all-start = ((bf16[8,16,4224]{2,1,0:T(8,128)(2,1)}), bf16[8,16,4224]{2,1,0:T(8,128)(2,1)}, u32[]{:S(2)}, u32[]{:S(2)}) async-start(bf16[8,16,4224]{2,1,0:T(8,128)(2,1)} %bitcast.2), calls=%async_computation | async-start | bytes 2162688 | tf_op jit(solution)/shard_map/all_to_all | solution.py:143
  66.5 0.0 collective-permute-done.4.refs_1_.refs_3_
  66.5 3.1 %shard_map.122 = (bf16[288,2048]{1,0:T(8,128)(2,1)}, bf16[288,2048]{1,0:T(8,128)(2,1)}) custom-call(bf16[576,2048]{1,0:T(8,128)(2,1)} %collective-permute-done.3.refs_0_.refs_4_, bf16[576,2048]{1,0:T(8,128)(2,1)} %collective-permute-done.4.refs_1_.refs_3_), custom_call_target="tpu_custom_call" | custom-call | flops 1 | bytes 1048576 | tf_op jit(solution)/shard_map/pallas_call | solution.py:77
  69.6 0.0 collective-permute-done.2.refs_1_
  69.6 3.5 %collective-permute-start.5 = (bf16[288,2048]{1,0:T(8,128)(2,1)}, bf16[288,2048]{1,0:T(8,128)(2,1)}, u32[]{:S(2)}, u32[]{:S(2)}) collective-permute-start(bf16[288,2048]{1,0:T(8,128)(2,1)} %get-tuple-element.37), channel_id=1, source_target_pairs={{0,128},{128,256},{256,384},{384,0},{1,129},{129,257},{257,385},{3... | collective-permute-start | bytes 3538952 | tf_op jit(solution)/shard_map/ppermute | solution.py:23
  73.2 2.3 %collective-permute-start.6 = (bf16[288,2048]{1,0:T(8,128)(2,1)}, bf16[288,2048]{1,0:T(8,128)(2,1)}, u32[]{:S(2)}, u32[]{:S(2)}) collective-permute-start(bf16[288,2048]{1,0:T(8,128)(2,1)} %get-tuple-element.38), channel_id=1, source_target_pairs={{0,384},{128,0},{256,128},{384,256},{1,385},{129,1},{257,129},{385... | collective-permute-start | bytes 3538952 | tf_op jit(solution)/shard_map/ppermute | solution.py:23
  75.5 2.9 %shard_map.123 = bf16[128,4224]{1,0:T(8,128)(2,1)} custom-call(bf16[16,128]{1,0:T(8,128)(2,1)S(1)} %fusion.2.pick_ref, bf16[64,4224]{1,0:T(8,128)(2,1)} %collective-permute-done.1.refs_0_, bf16[64,4224]{1,0:T(8,128)(2,1)} %collective-permute-done.2.refs_1_), custom_call_target="tpu_custom_call" | custom-call | flops 999999995904 | bytes 1048576 | tf_op jit(solution)/shard_map/pallas_call | solution.py:47
  78.4 4.5 %all-to-all-done = bf16[8,16,4224]{2,1,0:T(8,128)(2,1)} async-done(((bf16[8,16,4224]{2,1,0:T(8,128)(2,1)}), bf16[8,16,4224]{2,1,0:T(8,128)(2,1)}, u32[]{:S(2)}, u32[]{:S(2)}) %all-to-all-start) | async-done | bytes 1081376 | tf_op jit(solution)/shard_map/all_to_all | solution.py:143
  82.9 4.2 %all-to-all-start.1 = ((bf16[8,16,4224]{2,1,0:T(8,128)(2,1)}), bf16[8,16,4224]{2,1,0:T(8,128)(2,1)}, u32[]{:S(2)}, u32[]{:S(2)}) async-start(bf16[8,16,4224]{2,1,0:T(8,128)(2,1)} %bitcast.7), calls=%async_computation.1 | async-start | bytes 2162688 | tf_op jit(solution)/shard_map/all_to_all | solution.py:143
  87.2 0.8 fusion.perm_ref
  88.0 3.5 %collective-permute-start.8 = (bf16[128,4224]{1,0:T(8,128)(2,1)}, bf16[128,4224]{1,0:T(8,128)(2,1)}, u32[]{:S(2)}, u32[]{:S(2)}) collective-permute-start(bf16[128,4224]{1,0:T(8,128)(2,1)} %bitcast.3.refs_0_.refs_3_.refs_4_.refs_5_), channel_id=1, source_target_pairs={{0,128},{128,256},{256,384},{384,0},{1,129},{129,257},{257,385},{3... | collective-permute-start | bytes 3244040 | tf_op jit(solution)/shard_map/ppermute | solution.py:23
  91.5 2.3 %collective-permute-start.9 = (bf16[128,4224]{1,0:T(8,128)(2,1)}, bf16[128,4224]{1,0:T(8,128)(2,1)}, u32[]{:S(2)}, u32[]{:S(2)}) collective-permute-start(bf16[128,4224]{1,0:T(8,128)(2,1)} %bitcast.3.refs_0_.refs_3_.refs_4_.refs_5_), channel_id=1, source_target_pairs={{0,384},{128,0},{256,128},{384,256},{1,385},{129,1},{257,129},{385... | collective-permute-start | bytes 3244040 | tf_op jit(solution)/shard_map/ppermute | solution.py:23
  93.8 9.6 %all-to-all-done.1 = bf16[8,16,4224]{2,1,0:T(8,128)(2,1)} async-done(((bf16[8,16,4224]{2,1,0:T(8,128)(2,1)}), bf16[8,16,4224]{2,1,0:T(8,128)(2,1)}, u32[]{:S(2)}, u32[]{:S(2)}) %all-to-all-start.1) | async-done | bytes 1081376 | tf_op jit(solution)/shard_map/all_to_all | solution.py:143
  103.4 3.5 %collective-permute-start.10 = (bf16[128,4224]{1,0:T(8,128)(2,1)}, bf16[128,4224]{1,0:T(8,128)(2,1)}, u32[]{:S(2)}, u32[]{:S(2)}) collective-permute-start(bf16[128,4224]{1,0:T(8,128)(2,1)} %bitcast.8.refs_1_.refs_12_.refs_13_.refs_14_), channel_id=1, source_target_pairs={{0,128},{128,256},{256,384},{384,0},{1,129},{129,257},{257,385},{3... | collective-permute-start | bytes 3244040 | tf_op jit(solution)/shard_map/ppermute | solution.py:23
  107.0 2.3 %collective-permute-start.11 = (bf16[128,4224]{1,0:T(8,128)(2,1)}, bf16[128,4224]{1,0:T(8,128)(2,1)}, u32[]{:S(2)}, u32[]{:S(2)}) collective-permute-start(bf16[128,4224]{1,0:T(8,128)(2,1)} %bitcast.8.refs_1_.refs_12_.refs_13_.refs_14_), channel_id=1, source_target_pairs={{0,384},{128,0},{256,128},{384,256},{1,385},{129,1},{257,129},{385... | collective-permute-start | bytes 3244040 | tf_op jit(solution)/shard_map/ppermute | solution.py:23
  109.3 0.0 copy-start
  109.3 0.9 copy-done
  110.2 10.3 %shard_map.124 = (bf16[256,2176]{1,0:T(8,128)(2,1)S(1)}, bf16[576,256]{1,0:T(8,128)(2,1)}, bf16[576,256]{1,0:T(8,128)(2,1)}, bf16[576,256]{1,0:T(8,128)(2,1)}, bf16[576,256]{1,0:T(8,128)(2,1)}) custom-call(bf16[16,128]{1,0:T(8,128)(2,1)S(1)} %iota.42.own_ref, bf16[256,256]{1,0:T(8,128)(2,1)S(1)} %copy-done, ...), custom_call_target="tpu_custom_call" | custom-call | flops 999999995904 | bytes 1048576 | tf_op jit(solution)/shard_map/pallas_call | solution.py:47
  120.5 1.3 reshape.267
  121.8 10.8 %all-to-all-start.2 = ((bf16[128,2,2176]{2,1,0:T(2,128)(2,1)}), bf16[128,2,2176]{2,1,0:T(2,128)(2,1)}, u32[]{:S(2)}, u32[]{:S(2)}) async-start(bf16[128,2,2176]{2,1,0:T(2,128)(2,1)} %reshape.267), calls=%async_computation.2 | async-start | bytes 2228224 | tf_op jit(solution)/shard_map/all_to_all | solution.py:346
  132.7 3.4 %collective-permute-start.7 = (bf16[576,256]{1,0:T(8,128)(2,1)}, bf16[576,256]{1,0:T(8,128)(2,1)}, u32[]{:S(2)}, u32[]{:S(2)}) collective-permute-start(bf16[576,256]{1,0:T(8,128)(2,1)} %get-tuple-element.40), channel_id=1, source_target_pairs={{0,256},{128,384},{256,0},{384,128},{1,257},{129,385},{257,1},{385... | collective-permute-start | bytes 884744 | tf_op jit(solution)/shard_map/ppermute | solution.py:23
  136.0 0.0 collective-permute-done.8.refs_0_
  136.0 4.0 %collective-permute-start.14 = (bf16[576,256]{1,0:T(8,128)(2,1)}, bf16[576,256]{1,0:T(8,128)(2,1)}, u32[]{:S(2)}, u32[]{:S(2)}) collective-permute-start(bf16[576,256]{1,0:T(8,128)(2,1)} %get-tuple-element.44), channel_id=1, source_target_pairs={{0,128},{128,256},{256,384},{384,0},{1,129},{129,257},{257,385},{3... | collective-permute-start | bytes 884744 | tf_op jit(solution)/shard_map/ppermute | solution.py:23
  140.0 0.0 collective-permute-done.9.refs_1_
  140.0 2.5 %collective-permute-start.15 = (bf16[576,256]{1,0:T(8,128)(2,1)}, bf16[576,256]{1,0:T(8,128)(2,1)}, u32[]{:S(2)}, u32[]{:S(2)}) collective-permute-start(bf16[576,256]{1,0:T(8,128)(2,1)} %get-tuple-element.45), channel_id=1, source_target_pairs={{0,384},{128,0},{256,128},{384,256},{1,385},{129,1},{257,129},{385... | collective-permute-start | bytes 884744 | tf_op jit(solution)/shard_map/ppermute | solution.py:23
  142.5 9.5 %collective-permute-done.10.refs_2_ = bf16[128,4224]{1,0:T(8,128)(2,1)} collective-permute-done((bf16[128,4224]{1,0:T(8,128)(2,1)}, bf16[128,4224]{1,0:T(8,128)(2,1)}, u32[]{:S(2)}, u32[]{:S(2)}) %collective-permute-start.10) | collective-permute-done | bytes 1081376 | tf_op jit(solution)/shard_map/ppermute | solution.py:23
  152.0 6.0 %collective-permute-done.11.refs_3_ = bf16[128,4224]{1,0:T(8,128)(2,1)} collective-permute-done((bf16[128,4224]{1,0:T(8,128)(2,1)}, bf16[128,4224]{1,0:T(8,128)(2,1)}, u32[]{:S(2)}, u32[]{:S(2)}) %collective-permute-start.11) | collective-permute-done | bytes 1081376 | tf_op jit(solution)/shard_map/ppermute | solution.py:23
  158.1 2.0 %collective-permute-start.12 = (bf16[128,4224]{1,0:T(8,128)(2,1)}, bf16[128,4224]{1,0:T(8,128)(2,1)}, u32[]{:S(2)}, u32[]{:S(2)}) collective-permute-start(bf16[128,4224]{1,0:T(8,128)(2,1)} %get-tuple-element.41.refs_6_.refs_7_.refs_8_), channel_id=1, source_target_pairs={{0,128},{128,256},{256,384},{384,0},{1,129},{129,257},{257,385},{3... | collective-permute-start | bytes 3244040 | tf_op jit(solution)/shard_map/ppermute | solution.py:23
  160.1 3.9 %collective-permute-start.13 = (bf16[128,4224]{1,0:T(8,128)(2,1)}, bf16[128,4224]{1,0:T(8,128)(2,1)}, u32[]{:S(2)}, u32[]{:S(2)}) collective-permute-start(bf16[128,4224]{1,0:T(8,128)(2,1)} %get-tuple-element.42.refs_18_.refs_19_.refs_20_), channel_id=1, source_target_pairs={{0,384},{128,0},{256,128},{384,256},{1,385},{129,1},{257,129},{385... | collective-permute-start | bytes 3244040 | tf_op jit(solution)/shard_map/ppermute | solution.py:23
  164.1 0.0 collective-permute-done.14.refs_1_
  164.1 6.0 %shard_map.126.sums_ref = f32[576,2048]{1,0:T(8,128)S(1)} custom-call(f32[1,128]{1,0:T(1,128)S(1)} %compare_convert_fusion.own_ref, bf16[576,256]{1,0:T(8,128)(2,1)S(1)} %copy-done.3, bf16[576,256]{1,0:T(8,128)(2,1)} %collective-permute-done.14.refs_1_, bf16[576,256]{1,0:T(8,128)(2,1)} %collective-permute-done.15.refs_2_, ...), custom_call_target="tpu_custom_call" | custom-call | flops 999999995904 | bytes 1048576 | tf_op jit(solution)/shard_map/pallas_call | solution.py:47
  170.1 14.7 %collective-permute-done.12.first_ref = bf16[128,4224]{1,0:T(8,128)(2,1)} collective-permute-done((bf16[128,4224]{1,0:T(8,128)(2,1)}, bf16[128,4224]{1,0:T(8,128)(2,1)}, u32[]{:S(2)}, u32[]{:S(2)}) %collective-permute-start.12) | collective-permute-done | bytes 1081376 | tf_op jit(solution)/shard_map/ppermute | solution.py:23
  184.8 3.1 %collective-permute-done.13.second_ref = bf16[128,4224]{1,0:T(8,128)(2,1)} collective-permute-done((bf16[128,4224]{1,0:T(8,128)(2,1)}, bf16[128,4224]{1,0:T(8,128)(2,1)}, u32[]{:S(2)}, u32[]{:S(2)}) %collective-permute-start.13) | collective-permute-done | bytes 1081376 | tf_op jit(solution)/shard_map/ppermute | solution.py:23
  187.9 4.1 %shard_map.127 = (bf16[192,2048]{1,0:T(8,128)(2,1)}, bf16[192,2048]{1,0:T(8,128)(2,1)}, bf16[192,2048]{1,0:T(8,128)(2,1)}) custom-call(f32[1,128]{1,0:T(1,128)S(1)} %compare_convert_fusion.own_ref, bf16[576,256]{1,0:T(8,128)(2,1)} %collective-permute-done.7.acts_ref, bf16[128,4224]{1,0:T(8,128)(2,1)} %collective-permute-done.12.first_ref, ...), custom_call_target="tpu_custom_call" | custom-call | flops 1 | bytes 1048576 | tf_op jit(solution)/shard_map/pallas_call | solution.py:47
  192.0 1.5 reshape.268.home_ref
  193.5 1.3 shard_map.128
  (29 shorter events, 0.1 us)
Async XLA Ops:
  0.6 11.4 %copy-start.7 = (bf16[16,8]{0,1:T(8,128)(2,1)S(1)}, bf16[16,8]{0,1:T(8,128)(2,1)}, u32[]{:S(2)}) copy-start(bf16[16,8]{0,1:T(8,128)(2,1)} %param.11) | copy-start | bytes 772
  0.6 11.4 %copy-start.6 = (s32[16,8]{0,1:T(8,128)S(1)}, s32[16,8]{0,1:T(8,128)}, u32[]{:S(2)}) copy-start(s32[16,8]{0,1:T(8,128)} %param.12) | copy-start | bytes 1540
  2.3 64.1 %collective-permute-start.3 = (bf16[576,2048]{1,0:T(8,128)(2,1)S(1)}, bf16[576,2048]{1,0:T(8,128)(2,1)}, u32[]{:S(2)}, u32[]{:S(2)}) collective-permute-start(bf16[576,2048]{1,0:T(8,128)(2,1)S(1)} %shard_map.121.refs_2_), channel_id=1, source_target_pairs={{0,128},{128,256},{256,384},{384,0},{1,129},{129,257},{257,385},{3... | collective-permute-start | bytes 7077896 | tf_op jit(solution)/shard_map/ppermute | solution.py:23
  10.1 56.4 %collective-permute-start.4 = (bf16[576,2048]{1,0:T(8,128)(2,1)S(1)}, bf16[576,2048]{1,0:T(8,128)(2,1)}, u32[]{:S(2)}, u32[]{:S(2)}) collective-permute-start(bf16[576,2048]{1,0:T(8,128)(2,1)S(1)} %shard_map.121.refs_2_), channel_id=1, source_target_pairs={{0,384},{128,0},{256,128},{384,256},{1,385},{129,1},{257,129},{385... | collective-permute-start | bytes 7077896 | tf_op jit(solution)/shard_map/ppermute | solution.py:23
  12.1 29.5 %copy-start.1 = (s32[8,16]{1,0:T(8,128)}, s32[8,16]{1,0:T(8,128)S(1)}, u32[]{:S(2)}) copy-start(s32[8,16]{1,0:T(8,128)S(1)} %fusion.6.rank_ref) | copy-start | bytes 1540
  41.5 17.6 %copy-start.4 = (bf16[64,4224]{1,0:T(8,128)(2,1)}, bf16[64,4224]{1,0:T(8,128)(2,1)S(1)}, u32[]{:S(2)}) copy-start(bf16[64,4224]{1,0:T(8,128)(2,1)S(1)} %all_gather.3.refs_0_) | copy-start | bytes 1622020
  41.5 13.6 %collective-permute-start = (bf16[64,4224]{1,0:T(8,128)(2,1)S(1)}, bf16[64,4224]{1,0:T(8,128)(2,1)S(1)}, u32[]{:S(2)}, u32[]{:S(2)}) collective-permute-start(bf16[64,4224]{1,0:T(8,128)(2,1)S(1)} %all_gather.3.refs_0_), channel_id=1, source_target_pairs={{0,30},{2,0},{4,2},{6,4},{8,6},{10,8},{12,10},{14,12},{16,14},{18,... | collective-permute-start | bytes 1622024 | tf_op jit(solution)/shard_map/ppermute | solution.py:23
  47.0 22.6 %collective-permute-start.1 = (bf16[64,4224]{1,0:T(8,128)(2,1)S(1)}, bf16[64,4224]{1,0:T(8,128)(2,1)}, u32[]{:S(2)}, u32[]{:S(2)}) collective-permute-start(bf16[64,4224]{1,0:T(8,128)(2,1)S(1)} %all_gather.3.refs_0_), channel_id=1, source_target_pairs={{0,2},{2,4},{4,6},{6,8},{8,10},{10,12},{12,14},{14,16},{16,18},{18... | collective-permute-start | bytes 1622024 | tf_op jit(solution)/shard_map/ppermute | solution.py:23
  55.1 4.0 %copy-start.5 = (bf16[64,4224]{1,0:T(8,128)(2,1)}, bf16[64,4224]{1,0:T(8,128)(2,1)S(1)}, u32[]{:S(2)}) copy-start(bf16[64,4224]{1,0:T(8,128)(2,1)S(1)} %collective-permute-done.refs_1_) | copy-start | bytes 1622020
  55.1 14.5 %collective-permute-start.2 = (bf16[64,4224]{1,0:T(8,128)(2,1)S(1)}, bf16[64,4224]{1,0:T(8,128)(2,1)}, u32[]{:S(2)}, u32[]{:S(2)}) collective-permute-start(bf16[64,4224]{1,0:T(8,128)(2,1)S(1)} %all_gather.3.refs_0_), channel_id=1, source_target_pairs={{4,0},{30,2},{8,4},{2,6},{12,8},{6,10},{16,12},{10,14},{20,16},{14... | collective-permute-start | bytes 1622024 | tf_op jit(solution)/shard_map/ppermute | solution.py:314
  62.0 20.9 %all-to-all-start = ((bf16[8,16,4224]{2,1,0:T(8,128)(2,1)}), bf16[8,16,4224]{2,1,0:T(8,128)(2,1)}, u32[]{:S(2)}, u32[]{:S(2)}) async-start(bf16[8,16,4224]{2,1,0:T(8,128)(2,1)} %bitcast.2), calls=%async_computation | async-start | bytes 2162688 | tf_op jit(solution)/shard_map/all_to_all | solution.py:143
  69.6 37.4 %collective-permute-start.5 = (bf16[288,2048]{1,0:T(8,128)(2,1)}, bf16[288,2048]{1,0:T(8,128)(2,1)}, u32[]{:S(2)}, u32[]{:S(2)}) collective-permute-start(bf16[288,2048]{1,0:T(8,128)(2,1)} %get-tuple-element.37), channel_id=1, source_target_pairs={{0,128},{128,256},{256,384},{384,0},{1,129},{129,257},{257,385},{3... | collective-permute-start | bytes 3538952 | tf_op jit(solution)/shard_map/ppermute | solution.py:23
  73.2 36.1 %collective-permute-start.6 = (bf16[288,2048]{1,0:T(8,128)(2,1)}, bf16[288,2048]{1,0:T(8,128)(2,1)}, u32[]{:S(2)}, u32[]{:S(2)}) collective-permute-start(bf16[288,2048]{1,0:T(8,128)(2,1)} %get-tuple-element.38), channel_id=1, source_target_pairs={{0,384},{128,0},{256,128},{384,256},{1,385},{129,1},{257,129},{385... | collective-permute-start | bytes 3538952 | tf_op jit(solution)/shard_map/ppermute | solution.py:23
  82.9 20.6 %all-to-all-start.1 = ((bf16[8,16,4224]{2,1,0:T(8,128)(2,1)}), bf16[8,16,4224]{2,1,0:T(8,128)(2,1)}, u32[]{:S(2)}, u32[]{:S(2)}) async-start(bf16[8,16,4224]{2,1,0:T(8,128)(2,1)} %bitcast.7), calls=%async_computation.1 | async-start | bytes 2162688 | tf_op jit(solution)/shard_map/all_to_all | solution.py:143
  88.0 48.1 %collective-permute-start.8 = (bf16[128,4224]{1,0:T(8,128)(2,1)}, bf16[128,4224]{1,0:T(8,128)(2,1)}, u32[]{:S(2)}, u32[]{:S(2)}) collective-permute-start(bf16[128,4224]{1,0:T(8,128)(2,1)} %bitcast.3.refs_0_.refs_3_.refs_4_.refs_5_), channel_id=1, source_target_pairs={{0,128},{128,256},{256,384},{384,0},{1,129},{129,257},{257,385},{3... | collective-permute-start | bytes 3244040 | tf_op jit(solution)/shard_map/ppermute | solution.py:23
  91.5 48.5 %collective-permute-start.9 = (bf16[128,4224]{1,0:T(8,128)(2,1)}, bf16[128,4224]{1,0:T(8,128)(2,1)}, u32[]{:S(2)}, u32[]{:S(2)}) collective-permute-start(bf16[128,4224]{1,0:T(8,128)(2,1)} %bitcast.3.refs_0_.refs_3_.refs_4_.refs_5_), channel_id=1, source_target_pairs={{0,384},{128,0},{256,128},{384,256},{1,385},{129,1},{257,129},{385... | collective-permute-start | bytes 3244040 | tf_op jit(solution)/shard_map/ppermute | solution.py:23
  103.4 48.6 %collective-permute-start.10 = (bf16[128,4224]{1,0:T(8,128)(2,1)}, bf16[128,4224]{1,0:T(8,128)(2,1)}, u32[]{:S(2)}, u32[]{:S(2)}) collective-permute-start(bf16[128,4224]{1,0:T(8,128)(2,1)} %bitcast.8.refs_1_.refs_12_.refs_13_.refs_14_), channel_id=1, source_target_pairs={{0,128},{128,256},{256,384},{384,0},{1,129},{129,257},{257,385},{3... | collective-permute-start | bytes 3244040 | tf_op jit(solution)/shard_map/ppermute | solution.py:23
  107.0 51.1 %collective-permute-start.11 = (bf16[128,4224]{1,0:T(8,128)(2,1)}, bf16[128,4224]{1,0:T(8,128)(2,1)}, u32[]{:S(2)}, u32[]{:S(2)}) collective-permute-start(bf16[128,4224]{1,0:T(8,128)(2,1)} %bitcast.8.refs_1_.refs_12_.refs_13_.refs_14_), channel_id=1, source_target_pairs={{0,384},{128,0},{256,128},{384,256},{1,385},{129,1},{257,129},{385... | collective-permute-start | bytes 3244040 | tf_op jit(solution)/shard_map/ppermute | solution.py:23
  109.3 0.9 copy-start
  121.8 70.2 %all-to-all-start.2 = ((bf16[128,2,2176]{2,1,0:T(2,128)(2,1)}), bf16[128,2,2176]{2,1,0:T(2,128)(2,1)}, u32[]{:S(2)}, u32[]{:S(2)}) async-start(bf16[128,2,2176]{2,1,0:T(2,128)(2,1)} %reshape.267), calls=%async_computation.2 | async-start | bytes 2228224 | tf_op jit(solution)/shard_map/all_to_all | solution.py:346
  132.7 37.4 %collective-permute-start.7 = (bf16[576,256]{1,0:T(8,128)(2,1)}, bf16[576,256]{1,0:T(8,128)(2,1)}, u32[]{:S(2)}, u32[]{:S(2)}) collective-permute-start(bf16[576,256]{1,0:T(8,128)(2,1)} %get-tuple-element.40), channel_id=1, source_target_pairs={{0,256},{128,384},{256,0},{384,128},{1,257},{129,385},{257,1},{385... | collective-permute-start | bytes 884744 | tf_op jit(solution)/shard_map/ppermute | solution.py:23
  136.0 28.0 %collective-permute-start.14 = (bf16[576,256]{1,0:T(8,128)(2,1)}, bf16[576,256]{1,0:T(8,128)(2,1)}, u32[]{:S(2)}, u32[]{:S(2)}) collective-permute-start(bf16[576,256]{1,0:T(8,128)(2,1)} %get-tuple-element.44), channel_id=1, source_target_pairs={{0,128},{128,256},{256,384},{384,0},{1,129},{129,257},{257,385},{3... | collective-permute-start | bytes 884744 | tf_op jit(solution)/shard_map/ppermute | solution.py:23
  140.0 24.0 %collective-permute-start.15 = (bf16[576,256]{1,0:T(8,128)(2,1)}, bf16[576,256]{1,0:T(8,128)(2,1)}, u32[]{:S(2)}, u32[]{:S(2)}) collective-permute-start(bf16[576,256]{1,0:T(8,128)(2,1)} %get-tuple-element.45), channel_id=1, source_target_pairs={{0,384},{128,0},{256,128},{384,256},{1,385},{129,1},{257,129},{385... | collective-permute-start | bytes 884744 | tf_op jit(solution)/shard_map/ppermute | solution.py:23
  158.1 6.0 %copy-start.3 = (bf16[576,256]{1,0:T(8,128)(2,1)S(1)}, bf16[576,256]{1,0:T(8,128)(2,1)}, u32[]{:S(2)}) copy-start(bf16[576,256]{1,0:T(8,128)(2,1)} %get-tuple-element.43.refs_0_) | copy-start | bytes 884740
  158.1 26.7 %collective-permute-start.12 = (bf16[128,4224]{1,0:T(8,128)(2,1)}, bf16[128,4224]{1,0:T(8,128)(2,1)}, u32[]{:S(2)}, u32[]{:S(2)}) collective-permute-start(bf16[128,4224]{1,0:T(8,128)(2,1)} %get-tuple-element.41.refs_6_.refs_7_.refs_8_), channel_id=1, source_target_pairs={{0,128},{128,256},{256,384},{384,0},{1,129},{129,257},{257,385},{3... | collective-permute-start | bytes 3244040 | tf_op jit(solution)/shard_map/ppermute | solution.py:23
  160.1 27.8 %collective-permute-start.13 = (bf16[128,4224]{1,0:T(8,128)(2,1)}, bf16[128,4224]{1,0:T(8,128)(2,1)}, u32[]{:S(2)}, u32[]{:S(2)}) collective-permute-start(bf16[128,4224]{1,0:T(8,128)(2,1)} %get-tuple-element.42.refs_18_.refs_19_.refs_20_), channel_id=1, source_target_pairs={{0,384},{128,0},{256,128},{384,256},{1,385},{129,1},{257,129},{385... | collective-permute-start | bytes 3244040 | tf_op jit(solution)/shard_map/ppermute | solution.py:23
  192.0 1.5 copy-start.2
